TPU v7x, 32 devices: a whole 2x2x4 slice. The times are simulated.
32 devices in a mesh: row: 4 (over y, core), col: 8 (over z, x).
Axes of the slice: x: 2, y: 2, z: 4, core: 2. Of those that a mesh axis runs over, the one named last changes fastest.
Arguments:
- matrix_tiles: float32 [4, 32, 4, 256, 256], P('row', 'col'), as said below
- tile_rows: int32 [4, 32, 4], P('row', 'col'), may hold values from 0 to 7, as said below
- keep_rows: int32 [4, 32, 4], P('row', 'col'), may hold values from 0 to 7, as said below
- owners: int32 [4, 128, 1], P('row', 'col'), may hold values from 0 to 3; in each aligned block of 16 rows (0 to 15, 16 to 31, ..., all dimensions but the last counted through in order) at most 8 rows name the same one
Outputs:
- owned: float32 [4, 8, 32, 256, 256], P('row', 'col')
Inputs may be any that keep to these rules, and one draw needn't show every extreme that they name: `matrix_tiles`: every entry is positive. `tile_rows`: for each r and tile column j the 4 entries are distinct, and include j % 8 where j // 8 == r. `keep_rows`: for each r and tile column j the 4 entries are distinct, and include j % 8 where j // 8 == r. `owners`: among the 16 kept tiles of one row block and one column block, at most 8 go to the same owner.
All inputs are finite; a program needn't handle non-finite values.
Results may differ from a plain program's by a relative error of at most 0.000071.
Values sent between devices are 32-bit elements; how exact they have to be, the bound alone decides.
No kernel may reach another device: no remote copies, remote signals or barrier semaphores. Data moves between devices by JAX's collectives and lax.ppermute only.
A program may use at most 256 MiB of HBM per device.

v0:
```python
import jax
import jax.numpy as jnp
from jax import lax
from jax.sharding import PartitionSpec as P

TR = 8
KEEP = 4


def from_root(x, axis, root):
    mine = lax.axis_index(axis) == root
    return lax.psum(jnp.where(mine, x, jnp.zeros_like(x)), axis)


def section_product(running, a_panel, a_levels, b_panel, b_levels, section_index):
    columns = section_index * TR + b_levels
    chosen = jnp.take(a_panel, columns, axis=0)
    chosen_levels = jnp.take(a_levels, columns, axis=0)
    products = jnp.einsum("jzyab,jzbc->jzyac", chosen, b_panel, precision=lax.Precision.HIGHEST)
    selector = (chosen_levels[..., None] == jnp.arange(TR, dtype=jnp.int32)).astype(jnp.float32)
    return running + jnp.einsum(
        "jzyl,jzyac->ljac", selector, products, precision=lax.Precision.HIGHEST
    )


def on_device(matrix_tiles, tile_rows, keep_rows, owners):
    blocks = matrix_tiles.shape[1]
    width = matrix_tiles.shape[3]
    row_count = lax.axis_size("row")
    a_panel, a_levels = (
        lax.all_gather(matrix_tiles, "col", axis=1, tiled=True),
        lax.all_gather(tile_rows, "col", axis=1, tiled=True),
    )
    a_panel = a_panel[0]
    a_levels = a_levels[0]
    expanded = jnp.zeros((TR, blocks, width, width), jnp.float32)
    for section_index in range(row_count):
        b_panel, b_levels = (
            from_root(matrix_tiles[0], "row", section_index),
            from_root(tile_rows[0], "row", section_index),
        )
        expanded = section_product(expanded, a_panel, a_levels, b_panel, b_levels, section_index)
    kept = expanded[keep_rows[0], jnp.arange(blocks, dtype=jnp.int32)[:, None]]
    inflated = kept * kept
    flat = inflated.reshape(blocks * KEEP, width, width)
    column_ids = jnp.repeat(jnp.arange(blocks, dtype=jnp.int32), KEEP)
    most = blocks * KEEP // 2
    slots = row_count * most
    targets = owners[0, :, 0]
    items = targets.shape[0]
    order = jnp.arange(items, dtype=jnp.int32)
    earlier = jnp.sum(
        ((targets[None, :] == targets[:, None]) & (order[None, :] < order[:, None])).astype(
            jnp.int32
        ),
        axis=1,
    )
    slot_index = targets * most + earlier
    placing = slot_index[:, None] == jnp.arange(slots, dtype=jnp.int32)[None, :]
    outgoing = jnp.einsum(
        "fs,fab->sab", placing.astype(jnp.float32), flat, precision=lax.Precision.HIGHEST
    )
    outgoing_ids = jnp.sum(placing.astype(jnp.int32) * (column_ids[:, None] + 1), axis=0) - 1
    arrived, arrived_ids = (
        lax.all_to_all(outgoing, "row", split_axis=0, concat_axis=0, tiled=True),
        lax.all_to_all(outgoing_ids, "row", split_axis=0, concat_axis=0, tiled=True),
    )
    selector = (arrived_ids[:, None] == jnp.arange(blocks, dtype=jnp.int32)[None, :]).astype(
        jnp.float32
    )
    partial_sums = jnp.einsum("sj,sab->jb", selector, arrived, precision=lax.Precision.HIGHEST)
    totals = lax.psum(partial_sums, "row")
    denominators = jnp.einsum("sj,jb->sb", selector, totals, precision=lax.Precision.HIGHEST)
    present = arrived_ids >= 0
    safe_totals = jnp.where(present[:, None], denominators, 1.0)
    order_scale = float(row_count * TR * width)
    owned = order_scale * arrived / safe_totals[:, None, :]
    return owned[None, None]


def solution(mesh):
    placed = (
        P("row", "col", None, None, None),
        P("row", "col", None),
        P("row", "col", None),
        P("row", "col", None),
    )
    return jax.shard_map(
        on_device,
        mesh=mesh,
        in_specs=placed,
        out_specs=P("row", "col", None, None, None),
        check_vma=False,
    )
```

profile of v0, /device:TPU:0, one launch (start us, length us, event | category | flops | bytes accessed | tf_op | source)
XLA Modules:
  0.0 1088.5 jit_solution(15448127848709581992)
XLA Ops:
  7.4 0.0 all-gather.2.cloned.1.call-start
  7.4 0.7 all-gather.2.cloned.1.call-update
  8.1 0.0 all-reduce.4.cloned.1.call-start
  8.2 8.6 select_bitcast_fusion.3
  16.7 0.0 all-reduce.4.cloned.1.call-update
  16.8 0.1 add.95
  16.8 0.5 copy-done.5
  17.4 0.2 convert_reduce_fusion
  17.6 0.1 select_reduce_fusion
  17.7 0.7 sub.7
  18.3 4.2 all-to-all-start.1
  22.6 0.0 copy-done.3
  22.6 5.5 all-reduce
  28.1 0.1 reshape.208
  28.2 64.4 %all_gather.7 = s32[1,32,4]{2,0,1:T(1,128)S(1)} all-gather(s32[1,4,4]{2,0,1:T(1,128)S(1)} %bitcast.117), channel_id=1, replica_groups=mesh['row'=4,'col'=8] {'col'}, dimensions={1}, use_global_device_ids=true | all-gather | bytes 576 | tf_op jit(solution)/shard_map/all_gather | solution.py:32
  92.6 0.1 copy.59
  92.6 0.1 copy.60
  92.7 0.6 gather_fusion.4
  93.3 0.1 copy.93
  93.4 0.1 copy.66
  93.6 0.1 reshape.216
  93.6 0.6 gather_fusion.6
  94.2 0.1 copy.94
  94.3 0.1 copy.70
  94.5 0.1 reshape.200
  94.5 0.1 reshape.224
  94.6 0.6 gather_fusion.8
  95.2 0.1 copy.95
  95.3 0.1 copy.74
  95.4 0.6 gather_fusion.2
  96.0 0.1 copy.92
  96.1 0.1 copy.62
  96.2 0.0 copy-done.4
  96.3 0.1 reshape.176
  96.3 554.2 %all-gather.2.cloned.1.call-done = f32[1,32,4,256,256]{4,3,2,0,1:T(8,128)} async-done(((f32[1,4,4,256,256]{4,3,2,0,1:T(8,128)}), f32[1,32,4,256,256]{4,3,2,0,1:T(8,128)}) %all-gather.2.cloned.1.call-update) | async-done | bytes 33554448 | tf_op jit(solution)/shard_map/all_gather | solution.py:31
  650.5 12.1 %gather_fusion.3 = f32[16,4,256,256]{3,2,1,0:T(8,128)} fusion(f32[32,4,256,256]{3,2,1,0:T(8,128)} %bitcast.103, s32[1024]{0:T(1024)S(1)} %pad_clamp_fusion.2), kind=kCustom, calls=%fused_computation.2.clone | custom fusion | bytes 33554496 | tf_op jit(solution)/shard_map/jit(_take)/gather | solution.py:17
  662.7 12.2 %gather_fusion.5 = f32[16,4,256,256]{3,2,1,0:T(8,128)} fusion(f32[32,4,256,256]{3,2,1,0:T(8,128)} %bitcast.104, s32[1024]{0:T(1024)S(1)} %pad_clamp_fusion.1), kind=kCustom, calls=%fused_computation.3.clone | custom fusion | bytes 33554496 | tf_op jit(solution)/shard_map/jit(_take)/gather | solution.py:17
  674.9 12.4 %gather_fusion.1 = f32[16,4,256,256]{3,2,1,0:T(8,128)} fusion(f32[32,4,256,256]{3,2,1,0:T(8,128)} %bitcast.105, s32[1024]{0:T(1024)S(1)} %pad_clamp_fusion.3), kind=kCustom, calls=%fused_computation.clone | custom fusion | bytes 33554496 | tf_op jit(solution)/shard_map/jit(_take)/gather | solution.py:17
  687.3 11.9 %gather_fusion.7 = f32[16,4,256,256]{3,2,1,0:T(8,128)} fusion(f32[32,4,256,256]{3,2,1,0:T(8,128)} %bitcast.106, s32[1024]{0:T(1024)S(1)} %pad_clamp_fusion), kind=kCustom, calls=%fused_computation.4.clone | custom fusion | bytes 33554496 | tf_op jit(solution)/shard_map/jit(_take)/gather | solution.py:17
  699.2 23.2 %fusion.12 = f32[4,4,4,256,256]{4,3,2,1,0:T(8,128)} fusion(f32[4,4,4,256,256]{4,3,2,1,0:T(8,128)} %bitcast.110, pred[4,4]{1,0:T(4,128)(4,1)S(1)} %get-tuple-element.29, f32[4,4,256,256]{3,2,1,0:T(8,128)} %get-tuple-element.13), kind=kOutput, calls=%fused_computation.21 | convolution fusion | flops 12889096192 | bytes 37748752 | tf_op jit(solution)/shard_map/jzyab,jzbc->jzyac/dot_general | solution.py:19
  722.4 34.3 %fusion.4 = f32[4,256,256,8,1]{2,3,4,1,0:T(8,128)} fusion(f32[4,4,4,256,256]{4,3,2,1,0:T(8,128)} %fusion.12, s32[4,4,4]{2,1,0:T(4,128)S(1)} %copy.66), kind=kOutput, calls=%fused_computation.13 | convolution fusion | flops 402653696 | bytes 25166080 | tf_op jit(solution)/shard_map/jzyl,jzyac->ljac/dot_general | solution.py:21
  756.6 0.0 copy-done.2
  756.6 21.8 %fusion.10 = f32[4,4,4,256,256]{4,3,2,1,0:T(8,128)} fusion(f32[4,4,4,256,256]{4,3,2,1,0:T(8,128)} %bitcast.109, pred[4,4]{1,0:T(4,128)(4,1)S(1)} %get-tuple-element.28, f32[4,4,256,256]{3,2,1,0:T(8,128)S(1)} %copy-done.2), kind=kOutput, calls=%fused_computation.19 | convolution fusion | flops 12889096192 | bytes 37748752 | tf_op jit(solution)/shard_map/jzyab,jzbc->jzyac/dot_general | solution.py:19
  778.5 33.9 %fusion.2 = f32[4,256,256,8,1]{2,3,4,1,0:T(8,128)} fusion(f32[4,4,4,256,256]{4,3,2,1,0:T(8,128)} %fusion.10, s32[4,4,4]{2,1,0:T(4,128)S(1)} %copy.70), kind=kOutput, calls=%fused_computation.11 | convolution fusion | flops 402653696 | bytes 25166080 | tf_op jit(solution)/shard_map/jzyl,jzyac->ljac/dot_general | solution.py:21
  812.3 23.3 %fusion.14 = f32[4,4,4,256,256]{4,3,2,1,0:T(8,128)} fusion(f32[4,4,4,256,256]{4,3,2,1,0:T(8,128)} %bitcast.108, pred[4,4]{1,0:T(4,128)(4,1)S(1)} %get-tuple-element.30, f32[4,4,256,256]{3,2,1,0:T(8,128)} %get-tuple-element.14), kind=kOutput, calls=%fused_computation.23 | convolution fusion | flops 12889096192 | bytes 37748752 | tf_op jit(solution)/shard_map/jzyab,jzbc->jzyac/dot_general | solution.py:19
  835.7 21.8 %fusion.8 = f32[4,4,4,256,256]{4,3,2,1,0:T(8,128)} fusion(f32[4,4,4,256,256]{4,3,2,1,0:T(8,128)} %bitcast.107, pred[4,4]{1,0:T(4,128)(4,1)S(1)} %get-tuple-element.27, f32[4,4,256,256]{3,2,1,0:T(8,128)S(1)} %copy-done.1), kind=kOutput, calls=%fused_computation.17 | convolution fusion | flops 12889096192 | bytes 37748752 | tf_op jit(solution)/shard_map/jzyab,jzbc->jzyac/dot_general | solution.py:19
  857.5 33.9 %fusion = f32[4,256,256,8,1]{2,3,4,1,0:T(8,128)} fusion(f32[4,4,4,256,256]{4,3,2,1,0:T(8,128)} %fusion.8, s32[4,4,4]{2,1,0:T(4,128)S(1)} %copy.74), kind=kOutput, calls=%fused_computation.9 | convolution fusion | flops 402653696 | bytes 25166080 | tf_op jit(solution)/shard_map/jzyl,jzyac->ljac/dot_general | solution.py:21
  891.4 38.8 %fusion.16 = f32[8,4,256,256]{3,0,2,1:T(8,128)} fusion(f32[4,256,256,8,1]{2,3,4,1,0:T(8,128)} %fusion, f32[4,256,256,8,1]{2,3,4,1,0:T(8,128)S(1)} %copy-done, f32[4,256,256,8,1]{2,3,4,1,0:T(8,128)} %fusion.4, f32[4,4,4,256,256]{4,3,2,1,0:T(8,128)} %fusion.14, s32[4,4,4]{2,1,0:T(4,128)S(1)} %copy.62), kind=kOutput, calls=%fused_computation.26 | convolution fusion | flops 408945152 | bytes 50331904 | tf_op jit(solution)/shard_map/jzyl,jzyac->ljac/dot_general | solution.py:21
  930.2 9.3 copy.76
  939.5 6.2 gather_fusion
  945.7 4.0 mul.35
  949.7 5.7 fusion.29
  955.5 8.4 copy.78
  963.9 0.0 all-to-all-done.1
  963.9 5.6 all-to-all-start
  969.5 0.6 broadcast.286
  970.1 0.7 reduce.3
  970.8 0.1 all_to_all.11
  970.9 91.8 %all-to-all-done = f32[32,256,256]{2,1,0:T(8,128)} async-done(((f32[32,256,256]{2,1,0:T(8,128)}), f32[32,256,256]{2,1,0:T(8,128)}, u32[]{:S(2)}, u32[]{:S(2)}) %all-to-all-start) | async-done | bytes 8388640 | tf_op jit(solution)/shard_map/all_to_all | solution.py:65
  1062.7 4.0 reduce_sum.29
  1066.7 0.3 fusion.41
  1066.9 5.7 psum.71
  1072.7 0.2 convolution_select_fusion
  1072.9 8.0 divide_bitcast_fusion
  (27 shorter events, 0.1 us)
Async XLA Ops:
  7.4 643.2 %all-gather.2.cloned.1.call-start = ((), (), s32[]{:S(2)}) async-start(), calls=%async_computation.2 | async-start | bytes 37748736 | tf_op jit(solution)/shard_map/all_gather | solution.py:31
  8.1 691.1 %all-reduce.4.cloned.1.call-start = ((), (), s32[]{:S(2)}) async-start(), calls=%async_computation.3 | async-start | bytes 33554432 | tf_op jit(solution)/shard_map/psum | solution.py:12
  16.7 0.7 copy-start.5
  16.7 5.9 copy-start.3
  16.7 79.5 %copy-start.4 = (s32[1,4,4]{2,1,0:T(4,128)S(1)}, s32[1,4,4]{2,1,0:T(4,128)}, u32[]{:S(2)}) copy-start(s32[1,4,4]{2,1,0:T(4,128)} %param.10) | copy-start | bytes 196
  18.3 945.6 %all-to-all-start.1 = ((s32[4,8,1]{1,2,0:T(1,128)}), s32[4,8,1]{1,2,0:T(1,128)S(1)}, u32[]{:S(2)}, u32[]{:S(2)}) async-start(s32[4,8,1]{1,2,0:T(1,128)} %bitcast.48), calls=%async_computation.1 | async-start | bytes 4096 | tf_op jit(solution)/shard_map/all_to_all | solution.py:66
  722.4 34.3 %copy-start.2 = (f32[4,4,256,256]{3,2,1,0:T(8,128)S(1)}, f32[4,4,256,256]{3,2,1,0:T(8,128)}, u32[]{:S(2)}) copy-start(f32[4,4,256,256]{3,2,1,0:T(8,128)} %get-tuple-element.12) | copy-start | bytes 12582916
  812.3 23.4 %copy-start.1 = (f32[4,4,256,256]{3,2,1,0:T(8,128)S(1)}, f32[4,4,256,256]{3,2,1,0:T(8,128)}, u32[]{:S(2)}) copy-start(f32[4,4,256,256]{3,2,1,0:T(8,128)} %get-tuple-element.11) | copy-start | bytes 12582916
  857.5 33.9 %copy-start = (f32[4,256,256,8,1]{2,3,4,1,0:T(8,128)S(1)}, f32[4,256,256,8,1]{2,3,4,1,0:T(8,128)}, u32[]{:S(2)}) copy-start(f32[4,256,256,8,1]{2,3,4,1,0:T(8,128)} %fusion.2) | copy-start | bytes 25165828
  963.9 98.8 %all-to-all-start = ((f32[32,256,256]{2,1,0:T(8,128)}), f32[32,256,256]{2,1,0:T(8,128)}, u32[]{:S(2)}, u32[]{:S(2)}) async-start(f32[32,256,256]{2,1,0:T(8,128)} %copy.78), calls=%async_computation | async-start | bytes 16777216 | tf_op jit(solution)/shard_map/all_to_all | solution.py:65
Sparse Core Ops, SparseCore 0:
  9.7 640.7 all-gather.1
Sparse Core Ops, SparseCore 1:
  16.8 292.5 all-reduce.3
where the time goes:
time: 1100 us; the launch traced here: 1090 us
  waiting for transfers between devices  647 us (59%)
  matrix products  237 us (22%)
  local copies, waits for them, and re-layouts  78.3 us (7%)
  blocking collectives  75.6 us (7%)
  other arithmetic  25.7 us (2%)
  between operations  15.2 us (1%)
    all_gather x1, waiting for transfers between devices, on_device(): lax.all_gather(matrix_tiles, 'col', axis=1, tiled=True)  554 us
    dot_general x4, matrix products, section_product(): jnp.einsum('jzyl,jzyac->ljac', selector, products, precision=lax.Precisio...  141 us
    all_to_all x1, waiting for transfers between devices, on_device(): lax.all_to_all(outgoing, 'row', split_axis=0, concat_axis=0, tiled=True)  91.8 us
    dot_general x4, matrix products, section_product(): jnp.einsum('jzyab,jzbc->jzyac', chosen, b_panel, precision=lax.Precision....  90.1 us
    all_gather x1, blocking collectives, on_device(): lax.all_gather(tile_rows, 'col', axis=1, tiled=True)  64.4 us
    gather x4, local copies, waits for them, and re-layouts, section_product(): chosen = jnp.take(a_panel, columns, axis=0)  48.6 us
  transfers between devices with their start and end apart: 4, of which 2 were waited for; matrix products, arithmetic and copies ran while one was open for 30% of the time, Pallas kernels for 0%

commit v1 on v0

v1 whole, which is shorter than its diff:
```python
import functools

import jax
import jax.numpy as jnp
from jax import lax
from jax.experimental import pallas as pl
from jax.experimental.pallas import tpu as pltpu
from jax.sharding import PartitionSpec as P

TR = 8
CHUNKS = (64, 64, 64, 32, 32)
VMEM = 56 * 1024 * 1024


def split(x):
    high = x.astype(jnp.bfloat16)
    low = (x - high.astype(jnp.float32)).astype(jnp.bfloat16)
    return high, low


def place_kernel(x_ref, *refs):
    o_ref = refs[-1]
    for z in range(x_ref.shape[1]):
        high, low = split(x_ref[0, z])
        o_ref[0, 0, 0, z, 0] = high
        o_ref[0, 0, 0, z, 1] = low


def place(x, buffer, group, relative):
    blocks, count, width = x.shape[0], x.shape[1], x.shape[2]
    out = jax.ShapeDtypeStruct((2, blocks, 4, count, 2, width, width), jnp.bfloat16)
    in_specs = [pl.BlockSpec((1, count, width, width), lambda j: (j, 0, 0, 0))]
    args = [x]
    aliases = {}
    if buffer is not None:
        in_specs.append(pl.BlockSpec(memory_space=pl.ANY))
        args.append(buffer)
        aliases = {1: 0}
    return pl.pallas_call(
        place_kernel,
        grid=(blocks,),
        out_shape=out,
        in_specs=in_specs,
        out_specs=pl.BlockSpec(
            (1, 1, 1, count, 2, width, width),
            lambda j: (group, j, relative, 0, 0, 0, 0),
        ),
        input_output_aliases=aliases,
        compiler_params=pltpu.CompilerParams(vmem_limit_bytes=VMEM),
        cost_estimate=pl.CostEstimate(flops=x.size, bytes_accessed=8 * x.size, transcendentals=0),
        name="place",
    )(*args)


def product_kernel(line, columns, me_ref, meta_ref, b_ref, *refs):
    parts = 2 * line - 1
    a_refs = refs[:parts]
    other_ref, own_ref, raw, halves, total, sems = refs[parts:]
    group, j = pl.program_id(0), pl.program_id(1)
    blocks, count, rows, width = a_refs[0].shape
    record = 3 * blocks * count
    r, c = me_ref[0], me_ref[1]
    q, p = c // 2, c % 2

    def base(rr, cc):
        return (rr * columns + cc) * record

    @pl.when((group == 0) & (j == 0))
    def _():
        def each(act):
            for i in range(parts):
                at = q + i - (line - 1)

                @pl.when((at >= 0) & (at < line))
                def _():
                    act(pltpu.make_async_copy(a_refs[i], raw.at[at], sems.at[i]))

        each(lambda copy: copy.start())
        each(lambda copy: copy.wait())

        def convert(i, _):
            for y in range(count):
                high, low = split(raw[i // blocks, i % blocks, y])
                halves[i, y * rows : (y + 1) * rows, 0:width] = high
                halves[i, y * rows : (y + 1) * rows, width : 2 * width] = low
            return 0

        lax.fori_loop(0, line * blocks, convert, 0)

    total[...] = jnp.zeros_like(total)
    target = jnp.where(group == 0, c + 1 - 2 * p, c)

    def step(t, _):
        rr = jnp.bitwise_xor(r, t // count)
        k = rr * TR + meta_ref[base(rr, target) + j * count + t % count]
        ck = k // blocks

        @pl.when(ck % 2 == p)
        def _():
            kk = k % blocks
            at = (ck // 2) * blocks + kk
            high = halves[at, :, 0:width]
            both = halves[at]
            b_high = b_ref[0, 0, t // count, t % count, 0]
            b_low = b_ref[0, 0, t // count, t % count, 1]
            product = jnp.dot(
                jnp.concatenate([both, high], axis=1),
                jnp.concatenate([b_high, b_high, b_low], axis=0),
                preferred_element_type=jnp.float32,
            )
            levels = base(r, ck) + kk * count
            for y in range(count):
                total[meta_ref[levels + y]] += product[y * rows : (y + 1) * rows]

        return 0

    lax.fori_loop(0, 4 * count, step, 0)
    keeps = base(r, target) + blocks * count + j * count

    @pl.when(group == 0)
    def _():
        for m in range(count):
            other_ref[0, m] = total[meta_ref[keeps + m]]

    @pl.when(group == 1)
    def _():
        for m in range(count):
            own_ref[0, m] = total[meta_ref[keeps + m]]


def product(me, meta, panel, parts, line, columns):
    blocks, count, rows, width = parts[0].shape
    out = jax.ShapeDtypeStruct((blocks, count, rows, width), jnp.float32)
    smem = pl.BlockSpec(memory_space=pltpu.SMEM)
    return pl.pallas_call(
        functools.partial(product_kernel, line, columns),
        grid=(2, blocks),
        out_shape=(out, out),
        in_specs=[
            smem,
            smem,
            pl.BlockSpec(
                (1, 1, 4, count, 2, width, width), lambda g, j: (g, j, 0, 0, 0, 0, 0)
            ),
        ]
        + [pl.BlockSpec(memory_space=pl.ANY)] * len(parts),
        out_specs=(
            pl.BlockSpec(
                (1, count, rows, width), lambda g, j: (jnp.where(g == 0, j, blocks - 1), 0, 0, 0)
            ),
            pl.BlockSpec((1, count, rows, width), lambda g, j: (jnp.where(g == 0, 0, j), 0, 0, 0)),
        ),
        scratch_shapes=[
            pltpu.VMEM((line, blocks, count, rows, width), jnp.float32),
            pltpu.VMEM((line * blocks, count * rows, 2 * width), jnp.bfloat16),
            pltpu.VMEM((TR, rows, width), jnp.float32),
            pltpu.SemaphoreType.DMA((len(parts),)),
        ],
        compiler_params=pltpu.CompilerParams(vmem_limit_bytes=VMEM),
        cost_estimate=pl.CostEstimate(
            flops=3 * 2 * 16 * blocks * count * rows * width * width,
            bytes_accessed=2 * panel.size,
            transcendentals=0,
        ),
        name="product",
    )(me, meta, panel, *parts)


def owned_kernel(columns, sizes, scale, me_ref, meta_ref, sums_ref, *refs):
    chunks = len(sizes)
    sources = refs[: 4 * chunks]
    out_ref, slots, whose, in_sems, out_sems = refs[4 * chunks :]
    blocks, count = sources[0].shape[:2]
    items = blocks * count
    most = items // 2
    record = 3 * items
    r, c = me_ref[0], me_ref[1]
    starts = [sum(sizes[:h]) for h in range(chunks)]

    for s in range(4 * most):
        whose[s] = -1
    for relative in range(4):
        rr = jnp.bitwise_xor(r, relative)

        def place_item(f, n, relative=relative, rr=rr):
            mine = meta_ref[(rr * columns + c) * record + 2 * items + f] == r

            @pl.when(mine)
            def _():
                slot = rr * most + n
                whose[slot] = f // count
                for h in range(chunks):
                    pltpu.make_async_copy(
                        sources[4 * h + relative].at[f // count, f % count],
                        slots.at[slot, pl.ds(starts[h], sizes[h])],
                        in_sems.at[slot],
                    ).start()

            return n + mine.astype(jnp.int32)

        lax.fori_loop(0, items, place_item, jnp.int32(0))

    factors = scale / sums_ref[...]

    def finish(s, _):
        j = whose[s]

        @pl.when(j < 0)
        def _():
            slots[s] = jnp.zeros(slots.shape[1:], jnp.float32)

        for jj in range(blocks):

            @pl.when(j == jj)
            def _():
                pltpu.make_async_copy(slots.at[s], slots.at[s], in_sems.at[s]).wait()
                slots[s] = slots[s] * factors[jj : jj + 1]

        pltpu.make_async_copy(slots.at[s], out_ref.at[s], out_sems.at[s]).start()
        return 0

    lax.fori_loop(0, 4 * most, finish, 0)

    def drain(s, _):
        pltpu.make_async_copy(slots.at[s], out_ref.at[s], out_sems.at[s]).wait()
        return 0

    lax.fori_loop(0, 4 * most, drain, 0)


def owned_tiles(me, meta, sums, sources, columns, sizes, scale):
    blocks, count, _, width = sources[0].shape
    most = blocks * count // 2
    smem = pl.BlockSpec(memory_space=pltpu.SMEM)
    return pl.pallas_call(
        functools.partial(owned_kernel, columns, sizes, scale),
        out_shape=jax.ShapeDtypeStruct((4 * most, width, width), jnp.float32),
        in_specs=[smem, smem, pl.BlockSpec(memory_space=pltpu.VMEM)]
        + [pl.BlockSpec(memory_space=pl.ANY)] * len(sources),
        out_specs=pl.BlockSpec(memory_space=pl.ANY),
        scratch_shapes=[
            pltpu.VMEM((4 * most, width, width), jnp.float32),
            pltpu.SMEM((4 * most,), jnp.int32),
            pltpu.SemaphoreType.DMA((4 * most,)),
            pltpu.SemaphoreType.DMA((4 * most,)),
        ],
        compiler_params=pltpu.CompilerParams(vmem_limit_bytes=VMEM),
        cost_estimate=pl.CostEstimate(
            flops=4 * most * width * width,
            bytes_accessed=32 * most * width * width,
            transcendentals=0,
        ),
        name="owned",
    )(me, meta, sums, *sources)


def on_device(columns, matrix_tiles, tile_rows, keep_rows, owners):
    tiles = matrix_tiles[0]
    blocks, count, width = tiles.shape[0], tiles.shape[1], tiles.shape[2]
    line = columns // 2
    r, c = lax.axis_index("row"), lax.axis_index("col")
    me = jnp.stack([r, c]).astype(jnp.int32)

    core = functools.partial(lax.ppermute, axis_name="row", perm=[(i, i ^ 1) for i in range(4)])
    across = functools.partial(lax.ppermute, axis_name="row", perm=[(i, i ^ 2) for i in range(4)])
    pair = functools.partial(
        lax.ppermute, axis_name="col", perm=[(i, i ^ 1) for i in range(columns)]
    )

    def up(x, hop):
        return lax.ppermute(x, "col", [(i, i + 2) for i in range(2 * hop, columns - 2)])

    def down(x, hop):
        return lax.ppermute(x, "col", [(i + 2, i) for i in range(0, columns - 2 - 2 * hop)])

    sizes = tuple(size * width // sum(CHUNKS) for size in CHUNKS)
    starts = [sum(sizes[:h]) for h in range(len(sizes))]

    def gather(h):
        own = tiles[:, :, starts[h] : starts[h] + sizes[h]]
        below, above = [], []
        rising = falling = own
        for hop in range(line - 1):
            rising, falling = up(rising, hop), down(falling, hop)
            below.append(rising)
            above.append(falling)
        return below[::-1] + [own] + above

    mine = jnp.concatenate(
        [tile_rows.reshape(-1), keep_rows.reshape(-1), owners.reshape(-1)]
    )
    meta = lax.all_gather(mine, ("row", "col"), axis=0, tiled=True)

    gathered = [gather(h) for h in range(len(sizes))]

    half = width // 2
    b_pair, b_across = pair(tiles), across(tiles)
    b_diagonal = jnp.concatenate(
        [across(b_pair[:, :, :half]), pair(b_across[:, :, half:])], axis=2
    )
    shards = [
        (tiles, 1, 0),
        (core(tiles), 1, 1),
        (b_pair, 0, 0),
        (b_across, 1, 2),
        (core(b_pair), 0, 1),
        (core(b_across), 1, 3),
        (b_diagonal, 0, 2),
        (core(b_diagonal), 0, 3),
    ]
    panel = None
    for shard, group, relative in shards:
        panel = place(shard, panel, group, relative)

    sums = jnp.zeros((blocks, width), jnp.float32)
    sources = []
    for h in range(len(sizes)):
        other, own = product(me, meta, panel, gathered[h], line, columns)
        kept = own + pair(other)
        inflated = kept * kept
        opposite = across(inflated)
        four = [inflated, core(inflated), opposite, core(opposite)]
        sources += four
        sums = sums + sum(jnp.sum(x, axis=(1, 2)) for x in four)
    scale = float(4 * TR * width)
    owned = owned_tiles(me, meta, sums, sources, columns, sizes, scale)
    return owned[None, None]


def solution(mesh):
    placed = (
        P("row", "col", None, None, None),
        P("row", "col", None),
        P("row", "col", None),
        P("row", "col", None),
    )
    return jax.shard_map(
        functools.partial(on_device, mesh.shape["col"]),
        mesh=mesh,
        in_specs=placed,
        out_specs=P("row", "col", None, None, None),
        check_vma=False,
    )
```

time: 1100 us -> 643 us (0.58)
  waiting for transfers between devices: 647 us -> 264 us
  matrix products: 237 us -> 0 us
  Pallas kernels: 0 us -> 176 us
  starting transfers between devices: 9.92 us -> 82.4 us
  local copies, waits for them, and re-layouts: 78.3 us -> 13.3 us
  between operations: 15.2 us -> 1.25 us
    all_gather x1 -> x0, waiting for transfers between devices: 554 us -> none  [on_device(): lax.all_gather(matrix_tiles, 'col', axis=1, tiled=True)]
    ppermute x0 -> x58, waiting for transfers between devices: none -> 264 us  [the longest x15 121 us: down(): lax.ppermute(x, 'col', [(i + 2, i) for i in range(0, columns - 2 - 2 * ho...]
    dot_general x11 -> x0, matrix products: 237 us -> none  [the longest x4 141 us: section_product(): jnp.einsum('jzyl,jzyac->ljac', selector, products, precision=lax.Precisio...]
    pallas_call x0 -> x14, Pallas kernels: none -> 176 us  [the longest x5 131 us: product(): pl.pallas_call(functools.partial(product_kernel, line, columns), grid=(2,...]
    all_to_all x2 -> x0, waiting for transfers between devices: 91.8 us -> none  [the longest x1 91.8 us: on_device(): lax.all_to_all(outgoing, 'row', split_axis=0, concat_axis=0, tiled=True)]
    ppermute x0 -> x58, starting transfers between devices: none -> 82.4 us  [the longest x15 32.8 us: up(): lax.ppermute(x, 'col', [(i, i + 2) for i in range(2 * hop, columns - 2)])]
    unnamed x0 -> x1, blocking collectives: none -> 81.9 us
    all_gather x1 -> x0, blocking collectives: 64.4 us -> none  [on_device(): lax.all_gather(tile_rows, 'col', axis=1, tiled=True)]
  transfers between devices with their start and end apart: 4 -> 58, of which waited for: 2 -> 16; matrix products, arithmetic and copies ran while one was open for 30% -> 4% of each run, Pallas kernels for 0% -> 27%
where the time goes in v1:
time: 643 us; the launch traced here: 641 us
  waiting for transfers between devices  264 us (41%)
  Pallas kernels  176 us (27%)
  starting transfers between devices  82.4 us (13%)
  blocking collectives  81.9 us (13%)
  other arithmetic  21.4 us (3%)
  local copies, waits for them, and re-layouts  13.3 us (2%)
    pallas_call x5, Pallas kernels, product(): pl.pallas_call(functools.partial(product_kernel, line, columns), grid=(2,...  131 us
    ppermute x15, waiting for transfers between devices, down(): lax.ppermute(x, 'col', [(i + 2, i) for i in range(0, columns - 2 - 2 * ho...  121 us
    unnamed x1, blocking collectives  81.9 us
    ppermute x5, waiting for transfers between devices, on_device(): opposite = across(inflated)  62.1 us
    ppermute x2, waiting for transfers between devices, on_device(): b_pair, b_across = (pair(tiles), across(tiles))  54.7 us
    pallas_call x8, Pallas kernels, place(): pl.pallas_call(place_kernel, grid=(blocks,), out_shape=out, in_specs=in_s...  39.4 us
    ppermute x15, starting transfers between devices, up(): lax.ppermute(x, 'col', [(i, i + 2) for i in range(2 * hop, columns - 2)])  32.8 us
    reduce_sum x20, other arithmetic, on_device(): sums = sums + sum((jnp.sum(x, axis=(1, 2)) for x in four))  19.9 us
  transfers between devices with their start and end apart: 58, of which 16 were waited for; matrix products, arithmetic and copies ran while one was open for 4% of the time, Pallas kernels for 27%

profile of v1, /device:TPU:0, one launch (start us, length us, event | category | flops | bytes accessed | tf_op | source)
XLA Modules:
  0.0 640.7 jit_solution(15802838054530529291)
XLA Ops:
  0.0 2.9 collective-permute-start
  2.9 1.5 collective-permute-start.2
  4.5 1.3 fusion.6
  5.8 3.5 collective-permute-start.38
  9.3 1.3 collective-permute-start.41
  10.6 4.6 collective-permute-start.48
  15.2 6.4 %collective-permute-done.38.refs_2_ = f32[4,4,32,256]{3,2,1,0:T(8,128)S(1)} collective-permute-done((f32[4,4,32,256]{3,2,1,0:T(8,128)S(1)}, f32[4,4,32,256]{3,2,1,0:T(8,128)S(1)}, u32[]{:S(2)}, u32[]{:S(2)}) %collective-permute-start.38) | collective-permute-done | bytes 524320 | tf_op jit(solution)/shard_map/ppermute | solution.py:271
  22.9 2.2 fusion.5
  25.2 5.1 collective-permute-start.8
  30.3 2.6 collective-permute-done.48.refs_2_
  34.2 1.5 collective-permute-done.51.refs_4_
  35.7 3.6 collective-permute-start.18
  39.3 54.4 %collective-permute-done.x_ref = f32[4,4,256,256]{3,2,1,0:T(8,128)S(1)} collective-permute-done((f32[4,4,256,256]{3,2,1,0:T(8,128)}, f32[4,4,256,256]{3,2,1,0:T(8,128)S(1)}, u32[]{:S(2)}, u32[]{:S(2)}) %collective-permute-start) | collective-permute-done | bytes 4194336 | tf_op jit(solution)/shard_map/ppermute | solution.py:297
  95.3 5.5 collective-permute-start.28
  101.0 1.8 slice.29
  102.9 1.8 collective-permute-start.1
  104.8 1.5 collective-permute-start.3
  107.6 14.1 %collective-permute-done.21.refs_4_ = f32[4,4,64,256]{3,2,1,0:T(8,128)S(1)} collective-permute-done((f32[4,4,64,256]{3,2,1,0:T(8,128)S(1)}, f32[4,4,64,256]{3,2,1,0:T(8,128)S(1)}, u32[]{:S(2)}, u32[]{:S(2)}) %collective-permute-start.21) | collective-permute-done | bytes 1048608 | tf_op jit(solution)/shard_map/ppermute | solution.py:274
  123.7 20.6 %collective-permute-done.31.refs_4_ = f32[4,4,64,256]{3,2,1,0:T(8,128)} collective-permute-done((f32[4,4,64,256]{3,2,1,0:T(8,128)S(1)}, f32[4,4,64,256]{3,2,1,0:T(8,128)}, u32[]{:S(2)}, u32[]{:S(2)}) %collective-permute-start.31) | collective-permute-done | bytes 1048608 | tf_op jit(solution)/shard_map/ppermute | solution.py:274
  145.7 8.1 %collective-permute-done.42.refs_5_ = f32[4,4,32,256]{3,2,1,0:T(8,128)S(1)} collective-permute-done((f32[4,4,32,256]{3,2,1,0:T(8,128)S(1)}, f32[4,4,32,256]{3,2,1,0:T(8,128)S(1)}, u32[]{:S(2)}, u32[]{:S(2)}) %collective-permute-start.42) | collective-permute-done | bytes 524320 | tf_op jit(solution)/shard_map/ppermute | solution.py:274
  157.8 1.5 constant_dynamic-update-slice_fusion.1
  159.2 1.5 constant_dynamic-update-slice_fusion.x_ref
  160.8 30.5 %collective-permute-done.43.refs_6_ = f32[4,4,32,256]{3,2,1,0:T(8,128)S(1)} collective-permute-done((f32[4,4,32,256]{3,2,1,0:T(8,128)S(1)}, f32[4,4,32,256]{3,2,1,0:T(8,128)S(1)}, u32[]{:S(2)}, u32[]{:S(2)}) %collective-permute-start.43) | collective-permute-done | bytes 524320 | tf_op jit(solution)/shard_map/ppermute | solution.py:274
  191.8 1.7 collective-permute-start.19
  194.7 46.4 %collective-permute-done.22.refs_5_ = f32[4,4,64,256]{3,2,1,0:T(8,128)} collective-permute-done((f32[4,4,64,256]{3,2,1,0:T(8,128)S(1)}, f32[4,4,64,256]{3,2,1,0:T(8,128)}, u32[]{:S(2)}, u32[]{:S(2)}) %collective-permute-start.22) | collective-permute-done | bytes 1048608 | tf_op jit(solution)/shard_map/ppermute | solution.py:274
  243.2 2.1 collective-permute-start.29
  245.3 2.1 copy-done.2
  248.9 1.6 collective-permute-start.20
  252.0 4.9 place.8.refs_0_
  256.9 81.9 %all-reduce.meta_ref = s32[1536]{0:T(1024)} all-reduce(s32[1536]{0:T(1024)S(1)} %add_dynamic-update-slice_fusion), channel_id=1, replica_groups=mesh['row'=4,'col'=8] {'row','col'}, use_global_device_ids=true, to_apply=%add | all-reduce | flops 1536 | bytes 12288
  339.5 4.9 place.9.refs_0_
  344.4 4.9 place.10.refs_0_
  349.3 4.9 place.11.refs_0_
  354.2 4.9 place.12.refs_0_
  359.0 5.0 place.13.refs_0_
  364.0 4.9 place.14.refs_0_
  369.0 5.1 place.15.b_ref
  375.3 27.6 %product.5 = (f32[4,4,64,256]{3,2,1,0:T(8,128)}, f32[4,4,64,256]{3,2,1,0:T(8,128)}) custom-call(s32[2]{0:T(128)} %pad_add_fusion.me_ref, s32[1536]{0:T(1024)} %all-reduce.meta_ref, bf16[2,4,4,4,2,256,256]{6,5,4,3,2,1,0:T(8,128)(2,1)} %place.15.b_ref, f32[4,4,64,256]{3,2,1,0:T(8,128)} %copy-done.27, f32[4,4,64,256]{3,2,1,0:T(8,128)} %copy-done.26, ...), custom_call_target="tpu_custom_call" | custom-call | flops 6442450944 | bytes 33554432 | tf_op jit(solution)/shard_map/product/pallas_call | solution.py:135
  405.1 24.0 %product.8 = (f32[4,4,32,256]{3,2,1,0:T(8,128)}, f32[4,4,32,256]{3,2,1,0:T(8,128)}) custom-call(s32[2]{0:T(128)} %pad_add_fusion.me_ref, s32[1536]{0:T(1024)} %all-reduce.meta_ref, bf16[2,4,4,4,2,256,256]{6,5,4,3,2,1,0:T(8,128)(2,1)} %place.15.b_ref, f32[4,4,32,256]{3,2,1,0:T(8,128)} %copy-done.43, f32[4,4,32,256]{3,2,1,0:T(8,128)} %copy-done.41, ...), custom_call_target="tpu_custom_call" | custom-call | flops 3221225472 | bytes 33554432 | tf_op jit(solution)/shard_map/product/pallas_call | solution.py:135
  429.8 1.5 collective-permute-start.53
  431.3 5.9 collective-permute-start.14
  437.2 27.6 %product.6 = (f32[4,4,64,256]{3,2,1,0:T(8,128)}, f32[4,4,64,256]{3,2,1,0:T(8,128)}) custom-call(s32[2]{0:T(128)} %pad_add_fusion.me_ref, s32[1536]{0:T(1024)} %all-reduce.meta_ref, bf16[2,4,4,4,2,256,256]{6,5,4,3,2,1,0:T(8,128)(2,1)} %place.15.b_ref, f32[4,4,64,256]{3,2,1,0:T(8,128)} %collective-permute-done.20.refs_0_, ...), custom_call_target="tpu_custom_call" | custom-call | flops 6442450944 | bytes 33554432 | tf_op jit(solution)/shard_map/product/pallas_call | solution.py:135
  464.9 2.2 collective-permute-start.24
  467.9 24.0 %product.9 = (f32[4,4,32,256]{3,2,1,0:T(8,128)}, f32[4,4,32,256]{3,2,1,0:T(8,128)}) custom-call(s32[2]{0:T(128)} %pad_add_fusion.me_ref, s32[1536]{0:T(1024)} %all-reduce.meta_ref, bf16[2,4,4,4,2,256,256]{6,5,4,3,2,1,0:T(8,128)(2,1)} %place.15.b_ref, f32[4,4,32,256]{3,2,1,0:T(8,128)} %copy-done.46, f32[4,4,32,256]{3,2,1,0:T(8,128)} %copy-done.39, ...), custom_call_target="tpu_custom_call" | custom-call | flops 3221225472 | bytes 33554432 | tf_op jit(solution)/shard_map/product/pallas_call | solution.py:135
  491.9 2.7 collective-permute-start.54
  495.6 27.6 %product.7 = (f32[4,4,64,256]{3,2,1,0:T(8,128)}, f32[4,4,64,256]{3,2,1,0:T(8,128)}) custom-call(s32[2]{0:T(128)} %pad_add_fusion.me_ref, s32[1536]{0:T(1024)} %all-reduce.meta_ref, bf16[2,4,4,4,2,256,256]{6,5,4,3,2,1,0:T(8,128)(2,1)} %place.15.b_ref, f32[4,4,64,256]{3,2,1,0:T(8,128)} %copy-done.28, f32[4,4,64,256]{3,2,1,0:T(8,128)} %collective-permute-done.29.refs_1_, ...), custom_call_target="tpu_custom_call" | custom-call | flops 6442450944 | bytes 33554432 | tf_op jit(solution)/shard_map/product/pallas_call | solution.py:135
  523.3 3.0 collective-permute-start.34
  531.0 1.4 fusion.1
  532.4 15.3 %collective-permute-done.34 = f32[4,4,64,256]{3,2,1,0:T(8,128)S(1)} collective-permute-done((f32[4,4,64,256]{3,2,1,0:T(8,128)}, f32[4,4,64,256]{3,2,1,0:T(8,128)S(1)}, u32[]{:S(2)}, u32[]{:S(2)}) %collective-permute-start.34) | collective-permute-done | bytes 1048608 | tf_op jit(solution)/shard_map/ppermute | solution.py:319
  547.7 1.5 collective-permute-start.16
  550.9 1.4 collective-permute-done.56.refs_18_
  552.4 1.3 collective-permute-start.26
  554.4 1.9 collective-permute-done.57.refs_19_
  556.5 18.4 %collective-permute-done.16.refs_2_ = f32[4,4,64,256]{3,2,1,0:T(8,128)S(1)} collective-permute-done((f32[4,4,64,256]{3,2,1,0:T(8,128)S(1)}, f32[4,4,64,256]{3,2,1,0:T(8,128)S(1)}, u32[]{:S(2)}, u32[]{:S(2)}) %collective-permute-start.16) | collective-permute-done | bytes 1048608 | tf_op jit(solution)/shard_map/ppermute | solution.py:321
  575.4 22.1 %collective-permute-done.26.refs_6_ = f32[4,4,64,256]{3,2,1,0:T(8,128)} collective-permute-done((f32[4,4,64,256]{3,2,1,0:T(8,128)S(1)}, f32[4,4,64,256]{3,2,1,0:T(8,128)}, u32[]{:S(2)}, u32[]{:S(2)}) %collective-permute-start.26) | collective-permute-done | bytes 1048608 | tf_op jit(solution)/shard_map/ppermute | solution.py:321
  597.4 20.2 %collective-permute-done.36.refs_10_ = f32[4,4,64,256]{3,2,1,0:T(8,128)} collective-permute-done((f32[4,4,64,256]{3,2,1,0:T(8,128)}, f32[4,4,64,256]{3,2,1,0:T(8,128)}, u32[]{:S(2)}, u32[]{:S(2)}) %collective-permute-start.36) | collective-permute-done | bytes 1048608 | tf_op jit(solution)/shard_map/ppermute | solution.py:321
  624.5 1.3 reduce_sum.186
  625.8 1.3 reduce_sum.190
  627.2 1.3 reduce_sum.185
  628.6 1.3 reduce_sum.189
  629.9 1.3 reduce_sum.183
  631.2 1.3 reduce_sum.187
  632.5 1.3 reduce_sum.191
  634.4 6.1 owned.1
  (205 shorter events, 41.5 us)
Async XLA Ops:
  0.0 93.7 %collective-permute-start = (f32[4,4,256,256]{3,2,1,0:T(8,128)}, f32[4,4,256,256]{3,2,1,0:T(8,128)S(1)}, u32[]{:S(2)}, u32[]{:S(2)}) collective-permute-start(f32[4,4,256,256]{3,2,1,0:T(8,128)} %bitcast.5), channel_id=1, source_target_pairs={{0,1},{1,0},{2,3},{3,2},{4,5},{5,4},{6,7},{7,6},{8,9},{9,8},{10,11... | collective-permute-start | bytes 12582920 | tf_op jit(solution)/shard_map/ppermute | solution.py:297
  2.9 92.3 %collective-permute-start.2 = (f32[4,4,256,256]{3,2,1,0:T(8,128)}, f32[4,4,256,256]{3,2,1,0:T(8,128)}, u32[]{:S(2)}, u32[]{:S(2)}) collective-permute-start(f32[4,4,256,256]{3,2,1,0:T(8,128)} %bitcast.6), channel_id=1, source_target_pairs={{0,16},{8,24},{16,0},{24,8},{1,17},{9,25},{17,1},{25,9},{2,18},{10... | collective-permute-start | bytes 12582920 | tf_op jit(solution)/shard_map/ppermute | solution.py:297
  5.8 15.9 %collective-permute-start.38 = (f32[4,4,32,256]{3,2,1,0:T(8,128)S(1)}, f32[4,4,32,256]{3,2,1,0:T(8,128)S(1)}, u32[]{:S(2)}, u32[]{:S(2)}) collective-permute-start(f32[4,4,32,256]{3,2,1,0:T(8,128)S(1)} %get-tuple-element.38.refs_3_), channel_id=1, source_target_pairs={{0,2},{1,3},{2,4},{3,5},{4,6},{5,7},{8,10},{9,11},{10,12},{11,13},... | collective-permute-start | bytes 1572872 | tf_op jit(solution)/shard_map/ppermute | solution.py:271
  9.3 15.9 %collective-permute-start.41 = (f32[4,4,32,256]{3,2,1,0:T(8,128)S(1)}, f32[4,4,32,256]{3,2,1,0:T(8,128)S(1)}, u32[]{:S(2)}, u32[]{:S(2)}) collective-permute-start(f32[4,4,32,256]{3,2,1,0:T(8,128)S(1)} %get-tuple-element.38.refs_3_), channel_id=1, source_target_pairs={{2,0},{3,1},{4,2},{5,3},{6,4},{7,5},{10,8},{11,9},{12,10},{13,11},... | collective-permute-start | bytes 1572872 | tf_op jit(solution)/shard_map/ppermute | solution.py:274
  10.6 22.3 %collective-permute-start.48 = (f32[4,4,32,256]{3,2,1,0:T(8,128)S(1)}, f32[4,4,32,256]{3,2,1,0:T(8,128)S(1)}, u32[]{:S(2)}, u32[]{:S(2)}) collective-permute-start(f32[4,4,32,256]{3,2,1,0:T(8,128)S(1)} %get-tuple-element.39.refs_3_), channel_id=1, source_target_pairs={{0,2},{1,3},{2,4},{3,5},{4,6},{5,7},{8,10},{9,11},{10,12},{11,13},... | collective-permute-start | bytes 1572872 | tf_op jit(solution)/shard_map/ppermute | solution.py:271
  21.6 14.0 %collective-permute-start.51 = (f32[4,4,32,256]{3,2,1,0:T(8,128)S(1)}, f32[4,4,32,256]{3,2,1,0:T(8,128)S(1)}, u32[]{:S(2)}, u32[]{:S(2)}) collective-permute-start(f32[4,4,32,256]{3,2,1,0:T(8,128)S(1)} %get-tuple-element.39.refs_3_), channel_id=1, source_target_pairs={{2,0},{3,1},{4,2},{5,3},{6,4},{7,5},{10,8},{11,9},{12,10},{13,11},... | collective-permute-start | bytes 1572872 | tf_op jit(solution)/shard_map/ppermute | solution.py:274
  25.2 77.7 %collective-permute-start.8 = (f32[4,4,64,256]{3,2,1,0:T(8,128)S(1)}, f32[4,4,64,256]{3,2,1,0:T(8,128)S(1)}, u32[]{:S(2)}, u32[]{:S(2)}) collective-permute-start(f32[4,4,64,256]{3,2,1,0:T(8,128)S(1)} %get-tuple-element.35.refs_3_), channel_id=1, source_target_pairs={{0,2},{1,3},{2,4},{3,5},{4,6},{5,7},{8,10},{9,11},{10,12},{11,13},... | collective-permute-start | bytes 3145736 | tf_op jit(solution)/shard_map/ppermute | solution.py:271
  32.9 71.9 %collective-permute-start.11 = (f32[4,4,64,256]{3,2,1,0:T(8,128)S(1)}, f32[4,4,64,256]{3,2,1,0:T(8,128)S(1)}, u32[]{:S(2)}, u32[]{:S(2)}) collective-permute-start(f32[4,4,64,256]{3,2,1,0:T(8,128)S(1)} %get-tuple-element.35.refs_3_), channel_id=1, source_target_pairs={{2,0},{3,1},{4,2},{5,3},{6,4},{7,5},{10,8},{11,9},{12,10},{13,11},... | collective-permute-start | bytes 3145736 | tf_op jit(solution)/shard_map/ppermute | solution.py:274
  35.7 70.6 %collective-permute-start.18 = (f32[4,4,64,256]{3,2,1,0:T(8,128)S(1)}, f32[4,4,64,256]{3,2,1,0:T(8,128)S(1)}, u32[]{:S(2)}, u32[]{:S(2)}) collective-permute-start(f32[4,4,64,256]{3,2,1,0:T(8,128)S(1)} %get-tuple-element.37.refs_3_), channel_id=1, source_target_pairs={{0,2},{1,3},{2,4},{3,5},{4,6},{5,7},{8,10},{9,11},{10,12},{11,13},... | collective-permute-start | bytes 3145736 | tf_op jit(solution)/shard_map/ppermute | solution.py:271
  93.7 28.0 %collective-permute-start.21 = (f32[4,4,64,256]{3,2,1,0:T(8,128)S(1)}, f32[4,4,64,256]{3,2,1,0:T(8,128)S(1)}, u32[]{:S(2)}, u32[]{:S(2)}) collective-permute-start(f32[4,4,64,256]{3,2,1,0:T(8,128)S(1)} %get-tuple-element.37.refs_3_), channel_id=1, source_target_pairs={{2,0},{3,1},{4,2},{5,3},{6,4},{7,5},{10,8},{11,9},{12,10},{13,11},... | collective-permute-start | bytes 3145736 | tf_op jit(solution)/shard_map/ppermute | solution.py:274
  95.3 27.1 %collective-permute-start.28 = (f32[4,4,64,256]{3,2,1,0:T(8,128)S(1)}, f32[4,4,64,256]{3,2,1,0:T(8,128)}, u32[]{:S(2)}, u32[]{:S(2)}) collective-permute-start(f32[4,4,64,256]{3,2,1,0:T(8,128)S(1)} %get-tuple-element.36.refs_3_), channel_id=1, source_target_pairs={{0,2},{1,3},{2,4},{3,5},{4,6},{5,7},{8,10},{9,11},{10,12},{11,13},... | collective-permute-start | bytes 3145736 | tf_op jit(solution)/shard_map/ppermute | solution.py:271
  102.9 145.9 %copy-start.50 = (s32[1,4,4]{2,1,0:T(4,128)S(1)}, s32[1,4,4]{2,1,0:T(4,128)}, u32[]{:S(2)}) copy-start(s32[1,4,4]{2,1,0:T(4,128)} %param.6) | copy-start | bytes 196
  102.9 145.9 %copy-start.51 = (s32[1,4,4]{2,1,0:T(4,128)S(1)}, s32[1,4,4]{2,1,0:T(4,128)}, u32[]{:S(2)}) copy-start(s32[1,4,4]{2,1,0:T(4,128)} %param.5) | copy-start | bytes 196
  102.9 149.0 %copy-start.52 = (s32[1,16,1]{1,2,0:T(1,128)S(1)}, s32[1,16,1]{1,2,0:T(1,128)}, u32[]{:S(2)}) copy-start(s32[1,16,1]{1,2,0:T(1,128)} %param.7) | copy-start | bytes 196
  102.9 145.7 %copy-start.24 = (f32[4,4,64,256]{3,2,1,0:T(8,128)}, f32[4,4,64,256]{3,2,1,0:T(8,128)S(1)}, u32[]{:S(2)}) copy-start(f32[4,4,64,256]{3,2,1,0:T(8,128)S(1)} %collective-permute-done.8.refs_2_) | copy-start | bytes 3145732
  102.9 54.2 %collective-permute-start.1 = (f32[4,4,128,256]{3,2,1,0:T(8,128)S(1)}, f32[4,4,128,256]{3,2,1,0:T(8,128)S(1)}, u32[]{:S(2)}, u32[]{:S(2)}) collective-permute-start(f32[4,4,128,256]{3,2,1,0:T(8,128)S(1)} %slice.28), channel_id=1, source_target_pairs={{0,16},{8,24},{16,0},{24,8},{1,17},{9,25},{17,1},{25,9},{2,18},{10... | collective-permute-start | bytes 6291464 | tf_op jit(solution)/shard_map/ppermute | solution.py:299
  104.8 143.9 %copy-start.25 = (f32[4,4,64,256]{3,2,1,0:T(8,128)}, f32[4,4,64,256]{3,2,1,0:T(8,128)S(1)}, u32[]{:S(2)}) copy-start(f32[4,4,64,256]{3,2,1,0:T(8,128)S(1)} %collective-permute-done.11.refs_4_) | copy-start | bytes 3145732
  104.8 52.5 %collective-permute-start.3 = (f32[4,4,128,256]{3,2,1,0:T(8,128)S(1)}, f32[4,4,128,256]{3,2,1,0:T(8,128)S(1)}, u32[]{:S(2)}, u32[]{:S(2)}) collective-permute-start(f32[4,4,128,256]{3,2,1,0:T(8,128)S(1)} %slice.29), channel_id=1, source_target_pairs={{0,1},{1,0},{2,3},{3,2},{4,5},{5,4},{6,7},{7,6},{8,9},{9,8},{10,11... | collective-permute-start | bytes 6291464 | tf_op jit(solution)/shard_map/ppermute | solution.py:299
  106.3 142.4 %copy-start.22 = (f32[4,4,64,256]{3,2,1,0:T(8,128)}, f32[4,4,64,256]{3,2,1,0:T(8,128)S(1)}, u32[]{:S(2)}) copy-start(f32[4,4,64,256]{3,2,1,0:T(8,128)S(1)} %collective-permute-done.18.refs_2_) | copy-start | bytes 3145732
  106.3 38.0 %collective-permute-start.31 = (f32[4,4,64,256]{3,2,1,0:T(8,128)S(1)}, f32[4,4,64,256]{3,2,1,0:T(8,128)}, u32[]{:S(2)}, u32[]{:S(2)}) collective-permute-start(f32[4,4,64,256]{3,2,1,0:T(8,128)S(1)} %get-tuple-element.36.refs_3_), channel_id=1, source_target_pairs={{2,0},{3,1},{4,2},{5,3},{6,4},{7,5},{10,8},{11,9},{12,10},{13,11},... | collective-permute-start | bytes 3145736 | tf_op jit(solution)/shard_map/ppermute | solution.py:274
  121.7 23.3 %collective-permute-start.39 = (f32[4,4,32,256]{3,2,1,0:T(8,128)S(1)}, f32[4,4,32,256]{3,2,1,0:T(8,128)S(1)}, u32[]{:S(2)}, u32[]{:S(2)}) collective-permute-start(f32[4,4,32,256]{3,2,1,0:T(8,128)S(1)} %collective-permute-done.38.refs_2_), channel_id=1, source_target_pairs={{2,4},{3,5},{4,6},{5,7},{10,12},{11,13},{12,14},{13,15},{18,20},{1... | collective-permute-start | bytes 1572872 | tf_op jit(solution)/shard_map/ppermute | solution.py:271
  122.4 31.4 %collective-permute-start.42 = (f32[4,4,32,256]{3,2,1,0:T(8,128)S(1)}, f32[4,4,32,256]{3,2,1,0:T(8,128)S(1)}, u32[]{:S(2)}, u32[]{:S(2)}) collective-permute-start(f32[4,4,32,256]{3,2,1,0:T(8,128)S(1)} %collective-permute-done.41.refs_4_), channel_id=1, source_target_pairs={{2,0},{3,1},{4,2},{5,3},{10,8},{11,9},{12,10},{13,11},{18,16},{19,... | collective-permute-start | bytes 1572872 | tf_op jit(solution)/shard_map/ppermute | solution.py:274
  144.3 10.2 %collective-permute-start.49 = (f32[4,4,32,256]{3,2,1,0:T(8,128)S(1)}, f32[4,4,32,256]{3,2,1,0:T(8,128)S(1)}, u32[]{:S(2)}, u32[]{:S(2)}) collective-permute-start(f32[4,4,32,256]{3,2,1,0:T(8,128)S(1)} %collective-permute-done.48.refs_2_), channel_id=1, source_target_pairs={{2,4},{3,5},{4,6},{5,7},{10,12},{11,13},{12,14},{13,15},{18,20},{1... | collective-permute-start | bytes 1572872 | tf_op jit(solution)/shard_map/ppermute | solution.py:271
  145.0 10.8 %collective-permute-start.40 = (f32[4,4,32,256]{3,2,1,0:T(8,128)S(1)}, f32[4,4,32,256]{3,2,1,0:T(8,128)S(1)}, u32[]{:S(2)}, u32[]{:S(2)}) collective-permute-start(f32[4,4,32,256]{3,2,1,0:T(8,128)S(1)} %collective-permute-done.39.refs_1_), channel_id=1, source_target_pairs={{4,6},{5,7},{12,14},{13,15},{20,22},{21,23},{28,30},{29,31}} | collective-permute-start | bytes 1572872 | tf_op jit(solution)/shard_map/ppermute | solution.py:271
  153.8 37.5 %collective-permute-start.9 = (f32[4,4,64,256]{3,2,1,0:T(8,128)S(1)}, f32[4,4,64,256]{3,2,1,0:T(8,128)S(1)}, u32[]{:S(2)}, u32[]{:S(2)}) collective-permute-start(f32[4,4,64,256]{3,2,1,0:T(8,128)S(1)} %collective-permute-done.8.refs_2_), channel_id=1, source_target_pairs={{2,4},{3,5},{4,6},{5,7},{10,12},{11,13},{12,14},{13,15},{18,20},{1... | collective-permute-start | bytes 3145736 | tf_op jit(solution)/shard_map/ppermute | solution.py:271
  154.5 37.3 %collective-permute-start.12 = (f32[4,4,64,256]{3,2,1,0:T(8,128)S(1)}, f32[4,4,64,256]{3,2,1,0:T(8,128)}, u32[]{:S(2)}, u32[]{:S(2)}) collective-permute-start(f32[4,4,64,256]{3,2,1,0:T(8,128)S(1)} %collective-permute-done.11.refs_4_), channel_id=1, source_target_pairs={{2,0},{3,1},{4,2},{5,3},{10,8},{11,9},{12,10},{13,11},{18,16},{19,... | collective-permute-start | bytes 3145736 | tf_op jit(solution)/shard_map/ppermute | solution.py:274
  155.8 35.4 %collective-permute-start.43 = (f32[4,4,32,256]{3,2,1,0:T(8,128)S(1)}, f32[4,4,32,256]{3,2,1,0:T(8,128)S(1)}, u32[]{:S(2)}, u32[]{:S(2)}) collective-permute-start(f32[4,4,32,256]{3,2,1,0:T(8,128)S(1)} %collective-permute-done.42.refs_5_), channel_id=1, source_target_pairs={{2,0},{3,1},{10,8},{11,9},{18,16},{19,17},{26,24},{27,25}} | collective-permute-start | bytes 1572872 | tf_op jit(solution)/shard_map/ppermute | solution.py:274
  157.2 86.0 %collective-permute-start.7 = (f32[4,4,256,256]{3,2,1,0:T(8,128)S(1)}, f32[4,4,256,256]{3,2,1,0:T(8,128)S(1)}, u32[]{:S(2)}, u32[]{:S(2)}) collective-permute-start(f32[4,4,256,256]{3,2,1,0:T(8,128)S(1)} %bitcast.10), channel_id=1, source_target_pairs={{0,8},{8,0},{16,24},{24,16},{1,9},{9,1},{17,25},{25,17},{2,10},{10... | collective-permute-start | bytes 12582920 | tf_op jit(solution)/shard_map/ppermute | solution.py:303
  157.3 88.0 %collective-permute-start.6 = (f32[4,4,256,256]{3,2,1,0:T(8,128)S(1)}, f32[4,4,256,256]{3,2,1,0:T(8,128)S(1)}, u32[]{:S(2)}, u32[]{:S(2)}) collective-permute-start(f32[4,4,256,256]{3,2,1,0:T(8,128)S(1)} %collective-permute-done.x_ref), channel_id=1, source_target_pairs={{0,8},{8,0},{16,24},{24,16},{1,9},{9,1},{17,25},{25,17},{2,10},{10... | collective-permute-start | bytes 12582920 | tf_op jit(solution)/shard_map/ppermute | solution.py:306
  191.3 57.7 %collective-permute-start.5 = (f32[4,4,256,256]{3,2,1,0:T(8,128)}, f32[4,4,256,256]{3,2,1,0:T(8,128)}, u32[]{:S(2)}, u32[]{:S(2)}) collective-permute-start(f32[4,4,256,256]{3,2,1,0:T(8,128)} %collective-permute-done.2.x_ref), channel_id=1, source_target_pairs={{0,8},{8,0},{16,24},{24,16},{1,9},{9,1},{17,25},{25,17},{2,10},{10... | collective-permute-start | bytes 12582920 | tf_op jit(solution)/shard_map/ppermute | solution.py:307
  191.3 59.3 %collective-permute-start.4 = (f32[4,4,256,256]{3,2,1,0:T(8,128)}, f32[4,4,256,256]{3,2,1,0:T(8,128)}, u32[]{:S(2)}, u32[]{:S(2)}) collective-permute-start(f32[4,4,256,256]{3,2,1,0:T(8,128)} %constant_dynamic-update-slice_fusion.x_ref), channel_id=1, source_target_pairs={{0,8},{8,0},{16,24},{24,16},{1,9},{9,1},{17,25},{25,17},{2,10},{10... | collective-permute-start | bytes 12582920 | tf_op jit(solution)/shard_map/ppermute | solution.py:309
  191.8 1.7 collective-permute-start.19
  193.5 47.7 %collective-permute-start.22 = (f32[4,4,64,256]{3,2,1,0:T(8,128)S(1)}, f32[4,4,64,256]{3,2,1,0:T(8,128)}, u32[]{:S(2)}, u32[]{:S(2)}) collective-permute-start(f32[4,4,64,256]{3,2,1,0:T(8,128)S(1)} %collective-permute-done.21.refs_4_), channel_id=1, source_target_pairs={{2,0},{3,1},{4,2},{5,3},{10,8},{11,9},{12,10},{13,11},{18,16},{19,... | collective-permute-start | bytes 3145736 | tf_op jit(solution)/shard_map/ppermute | solution.py:274
  241.1 0.7 collective-permute-start.10
  241.9 132.2 %collective-permute-start.13 = (f32[4,4,64,256]{3,2,1,0:T(8,128)}, f32[4,4,64,256]{3,2,1,0:T(8,128)}, u32[]{:S(2)}, u32[]{:S(2)}) collective-permute-start(f32[4,4,64,256]{3,2,1,0:T(8,128)} %collective-permute-done.12.refs_5_), channel_id=1, source_target_pairs={{2,0},{3,1},{10,8},{11,9},{18,16},{19,17},{26,24},{27,25}} | collective-permute-start | bytes 3145736 | tf_op jit(solution)/shard_map/ppermute | solution.py:274
  243.2 159.8 %collective-permute-start.29 = (f32[4,4,64,256]{3,2,1,0:T(8,128)}, f32[4,4,64,256]{3,2,1,0:T(8,128)}, u32[]{:S(2)}, u32[]{:S(2)}) collective-permute-start(f32[4,4,64,256]{3,2,1,0:T(8,128)} %collective-permute-done.28.refs_2_), channel_id=1, source_target_pairs={{2,4},{3,5},{4,6},{5,7},{10,12},{11,13},{12,14},{13,15},{18,20},{1... | collective-permute-start | bytes 3145736 | tf_op jit(solution)/shard_map/ppermute | solution.py:271
  247.3 156.5 %collective-permute-start.32 = (f32[4,4,64,256]{3,2,1,0:T(8,128)}, f32[4,4,64,256]{3,2,1,0:T(8,128)}, u32[]{:S(2)}, u32[]{:S(2)}) collective-permute-start(f32[4,4,64,256]{3,2,1,0:T(8,128)} %collective-permute-done.31.refs_4_), channel_id=1, source_target_pairs={{2,0},{3,1},{4,2},{5,3},{10,8},{11,9},{12,10},{13,11},{18,16},{19,... | collective-permute-start | bytes 3145736 | tf_op jit(solution)/shard_map/ppermute | solution.py:274
  248.9 180.9 %collective-permute-start.20 = (f32[4,4,64,256]{3,2,1,0:T(8,128)}, f32[4,4,64,256]{3,2,1,0:T(8,128)}, u32[]{:S(2)}, u32[]{:S(2)}) collective-permute-start(f32[4,4,64,256]{3,2,1,0:T(8,128)} %collective-permute-done.19.refs_1_), channel_id=1, source_target_pairs={{4,6},{5,7},{12,14},{13,15},{20,22},{21,23},{28,30},{29,31}} | collective-permute-start | bytes 3145736 | tf_op jit(solution)/shard_map/ppermute | solution.py:271
  250.5 180.8 %collective-permute-start.23 = (f32[4,4,64,256]{3,2,1,0:T(8,128)}, f32[4,4,64,256]{3,2,1,0:T(8,128)}, u32[]{:S(2)}, u32[]{:S(2)}) collective-permute-start(f32[4,4,64,256]{3,2,1,0:T(8,128)} %collective-permute-done.22.refs_5_), channel_id=1, source_target_pairs={{2,0},{3,1},{10,8},{11,9},{18,16},{19,17},{26,24},{27,25}} | collective-permute-start | bytes 3145736 | tf_op jit(solution)/shard_map/ppermute | solution.py:274
  374.0 55.1 %collective-permute-start.52 = (f32[4,4,32,256]{3,2,1,0:T(8,128)S(1)}, f32[4,4,32,256]{3,2,1,0:T(8,128)S(1)}, u32[]{:S(2)}, u32[]{:S(2)}) collective-permute-start(f32[4,4,32,256]{3,2,1,0:T(8,128)S(1)} %copy-done.36), channel_id=1, source_target_pairs={{2,0},{3,1},{4,2},{5,3},{10,8},{11,9},{12,10},{13,11},{18,16},{19,... | collective-permute-start | bytes 1572872 | tf_op jit(solution)/shard_map/ppermute | solution.py:274
  403.0 88.9 %collective-permute-start.30 = (f32[4,4,64,256]{3,2,1,0:T(8,128)}, f32[4,4,64,256]{3,2,1,0:T(8,128)S(1)}, u32[]{:S(2)}, u32[]{:S(2)}) collective-permute-start(f32[4,4,64,256]{3,2,1,0:T(8,128)} %collective-permute-done.29.refs_1_), channel_id=1, source_target_pairs={{4,6},{5,7},{12,14},{13,15},{20,22},{21,23},{28,30},{29,31}} | collective-permute-start | bytes 3145736 | tf_op jit(solution)/shard_map/ppermute | solution.py:271
  403.8 90.8 %collective-permute-start.33 = (f32[4,4,64,256]{3,2,1,0:T(8,128)}, f32[4,4,64,256]{3,2,1,0:T(8,128)S(1)}, u32[]{:S(2)}, u32[]{:S(2)}) collective-permute-start(f32[4,4,64,256]{3,2,1,0:T(8,128)} %collective-permute-done.32.refs_5_), channel_id=1, source_target_pairs={{2,0},{3,1},{10,8},{11,9},{18,16},{19,17},{26,24},{27,25}} | collective-permute-start | bytes 3145736 | tf_op jit(solution)/shard_map/ppermute | solution.py:274
  429.1 35.7 %collective-permute-start.50 = (f32[4,4,32,256]{3,2,1,0:T(8,128)S(1)}, f32[4,4,32,256]{3,2,1,0:T(8,128)S(1)}, u32[]{:S(2)}, u32[]{:S(2)}) collective-permute-start(f32[4,4,32,256]{3,2,1,0:T(8,128)S(1)} %copy-done.40), channel_id=1, source_target_pairs={{4,6},{5,7},{12,14},{13,15},{20,22},{21,23},{28,30},{29,31}} | collective-permute-start | bytes 1572872 | tf_op jit(solution)/shard_map/ppermute | solution.py:271
  429.8 37.2 %collective-permute-start.53 = (f32[4,4,32,256]{3,2,1,0:T(8,128)S(1)}, f32[4,4,32,256]{3,2,1,0:T(8,128)S(1)}, u32[]{:S(2)}, u32[]{:S(2)}) collective-permute-start(f32[4,4,32,256]{3,2,1,0:T(8,128)S(1)} %collective-permute-done.52.refs_5_), channel_id=1, source_target_pairs={{2,0},{3,1},{10,8},{11,9},{18,16},{19,17},{26,24},{27,25}} | collective-permute-start | bytes 1572872 | tf_op jit(solution)/shard_map/ppermute | solution.py:274
  431.3 97.2 %collective-permute-start.14 = (f32[4,4,64,256]{3,2,1,0:T(8,128)}, f32[4,4,64,256]{3,2,1,0:T(8,128)S(1)}, u32[]{:S(2)}, u32[]{:S(2)}) collective-permute-start(f32[4,4,64,256]{3,2,1,0:T(8,128)} %get-tuple-element.16), channel_id=1, source_target_pairs={{0,1},{1,0},{2,3},{3,2},{4,5},{5,4},{6,7},{7,6},{8,9},{9,8},{10,11... | collective-permute-start | bytes 3145736 | tf_op jit(solution)/shard_map/ppermute | solution.py:319
  464.9 65.1 %collective-permute-start.24 = (f32[4,4,64,256]{3,2,1,0:T(8,128)}, f32[4,4,64,256]{3,2,1,0:T(8,128)S(1)}, u32[]{:S(2)}, u32[]{:S(2)}) collective-permute-start(f32[4,4,64,256]{3,2,1,0:T(8,128)} %get-tuple-element.18), channel_id=1, source_target_pairs={{0,1},{1,0},{2,3},{3,2},{4,5},{5,4},{6,7},{7,6},{8,9},{9,8},{10,11... | collective-permute-start | bytes 3145736 | tf_op jit(solution)/shard_map/ppermute | solution.py:319
  467.1 59.2 %collective-permute-start.44 = (f32[4,4,32,256]{3,2,1,0:T(8,128)}, f32[4,4,32,256]{3,2,1,0:T(8,128)}, u32[]{:S(2)}, u32[]{:S(2)}) collective-permute-start(f32[4,4,32,256]{3,2,1,0:T(8,128)} %get-tuple-element.22), channel_id=1, source_target_pairs={{0,1},{1,0},{2,3},{3,2},{4,5},{5,4},{6,7},{7,6},{8,9},{9,8},{10,11... | collective-permute-start | bytes 1572872 | tf_op jit(solution)/shard_map/ppermute | solution.py:319
  491.9 36.5 %collective-permute-start.54 = (f32[4,4,32,256]{3,2,1,0:T(8,128)}, f32[4,4,32,256]{3,2,1,0:T(8,128)S(1)}, u32[]{:S(2)}, u32[]{:S(2)}) collective-permute-start(f32[4,4,32,256]{3,2,1,0:T(8,128)} %get-tuple-element.24), channel_id=1, source_target_pairs={{0,1},{1,0},{2,3},{3,2},{4,5},{5,4},{6,7},{7,6},{8,9},{9,8},{10,11... | collective-permute-start | bytes 1572872 | tf_op jit(solution)/shard_map/ppermute | solution.py:319
  523.3 24.4 %collective-permute-start.34 = (f32[4,4,64,256]{3,2,1,0:T(8,128)}, f32[4,4,64,256]{3,2,1,0:T(8,128)S(1)}, u32[]{:S(2)}, u32[]{:S(2)}) collective-permute-start(f32[4,4,64,256]{3,2,1,0:T(8,128)} %get-tuple-element.20), channel_id=1, source_target_pairs={{0,1},{1,0},{2,3},{3,2},{4,5},{5,4},{6,7},{7,6},{8,9},{9,8},{10,11... | collective-permute-start | bytes 3145736 | tf_op jit(solution)/shard_map/ppermute | solution.py:319
  527.5 21.7 %collective-permute-start.46 = (f32[4,4,32,256]{3,2,1,0:T(8,128)S(1)}, f32[4,4,32,256]{3,2,1,0:T(8,128)S(1)}, u32[]{:S(2)}, u32[]{:S(2)}) collective-permute-start(f32[4,4,32,256]{3,2,1,0:T(8,128)S(1)} %get-tuple-element.32.refs_12_), channel_id=1, source_target_pairs={{0,16},{8,24},{16,0},{24,8},{1,17},{9,25},{17,1},{25,9},{2,18},{10... | collective-permute-start | bytes 1572872 | tf_op jit(solution)/shard_map/ppermute | solution.py:321
  528.4 21.9 %collective-permute-start.45 = (f32[4,4,32,256]{3,2,1,0:T(8,128)S(1)}, f32[4,4,32,256]{3,2,1,0:T(8,128)S(1)}, u32[]{:S(2)}, u32[]{:S(2)}) collective-permute-start(f32[4,4,32,256]{3,2,1,0:T(8,128)S(1)} %get-tuple-element.32.refs_12_), channel_id=1, source_target_pairs={{0,8},{8,0},{16,24},{24,16},{1,9},{9,1},{17,25},{25,17},{2,10},{10... | collective-permute-start | bytes 1572872 | tf_op jit(solution)/shard_map/ppermute | solution.py:322
  528.5 23.8 %collective-permute-start.56 = (f32[4,4,32,256]{3,2,1,0:T(8,128)S(1)}, f32[4,4,32,256]{3,2,1,0:T(8,128)S(1)}, u32[]{:S(2)}, u32[]{:S(2)}) collective-permute-start(f32[4,4,32,256]{3,2,1,0:T(8,128)S(1)} %get-tuple-element.34.refs_16_), channel_id=1, source_target_pairs={{0,16},{8,24},{16,0},{24,8},{1,17},{9,25},{17,1},{25,9},{2,18},{10... | collective-permute-start | bytes 1572872 | tf_op jit(solution)/shard_map/ppermute | solution.py:321
  530.0 23.7 %collective-permute-start.55 = (f32[4,4,32,256]{3,2,1,0:T(8,128)S(1)}, f32[4,4,32,256]{3,2,1,0:T(8,128)S(1)}, u32[]{:S(2)}, u32[]{:S(2)}) collective-permute-start(f32[4,4,32,256]{3,2,1,0:T(8,128)S(1)} %get-tuple-element.34.refs_16_), channel_id=1, source_target_pairs={{0,8},{8,0},{16,24},{24,16},{1,9},{9,1},{17,25},{25,17},{2,10},{10... | collective-permute-start | bytes 1572872 | tf_op jit(solution)/shard_map/ppermute | solution.py:322
  547.7 27.2 %collective-permute-start.16 = (f32[4,4,64,256]{3,2,1,0:T(8,128)S(1)}, f32[4,4,64,256]{3,2,1,0:T(8,128)S(1)}, u32[]{:S(2)}, u32[]{:S(2)}) collective-permute-start(f32[4,4,64,256]{3,2,1,0:T(8,128)S(1)} %get-tuple-element.26.refs_0_), channel_id=1, source_target_pairs={{0,16},{8,24},{16,0},{24,8},{1,17},{9,25},{17,1},{25,9},{2,18},{10... | collective-permute-start | bytes 3145736 | tf_op jit(solution)/shard_map/ppermute | solution.py:321
  549.2 5.2 collective-permute-start.47
  550.4 24.5 %collective-permute-start.15 = (f32[4,4,64,256]{3,2,1,0:T(8,128)S(1)}, f32[4,4,64,256]{3,2,1,0:T(8,128)S(1)}, u32[]{:S(2)}, u32[]{:S(2)}) collective-permute-start(f32[4,4,64,256]{3,2,1,0:T(8,128)S(1)} %get-tuple-element.26.refs_0_), channel_id=1, source_target_pairs={{0,8},{8,0},{16,24},{24,16},{1,9},{9,1},{17,25},{25,17},{2,10},{10... | collective-permute-start | bytes 3145736 | tf_op jit(solution)/shard_map/ppermute | solution.py:322
  552.4 45.0 %collective-permute-start.26 = (f32[4,4,64,256]{3,2,1,0:T(8,128)S(1)}, f32[4,4,64,256]{3,2,1,0:T(8,128)}, u32[]{:S(2)}, u32[]{:S(2)}) collective-permute-start(f32[4,4,64,256]{3,2,1,0:T(8,128)S(1)} %get-tuple-element.28.refs_4_), channel_id=1, source_target_pairs={{0,16},{8,24},{16,0},{24,8},{1,17},{9,25},{17,1},{25,9},{2,18},{10... | collective-permute-start | bytes 3145736 | tf_op jit(solution)/shard_map/ppermute | solution.py:321
  553.7 64.0 %collective-permute-start.36 = (f32[4,4,64,256]{3,2,1,0:T(8,128)}, f32[4,4,64,256]{3,2,1,0:T(8,128)}, u32[]{:S(2)}, u32[]{:S(2)}) collective-permute-start(f32[4,4,64,256]{3,2,1,0:T(8,128)} %get-tuple-element.30.refs_8_), channel_id=1, source_target_pairs={{0,16},{8,24},{16,0},{24,8},{1,17},{9,25},{17,1},{25,9},{2,18},{10... | collective-permute-start | bytes 3145736 | tf_op jit(solution)/shard_map/ppermute | solution.py:321
  554.4 1.9 collective-permute-start.57
  556.3 70.9 %collective-permute-start.25 = (f32[4,4,64,256]{3,2,1,0:T(8,128)S(1)}, f32[4,4,64,256]{3,2,1,0:T(8,128)}, u32[]{:S(2)}, u32[]{:S(2)}) collective-permute-start(f32[4,4,64,256]{3,2,1,0:T(8,128)S(1)} %get-tuple-element.28.refs_4_), channel_id=1, source_target_pairs={{0,8},{8,0},{16,24},{24,16},{1,9},{9,1},{17,25},{25,17},{2,10},{10... | collective-permute-start | bytes 3145736 | tf_op jit(solution)/shard_map/ppermute | solution.py:322
  574.8 53.7 %collective-permute-start.35 = (f32[4,4,64,256]{3,2,1,0:T(8,128)}, f32[4,4,64,256]{3,2,1,0:T(8,128)}, u32[]{:S(2)}, u32[]{:S(2)}) collective-permute-start(f32[4,4,64,256]{3,2,1,0:T(8,128)} %get-tuple-element.30.refs_8_), channel_id=1, source_target_pairs={{0,8},{8,0},{16,24},{24,16},{1,9},{9,1},{17,25},{25,17},{2,10},{10... | collective-permute-start | bytes 3145736 | tf_op jit(solution)/shard_map/ppermute | solution.py:322
  574.9 55.0 %collective-permute-start.17 = (f32[4,4,64,256]{3,2,1,0:T(8,128)S(1)}, f32[4,4,64,256]{3,2,1,0:T(8,128)}, u32[]{:S(2)}, u32[]{:S(2)}) collective-permute-start(f32[4,4,64,256]{3,2,1,0:T(8,128)S(1)} %collective-permute-done.16.refs_2_), channel_id=1, source_target_pairs={{0,8},{8,0},{16,24},{24,16},{1,9},{9,1},{17,25},{25,17},{2,10},{10... | collective-permute-start | bytes 3145736 | tf_op jit(solution)/shard_map/ppermute | solution.py:322
  597.4 33.8 %collective-permute-start.27 = (f32[4,4,64,256]{3,2,1,0:T(8,128)}, f32[4,4,64,256]{3,2,1,0:T(8,128)}, u32[]{:S(2)}, u32[]{:S(2)}) collective-permute-start(f32[4,4,64,256]{3,2,1,0:T(8,128)} %collective-permute-done.26.refs_6_), channel_id=1, source_target_pairs={{0,8},{8,0},{16,24},{24,16},{1,9},{9,1},{17,25},{25,17},{2,10},{10... | collective-permute-start | bytes 3145736 | tf_op jit(solution)/shard_map/ppermute | solution.py:322
  617.7 14.8 %collective-permute-start.37 = (f32[4,4,64,256]{3,2,1,0:T(8,128)}, f32[4,4,64,256]{3,2,1,0:T(8,128)}, u32[]{:S(2)}, u32[]{:S(2)}) collective-permute-start(f32[4,4,64,256]{3,2,1,0:T(8,128)} %collective-permute-done.36.refs_10_), channel_id=1, source_target_pairs={{0,8},{8,0},{16,24},{24,16},{1,9},{9,1},{17,25},{25,17},{2,10},{10... | collective-permute-start | bytes 3145736 | tf_op jit(solution)/shard_map/ppermute | solution.py:322
  (47 other events, 2198.7 us)

commit v2 on v1

v2 whole, which is shorter than its diff:
```python
import functools

import jax
import jax.numpy as jnp
from jax import lax
from jax.experimental import pallas as pl
from jax.experimental.pallas import tpu as pltpu
from jax.sharding import PartitionSpec as P

TR = 8
CHUNKS = (128, 64, 32, 32)
ROWS = 64
FIELDS = 8
RING = 16
MODE = 0
VMEM = 56 * 1024 * 1024


def split(x):
    high = x.astype(jnp.bfloat16)
    low = (x - high.astype(jnp.float32)).astype(jnp.bfloat16)
    return high, low


def place_kernel(pieces, *refs):
    o_ref, mark_ref = refs[-2:]
    mark_ref[...] = jnp.zeros_like(mark_ref)
    start = 0
    for x_ref in refs[:pieces]:
        count, rows = x_ref.shape[1:3]
        for z in range(count):
            high, low = split(x_ref[0, z])
            o_ref[0, 0, 0, z, 0, start : start + rows] = high
            o_ref[0, 0, 0, z, 1, start : start + rows] = low
        start += rows


def place(pieces, buffer, group, relative, rows):
    blocks, count, _, width = pieces[0].shape
    out = jax.ShapeDtypeStruct((2, blocks, 4, count, 2, width, width), jnp.bfloat16)
    in_specs = [pl.BlockSpec((1, count, rows, width), lambda j: (j, 0, 0, 0)) for _ in pieces]
    args = list(pieces)
    aliases = {}
    if buffer is not None:
        in_specs.append(pl.BlockSpec(memory_space=pl.ANY))
        args.append(buffer)
        aliases = {len(pieces): 0}
    size = blocks * count * width * width
    return pl.pallas_call(
        functools.partial(place_kernel, len(pieces)),
        grid=(blocks,),
        out_shape=(out, jax.ShapeDtypeStruct((8, 128), jnp.float32)),
        in_specs=in_specs,
        out_specs=(
            pl.BlockSpec(
                (1, 1, 1, count, 2, width, width),
                lambda j: (group, j, relative, 0, 0, 0, 0),
            ),
            pl.BlockSpec((8, 128), lambda j: (0, 0)),
        ),
        input_output_aliases=aliases,
        compiler_params=pltpu.CompilerParams(vmem_limit_bytes=VMEM),
        cost_estimate=pl.CostEstimate(flops=size, bytes_accessed=8 * size, transcendentals=0),
        name="place",
    )(*args)


def plan_kernel(line, blocks, count, me_ref, meta_ref, levels_ref, plan_ref, kept_ref):
    items = blocks * count
    r, c = me_ref[0], me_ref[1]
    q, p = c // 2, c % 2

    def base(relative, group):
        return (relative * 2 + group) * 3 * items

    def write(n, tile, at, levels):
        plan_ref[FIELDS * n] = tile
        plan_ref[FIELDS * n + 1] = at
        for y in range(count):
            plan_ref[FIELDS * n + 2 + y] = levels(y)

    def column(row, n):
        group, j = row // blocks, row % blocks

        def entry(t, n):
            relative = t // count
            rr = jnp.bitwise_xor(r, relative)
            k = rr * TR + meta_ref[base(relative, group) + j * count + t % count]
            ck = k // blocks
            mine = ck % 2 == p
            levels = (ck // 2 - q + line - 1) * items + (k % blocks) * count
            write(
                n,
                row * 4 * count + t,
                (ck // 2) * blocks + k % blocks,
                lambda y: levels_ref[levels + y],
            )
            return n + mine.astype(jnp.int32)

        n = lax.fori_loop(0, 4 * count, entry, n)
        write(n, row * 4 * count, line * blocks, lambda y: jnp.int32(0))
        n = n + n % 2
        kept_ref[FIELDS * row] = n
        for m in range(count):
            kept_ref[FIELDS * row + 1 + m] = meta_ref[base(0, group) + items + j * count + m]
        return n

    lax.fori_loop(0, 2 * blocks, column, jnp.int32(0))


def make_plan(me, meta, levels, line, blocks, count):
    smem = pl.BlockSpec(memory_space=pltpu.SMEM)
    return pl.pallas_call(
        functools.partial(plan_kernel, line, blocks, count),
        out_shape=(
            jax.ShapeDtypeStruct((FIELDS * (2 * blocks * 4 * count + 2),), jnp.int32),
            jax.ShapeDtypeStruct((FIELDS * 2 * blocks,), jnp.int32),
        ),
        in_specs=[smem] * 3,
        out_specs=(smem, smem),
        name="plan",
    )(me, meta, levels)


def product_kernel(line, start, me_ref, plan_ref, kept_ref, b_ref, *refs):
    parts = 2 * line - 1
    a_refs = refs[:parts]
    other_ref, own_ref, raw, halves, total, ring, a_sems, b_sems = refs[parts:]
    group, j = pl.program_id(0), pl.program_id(1)
    blocks, count, rows, width = raw.shape[1:]
    last = 2 * blocks - 1
    row = group * blocks + j
    q = me_ref[1] // 2
    end = kept_ref[FIELDS * last]

    def fetch(n):
        tile = plan_ref[FIELDS * n]
        slot = n % RING
        return pltpu.make_async_copy(b_ref.at[tile], ring.at[slot], b_sems.at[slot])

    @pl.when(row == 0)
    def _():
        def each(act):
            for i in range(parts):
                at = q + i - (line - 1)

                @pl.when((at >= 0) & (at < line))
                def _():
                    rows_of = a_refs[i].at[:, :, start : start + rows]
                    act(pltpu.make_async_copy(rows_of, raw.at[at], a_sems.at[i]))

        each(lambda copy: copy.start())

        def begin(n, _):
            fetch(n).start()
            return 0

        lax.fori_loop(0, jnp.minimum(end, RING), begin, 0)
        halves[line * blocks] = jnp.zeros(halves.shape[1:], halves.dtype)
        each(lambda copy: copy.wait())

        def convert(i, _):
            for y in range(count):
                high, low = split(raw[i // blocks, i % blocks, y])
                halves[i, y * rows : (y + 1) * rows, 0:width] = high
                halves[i, y * rows : (y + 1) * rows, width : 2 * width] = low
            return 0

        lax.fori_loop(0, line * blocks, convert, 0)

    total[...] = jnp.zeros_like(total)
    first = jnp.where(row == 0, 0, kept_ref[FIELDS * jnp.maximum(row - 1, 0)])

    def multiply(n):
        a = halves[plan_ref[FIELDS * n + 1]]
        slot = n % RING
        b_high, b_low = ring[slot, 0], ring[slot, 1]
        if MODE == 0:
            return jnp.dot(
                jnp.concatenate([a, a[:, 0:width]], axis=1),
                jnp.concatenate([b_high, b_high, b_low], axis=0),
                preferred_element_type=jnp.float32,
            )
        if MODE == 1:
            dot = functools.partial(jnp.dot, preferred_element_type=jnp.float32)
            return dot(a[:, :width], b_high) + dot(a[:, width:], b_high) + dot(a[:, :width], b_low)
        bb = jnp.concatenate([b_high, b_high, b_low], axis=0)
        return jnp.concatenate(
            [
                jnp.dot(
                    jnp.concatenate(
                        [a[y * rows : (y + 1) * rows], a[y * rows : (y + 1) * rows, 0:width]], axis=1
                    ),
                    bb,
                    preferred_element_type=jnp.float32,
                )
                for y in range(count)
            ],
            axis=0,
        )

    def step(i, _):
        n = first + 2 * i
        fetch(n).wait()
        fetch(n + 1).wait()
        products = [multiply(n), multiply(n + 1)]
        for e in range(2):
            for y in range(count):
                level = plan_ref[FIELDS * (n + e) + 2 + y]
                total[level] += products[e][y * rows : (y + 1) * rows]

        @pl.when(n + RING < end)
        def _():
            fetch(n + RING).start()
            fetch(n + RING + 1).start()

        return 0

    lax.fori_loop(0, (kept_ref[FIELDS * row] - first) // 2, step, 0)

    @pl.when(group == 0)
    def _():
        for m in range(count):
            other_ref[0, m] = total[kept_ref[FIELDS * row + 1 + m]]

    @pl.when(group == 1)
    def _():
        for m in range(count):
            own_ref[0, m] = total[kept_ref[FIELDS * row + 1 + m]]


def product(me, plan, panel, parts, line, start, rows):
    blocks, count, _, width = parts[0].shape
    out = jax.ShapeDtypeStruct((blocks, count, rows, width), jnp.float32)
    smem = pl.BlockSpec(memory_space=pltpu.SMEM)
    return pl.pallas_call(
        functools.partial(product_kernel, line, start),
        grid=(2, blocks),
        out_shape=(out, out),
        in_specs=[smem] * 3 + [pl.BlockSpec(memory_space=pl.ANY)] * (1 + len(parts)),
        out_specs=(
            pl.BlockSpec(
                (1, count, rows, width), lambda g, j: (jnp.where(g == 0, j, blocks - 1), 0, 0, 0)
            ),
            pl.BlockSpec((1, count, rows, width), lambda g, j: (jnp.where(g == 0, 0, j), 0, 0, 0)),
        ),
        scratch_shapes=[
            pltpu.VMEM((line, blocks, count, rows, width), jnp.float32),
            pltpu.VMEM((line * blocks + 1, count * rows, 2 * width), jnp.bfloat16),
            pltpu.VMEM((TR, rows, width), jnp.float32),
            pltpu.VMEM((RING, 2, width, width), jnp.bfloat16),
            pltpu.SemaphoreType.DMA((len(parts),)),
            pltpu.SemaphoreType.DMA((RING,)),
        ],
        compiler_params=pltpu.CompilerParams(vmem_limit_bytes=VMEM),
        cost_estimate=pl.CostEstimate(
            flops=3 * 2 * 16 * blocks * count * rows * width * width,
            bytes_accessed=panel.size,
            transcendentals=0,
        ),
        name="product",
    )(me, *plan, panel.reshape(-1, 2, width, width), *parts)


def inflate_kernel(own_ref, other_ref, out_ref):
    count, rows = own_ref.shape[1:3]
    partial = jnp.zeros((8, own_ref.shape[3]), jnp.float32)
    for m in range(count):
        kept = own_ref[0, m] + other_ref[0, m]
        inflated = kept * kept
        out_ref[0, m * rows : (m + 1) * rows] = inflated
        for i in range(0, rows, 8):
            partial += inflated[i : i + 8]
    out_ref[0, count * rows :] = partial


def inflate(own, other):
    blocks, count, rows, width = own.shape
    spec = pl.BlockSpec((1, count, rows, width), lambda j: (j, 0, 0, 0))
    return pl.pallas_call(
        inflate_kernel,
        grid=(blocks,),
        out_shape=jax.ShapeDtypeStruct((blocks, count * rows + 8, width), jnp.float32),
        in_specs=[spec, spec],
        out_specs=pl.BlockSpec((1, count * rows + 8, width), lambda j: (j, 0, 0)),
        cost_estimate=pl.CostEstimate(
            flops=3 * own.size, bytes_accessed=12 * own.size, transcendentals=0
        ),
        name="inflate",
    )(own, other)


def owned_kernel(sizes, blocks, count, scale, me_ref, meta_ref, *refs):
    chunks = len(sizes)
    sources = refs[: 4 * chunks]
    out_ref, slots, partial, whose, in_sems, out_sems, sum_sems = refs[4 * chunks :]
    items = blocks * count
    most = items // 2
    r = me_ref[0]
    starts = [sum(sizes[:h]) for h in range(chunks)]

    def partials(act):
        for i in range(4 * chunks):
            rows = pl.ds(count * sizes[i // 4], 8)
            act(pltpu.make_async_copy(sources[i].at[:, rows], partial.at[i], sum_sems.at[i]))

    partials(lambda copy: copy.start())
    for s in range(4 * most):
        whose[s] = -1
    for relative in range(4):
        rr = jnp.bitwise_xor(r, relative)

        def place_item(f, n, relative=relative, rr=rr):
            mine = meta_ref[((relative * 2 + 1) * 3 + 2) * items + f] == r

            @pl.when(mine)
            def _():
                slot = rr * most + n
                whose[slot] = f // count
                for h in range(chunks):
                    pltpu.make_async_copy(
                        sources[4 * h + relative].at[
                            f // count, pl.ds(pl.multiple_of(f % count * sizes[h], 8), sizes[h])
                        ],
                        slots.at[slot, pl.ds(starts[h], sizes[h])],
                        in_sems.at[slot],
                    ).start()

            return n + mine.astype(jnp.int32)

        lax.fori_loop(0, items, place_item, jnp.int32(0))

    partials(lambda copy: copy.wait())
    factors = scale / jnp.sum(jnp.sum(partial[...], axis=0), axis=1)

    def finish(s, _):
        j = whose[s]

        @pl.when(j < 0)
        def _():
            slots[s] = jnp.zeros(slots.shape[1:], jnp.float32)

        for jj in range(blocks):

            @pl.when(j == jj)
            def _():
                pltpu.make_async_copy(slots.at[s], slots.at[s], in_sems.at[s]).wait()
                slots[s] = slots[s] * factors[jj : jj + 1]

        pltpu.make_async_copy(slots.at[s], out_ref.at[s], out_sems.at[s]).start()
        return 0

    lax.fori_loop(0, 4 * most, finish, 0)

    def drain(s, _):
        pltpu.make_async_copy(slots.at[s], out_ref.at[s], out_sems.at[s]).wait()
        return 0

    lax.fori_loop(0, 4 * most, drain, 0)


def owned_tiles(me, meta, sources, sizes, count, scale):
    blocks, _, width = sources[0].shape
    most = blocks * count // 2
    smem = pl.BlockSpec(memory_space=pltpu.SMEM)
    return pl.pallas_call(
        functools.partial(owned_kernel, sizes, blocks, count, scale),
        out_shape=jax.ShapeDtypeStruct((4 * most, width, width), jnp.float32),
        in_specs=[smem, smem]
        + [pl.BlockSpec(memory_space=pl.ANY)] * len(sources),
        out_specs=pl.BlockSpec(memory_space=pl.ANY),
        scratch_shapes=[
            pltpu.VMEM((4 * most, width, width), jnp.float32),
            pltpu.VMEM((len(sources), blocks, 8, width), jnp.float32),
            pltpu.SMEM((4 * most,), jnp.int32),
            pltpu.SemaphoreType.DMA((4 * most,)),
            pltpu.SemaphoreType.DMA((4 * most,)),
            pltpu.SemaphoreType.DMA((len(sources),)),
        ],
        compiler_params=pltpu.CompilerParams(vmem_limit_bytes=VMEM),
        cost_estimate=pl.CostEstimate(
            flops=4 * most * width * width,
            bytes_accessed=32 * most * width * width,
            transcendentals=0,
        ),
        name="owned",
    )(me, meta, *sources)


def on_device(columns, matrix_tiles, tile_rows, keep_rows, owners):
    tiles = matrix_tiles[0]
    blocks, count, width = tiles.shape[0], tiles.shape[1], tiles.shape[2]
    line = columns // 2
    r, c = lax.axis_index("row"), lax.axis_index("col")
    me = jnp.stack([r, c]).astype(jnp.int32)

    core = functools.partial(lax.ppermute, axis_name="row", perm=[(i, i ^ 1) for i in range(4)])
    across = functools.partial(lax.ppermute, axis_name="row", perm=[(i, i ^ 2) for i in range(4)])
    pair = functools.partial(
        lax.ppermute, axis_name="col", perm=[(i, i ^ 1) for i in range(columns)]
    )

    def up(x, hop):
        return lax.ppermute(x, "col", [(i, i + 2) for i in range(2 * hop, columns - 2)])

    def down(x, hop):
        return lax.ppermute(x, "col", [(i + 2, i) for i in range(0, columns - 2 - 2 * hop)])

    def apart(x, hop):
        rising = [(i, i + 2) for i in range(2 * hop, columns - 2)]
        falling = [(i + 2, i) for i in range(0, columns - 2 - 2 * hop)]
        return lax.ppermute(x, "col", rising + falling)

    sizes = tuple(size * width // sum(CHUNKS) for size in CHUNKS)
    starts = [sum(sizes[:h]) for h in range(len(sizes))]

    chunks, half = len(sizes), width // 2
    notes = jnp.stack([tile_rows[0], keep_rows[0], owners.reshape(blocks, count)], axis=2)
    notes = jnp.pad(notes, ((0, 0), (0, 0), (0, 5))).astype(jnp.float32)
    noted = jnp.broadcast_to(notes[..., None], (blocks, count, 8, width))
    own = [tiles[:, :, start : start + size] for start, size in zip(starts, sizes)]
    own[0] = jnp.concatenate([own[0], noted], axis=2)
    rest = tiles[:, :, half:]
    below, above = [[] for _ in sizes], [[] for _ in sizes]

    ticks = {}

    def at(tick, x):
        ticks.setdefault(tick, []).append(x)
        return x

    def after(tick, x):
        others = ticks.get(tick - 1, ())
        return lax.optimization_barrier((x, *others))[0] if others else x

    def send(tick, move, x, *more):
        return at(tick, move(after(tick, x), *more))

    swapped = []

    def swap(tick, x):
        if swapped:
            x = lax.optimization_barrier((x, swapped[-1]))[0]
        swapped.append(send(tick, core, x))
        return swapped[-1]

    base = line - 1
    hops = {}
    for h in range(chunks):
        for hop in range(line - 1):
            if h == 0:
                tick = hop
            else:
                tick = base + hop + (h - 1 if hop else max(h - 2, 0))
            hops.setdefault(tick, []).append((h, hop))

    panel = None
    sources, waiting, landed, flying = [], [], [], []

    def put(tick, pieces, group, relative):
        nonlocal panel
        panel, mark = place(pieces, panel, group, relative, half)
        at(tick, mark)

    tick = 0
    while tick <= max(hops) + 1 or waiting or landed or flying:
        for h, hop in hops.get(tick, ()):
            rising, falling = (below[h][-1], above[h][-1]) if hop else (own[h], own[h])
            if line - 1 - hop < hop:
                both = send(tick, apart, jnp.where(c // 2 >= hop, rising, falling), hop)
                below[h].append(both)
                above[h].append(both)
                continue
            below[h].append(send(tick, up, rising, hop))
            above[h].append(send(tick, down, falling, hop))
        if tick == 0:
            b_pair, b_across = [send(0, pair, own[0])], [send(0, across, own[0])]
            core_own = [swap(0, own[0]), swap(0, rest)]
            put(0, [own[0], rest], 1, 0)
            put(0, core_own, 1, 1)
        if tick == 1:
            b_pair.append(send(1, pair, rest))
            b_across.append(send(1, across, rest))
            core_pair, core_across = [swap(1, b_pair[0])], [swap(1, b_across[0])]
        if tick == 2:
            b_diagonal = [send(2, across, b_pair[0]), send(2, pair, b_across[1])]
            core_pair.append(swap(2, b_pair[1]))
            core_across.append(swap(2, b_across[1]))
            put(2, b_pair, 0, 0)
            put(2, b_across, 1, 2)
            put(2, core_pair, 0, 1)
            put(2, core_across, 1, 3)
        if tick == max(base, 3):
            core_diagonal = [swap(tick, x) for x in b_diagonal]
            put(tick, b_diagonal, 0, 2)
            put(tick, core_diagonal, 0, 3)
            known = [
                x[0][:, :, half : half + 3, 0]
                for x in (
                    b_pair,
                    own,
                    core_pair,
                    core_own,
                    b_diagonal,
                    b_across,
                    core_diagonal,
                    core_across,
                )
            ]
            meta = jnp.transpose(jnp.stack(known), (0, 3, 1, 2)).astype(jnp.int32).reshape(-1)
            levels = jnp.stack(
                [x[:, :, half, 0] for x in below[0][::-1] + [own[0]] + above[0]]
            )
            levels = levels.astype(jnp.int32).reshape(-1)
            plan = make_plan(me, meta, levels, line, blocks, count)
        for h in range(chunks):
            if tick == max(base, 3) if h == 0 else (h, line - 2) in hops.get(tick - 1, ()):
                gathered = below[h][::-1] + [own[h]] + above[h]
                for start in range(0, sizes[h], ROWS):
                    waiting.append((gathered, start, min(ROWS, sizes[h])))
        if flying and flying[0][0] < tick:
            _, mine, other = flying.pop(0)
            inflated = inflate(mine, other)
            opposite = send(tick, across, inflated)
            sources += [inflated, core(inflated), opposite, core(opposite)]
        if landed and landed[0][0] < tick:
            _, theirs, mine = landed.pop(0)
            flying.append((tick, mine, send(tick, pair, theirs)))
        many = len(waiting) if tick > max(hops) else 1
        for i, (gathered, start, rows) in enumerate(waiting[:many]):
            theirs, mine = product(me, plan, panel, gathered, line, start, rows)
            if i == 0:
                at(tick, theirs)
            landed.append((tick, theirs, mine))
        waiting = waiting[many:]
        tick += 1
    sizes = tuple(min(ROWS, size) for size in sizes for _ in range(0, size, ROWS))
    scale = float(4 * TR * width)
    owned = owned_tiles(me, meta, sources, sizes, count, scale)
    return owned[None, None]


def solution(mesh):
    placed = (
        P("row", "col", None, None, None),
        P("row", "col", None),
        P("row", "col", None),
        P("row", "col", None),
    )
    return jax.shard_map(
        functools.partial(on_device, mesh.shape["col"]),
        mesh=mesh,
        in_specs=placed,
        out_specs=P("row", "col", None, None, None),
        check_vma=False,
    )
```

time: 643 us -> 456 us (0.71)
  blocking collectives: 81.9 us -> 0 us
  waiting for transfers between devices: 264 us -> 200 us
  Pallas kernels: 176 us -> 153 us
  starting transfers between devices: 82.4 us -> 67.3 us
  other arithmetic: 21.4 us -> 7.51 us
  local copies, waits for them, and re-layouts: 13.3 us -> 24.2 us
    ppermute x15 -> x8, waiting for transfers between devices: 121 us -> 29.7 us  [down(): lax.ppermute(x, 'col', [(i + 2, i) for i in range(0, columns - 2 - 2 * ho...]
    unnamed x1 -> x0, blocking collectives: 81.9 us -> none
    ppermute x28 -> x38, waiting for transfers between devices: 134 us -> 169 us  [the longest x24 167 us: send(): return at(tick, move(after(tick, x), *more))]
    pallas_call x14 -> x20, Pallas kernels: 176 us -> 153 us  [the longest x5 82.7 us: product(): pl.pallas_call(functools.partial(product_kernel, line, start), grid=(2, b...]
    reduce_sum x20 -> x0, other arithmetic: 19.9 us -> none  [on_device(): sums = sums + sum((jnp.sum(x, axis=(1, 2)) for x in four))]
    slice x4 -> x22, local copies, waits for them, and re-layouts: 5.5 us -> 16.2 us  [the longest x14 7.03 us: on_device(): x[0][:, :, half:half + 3, 0]]
    ppermute x15 -> x8, starting transfers between devices: 19.5 us -> 10.3 us  [down(): lax.ppermute(x, 'col', [(i + 2, i) for i in range(0, columns - 2 - 2 * ho...]
    ppermute x15 -> x8, waiting for transfers between devices: 9.06 us -> 0.88 us  [up(): lax.ppermute(x, 'col', [(i, i + 2) for i in range(2 * hop, columns - 2)])]
  transfers between devices with their start and end apart: 58 -> 54, of which waited for: 16 -> 19; matrix products, arithmetic and copies ran while one was open for 4% -> 4% of each run, Pallas kernels for 27% -> 31%
where the time goes in v2:
time: 456 us; the launch traced here: 452 us
  waiting for transfers between devices  200 us (44%)
  Pallas kernels  153 us (34%)
  starting transfers between devices  67.3 us (15%)
  local copies, waits for them, and re-layouts  24.2 us (5%)
  other arithmetic  7.51 us (2%)
    ppermute x24, waiting for transfers between devices, send(): return at(tick, move(after(tick, x), *more))  167 us
    pallas_call x5, Pallas kernels, product(): pl.pallas_call(functools.partial(product_kernel, line, start), grid=(2, b...  82.7 us
    pallas_call x8, Pallas kernels, place(): pl.pallas_call(functools.partial(place_kernel, len(pieces)), grid=(blocks...  38.9 us
    ppermute x8, waiting for transfers between devices, down(): lax.ppermute(x, 'col', [(i + 2, i) for i in range(0, columns - 2 - 2 * ho...  29.7 us
    ppermute x8, starting transfers between devices, up(): lax.ppermute(x, 'col', [(i, i + 2) for i in range(2 * hop, columns - 2)])  25.5 us
    ppermute x24, starting transfers between devices, send(): return at(tick, move(after(tick, x), *more))  24.7 us
    pallas_call x5, Pallas kernels, inflate(): pl.pallas_call(inflate_kernel, grid=(blocks,), out_shape=jax.ShapeDtypeSt...  17.6 us
    ppermute x8, starting transfers between devices, down(): lax.ppermute(x, 'col', [(i + 2, i) for i in range(0, columns - 2 - 2 * ho...  10.3 us
  transfers between devices with their start and end apart: 54, of which 19 were waited for; matrix products, arithmetic and copies ran while one was open for 4% of the time, Pallas kernels for 31%

profile of v2, /device:TPU:0, one launch (start us, length us, event | category | flops | bytes accessed | tf_op | source)
XLA Modules:
  0.0 452.1 jit_solution(14630055891835884691)
XLA Ops:
  0.5 1.3 reduce.13
  2.7 3.9 fusion.1
  7.5 2.6 collective-permute-start
  10.0 1.5 collective-permute-start.5
  11.6 1.3 collective-permute-start.4
  12.9 4.7 %collective-permute-start.3 = (f32[4,4,136,256]{3,2,1,0:T(8,128)S(1)}, f32[4,4,136,256]{3,2,1,0:T(8,128)S(1)}, u32[]{:S(2)}, u32[]{:S(2)}) collective-permute-start(f32[4,4,136,256]{3,2,1,0:T(8,128)S(1)} %pad_maximum_fusion.refs_0_.refs_3_), channel_id=1, source_target_pairs={{0,2},{1,3},{2,4},{3,5},{4,6},{5,7},{8,10},{9,11},{10,12},{11,13},... | collective-permute-start | bytes 6684680 | tf_op jit(solution)/shard_map/ppermute | solution.py:404
  17.6 1.4 copy-done.13
  18.9 4.8 %place.8 = (bf16[2,4,4,4,2,256,256]{6,5,4,3,2,1,0:T(8,128)(2,1)}, f32[8,128]{1,0:T(8,128)}) custom-call(f32[4,4,136,256]{3,2,1,0:T(8,128)} %copy-done.1, f32[4,4,128,256]{3,2,1,0:T(8,128)} %get-tuple-element.82.refs_1_), custom_call_target="tpu_custom_call" | custom-call | flops 1048576 | bytes 8388608 | tf_op jit(solution)/shard_map/place/pallas_call | solution.py:49
  23.7 35.5 %collective-permute-done.refs_0_ = f32[4,4,136,256]{3,2,1,0:T(8,128)} collective-permute-done((f32[4,4,136,256]{3,2,1,0:T(8,128)S(1)}, f32[4,4,136,256]{3,2,1,0:T(8,128)}, u32[]{:S(2)}, u32[]{:S(2)}) %collective-permute-start) | collective-permute-done | bytes 2228256 | tf_op jit(solution)/shard_map/ppermute | solution.py:437
  59.2 4.8 %place.9 = (bf16[2,4,4,4,2,256,256]{6,5,4,3,2,1,0:T(8,128)(2,1)}, f32[8,128]{1,0:T(8,128)}) custom-call(f32[4,4,136,256]{3,2,1,0:T(8,128)} %copy-done.13, f32[4,4,128,256]{3,2,1,0:T(8,128)} %collective-permute-done.2.refs_1_, bf16[2,4,4,4,2,256,256]{6,5,4,3,2,1,0:T(8,128)(2,1)} %get-tuple-element.77.refs_2_), custom_call_target="tpu_custom_call", output_to_operand_aliasing={{0}: (2, {})} | custom-call | flops 1048576 | bytes 8388608 | tf_op jit(solution)/shard_map/place/pallas_call | solution.py:49
  64.9 4.7 %collective-permute-done.6.refs_0_ = f32[4,4,136,256]{3,2,1,0:T(8,128)} collective-permute-done((f32[4,4,136,256]{3,2,1,0:T(8,128)}, f32[4,4,136,256]{3,2,1,0:T(8,128)}, u32[]{:S(2)}, u32[]{:S(2)}) %collective-permute-start.6) | collective-permute-done | bytes 2228256 | tf_op jit(solution)/shard_map/ppermute | solution.py:437
  70.5 1.3 collective-permute-start.8
  72.9 1.5 collective-permute-start.10
  74.4 45.7 %collective-permute-done.9.refs_1_ = f32[4,4,128,256]{3,2,1,0:T(8,128)} collective-permute-done((f32[4,4,128,256]{3,2,1,0:T(8,128)}, f32[4,4,128,256]{3,2,1,0:T(8,128)}, u32[]{:S(2)}, u32[]{:S(2)}) %collective-permute-start.9) | collective-permute-done | bytes 2097184 | tf_op jit(solution)/shard_map/ppermute | solution.py:437
  120.8 5.7 %collective-permute-done.8.refs_5_ = f32[4,4,136,256]{3,2,1,0:T(8,128)} collective-permute-done((f32[4,4,136,256]{3,2,1,0:T(8,128)S(1)}, f32[4,4,136,256]{3,2,1,0:T(8,128)}, u32[]{:S(2)}, u32[]{:S(2)}) %collective-permute-start.8) | collective-permute-done | bytes 2228256 | tf_op jit(solution)/shard_map/ppermute | solution.py:407
  127.0 3.3 broadcast_select_fusion
  130.3 1.3 collective-permute-start.15
  133.0 4.8 %place.10 = (bf16[2,4,4,4,2,256,256]{6,5,4,3,2,1,0:T(8,128)(2,1)}, f32[8,128]{1,0:T(8,128)}) custom-call(f32[4,4,136,256]{3,2,1,0:T(8,128)} %collective-permute-done.refs_0_, f32[4,4,128,256]{3,2,1,0:T(8,128)} %collective-permute-done.9.refs_1_, bf16[2,4,4,4,2,256,256]{6,5,4,3,2,1,0:T(8,128)(2,1)} %get-tuple-element.93.refs_2_), custom_call_target="tpu_custom_call", output_to_operand_aliasing={{0}: (2, {})} | custom-call | flops 1048576 | bytes 8388608 | tf_op jit(solution)/shard_map/place/pallas_call | solution.py:49
  137.8 4.9 %place.11 = (bf16[2,4,4,4,2,256,256]{6,5,4,3,2,1,0:T(8,128)(2,1)}, f32[8,128]{1,0:T(8,128)}) custom-call(f32[4,4,136,256]{3,2,1,0:T(8,128)} %collective-permute-done.5.refs_0_, f32[4,4,128,256]{3,2,1,0:T(8,128)} %collective-permute-done.10.refs_1_, bf16[2,4,4,4,2,256,256]{6,5,4,3,2,1,0:T(8,128)(2,1)} %get-tuple-element.95.refs_2_), custom_call_target="tpu_custom_call", output_to_operand_aliasing={{0}: (2, {})} | custom-call | flops 1048576 | bytes 8388608 | tf_op jit(solution)/shard_map/place/pallas_call | solution.py:49
  142.6 4.8 %place.12 = (bf16[2,4,4,4,2,256,256]{6,5,4,3,2,1,0:T(8,128)(2,1)}, f32[8,128]{1,0:T(8,128)}) custom-call(f32[4,4,136,256]{3,2,1,0:T(8,128)} %collective-permute-done.6.refs_0_, f32[4,4,128,256]{3,2,1,0:T(8,128)} %collective-permute-done.13.refs_1_, bf16[2,4,4,4,2,256,256]{6,5,4,3,2,1,0:T(8,128)(2,1)} %get-tuple-element.97.refs_2_), custom_call_target="tpu_custom_call", output_to_operand_aliasing={{0}: (2, {})} | custom-call | flops 1048576 | bytes 8388608 | tf_op jit(solution)/shard_map/place/pallas_call | solution.py:49
  147.4 30.2 %collective-permute-done.12.refs_0_ = f32[4,4,136,256]{3,2,1,0:T(8,128)} collective-permute-done((f32[4,4,136,256]{3,2,1,0:T(8,128)}, f32[4,4,136,256]{3,2,1,0:T(8,128)}, u32[]{:S(2)}, u32[]{:S(2)}) %collective-permute-start.12) | collective-permute-done | bytes 2228256 | tf_op jit(solution)/shard_map/ppermute | solution.py:437
  177.7 5.2 %place.13 = (bf16[2,4,4,4,2,256,256]{6,5,4,3,2,1,0:T(8,128)(2,1)}, f32[8,128]{1,0:T(8,128)}) custom-call(f32[4,4,136,256]{3,2,1,0:T(8,128)} %copy-done.14, f32[4,4,128,256]{3,2,1,0:T(8,128)} %collective-permute-done.14.refs_1_, bf16[2,4,4,4,2,256,256]{6,5,4,3,2,1,0:T(8,128)(2,1)} %get-tuple-element.99.refs_2_), custom_call_target="tpu_custom_call", output_to_operand_aliasing={{0}: (2, {})} | custom-call | flops 1048576 | bytes 8388608 | tf_op jit(solution)/shard_map/place/pallas_call | solution.py:49
  183.8 1.2 fusion
  196.2 1.3 collective-permute-start.22
  197.5 5.4 %collective-permute-start.21 = (f32[4,4,32,256]{3,2,1,0:T(8,128)}, f32[4,4,32,256]{3,2,1,0:T(8,128)}, u32[]{:S(2)}, u32[]{:S(2)}) collective-permute-start(f32[4,4,32,256]{3,2,1,0:T(8,128)} %get-tuple-element.112.refs_3_), channel_id=1, source_target_pairs={{0,2},{1,3},{2,4},{3,5},{4,6},{5,7},{8,10},{9,11},{10,12},{11,13},... | collective-permute-start | bytes 1572872 | tf_op jit(solution)/shard_map/ppermute | solution.py:404
  202.9 1.3 collective-permute-start.20
  204.2 5.5 %collective-permute-start.19 = (f32[4,4,64,256]{3,2,1,0:T(8,128)S(1)}, f32[4,4,64,256]{3,2,1,0:T(8,128)}, u32[]{:S(2)}, u32[]{:S(2)}) collective-permute-start(f32[4,4,64,256]{3,2,1,0:T(8,128)S(1)} %slice.95.refs_3_), channel_id=1, source_target_pairs={{0,2},{1,3},{2,4},{3,5},{4,6},{5,7},{8,10},{9,11},{10,12},{11,13},... | collective-permute-start | bytes 3145736 | tf_op jit(solution)/shard_map/ppermute | solution.py:404
  209.7 4.8 %place.14 = (bf16[2,4,4,4,2,256,256]{6,5,4,3,2,1,0:T(8,128)(2,1)}, f32[8,128]{1,0:T(8,128)}) custom-call(f32[4,4,136,256]{3,2,1,0:T(8,128)} %collective-permute-done.12.refs_0_, f32[4,4,128,256]{3,2,1,0:T(8,128)} %collective-permute-done.16.refs_1_, bf16[2,4,4,4,2,256,256]{6,5,4,3,2,1,0:T(8,128)(2,1)} %get-tuple-element.106.refs_2_), custom_call_target="tpu_custom_call", output_to_operand_aliasing={{0}: (2, {})} | custom-call | flops 1048576 | bytes 8388608 | tf_op jit(solution)/shard_map/place/pallas_call | solution.py:49
  216.2 5.9 %plan.1 = (s32[1040]{0:T(1024)}, s32[64]{0:T(128)}) custom-call(s32[2]{0:T(128)} %pad_add_fusion.1.me_ref, s32[384]{0:T(512)} %reshape.16.meta_ref, s32[112]{0:T(128)} %convert_element_type.20.levels_ref), custom_call_target="tpu_custom_call" | custom-call | tf_op jit(solution)/shard_map/plan/pallas_call | solution.py:113
  222.1 1.3 copy-done.22
  223.4 4.9 %place.15 = (bf16[2,4,4,4,2,256,256]{6,5,4,3,2,1,0:T(8,128)(2,1)}, f32[8,128]{1,0:T(8,128)}) custom-call(f32[4,4,136,256]{3,2,1,0:T(8,128)} %collective-permute-done.17.refs_0_, f32[4,4,128,256]{3,2,1,0:T(8,128)} %copy-done.22, bf16[2,4,4,4,2,256,256]{6,5,4,3,2,1,0:T(8,128)(2,1)} %get-tuple-element.107.refs_2_), custom_call_target="tpu_custom_call", output_to_operand_aliasing={{0}: (2, {})} | custom-call | flops 1048576 | bytes 8388608 | tf_op jit(solution)/shard_map/place/pallas_call | solution.py:49
  228.3 18.4 %product.5 = (f32[4,4,64,256]{3,2,1,0:T(8,128)}, f32[4,4,64,256]{3,2,1,0:T(8,128)}) custom-call(s32[2]{0:T(128)} %pad_add_fusion.1.me_ref, s32[1040]{0:T(1024)} %get-tuple-element.102.plan_ref, s32[64]{0:T(128)} %get-tuple-element.103.kept_ref, bf16[128,2,256,256]{3,2,1,0:T(8,128)(2,1)} %bitcast.43, f32[4,4,136,256]{3,2,1,0:T(8,128)} %copy-done, ...), custom_call_target="tpu_custom_call" | custom-call | flops 6442450944 | bytes 16777216 | tf_op jit(solution)/shard_map/product/pallas_call | solution.py:236
  246.8 3.6 collective-permute-start.23
  251.1 1.3 collective-permute-start.26
  252.4 1.3 collective-permute-start.28
  253.7 7.0 %collective-permute-start.27 = (f32[4,4,32,256]{3,2,1,0:T(8,128)S(1)}, f32[4,4,32,256]{3,2,1,0:T(8,128)S(1)}, u32[]{:S(2)}, u32[]{:S(2)}) collective-permute-start(f32[4,4,32,256]{3,2,1,0:T(8,128)S(1)} %copy-done.21), channel_id=1, source_target_pairs={{0,2},{1,3},{2,4},{3,5},{4,6},{5,7},{8,10},{9,11},{10,12},{11,13},... | collective-permute-start | bytes 1572872 | tf_op jit(solution)/shard_map/ppermute | solution.py:404
  260.7 18.3 %product.6 = (f32[4,4,64,256]{3,2,1,0:T(8,128)}, f32[4,4,64,256]{3,2,1,0:T(8,128)}) custom-call(s32[2]{0:T(128)} %pad_add_fusion.1.me_ref, s32[1040]{0:T(1024)} %get-tuple-element.102.plan_ref, s32[64]{0:T(128)} %get-tuple-element.103.kept_ref, bf16[128,2,256,256]{3,2,1,0:T(8,128)(2,1)} %bitcast.44, f32[4,4,136,256]{3,2,1,0:T(8,128)} %copy-done, ...), custom_call_target="tpu_custom_call" | custom-call | flops 6442450944 | bytes 16777216 | tf_op jit(solution)/shard_map/product/pallas_call | solution.py:236
  279.0 11.1 %collective-permute-done.28.refs_4_ = f32[4,4,32,256]{3,2,1,0:T(8,128)S(1)} collective-permute-done((f32[4,4,32,256]{3,2,1,0:T(8,128)S(1)}, f32[4,4,32,256]{3,2,1,0:T(8,128)S(1)}, u32[]{:S(2)}, u32[]{:S(2)}) %collective-permute-start.28) | collective-permute-done | bytes 524320 | tf_op jit(solution)/shard_map/ppermute | solution.py:407
  291.4 3.7 inflate.5.refs_0_
  297.6 1.3 collective-permute-start.33
  299.6 1.3 collective-permute-start.35
  300.9 17.5 %collective-permute-done.31.other_ref = f32[4,4,64,256]{3,2,1,0:T(8,128)} collective-permute-done((f32[4,4,64,256]{3,2,1,0:T(8,128)}, f32[4,4,64,256]{3,2,1,0:T(8,128)}, u32[]{:S(2)}, u32[]{:S(2)}) %collective-permute-start.31) | collective-permute-done | bytes 1048608 | tf_op jit(solution)/shard_map/ppermute | solution.py:437
  318.4 3.7 inflate.6.refs_4_
  322.0 11.5 %collective-permute-done.35.refs_5_ = f32[4,4,32,256]{3,2,1,0:T(8,128)S(1)} collective-permute-done((f32[4,4,32,256]{3,2,1,0:T(8,128)}, f32[4,4,32,256]{3,2,1,0:T(8,128)S(1)}, u32[]{:S(2)}, u32[]{:S(2)}) %collective-permute-start.35) | collective-permute-done | bytes 524320 | tf_op jit(solution)/shard_map/ppermute | solution.py:407
  334.4 1.3 collective-permute-start.38
  336.4 1.3 collective-permute-start.40
  337.8 18.3 %product.7 = (f32[4,4,64,256]{3,2,1,0:T(8,128)}, f32[4,4,64,256]{3,2,1,0:T(8,128)}) custom-call(s32[2]{0:T(128)} %pad_add_fusion.1.me_ref, s32[1040]{0:T(1024)} %get-tuple-element.102.plan_ref, s32[64]{0:T(128)} %get-tuple-element.103.kept_ref, bf16[128,2,256,256]{3,2,1,0:T(8,128)(2,1)} %bitcast.45, f32[4,4,64,256]{3,2,1,0:T(8,128)} %copy-done.9, ...), custom_call_target="tpu_custom_call" | custom-call | flops 6442450944 | bytes 16777216 | tf_op jit(solution)/shard_map/product/pallas_call | solution.py:236
  356.2 1.3 collective-permute-done.40.refs_5_
  357.5 2.9 collective-permute-start.41
  360.5 1.5 collective-permute-start.43
  362.0 13.9 %product.8 = (f32[4,4,32,256]{3,2,1,0:T(8,128)}, f32[4,4,32,256]{3,2,1,0:T(8,128)}) custom-call(s32[2]{0:T(128)} %pad_add_fusion.1.me_ref, s32[1040]{0:T(1024)} %get-tuple-element.102.plan_ref, s32[64]{0:T(128)} %get-tuple-element.103.kept_ref, bf16[128,2,256,256]{3,2,1,0:T(8,128)(2,1)} %bitcast.46, f32[4,4,32,256]{3,2,1,0:T(8,128)} %copy-done.15, ...), custom_call_target="tpu_custom_call" | custom-call | flops 3221225472 | bytes 16777216 | tf_op jit(solution)/shard_map/product/pallas_call | solution.py:236
  375.9 4.1 collective-permute-done.41.other_ref
  381.0 3.6 inflate.7.refs_8_
  385.7 1.7 collective-permute-start.46
  387.5 13.9 %product.9 = (f32[4,4,32,256]{3,2,1,0:T(8,128)}, f32[4,4,32,256]{3,2,1,0:T(8,128)}) custom-call(s32[2]{0:T(128)} %pad_add_fusion.1.me_ref, s32[1040]{0:T(1024)} %get-tuple-element.102.plan_ref, s32[64]{0:T(128)} %get-tuple-element.103.kept_ref, bf16[128,2,256,256]{3,2,1,0:T(8,128)(2,1)} %bitcast.47, f32[4,4,32,256]{3,2,1,0:T(8,128)} %copy-done.16, ...), custom_call_target="tpu_custom_call" | custom-call | flops 3221225472 | bytes 16777216 | tf_op jit(solution)/shard_map/product/pallas_call | solution.py:236
  401.4 4.7 %collective-permute-done.44.refs_10_ = f32[4,264,256]{2,1,0:T(8,128)S(1)} collective-permute-done((f32[4,264,256]{2,1,0:T(8,128)}, f32[4,264,256]{2,1,0:T(8,128)S(1)}, u32[]{:S(2)}, u32[]{:S(2)}) %collective-permute-start.44) | collective-permute-done | bytes 1081376 | tf_op jit(solution)/shard_map/ppermute | solution.py:437
  406.1 1.5 collective-permute-start.50
  408.1 3.3 inflate.8.refs_12_
  412.4 3.9 collective-permute-done.50.other_ref
  416.4 3.3 inflate.9.refs_16_
  419.7 6.6 %collective-permute-done.48.refs_14_ = f32[4,136,256]{2,1,0:T(8,128)} collective-permute-done((f32[4,136,256]{2,1,0:T(8,128)}, f32[4,136,256]{2,1,0:T(8,128)}, u32[]{:S(2)}, u32[]{:S(2)}) %collective-permute-start.48) | collective-permute-done | bytes 557088 | tf_op jit(solution)/shard_map/ppermute | solution.py:437
  428.6 12.9 %collective-permute-done.52.refs_18_ = f32[4,136,256]{2,1,0:T(8,128)S(1)} collective-permute-done((f32[4,136,256]{2,1,0:T(8,128)}, f32[4,136,256]{2,1,0:T(8,128)S(1)}, u32[]{:S(2)}, u32[]{:S(2)}) %collective-permute-start.52) | collective-permute-done | bytes 557088 | tf_op jit(solution)/shard_map/ppermute | solution.py:437
  441.7 1.9 collective-permute-done.53.refs_19_
  444.4 7.5 %owned.1 = f32[32,256,256]{2,1,0:T(8,128)} custom-call(s32[2]{0:T(128)} %pad_add_fusion.1.me_ref, s32[384]{0:T(512)} %reshape.16.meta_ref, f32[4,264,256]{2,1,0:T(8,128)} %inflate.5.refs_0_, f32[4,264,256]{2,1,0:T(8,128)} %collective-permute-done.24.refs_1_, f32[4,264,256]{2,1,0:T(8,128)} %collective-permute-done.29.refs_2_, ...), custom_call_target="tpu_custom_call" | custom-call | flops 2097152 | bytes 16777216 | tf_op jit(solution)/shard_map/owned/pallas_call | solution.py:366
  (194 shorter events, 35.2 us)
Async XLA Ops:
  7.0 10.6 %collective-permute-start.1 = (f32[4,4,136,256]{3,2,1,0:T(8,128)S(1)}, f32[4,4,136,256]{3,2,1,0:T(8,128)S(1)}, u32[]{:S(2)}, u32[]{:S(2)}) collective-permute-start(f32[4,4,136,256]{3,2,1,0:T(8,128)S(1)} %pad_maximum_fusion.refs_0_.refs_3_), channel_id=1, source_target_pairs={{0,8},{8,0},{16,24},{24,16},{1,9},{9,1},{17,25},{25,17},{2,10},{10... | collective-permute-start | bytes 6684680 | tf_op jit(solution)/shard_map/ppermute | solution.py:437
  7.5 51.7 %collective-permute-start = (f32[4,4,136,256]{3,2,1,0:T(8,128)S(1)}, f32[4,4,136,256]{3,2,1,0:T(8,128)}, u32[]{:S(2)}, u32[]{:S(2)}) collective-permute-start(f32[4,4,136,256]{3,2,1,0:T(8,128)S(1)} %pad_maximum_fusion.refs_0_.refs_3_), channel_id=1, source_target_pairs={{0,1},{1,0},{2,3},{3,2},{4,5},{5,4},{6,7},{7,6},{8,9},{9,8},{10,11... | collective-permute-start | bytes 6684680 | tf_op jit(solution)/shard_map/ppermute | solution.py:437
  10.0 53.9 %collective-permute-start.5 = (f32[4,4,136,256]{3,2,1,0:T(8,128)S(1)}, f32[4,4,136,256]{3,2,1,0:T(8,128)}, u32[]{:S(2)}, u32[]{:S(2)}) collective-permute-start(f32[4,4,136,256]{3,2,1,0:T(8,128)S(1)} %pad_maximum_fusion.refs_0_.refs_3_), channel_id=1, source_target_pairs={{0,16},{8,24},{16,0},{24,8},{1,17},{9,25},{17,1},{25,9},{2,18},{10... | collective-permute-start | bytes 6684680 | tf_op jit(solution)/shard_map/ppermute | solution.py:437
  11.6 52.4 %collective-permute-start.4 = (f32[4,4,136,256]{3,2,1,0:T(8,128)S(1)}, f32[4,4,136,256]{3,2,1,0:T(8,128)S(1)}, u32[]{:S(2)}, u32[]{:S(2)}) collective-permute-start(f32[4,4,136,256]{3,2,1,0:T(8,128)S(1)} %pad_maximum_fusion.refs_0_.refs_3_), channel_id=1, source_target_pairs={{2,0},{3,1},{4,2},{5,3},{6,4},{7,5},{10,8},{11,9},{12,10},{13,11},... | collective-permute-start | bytes 6684680 | tf_op jit(solution)/shard_map/ppermute | solution.py:407
  12.9 52.0 %collective-permute-start.3 = (f32[4,4,136,256]{3,2,1,0:T(8,128)S(1)}, f32[4,4,136,256]{3,2,1,0:T(8,128)S(1)}, u32[]{:S(2)}, u32[]{:S(2)}) collective-permute-start(f32[4,4,136,256]{3,2,1,0:T(8,128)S(1)} %pad_maximum_fusion.refs_0_.refs_3_), channel_id=1, source_target_pairs={{0,2},{1,3},{2,4},{3,5},{4,6},{5,7},{8,10},{9,11},{10,12},{11,13},... | collective-permute-start | bytes 6684680 | tf_op jit(solution)/shard_map/ppermute | solution.py:404
  18.9 40.3 %collective-permute-start.2 = (f32[4,4,128,256]{3,2,1,0:T(8,128)}, f32[4,4,128,256]{3,2,1,0:T(8,128)}, u32[]{:S(2)}, u32[]{:S(2)}) collective-permute-start(f32[4,4,128,256]{3,2,1,0:T(8,128)} %get-tuple-element.82.refs_1_), channel_id=1, source_target_pairs={{0,8},{8,0},{16,24},{24,16},{1,9},{9,1},{17,25},{25,17},{2,10},{10... | collective-permute-start | bytes 6291464 | tf_op jit(solution)/shard_map/ppermute | solution.py:437
  64.0 56.8 %copy-start.4 = (f32[4,4,136,256]{3,2,1,0:T(8,128)}, f32[4,4,136,256]{3,2,1,0:T(8,128)S(1)}, u32[]{:S(2)}) copy-start(f32[4,4,136,256]{3,2,1,0:T(8,128)S(1)} %collective-permute-done.4.refs_4_) | copy-start | bytes 6684676
  64.9 4.7 %collective-permute-start.6 = (f32[4,4,136,256]{3,2,1,0:T(8,128)}, f32[4,4,136,256]{3,2,1,0:T(8,128)}, u32[]{:S(2)}, u32[]{:S(2)}) collective-permute-start(f32[4,4,136,256]{3,2,1,0:T(8,128)} %collective-permute-done.refs_0_), channel_id=1, source_target_pairs={{0,8},{8,0},{16,24},{24,16},{1,9},{9,1},{17,25},{25,17},{2,10},{10... | collective-permute-start | bytes 6684680 | tf_op jit(solution)/shard_map/ppermute | solution.py:437
  69.6 50.5 %collective-permute-start.11 = (f32[4,4,136,256]{3,2,1,0:T(8,128)}, f32[4,4,136,256]{3,2,1,0:T(8,128)S(1)}, u32[]{:S(2)}, u32[]{:S(2)}) collective-permute-start(f32[4,4,136,256]{3,2,1,0:T(8,128)} %collective-permute-done.5.refs_0_), channel_id=1, source_target_pairs={{0,8},{8,0},{16,24},{24,16},{1,9},{9,1},{17,25},{25,17},{2,10},{10... | collective-permute-start | bytes 6684680 | tf_op jit(solution)/shard_map/ppermute | solution.py:437
  69.7 51.1 %collective-permute-start.7 = (f32[4,4,136,256]{3,2,1,0:T(8,128)}, f32[4,4,136,256]{3,2,1,0:T(8,128)S(1)}, u32[]{:S(2)}, u32[]{:S(2)}) collective-permute-start(f32[4,4,136,256]{3,2,1,0:T(8,128)} %copy-done.5), channel_id=1, source_target_pairs={{2,4},{3,5},{4,6},{5,7},{10,12},{11,13},{12,14},{13,15},{18,20},{1... | collective-permute-start | bytes 6684680 | tf_op jit(solution)/shard_map/ppermute | solution.py:404
  70.5 56.0 %collective-permute-start.8 = (f32[4,4,136,256]{3,2,1,0:T(8,128)S(1)}, f32[4,4,136,256]{3,2,1,0:T(8,128)}, u32[]{:S(2)}, u32[]{:S(2)}) collective-permute-start(f32[4,4,136,256]{3,2,1,0:T(8,128)S(1)} %collective-permute-done.4.refs_4_), channel_id=1, source_target_pairs={{2,0},{3,1},{4,2},{5,3},{10,8},{11,9},{12,10},{13,11},{18,16},{19,... | collective-permute-start | bytes 6684680 | tf_op jit(solution)/shard_map/ppermute | solution.py:407
  71.8 48.3 %collective-permute-start.9 = (f32[4,4,128,256]{3,2,1,0:T(8,128)}, f32[4,4,128,256]{3,2,1,0:T(8,128)}, u32[]{:S(2)}, u32[]{:S(2)}) collective-permute-start(f32[4,4,128,256]{3,2,1,0:T(8,128)} %get-tuple-element.82.refs_1_), channel_id=1, source_target_pairs={{0,1},{1,0},{2,3},{3,2},{4,5},{5,4},{6,7},{7,6},{8,9},{9,8},{10,11... | collective-permute-start | bytes 6291464 | tf_op jit(solution)/shard_map/ppermute | solution.py:437
  72.9 47.9 %collective-permute-start.10 = (f32[4,4,128,256]{3,2,1,0:T(8,128)}, f32[4,4,128,256]{3,2,1,0:T(8,128)}, u32[]{:S(2)}, u32[]{:S(2)}) collective-permute-start(f32[4,4,128,256]{3,2,1,0:T(8,128)} %get-tuple-element.82.refs_1_), channel_id=1, source_target_pairs={{0,16},{8,24},{16,0},{24,8},{1,17},{9,25},{17,1},{25,9},{2,18},{10... | collective-permute-start | bytes 6291464 | tf_op jit(solution)/shard_map/ppermute | solution.py:437
  126.5 5.1 %collective-permute-start.13 = (f32[4,4,128,256]{3,2,1,0:T(8,128)}, f32[4,4,128,256]{3,2,1,0:T(8,128)}, u32[]{:S(2)}, u32[]{:S(2)}) collective-permute-start(f32[4,4,128,256]{3,2,1,0:T(8,128)} %collective-permute-done.9.refs_1_), channel_id=1, source_target_pairs={{0,8},{8,0},{16,24},{24,16},{1,9},{9,1},{17,25},{25,17},{2,10},{10... | collective-permute-start | bytes 6291464 | tf_op jit(solution)/shard_map/ppermute | solution.py:437
  126.5 51.2 %collective-permute-start.12 = (f32[4,4,136,256]{3,2,1,0:T(8,128)}, f32[4,4,136,256]{3,2,1,0:T(8,128)}, u32[]{:S(2)}, u32[]{:S(2)}) collective-permute-start(f32[4,4,136,256]{3,2,1,0:T(8,128)} %collective-permute-done.refs_0_), channel_id=1, source_target_pairs={{0,16},{8,24},{16,0},{24,8},{1,17},{9,25},{17,1},{25,9},{2,18},{10... | collective-permute-start | bytes 6684680 | tf_op jit(solution)/shard_map/ppermute | solution.py:437
  130.3 52.7 %collective-permute-start.15 = (f32[4,4,136,256]{3,2,1,0:T(8,128)}, f32[4,4,136,256]{3,2,1,0:T(8,128)S(1)}, u32[]{:S(2)}, u32[]{:S(2)}) collective-permute-start(f32[4,4,136,256]{3,2,1,0:T(8,128)} %broadcast_select_fusion), channel_id=1, source_target_pairs={{4,6},{5,7},{2,0},{3,1},{12,14},{13,15},{10,8},{11,9},{20,22},{21,... | collective-permute-start | bytes 6684680 | tf_op jit(solution)/shard_map/ppermute | solution.py:412
  131.6 46.0 %collective-permute-start.14 = (f32[4,4,128,256]{3,2,1,0:T(8,128)}, f32[4,4,128,256]{3,2,1,0:T(8,128)}, u32[]{:S(2)}, u32[]{:S(2)}) collective-permute-start(f32[4,4,128,256]{3,2,1,0:T(8,128)} %collective-permute-done.10.refs_1_), channel_id=1, source_target_pairs={{0,8},{8,0},{16,24},{24,16},{1,9},{9,1},{17,25},{25,17},{2,10},{10... | collective-permute-start | bytes 6291464 | tf_op jit(solution)/shard_map/ppermute | solution.py:437
  131.9 50.9 %collective-permute-start.16 = (f32[4,4,128,256]{3,2,1,0:T(8,128)}, f32[4,4,128,256]{3,2,1,0:T(8,128)}, u32[]{:S(2)}, u32[]{:S(2)}) collective-permute-start(f32[4,4,128,256]{3,2,1,0:T(8,128)} %collective-permute-done.10.refs_1_), channel_id=1, source_target_pairs={{0,1},{1,0},{2,3},{3,2},{4,5},{5,4},{6,7},{7,6},{8,9},{9,8},{10,11... | collective-permute-start | bytes 6291464 | tf_op jit(solution)/shard_map/ppermute | solution.py:437
  183.0 11.0 %collective-permute-start.17 = (f32[4,4,136,256]{3,2,1,0:T(8,128)}, f32[4,4,136,256]{3,2,1,0:T(8,128)}, u32[]{:S(2)}, u32[]{:S(2)}) collective-permute-start(f32[4,4,136,256]{3,2,1,0:T(8,128)} %collective-permute-done.12.refs_0_), channel_id=1, source_target_pairs={{0,8},{8,0},{16,24},{24,16},{1,9},{9,1},{17,25},{25,17},{2,10},{10... | collective-permute-start | bytes 6684680 | tf_op jit(solution)/shard_map/ppermute | solution.py:437
  183.8 30.7 %copy-start.10 = (f32[4,4,64,256]{3,2,1,0:T(8,128)}, f32[4,4,64,256]{3,2,1,0:T(8,128)S(1)}, u32[]{:S(2)}) copy-start(f32[4,4,64,256]{3,2,1,0:T(8,128)S(1)} %slice.95.refs_3_) | copy-start | bytes 3145732
  194.0 28.1 %collective-permute-start.18 = (f32[4,4,128,256]{3,2,1,0:T(8,128)}, f32[4,4,128,256]{3,2,1,0:T(8,128)S(1)}, u32[]{:S(2)}, u32[]{:S(2)}) collective-permute-start(f32[4,4,128,256]{3,2,1,0:T(8,128)} %collective-permute-done.16.refs_1_), channel_id=1, source_target_pairs={{0,8},{8,0},{16,24},{24,16},{1,9},{9,1},{17,25},{25,17},{2,10},{10... | collective-permute-start | bytes 6291464 | tf_op jit(solution)/shard_map/ppermute | solution.py:437
  196.2 50.5 %collective-permute-start.22 = (f32[4,4,32,256]{3,2,1,0:T(8,128)}, f32[4,4,32,256]{3,2,1,0:T(8,128)}, u32[]{:S(2)}, u32[]{:S(2)}) collective-permute-start(f32[4,4,32,256]{3,2,1,0:T(8,128)} %get-tuple-element.112.refs_3_), channel_id=1, source_target_pairs={{2,0},{3,1},{4,2},{5,3},{6,4},{7,5},{10,8},{11,9},{12,10},{13,11},... | collective-permute-start | bytes 1572872 | tf_op jit(solution)/shard_map/ppermute | solution.py:407
  197.5 49.2 %collective-permute-start.21 = (f32[4,4,32,256]{3,2,1,0:T(8,128)}, f32[4,4,32,256]{3,2,1,0:T(8,128)}, u32[]{:S(2)}, u32[]{:S(2)}) collective-permute-start(f32[4,4,32,256]{3,2,1,0:T(8,128)} %get-tuple-element.112.refs_3_), channel_id=1, source_target_pairs={{0,2},{1,3},{2,4},{3,5},{4,6},{5,7},{8,10},{9,11},{10,12},{11,13},... | collective-permute-start | bytes 1572872 | tf_op jit(solution)/shard_map/ppermute | solution.py:404
  202.9 43.9 %collective-permute-start.20 = (f32[4,4,64,256]{3,2,1,0:T(8,128)S(1)}, f32[4,4,64,256]{3,2,1,0:T(8,128)}, u32[]{:S(2)}, u32[]{:S(2)}) collective-permute-start(f32[4,4,64,256]{3,2,1,0:T(8,128)S(1)} %slice.95.refs_3_), channel_id=1, source_target_pairs={{2,0},{3,1},{4,2},{5,3},{6,4},{7,5},{10,8},{11,9},{12,10},{13,11},... | collective-permute-start | bytes 3145736 | tf_op jit(solution)/shard_map/ppermute | solution.py:407
  204.2 42.6 %collective-permute-start.19 = (f32[4,4,64,256]{3,2,1,0:T(8,128)S(1)}, f32[4,4,64,256]{3,2,1,0:T(8,128)}, u32[]{:S(2)}, u32[]{:S(2)}) collective-permute-start(f32[4,4,64,256]{3,2,1,0:T(8,128)S(1)} %slice.95.refs_3_), channel_id=1, source_target_pairs={{0,2},{1,3},{2,4},{3,5},{4,6},{5,7},{8,10},{9,11},{10,12},{11,13},... | collective-permute-start | bytes 3145736 | tf_op jit(solution)/shard_map/ppermute | solution.py:404
  228.3 24.0 %copy-start.21 = (f32[4,4,32,256]{3,2,1,0:T(8,128)S(1)}, f32[4,4,32,256]{3,2,1,0:T(8,128)}, u32[]{:S(2)}) copy-start(f32[4,4,32,256]{3,2,1,0:T(8,128)} %get-tuple-element.118.refs_3_) | copy-start | bytes 1572868
  246.8 43.3 %collective-permute-start.23 = (f32[4,4,64,256]{3,2,1,0:T(8,128)}, f32[4,4,64,256]{3,2,1,0:T(8,128)S(1)}, u32[]{:S(2)}, u32[]{:S(2)}) collective-permute-start(f32[4,4,64,256]{3,2,1,0:T(8,128)} %get-tuple-element.115), channel_id=1, source_target_pairs={{0,1},{1,0},{2,3},{3,2},{4,5},{5,4},{6,7},{7,6},{8,9},{9,8},{10,11... | collective-permute-start | bytes 3145736 | tf_op jit(solution)/shard_map/ppermute | solution.py:437
  250.4 39.8 %collective-permute-start.25 = (f32[4,4,64,256]{3,2,1,0:T(8,128)}, f32[4,4,64,256]{3,2,1,0:T(8,128)S(1)}, u32[]{:S(2)}, u32[]{:S(2)}) collective-permute-start(f32[4,4,64,256]{3,2,1,0:T(8,128)} %collective-permute-done.19.refs_2_), channel_id=1, source_target_pairs={{2,4},{3,5},{4,6},{5,7},{10,12},{11,13},{12,14},{13,15},{18,20},{1... | collective-permute-start | bytes 3145736 | tf_op jit(solution)/shard_map/ppermute | solution.py:404
  251.1 39.1 %collective-permute-start.26 = (f32[4,4,64,256]{3,2,1,0:T(8,128)}, f32[4,4,64,256]{3,2,1,0:T(8,128)S(1)}, u32[]{:S(2)}, u32[]{:S(2)}) collective-permute-start(f32[4,4,64,256]{3,2,1,0:T(8,128)} %collective-permute-done.20.refs_4_), channel_id=1, source_target_pairs={{2,0},{3,1},{4,2},{5,3},{10,8},{11,9},{12,10},{13,11},{18,16},{19,... | collective-permute-start | bytes 3145736 | tf_op jit(solution)/shard_map/ppermute | solution.py:407
  252.4 37.7 %collective-permute-start.28 = (f32[4,4,32,256]{3,2,1,0:T(8,128)S(1)}, f32[4,4,32,256]{3,2,1,0:T(8,128)S(1)}, u32[]{:S(2)}, u32[]{:S(2)}) collective-permute-start(f32[4,4,32,256]{3,2,1,0:T(8,128)S(1)} %copy-done.21), channel_id=1, source_target_pairs={{2,0},{3,1},{4,2},{5,3},{6,4},{7,5},{10,8},{11,9},{12,10},{13,11},... | collective-permute-start | bytes 1572872 | tf_op jit(solution)/shard_map/ppermute | solution.py:407
  253.7 36.4 %collective-permute-start.27 = (f32[4,4,32,256]{3,2,1,0:T(8,128)S(1)}, f32[4,4,32,256]{3,2,1,0:T(8,128)S(1)}, u32[]{:S(2)}, u32[]{:S(2)}) collective-permute-start(f32[4,4,32,256]{3,2,1,0:T(8,128)S(1)} %copy-done.21), channel_id=1, source_target_pairs={{0,2},{1,3},{2,4},{3,5},{4,6},{5,7},{8,10},{9,11},{10,12},{11,13},... | collective-permute-start | bytes 1572872 | tf_op jit(solution)/shard_map/ppermute | solution.py:404
  295.1 23.2 %collective-permute-start.31 = (f32[4,4,64,256]{3,2,1,0:T(8,128)}, f32[4,4,64,256]{3,2,1,0:T(8,128)}, u32[]{:S(2)}, u32[]{:S(2)}) collective-permute-start(f32[4,4,64,256]{3,2,1,0:T(8,128)} %get-tuple-element.122), channel_id=1, source_target_pairs={{0,1},{1,0},{2,3},{3,2},{4,5},{5,4},{6,7},{7,6},{8,9},{9,8},{10,11... | collective-permute-start | bytes 3145736 | tf_op jit(solution)/shard_map/ppermute | solution.py:437
  295.4 38.2 %collective-permute-start.29 = (f32[4,264,256]{2,1,0:T(8,128)}, f32[4,264,256]{2,1,0:T(8,128)}, u32[]{:S(2)}, u32[]{:S(2)}) collective-permute-start(f32[4,264,256]{2,1,0:T(8,128)} %inflate.5.refs_0_), channel_id=1, source_target_pairs={{0,16},{8,24},{16,0},{24,8},{1,17},{9,25},{17,1},{25,9},{2,18},{10... | collective-permute-start | bytes 3244040 | tf_op jit(solution)/shard_map/ppermute | solution.py:437
  297.6 36.0 %collective-permute-start.33 = (f32[4,4,64,256]{3,2,1,0:T(8,128)}, f32[4,4,64,256]{3,2,1,0:T(8,128)S(1)}, u32[]{:S(2)}, u32[]{:S(2)}) collective-permute-start(f32[4,4,64,256]{3,2,1,0:T(8,128)} %broadcast_select_fusion.1), channel_id=1, source_target_pairs={{4,6},{5,7},{2,0},{3,1},{12,14},{13,15},{10,8},{11,9},{20,22},{21,... | collective-permute-start | bytes 3145736 | tf_op jit(solution)/shard_map/ppermute | solution.py:412
  298.9 23.1 %collective-permute-start.34 = (f32[4,4,32,256]{3,2,1,0:T(8,128)}, f32[4,4,32,256]{3,2,1,0:T(8,128)S(1)}, u32[]{:S(2)}, u32[]{:S(2)}) collective-permute-start(f32[4,4,32,256]{3,2,1,0:T(8,128)} %collective-permute-done.21.refs_2_), channel_id=1, source_target_pairs={{2,4},{3,5},{4,6},{5,7},{10,12},{11,13},{12,14},{13,15},{18,20},{1... | collective-permute-start | bytes 1572872 | tf_op jit(solution)/shard_map/ppermute | solution.py:404
  299.6 34.0 %collective-permute-start.35 = (f32[4,4,32,256]{3,2,1,0:T(8,128)}, f32[4,4,32,256]{3,2,1,0:T(8,128)S(1)}, u32[]{:S(2)}, u32[]{:S(2)}) collective-permute-start(f32[4,4,32,256]{3,2,1,0:T(8,128)} %collective-permute-done.22.refs_4_), channel_id=1, source_target_pairs={{2,0},{3,1},{4,2},{5,3},{10,8},{11,9},{12,10},{13,11},{18,16},{19,... | collective-permute-start | bytes 1572872 | tf_op jit(solution)/shard_map/ppermute | solution.py:407
  318.4 18.1 %copy-start.35 = (f32[4,4,32,256]{3,2,1,0:T(8,128)S(1)}, f32[4,4,32,256]{3,2,1,0:T(8,128)}, u32[]{:S(2)}) copy-start(f32[4,4,32,256]{3,2,1,0:T(8,128)} %copy-done.34) | copy-start | bytes 1572868
  322.0 34.1 %copy-start.17 = (f32[4,4,32,256]{3,2,1,0:T(8,128)}, f32[4,4,32,256]{3,2,1,0:T(8,128)S(1)}, u32[]{:S(2)}) copy-start(f32[4,4,32,256]{3,2,1,0:T(8,128)S(1)} %collective-permute-done.34.refs_1_) | copy-start | bytes 1572868
  333.6 22.5 %copy-start.19 = (f32[4,4,32,256]{3,2,1,0:T(8,128)}, f32[4,4,32,256]{3,2,1,0:T(8,128)S(1)}, u32[]{:S(2)}) copy-start(f32[4,4,32,256]{3,2,1,0:T(8,128)S(1)} %collective-permute-done.35.refs_5_) | copy-start | bytes 1572868
  333.6 23.9 %collective-permute-start.36 = (f32[4,264,256]{2,1,0:T(8,128)}, f32[4,264,256]{2,1,0:T(8,128)S(1)}, u32[]{:S(2)}, u32[]{:S(2)}) collective-permute-start(f32[4,264,256]{2,1,0:T(8,128)} %inflate.6.refs_4_), channel_id=1, source_target_pairs={{0,16},{8,24},{16,0},{24,8},{1,17},{9,25},{17,1},{25,9},{2,18},{10... | collective-permute-start | bytes 3244040 | tf_op jit(solution)/shard_map/ppermute | solution.py:437
  334.4 21.7 %collective-permute-start.38 = (f32[4,4,32,256]{3,2,1,0:T(8,128)S(1)}, f32[4,4,32,256]{3,2,1,0:T(8,128)S(1)}, u32[]{:S(2)}, u32[]{:S(2)}) collective-permute-start(f32[4,4,32,256]{3,2,1,0:T(8,128)S(1)} %broadcast_select_fusion.3), channel_id=1, source_target_pairs={{4,6},{5,7},{2,0},{3,1},{12,14},{13,15},{10,8},{11,9},{20,22},{21,... | collective-permute-start | bytes 1572872 | tf_op jit(solution)/shard_map/ppermute | solution.py:412
  335.7 20.4 %collective-permute-start.39 = (f32[4,4,32,256]{3,2,1,0:T(8,128)}, f32[4,4,32,256]{3,2,1,0:T(8,128)S(1)}, u32[]{:S(2)}, u32[]{:S(2)}) collective-permute-start(f32[4,4,32,256]{3,2,1,0:T(8,128)} %copy-done.36), channel_id=1, source_target_pairs={{2,4},{3,5},{4,6},{5,7},{10,12},{11,13},{12,14},{13,15},{18,20},{1... | collective-permute-start | bytes 1572872 | tf_op jit(solution)/shard_map/ppermute | solution.py:404
  336.4 21.1 %collective-permute-start.40 = (f32[4,4,32,256]{3,2,1,0:T(8,128)S(1)}, f32[4,4,32,256]{3,2,1,0:T(8,128)S(1)}, u32[]{:S(2)}, u32[]{:S(2)}) collective-permute-start(f32[4,4,32,256]{3,2,1,0:T(8,128)S(1)} %copy-done.35), channel_id=1, source_target_pairs={{2,0},{3,1},{4,2},{5,3},{10,8},{11,9},{12,10},{13,11},{18,16},{19,... | collective-permute-start | bytes 1572872 | tf_op jit(solution)/shard_map/ppermute | solution.py:407
  357.5 18.4 %copy-start.20 = (f32[4,4,32,256]{3,2,1,0:T(8,128)}, f32[4,4,32,256]{3,2,1,0:T(8,128)S(1)}, u32[]{:S(2)}) copy-start(f32[4,4,32,256]{3,2,1,0:T(8,128)S(1)} %collective-permute-done.40.refs_5_) | copy-start | bytes 1572868
  357.5 18.4 %copy-start.23 = (f32[4,264,256]{2,1,0:T(8,128)}, f32[4,264,256]{2,1,0:T(8,128)S(1)}, u32[]{:S(2)}) copy-start(f32[4,264,256]{2,1,0:T(8,128)S(1)} %collective-permute-done.36.refs_6_) | copy-start | bytes 3244036
  357.5 22.5 %collective-permute-start.41 = (f32[4,4,64,256]{3,2,1,0:T(8,128)}, f32[4,4,64,256]{3,2,1,0:T(8,128)S(1)}, u32[]{:S(2)}, u32[]{:S(2)}) collective-permute-start(f32[4,4,64,256]{3,2,1,0:T(8,128)} %get-tuple-element.132), channel_id=1, source_target_pairs={{0,1},{1,0},{2,3},{3,2},{4,5},{5,4},{6,7},{7,6},{8,9},{9,8},{10,11... | collective-permute-start | bytes 3145736 | tf_op jit(solution)/shard_map/ppermute | solution.py:437
  360.5 24.1 %collective-permute-start.43 = (f32[4,4,32,256]{3,2,1,0:T(8,128)S(1)}, f32[4,4,32,256]{3,2,1,0:T(8,128)S(1)}, u32[]{:S(2)}, u32[]{:S(2)}) collective-permute-start(f32[4,4,32,256]{3,2,1,0:T(8,128)S(1)} %broadcast_select_fusion.2), channel_id=1, source_target_pairs={{4,6},{5,7},{2,0},{3,1},{12,14},{13,15},{10,8},{11,9},{20,22},{21,... | collective-permute-start | bytes 1572872 | tf_op jit(solution)/shard_map/ppermute | solution.py:412
  384.6 22.9 %copy-start.7 = (f32[4,264,256]{2,1,0:T(8,128)S(1)}, f32[4,264,256]{2,1,0:T(8,128)}, u32[]{:S(2)}) copy-start(f32[4,264,256]{2,1,0:T(8,128)} %inflate.6.refs_4_) | copy-start | bytes 3244036
  384.6 21.5 %collective-permute-start.44 = (f32[4,264,256]{2,1,0:T(8,128)}, f32[4,264,256]{2,1,0:T(8,128)S(1)}, u32[]{:S(2)}, u32[]{:S(2)}) collective-permute-start(f32[4,264,256]{2,1,0:T(8,128)} %inflate.7.refs_8_), channel_id=1, source_target_pairs={{0,16},{8,24},{16,0},{24,8},{1,17},{9,25},{17,1},{25,9},{2,18},{10... | collective-permute-start | bytes 3244040 | tf_op jit(solution)/shard_map/ppermute | solution.py:437
  385.7 15.6 %collective-permute-start.46 = (f32[4,4,32,256]{3,2,1,0:T(8,128)}, f32[4,4,32,256]{3,2,1,0:T(8,128)S(1)}, u32[]{:S(2)}, u32[]{:S(2)}) collective-permute-start(f32[4,4,32,256]{3,2,1,0:T(8,128)} %get-tuple-element.137), channel_id=1, source_target_pairs={{0,1},{1,0},{2,3},{3,2},{4,5},{5,4},{6,7},{7,6},{8,9},{9,8},{10,11... | collective-permute-start | bytes 1572872 | tf_op jit(solution)/shard_map/ppermute | solution.py:437
  387.4 38.9 %collective-permute-start.24 = (f32[4,264,256]{2,1,0:T(8,128)S(1)}, f32[4,264,256]{2,1,0:T(8,128)}, u32[]{:S(2)}, u32[]{:S(2)}) collective-permute-start(f32[4,264,256]{2,1,0:T(8,128)S(1)} %copy-done.6), channel_id=1, source_target_pairs={{0,8},{8,0},{16,24},{24,16},{1,9},{9,1},{17,25},{25,17},{2,10},{10... | collective-permute-start | bytes 3244040 | tf_op jit(solution)/shard_map/ppermute | solution.py:525
  401.3 26.1 %copy-start.8 = (f32[4,264,256]{2,1,0:T(8,128)S(1)}, f32[4,264,256]{2,1,0:T(8,128)}, u32[]{:S(2)}) copy-start(f32[4,264,256]{2,1,0:T(8,128)} %inflate.7.refs_8_) | copy-start | bytes 3244036
  406.1 10.3 %collective-permute-start.50 = (f32[4,4,32,256]{3,2,1,0:T(8,128)}, f32[4,4,32,256]{3,2,1,0:T(8,128)}, u32[]{:S(2)}, u32[]{:S(2)}) collective-permute-start(f32[4,4,32,256]{3,2,1,0:T(8,128)} %get-tuple-element.141), channel_id=1, source_target_pairs={{0,1},{1,0},{2,3},{3,2},{4,5},{5,4},{6,7},{7,6},{8,9},{9,8},{10,11... | collective-permute-start | bytes 1572872 | tf_op jit(solution)/shard_map/ppermute | solution.py:437
  407.5 19.8 %collective-permute-start.32 = (f32[4,264,256]{2,1,0:T(8,128)S(1)}, f32[4,264,256]{2,1,0:T(8,128)}, u32[]{:S(2)}, u32[]{:S(2)}) collective-permute-start(f32[4,264,256]{2,1,0:T(8,128)S(1)} %copy-done.7), channel_id=1, source_target_pairs={{0,8},{8,0},{16,24},{24,16},{1,9},{9,1},{17,25},{25,17},{2,10},{10... | collective-permute-start | bytes 3244040 | tf_op jit(solution)/shard_map/ppermute | solution.py:525
  407.6 20.1 %collective-permute-start.30 = (f32[4,264,256]{2,1,0:T(8,128)}, f32[4,264,256]{2,1,0:T(8,128)}, u32[]{:S(2)}, u32[]{:S(2)}) collective-permute-start(f32[4,264,256]{2,1,0:T(8,128)} %collective-permute-done.29.refs_2_), channel_id=1, source_target_pairs={{0,8},{8,0},{16,24},{24,16},{1,9},{9,1},{17,25},{25,17},{2,10},{10... | collective-permute-start | bytes 3244040 | tf_op jit(solution)/shard_map/ppermute | solution.py:525
  411.4 14.9 %collective-permute-start.48 = (f32[4,136,256]{2,1,0:T(8,128)}, f32[4,136,256]{2,1,0:T(8,128)}, u32[]{:S(2)}, u32[]{:S(2)}) collective-permute-start(f32[4,136,256]{2,1,0:T(8,128)} %inflate.8.refs_12_), channel_id=1, source_target_pairs={{0,16},{8,24},{16,0},{24,8},{1,17},{9,25},{17,1},{25,9},{2,18},{10... | collective-permute-start | bytes 1671176 | tf_op jit(solution)/shard_map/ppermute | solution.py:437
  416.4 11.5 %collective-permute-start.37 = (f32[4,264,256]{2,1,0:T(8,128)}, f32[4,264,256]{2,1,0:T(8,128)}, u32[]{:S(2)}, u32[]{:S(2)}) collective-permute-start(f32[4,264,256]{2,1,0:T(8,128)} %copy-done.23), channel_id=1, source_target_pairs={{0,8},{8,0},{16,24},{24,16},{1,9},{9,1},{17,25},{25,17},{2,10},{10... | collective-permute-start | bytes 3244040 | tf_op jit(solution)/shard_map/ppermute | solution.py:525
  426.3 2.2 collective-permute-start.47
  426.3 15.2 %collective-permute-start.52 = (f32[4,136,256]{2,1,0:T(8,128)}, f32[4,136,256]{2,1,0:T(8,128)S(1)}, u32[]{:S(2)}, u32[]{:S(2)}) collective-permute-start(f32[4,136,256]{2,1,0:T(8,128)} %inflate.9.refs_16_), channel_id=1, source_target_pairs={{0,16},{8,24},{16,0},{24,8},{1,17},{9,25},{17,1},{25,9},{2,18},{10... | collective-permute-start | bytes 1671176 | tf_op jit(solution)/shard_map/ppermute | solution.py:437
  427.4 14.2 %collective-permute-start.42 = (f32[4,264,256]{2,1,0:T(8,128)S(1)}, f32[4,264,256]{2,1,0:T(8,128)S(1)}, u32[]{:S(2)}, u32[]{:S(2)}) collective-permute-start(f32[4,264,256]{2,1,0:T(8,128)S(1)} %copy-done.8), channel_id=1, source_target_pairs={{0,8},{8,0},{16,24},{24,16},{1,9},{9,1},{17,25},{25,17},{2,10},{10... | collective-permute-start | bytes 3244040 | tf_op jit(solution)/shard_map/ppermute | solution.py:525
  427.6 14.0 %collective-permute-start.45 = (f32[4,264,256]{2,1,0:T(8,128)}, f32[4,264,256]{2,1,0:T(8,128)S(1)}, u32[]{:S(2)}, u32[]{:S(2)}) collective-permute-start(f32[4,264,256]{2,1,0:T(8,128)} %copy-done.24), channel_id=1, source_target_pairs={{0,8},{8,0},{16,24},{24,16},{1,9},{9,1},{17,25},{25,17},{2,10},{10... | collective-permute-start | bytes 3244040 | tf_op jit(solution)/shard_map/ppermute | solution.py:525
  427.9 13.7 %collective-permute-start.51 = (f32[4,136,256]{2,1,0:T(8,128)}, f32[4,136,256]{2,1,0:T(8,128)S(1)}, u32[]{:S(2)}, u32[]{:S(2)}) collective-permute-start(f32[4,136,256]{2,1,0:T(8,128)} %inflate.9.refs_16_), channel_id=1, source_target_pairs={{0,8},{8,0},{16,24},{24,16},{1,9},{9,1},{17,25},{25,17},{2,10},{10... | collective-permute-start | bytes 1671176 | tf_op jit(solution)/shard_map/ppermute | solution.py:525
  428.5 13.2 %collective-permute-start.49 = (f32[4,136,256]{2,1,0:T(8,128)}, f32[4,136,256]{2,1,0:T(8,128)S(1)}, u32[]{:S(2)}, u32[]{:S(2)}) collective-permute-start(f32[4,136,256]{2,1,0:T(8,128)} %collective-permute-done.48.refs_14_), channel_id=1, source_target_pairs={{0,8},{8,0},{16,24},{24,16},{1,9},{9,1},{17,25},{25,17},{2,10},{10... | collective-permute-start | bytes 1671176 | tf_op jit(solution)/shard_map/ppermute | solution.py:525
  441.6 2.0 collective-permute-start.53
  (28 other events, 131.2 us)

commit v3 on v2

v3 whole, which is shorter than its diff:
```python
import functools

import jax
import jax.numpy as jnp
from jax import lax
from jax.experimental import pallas as pl
from jax.experimental.pallas import tpu as pltpu
from jax.sharding import PartitionSpec as P

TR = 8
CHUNKS = (128, 64, 64)
ROWS = (64, 64, 32)
FIELDS = 8
RING = 16
VMEM = 56 * 1024 * 1024


def arrival(q, source):
    steps = jnp.abs(source - q)
    link = (q + (source < q)) % 2
    return jnp.where(steps == 0, 0, 2 * steps - 1 + link)


def split(x):
    high = x.astype(jnp.bfloat16)
    low = (x - high.astype(jnp.float32)).astype(jnp.bfloat16)
    return high, low


def place_kernel(parts, *refs):
    o_ref, mark_ref = refs[-2:]
    mark_ref[...] = jnp.zeros_like(mark_ref)
    count = o_ref.shape[3]
    start = 0
    for x_ref in refs[:parts]:
        rows = x_ref.shape[0] // count
        for z in range(count):
            high, low = split(x_ref[z * rows : (z + 1) * rows])
            o_ref[0, 0, 0, z, 0, start : start + rows] = high
            o_ref[0, 0, 0, z, 1, start : start + rows] = low
        start += rows


def place(parts, buffer, group, relative, blocks, count):
    width = parts[0][0].shape[1]
    out = jax.ShapeDtypeStruct((2, blocks, 4, count, 2, width, width), jnp.bfloat16)
    in_specs = [
        pl.BlockSpec((count * rows, width), lambda j, first=first: (first // count + j, 0))
        for _, rows, first in parts
    ]
    args = [x for x, _, _ in parts]
    aliases = {}
    if buffer is not None:
        in_specs.append(pl.BlockSpec(memory_space=pl.ANY))
        args.append(buffer)
        aliases = {len(parts): 0}
    size = blocks * count * width * width
    return pl.pallas_call(
        functools.partial(place_kernel, len(parts)),
        grid=(blocks,),
        out_shape=(out, jax.ShapeDtypeStruct((8, 128), jnp.float32)),
        in_specs=in_specs,
        out_specs=(
            pl.BlockSpec(
                (1, 1, 1, count, 2, width, width), lambda j: (group, j, relative, 0, 0, 0, 0)
            ),
            pl.BlockSpec((8, 128), lambda j: (0, 0)),
        ),
        input_output_aliases=aliases,
        compiler_params=pltpu.CompilerParams(vmem_limit_bytes=VMEM),
        cost_estimate=pl.CostEstimate(flops=size, bytes_accessed=8 * size, transcendentals=0),
        name="place",
    )(*args)


def plan_kernel(line, blocks, count, me_ref, *refs):
    items = blocks * count
    known, shards = refs[:8], refs[8:-3]
    plan_ref, kept_ref, levels_ref = refs[-3:]
    r, c = me_ref[0], me_ref[1]
    q, p = c // 2, c % 2

    for i, shard in enumerate(shards):

        def note(j, _, i=i, shard=shard):
            levels_ref[i * items + j] = shard[0, j].astype(jnp.int32)
            return 0

        lax.fori_loop(0, items, note, 0)

    def write(n, tile, at, levels):
        plan_ref[FIELDS * n] = tile
        plan_ref[FIELDS * n + 1] = at
        for y in range(count):
            plan_ref[FIELDS * n + 2 + y] = levels(y)

    n = jnp.int32(0)
    for group in range(2):

        def column(j, n, group=group):
            row = group * blocks + j
            for relative in range(4):
                rr = jnp.bitwise_xor(r, relative)

                def entry(z, n, relative=relative, rr=rr):
                    noted = known[2 * relative + group][0, j * count + z]
                    k = rr * TR + noted.astype(jnp.int32)
                    ck = k // blocks
                    levels = arrival(q, ck // 2) * items + (k % blocks) * count
                    mine = ck % 2 == p
                    write(
                        n,
                        (row * 4 + relative) * count + z,
                        (ck // 2) * blocks + k % blocks,
                        lambda y: levels_ref[jnp.where(mine, levels + y, 0)],
                    )
                    return n + mine.astype(jnp.int32)

                n = lax.fori_loop(0, count, entry, n)
            write(n, row * 4 * count, line * blocks, lambda y: jnp.int32(0))
            n = n + n % 2
            kept_ref[FIELDS * row] = n
            for m in range(count):
                noted = known[group][0, items + j * count + m]
                kept_ref[FIELDS * row + 1 + m] = noted.astype(jnp.int32)
            return n

        n = lax.fori_loop(0, blocks, column, n)


def noted(x, row):
    return x, pl.BlockSpec((8, 128), lambda *_: (row // 8, 0), memory_space=pltpu.SMEM)


def make_plan(me, known, shards, line, blocks, count):
    smem = pl.BlockSpec(memory_space=pltpu.SMEM)
    args, specs = zip(*known, *shards)
    return pl.pallas_call(
        functools.partial(plan_kernel, line, blocks, count),
        grid=(1,),
        out_shape=(
            jax.ShapeDtypeStruct((FIELDS * (2 * blocks * 4 * count + 2),), jnp.int32),
            jax.ShapeDtypeStruct((FIELDS * 2 * blocks,), jnp.int32),
        ),
        in_specs=[smem, *specs],
        out_specs=(smem, smem),
        scratch_shapes=[pltpu.SMEM(((2 * line - 2) * blocks * count,), jnp.int32)],
        name="plan",
    )(me, *args)


def product_kernel(line, grid_blocks, part, me_ref, plan_ref, kept_ref, b_ref, *refs):
    parts = 2 * line - 2
    a_refs = refs[:parts]
    other_ref, own_ref, raw, halves, total, ring, a_sems, b_sems = refs[parts:]
    group, j = pl.program_id(0), pl.program_id(1)
    blocks, count, rows, width = (grid_blocks, *other_ref.shape[1:])
    size = blocks * count * rows
    last = 2 * blocks - 1
    row = group * blocks + j
    q = me_ref[1] // 2
    end = kept_ref[FIELDS * last]

    def fetch(n):
        tile = plan_ref[FIELDS * n]
        slot = n % RING
        return pltpu.make_async_copy(b_ref.at[tile], ring.at[slot], b_sems.at[slot])

    @pl.when(row == 0)
    def _():
        def each(act):
            for i in range(parts):
                steps, link = (i + 1) // 2, (i + 1) % 2
                source = q if i == 0 else jnp.where(q % 2 == link, q + steps, q - steps)

                @pl.when((source >= 0) & (source < line))
                def _():
                    rows_of = a_refs[i].at[part * size : (part + 1) * size]
                    to = raw.at[pl.ds(pl.multiple_of(source * size, size), size)]
                    act(pltpu.make_async_copy(rows_of, to, a_sems.at[i]))

        each(lambda copy: copy.start())

        def begin(n, _):
            fetch(n).start()
            return 0

        lax.fori_loop(0, jnp.minimum(end, RING), begin, 0)
        halves[line * blocks] = jnp.zeros(halves.shape[1:], halves.dtype)
        each(lambda copy: copy.wait())

        def convert(i, _):
            first = pl.multiple_of(i * count * rows, count * rows)
            high, low = split(raw[pl.ds(first, count * rows)])
            halves[i, 0 : count * rows] = high
            halves[i, count * rows :] = low
            return 0

        lax.fori_loop(0, line * blocks, convert, 0)

    total[...] = jnp.zeros_like(total)
    first = jnp.where(row == 0, 0, kept_ref[FIELDS * jnp.maximum(row - 1, 0)])

    def multiply(n):
        a = halves[plan_ref[FIELDS * n + 1]]
        slot = n % RING
        b_high, b_low = ring[slot, 0], ring[slot, 1]
        dot = functools.partial(jnp.dot, preferred_element_type=jnp.float32)
        by_high = dot(a, b_high)
        return by_high[: count * rows] + by_high[count * rows :] + dot(a[: count * rows], b_low)

    def step(i, _):
        n = first + 2 * i
        fetch(n).wait()
        fetch(n + 1).wait()
        products = [multiply(n), multiply(n + 1)]
        for e in range(2):
            for y in range(count):
                level = plan_ref[FIELDS * (n + e) + 2 + y]
                total[level] += products[e][y * rows : (y + 1) * rows]

        @pl.when(n + RING < end)
        def _():
            fetch(n + RING).start()
            fetch(n + RING + 1).start()

        return 0

    lax.fori_loop(0, (kept_ref[FIELDS * row] - first) // 2, step, 0)

    @pl.when(group == 0)
    def _():
        for m in range(count):
            other_ref[0, m] = total[kept_ref[FIELDS * row + 1 + m]]

    @pl.when(group == 1)
    def _():
        for m in range(count):
            own_ref[0, m] = total[kept_ref[FIELDS * row + 1 + m]]


def product(me, plan, panel, parts, line, part, rows):
    blocks, count, width = panel.shape[1], panel.shape[3], panel.shape[6]
    out = jax.ShapeDtypeStruct((blocks, count, rows, width), jnp.float32)
    smem = pl.BlockSpec(memory_space=pltpu.SMEM)
    return pl.pallas_call(
        functools.partial(product_kernel, line, blocks, part),
        grid=(2, blocks),
        out_shape=(out, out),
        in_specs=[smem] * 3 + [pl.BlockSpec(memory_space=pl.ANY)] * (1 + len(parts)),
        out_specs=(
            pl.BlockSpec(
                (1, count, rows, width), lambda g, j: (jnp.where(g == 0, j, blocks - 1), 0, 0, 0)
            ),
            pl.BlockSpec((1, count, rows, width), lambda g, j: (jnp.where(g == 0, 0, j), 0, 0, 0)),
        ),
        scratch_shapes=[
            pltpu.VMEM((line * blocks * count * rows, width), jnp.float32),
            pltpu.VMEM((line * blocks + 1, 2 * count * rows, width), jnp.bfloat16),
            pltpu.VMEM((TR, rows, width), jnp.float32),
            pltpu.VMEM((RING, 2, width, width), jnp.bfloat16),
            pltpu.SemaphoreType.DMA((len(parts),)),
            pltpu.SemaphoreType.DMA((RING,)),
        ],
        compiler_params=pltpu.CompilerParams(vmem_limit_bytes=VMEM),
        cost_estimate=pl.CostEstimate(
            flops=3 * 2 * 16 * blocks * count * rows * width * width,
            bytes_accessed=panel.size,
            transcendentals=0,
        ),
        name="product",
    )(me, *plan, panel.reshape(-1, 2, width, width), *parts)


def inflate_kernel(own_ref, other_ref, out_ref):
    count, rows = own_ref.shape[1:3]
    partial = jnp.zeros((8, own_ref.shape[3]), jnp.float32)
    for m in range(count):
        kept = own_ref[0, m] + other_ref[0, m]
        inflated = kept * kept
        out_ref[0, m * rows : (m + 1) * rows] = inflated
        for i in range(0, rows, 8):
            partial += inflated[i : i + 8]
    out_ref[0, count * rows :] = partial


def inflate(own, other):
    blocks, count, rows, width = own.shape
    spec = pl.BlockSpec((1, count, rows, width), lambda j: (j, 0, 0, 0))
    return pl.pallas_call(
        inflate_kernel,
        grid=(blocks,),
        out_shape=jax.ShapeDtypeStruct((blocks, count * rows + 8, width), jnp.float32),
        in_specs=[spec, spec],
        out_specs=pl.BlockSpec((1, count * rows + 8, width), lambda j: (j, 0, 0)),
        cost_estimate=pl.CostEstimate(
            flops=3 * own.size, bytes_accessed=12 * own.size, transcendentals=0
        ),
        name="inflate",
    )(own, other)


def owned_kernel(sizes, blocks, count, scale, me_ref, *refs):
    chunks = len(sizes)
    notes, refs = refs[:4], refs[4:]
    sources = refs[: 4 * chunks]
    out_ref, slots, partial, whose, in_sems, out_sems, sum_sems = refs[4 * chunks :]
    items = blocks * count
    most = items // 2
    r = me_ref[0]
    starts = [sum(sizes[:h]) for h in range(chunks)]

    def partials(act):
        for i in range(4 * chunks):
            rows = pl.ds(count * sizes[i // 4], 8)
            act(pltpu.make_async_copy(sources[i].at[:, rows], partial.at[i], sum_sems.at[i]))

    partials(lambda copy: copy.start())
    for s in range(4 * most):
        whose[s] = -1
    for relative in range(4):
        rr = jnp.bitwise_xor(r, relative)

        def place_item(f, n, relative=relative, rr=rr):
            mine = notes[relative][0, 2 * items + f].astype(jnp.int32) == r

            @pl.when(mine)
            def _():
                slot = rr * most + n
                whose[slot] = f // count
                for h in range(chunks):
                    pltpu.make_async_copy(
                        sources[4 * h + relative].at[
                            f // count, pl.ds(pl.multiple_of(f % count * sizes[h], 8), sizes[h])
                        ],
                        slots.at[slot, pl.ds(starts[h], sizes[h])],
                        in_sems.at[slot],
                    ).start()

            return n + mine.astype(jnp.int32)

        lax.fori_loop(0, items, place_item, jnp.int32(0))

    partials(lambda copy: copy.wait())
    factors = scale / jnp.sum(jnp.sum(partial[...], axis=0), axis=1)

    def finish(s, _):
        j = whose[s]

        @pl.when(j < 0)
        def _():
            slots[s] = jnp.zeros(slots.shape[1:], jnp.float32)

        for jj in range(blocks):

            @pl.when(j == jj)
            def _():
                pltpu.make_async_copy(slots.at[s], slots.at[s], in_sems.at[s]).wait()
                slots[s] = slots[s] * factors[jj : jj + 1]

        pltpu.make_async_copy(slots.at[s], out_ref.at[s], out_sems.at[s]).start()
        return 0

    lax.fori_loop(0, 4 * most, finish, 0)

    def drain(s, _):
        pltpu.make_async_copy(slots.at[s], out_ref.at[s], out_sems.at[s]).wait()
        return 0

    lax.fori_loop(0, 4 * most, drain, 0)


def owned_tiles(me, notes, sources, sizes, count, scale):
    blocks, _, width = sources[0].shape
    most = blocks * count // 2
    smem = pl.BlockSpec(memory_space=pltpu.SMEM)
    return pl.pallas_call(
        functools.partial(owned_kernel, sizes, blocks, count, scale),
        grid=(1,),
        out_shape=jax.ShapeDtypeStruct((4 * most, width, width), jnp.float32),
        in_specs=[smem, *(spec for _, spec in notes)]
        + [pl.BlockSpec(memory_space=pl.ANY)] * len(sources),
        out_specs=pl.BlockSpec(memory_space=pl.ANY),
        scratch_shapes=[
            pltpu.VMEM((4 * most, width, width), jnp.float32),
            pltpu.VMEM((len(sources), blocks, 8, width), jnp.float32),
            pltpu.SMEM((4 * most,), jnp.int32),
            pltpu.SemaphoreType.DMA((4 * most,)),
            pltpu.SemaphoreType.DMA((4 * most,)),
            pltpu.SemaphoreType.DMA((len(sources),)),
        ],
        compiler_params=pltpu.CompilerParams(vmem_limit_bytes=VMEM),
        cost_estimate=pl.CostEstimate(
            flops=4 * most * width * width,
            bytes_accessed=32 * most * width * width,
            transcendentals=0,
        ),
        name="owned",
    )(me, *(x for x, _ in notes), *sources)


def on_device(columns, matrix_tiles, tile_rows, keep_rows, owners):
    tiles = matrix_tiles[0]
    blocks, count, width = tiles.shape[0], tiles.shape[1], tiles.shape[2]
    line = columns // 2
    r, c = lax.axis_index("row"), lax.axis_index("col")
    me = jnp.stack([r, c]).astype(jnp.int32)

    core = functools.partial(lax.ppermute, axis_name="row", perm=[(i, i ^ 1) for i in range(4)])
    across = functools.partial(lax.ppermute, axis_name="row", perm=[(i, i ^ 2) for i in range(4)])
    pair = functools.partial(
        lax.ppermute, axis_name="col", perm=[(i, i ^ 1) for i in range(columns)]
    )

    links = []
    for first in (0, 1):
        perm = []
        for i in range(4 * columns):
            rank = i % columns // 2
            to = rank + 1 if rank % 2 == first else rank - 1
            inside = 0 <= to < line
            perm.append((i, i + 2 * (to - rank) if inside else i ^ columns))
        links.append(functools.partial(lax.ppermute, axis_name=("row", "col"), perm=perm))

    sizes = tuple(size * width // sum(CHUNKS) for size in CHUNKS)
    starts = [sum(sizes[:h]) for h in range(len(sizes))]

    chunks, half = len(sizes), width // 2
    rows = [size * width // sum(CHUNKS) for size in ROWS]

    def cut(x, h):
        x = x[:, :, starts[h] : starts[h] + sizes[h]]
        x = x.reshape(blocks * count, sizes[h] // rows[h], rows[h], width)
        return jnp.swapaxes(x, 0, 1).reshape(-1, width)

    notes = jnp.concatenate([tile_rows.reshape(-1), keep_rows.reshape(-1), owners.reshape(-1)])
    notes = jnp.pad(notes.astype(jnp.float32), (0, width - notes.shape[0]))
    own = [jnp.concatenate([cut(tiles, 0), jnp.broadcast_to(notes, (8, width))])]
    came = [[] for _ in sizes]

    ticks = {}

    def at(tick, x):
        ticks.setdefault(tick, []).append(x)
        return x

    def tie(x, *others):
        return lax.optimization_barrier((x, *others))[0] if others else x

    def after(tick, x):
        return tie(x, *ticks.get(tick - 1, ()))

    def send(tick, move, x, *more):
        return at(tick, move(after(tick, x), *more))

    swapped = []

    def swap(tick, x):
        x = tie(x, *swapped[-1:])
        swapped.append(send(tick, core, x))
        return swapped[-1]

    base = line - 1
    hops = {}
    for h in range(chunks):
        for hop in range(line - 1):
            if h == 0:
                tick = hop
            else:
                tick = base + hop + (h - 1 if hop else max(h - 2, 0))
            hops.setdefault(tick, []).append((h, hop))

    panel = None
    sources, waiting, landed, flying = [], [], [], []

    def put(tick, group, relative, *parts):
        nonlocal panel
        panel, mark = place(parts, panel, group, relative, blocks, count)
        at(tick, mark)

    items = blocks * count
    upper, parts = sizes[0] * items, sizes[0] // rows[0]

    def halves(top, low):
        return (*((top, rows[0], part * items) for part in range(parts)), (low, half, 0))

    tick = 0
    while tick <= max(hops) + 1 or landed or flying:
        for h, hop in hops.get(tick, ()):
            if hop:
                operands = came[h][-1], came[h][-2]
            else:
                operands = own[h], own[h]
            for link in range(1 if hop == line - 2 else 2):
                came[h].append(send(tick, links[link], operands[link]))
        if tick == 0:
            whole = tiles.reshape(-1, width)
            rest = tiles[:, :, half:].reshape(-1, width)
            b_pair, b_across = send(0, pair, own[0]), send(0, across, own[0])
            core_own = swap(0, whole)
            put(0, 1, 0, (whole, width, 0))
        if tick == 1:
            pair_rest, across_rest = send(1, pair, rest), send(1, across, rest)
            core_pair, core_notes = swap(1, b_pair), swap(1, own[0][upper:])
            put(1, 1, 1, (core_own, width, 0))
            later = after(1, tiles)
            own += [at(1, cut(later, h)) for h in range(1, chunks)]
        if tick == 2:
            diagonal, diagonal_rest = send(2, across, b_pair), send(2, pair, across_rest)
            core_across, core_pair_rest = swap(2, b_across), swap(2, pair_rest)
            core_across_rest = swap(2, across_rest)
            put(2, 0, 0, *halves(b_pair, pair_rest))
            put(2, 1, 2, *halves(b_across, across_rest))
            put(3, 0, 1, *halves(core_pair, core_pair_rest))
            put(3, 1, 3, *halves(core_across, core_across_rest))
        if tick == max(base, 3):
            core_diagonal = swap(tick, diagonal)
            put(tick, 0, 2, *halves(diagonal, diagonal_rest))
            put(tick, 0, 3, *halves(core_diagonal, swap(tick, diagonal_rest)))
            known = [
                (b_pair, upper),
                (own[0], upper),
                (core_pair, upper),
                (core_notes, 0),
                (diagonal, upper),
                (b_across, upper),
                (core_diagonal, upper),
                (core_across, upper),
            ]
            known = [noted(x, i) for x, i in known]
            shards = [noted(x, upper) for x in [own[0], *came[0]]]
            plan = make_plan(me, known, shards, line, blocks, count)
        for h in range(chunks):
            if tick == max(base, 3) if h == 0 else (h, line - 2) in hops.get(tick - 1, ()):
                gathered = [own[h], *came[h]]
                waiting += [(gathered, i, rows[h]) for i in range(sizes[h] // rows[h])]
        if flying and flying[0][0] < tick:
            _, mine, other = flying.pop(0)
            inflated = inflate(mine, other)
            opposite = send(tick, across, inflated)
            sources += [inflated, core(inflated), opposite, core(opposite)]
        if landed and landed[0][0] < tick:
            _, theirs, mine = landed.pop(0)
            other = send(tick, pair, theirs)
            flying.append((tick, mine, other))
        if waiting and tick < max(hops) - 1:
            gathered, part, size = waiting.pop(0)
            theirs, mine = product(me, plan, panel, gathered, line, part, size)
            landed.append((tick, at(tick, theirs), mine))
        tick += 1
    theirs, queue = None, []
    for n, (gathered, part, size) in enumerate(waiting):
        theirs, mine = product(
            me if theirs is None else tie(me, theirs), plan, panel, gathered, line, part, size
        )
        other = pair(tie(theirs, other))
        queue.append((mine, other))
        done = [theirs, *(waiting[n + 1][0] if n + 1 < len(waiting) else ())]
        if n == 0 and len(waiting) > 1:
            continue
        for mine, ready in queue if n + 1 == len(waiting) else [queue.pop(0)]:
            inflated = inflate(mine, tie(ready, *done) if ready is not other else ready)
            opposite = across(tie(inflated, opposite))
            sources += [inflated, core(inflated), opposite, core(opposite)]
    sizes = tuple(rows[h] for h in range(chunks) for _ in range(0, sizes[h], rows[h]))
    scale = float(4 * TR * width)
    owned = owned_tiles(me, known[1::2], sources, sizes, count, scale)
    return owned[None, None]


def solution(mesh):
    placed = (
        P("row", "col", None, None, None),
        P("row", "col", None),
        P("row", "col", None),
        P("row", "col", None),
    )
    return jax.shard_map(
        functools.partial(on_device, mesh.shape["col"]),
        mesh=mesh,
        in_specs=placed,
        out_specs=P("row", "col", None, None, None),
        check_vma=False,
    )
```

time: 456 us -> 415 us (0.910)
  starting transfers between devices: 67.3 us -> 32.9 us
  local copies, waits for them, and re-layouts: 24.2 us -> 13 us
  other arithmetic: 7.51 us -> 0.86 us
  waiting for transfers between devices: 200 us -> 206 us
  Pallas kernels: 153 us -> 158 us
    ppermute x20 -> x6, starting transfers between devices: 41.2 us -> 5.77 us  [the longest x3 3.56 us: on_device(): opposite = across(tie(inflated, opposite))]
    slice x22 -> x2, local copies, waits for them, and re-layouts: 16.2 us -> 6.62 us  [the longest x1 3.95 us: on_device(): rest = tiles[:, :, half:].reshape(-1, width)]
    ppermute x24 -> x33, waiting for transfers between devices: 167 us -> 173 us  [send(): return at(tick, move(after(tick, x), *more))]
    pallas_call x14, Pallas kernels: 127 us -> 134 us  [the longest x5 87 us: product(): pl.pallas_call(functools.partial(product_kernel, line, blocks, part), gri...]
    select_n x4 -> x0, other arithmetic: 4.58 us -> none  [on_device(): both = send(tick, apart, jnp.where(c // 2 >= hop, rising, falling), hop)]
    ppermute x20 -> x6, waiting for transfers between devices: 30.7 us -> 29.3 us  [the longest x3 15.8 us: on_device(): opposite = across(tie(inflated, opposite))]
    ppermute x24 -> x33, starting transfers between devices: 24.7 us -> 25.6 us  [send(): return at(tick, move(after(tick, x), *more))]
  transfers between devices with their start and end apart: 54 -> 49, of which waited for: 19 -> 22; matrix products, arithmetic and copies ran while one was open for 4% -> 2% of each run, Pallas kernels for 31% -> 37%
where the time goes in v3:
time: 415 us; the launch traced here: 411 us
  waiting for transfers between devices  206 us (50%)
  Pallas kernels  158 us (38%)
  starting transfers between devices  32.9 us (8%)
  local copies, waits for them, and re-layouts  13 us (3%)
    ppermute x33, waiting for transfers between devices, send(): return at(tick, move(after(tick, x), *more))  173 us
    pallas_call x5, Pallas kernels, product(): pl.pallas_call(functools.partial(product_kernel, line, blocks, part), gri...  87 us
    pallas_call x8, Pallas kernels, place(): pl.pallas_call(functools.partial(place_kernel, len(parts)), grid=(blocks,...  39 us
    ppermute x33, starting transfers between devices, send(): return at(tick, move(after(tick, x), *more))  25.6 us
    pallas_call x5, Pallas kernels, inflate(): pl.pallas_call(inflate_kernel, grid=(blocks,), out_shape=jax.ShapeDtypeSt...  17.4 us
    ppermute x3, waiting for transfers between devices, on_device(): opposite = across(tie(inflated, opposite))  15.8 us
    ppermute x3, waiting for transfers between devices, on_device(): other = pair(tie(theirs, other))  13.4 us
  transfers between devices with their start and end apart: 49, of which 22 were waited for; matrix products, arithmetic and copies ran while one was open for 2% of the time, Pallas kernels for 37%

profile of v3, /device:TPU:0, one launch (start us, length us, event | category | flops | bytes accessed | tf_op | source)
XLA Modules:
  0.0 410.6 jit_solution(18419586064542112280)
XLA Ops:
  0.5 0.8 reshape.33
  1.2 0.8 reshape.34
  2.0 4.0 fusion.1
  6.8 2.6 collective-permute-start
  9.4 1.5 collective-permute-start.4
  10.9 3.1 collective-permute-start.2
  14.1 4.9 %place.8 = (bf16[2,4,4,4,2,256,256]{6,5,4,3,2,1,0:T(8,128)(2,1)}, f32[8,128]{1,0:T(8,128)}) custom-call(f32[4096,256]{1,0:T(8,128)} %bitcast.24), custom_call_target="tpu_custom_call" | custom-call | flops 1048576 | bytes 8388608 | tf_op jit(solution)/shard_map/place/pallas_call | solution.py:58
  19.0 37.0 %collective-permute-done.refs_0_.refs_1_ = f32[2056,256]{1,0:T(8,128)} collective-permute-done((f32[2056,256]{1,0:T(8,128)S(1)}, f32[2056,256]{1,0:T(8,128)}, u32[]{:S(2)}, u32[]{:S(2)}) %collective-permute-start) | collective-permute-done | bytes 2105376 | tf_op jit(solution)/shard_map/ppermute | solution.py:454
  56.0 1.4 collective-permute-done.4.refs_0_.refs_1_.refs_5_.refs_2_
  57.3 2.5 collective-permute-done.2.refs_9_.refs_1_
  59.8 1.7 collective-permute-start.7
  62.8 1.5 collective-permute-done.5.refs_2_.refs_0_.refs_1_
  64.5 2.7 fusion
  67.2 5.3 %place.9 = (bf16[2,4,4,4,2,256,256]{6,5,4,3,2,1,0:T(8,128)(2,1)}, f32[8,128]{1,0:T(8,128)}) custom-call(f32[4096,256]{1,0:T(8,128)} %collective-permute-done.1.refs_0_, bf16[2,4,4,4,2,256,256]{6,5,4,3,2,1,0:T(8,128)(2,1)} %get-tuple-element.85.refs_1_), custom_call_target="tpu_custom_call", output_to_operand_aliasing={{0}: (1, {})} | custom-call | flops 1048576 | bytes 8388608 | tf_op jit(solution)/shard_map/place/pallas_call | solution.py:58
  72.5 37.4 %collective-permute-done.10.refs_2_ = f32[2048,256]{1,0:T(8,128)} collective-permute-done((f32[2048,256]{1,0:T(8,128)}, f32[2048,256]{1,0:T(8,128)}, u32[]{:S(2)}, u32[]{:S(2)}) %collective-permute-start.10) | collective-permute-done | bytes 2097184 | tf_op jit(solution)/shard_map/ppermute | solution.py:454
  110.2 4.2 %collective-permute-done.11.refs_7_.refs_0_.refs_1_.refs_3_ = f32[2056,256]{1,0:T(8,128)S(1)} collective-permute-done((f32[2056,256]{1,0:T(8,128)S(1)}, f32[2056,256]{1,0:T(8,128)S(1)}, u32[]{:S(2)}, u32[]{:S(2)}) %collective-permute-start.11) | collective-permute-done | bytes 2105376 | tf_op jit(solution)/shard_map/ppermute | solution.py:454
  114.5 1.5 collective-permute-start.12
  116.1 1.9 collective-permute-start.15
  117.9 1.0 collective-permute-done.13.refs_2_
  119.6 4.8 %place.10 = (bf16[2,4,4,4,2,256,256]{6,5,4,3,2,1,0:T(8,128)(2,1)}, f32[8,128]{1,0:T(8,128)}) custom-call(f32[2056,256]{1,0:T(8,128)} %collective-permute-done.refs_0_.refs_1_, f32[2056,256]{1,0:T(8,128)} %collective-permute-done.refs_0_.refs_1_, f32[2048,256]{1,0:T(8,128)} %collective-permute-done.9.refs_2_, ...), custom_call_target="tpu_custom_call", output_to_operand_aliasing={{0}: (3, {})} | custom-call | flops 1048576 | bytes 8388608 | tf_op jit(solution)/shard_map/place/pallas_call | solution.py:58
  124.4 4.8 %place.11 = (bf16[2,4,4,4,2,256,256]{6,5,4,3,2,1,0:T(8,128)(2,1)}, f32[8,128]{1,0:T(8,128)}) custom-call(f32[2056,256]{1,0:T(8,128)} %copy-done.1, f32[2056,256]{1,0:T(8,128)} %copy-done.1, f32[2048,256]{1,0:T(8,128)} %collective-permute-done.10.refs_2_, bf16[2,4,4,4,2,256,256]{6,5,4,3,2,1,0:T(8,128)(2,1)} %get-tuple-element.99.refs_3_), custom_call_target="tpu_custom_call", output_to_operand_aliasing={{0}: (3, {})} | custom-call | flops 1048576 | bytes 8388608 | tf_op jit(solution)/shard_map/place/pallas_call | solution.py:58
  129.2 33.6 %collective-permute-done.12.refs_4_.refs_0_.refs_1_ = f32[2056,256]{1,0:T(8,128)S(1)} collective-permute-done((f32[2056,256]{1,0:T(8,128)}, f32[2056,256]{1,0:T(8,128)S(1)}, u32[]{:S(2)}, u32[]{:S(2)}) %collective-permute-start.12) | collective-permute-done | bytes 2105376 | tf_op jit(solution)/shard_map/ppermute | solution.py:454
  162.8 4.4 %collective-permute-done.16.refs_2_ = f32[2048,256]{1,0:T(8,128)} collective-permute-done((f32[2048,256]{1,0:T(8,128)}, f32[2048,256]{1,0:T(8,128)}, u32[]{:S(2)}, u32[]{:S(2)}) %collective-permute-start.16) | collective-permute-done | bytes 2097184 | tf_op jit(solution)/shard_map/ppermute | solution.py:454
  167.3 4.2 %collective-permute-done.17.refs_6_.refs_0_.refs_1_ = f32[2056,256]{1,0:T(8,128)S(1)} collective-permute-done((f32[2056,256]{1,0:T(8,128)S(1)}, f32[2056,256]{1,0:T(8,128)S(1)}, u32[]{:S(2)}, u32[]{:S(2)}) %collective-permute-start.17) | collective-permute-done | bytes 2105376 | tf_op jit(solution)/shard_map/ppermute | solution.py:454
  171.5 1.3 copy-done.6
  173.3 1.8 collective-permute-start.19
  175.1 1.7 collective-permute-start.21
  177.5 4.8 %place.12 = (bf16[2,4,4,4,2,256,256]{6,5,4,3,2,1,0:T(8,128)(2,1)}, f32[8,128]{1,0:T(8,128)}) custom-call(f32[2056,256]{1,0:T(8,128)} %collective-permute-done.5.refs_2_.refs_0_.refs_1_, f32[2056,256]{1,0:T(8,128)} %collective-permute-done.5.refs_2_.refs_0_.refs_1_, f32[2048,256]{1,0:T(8,128)} %collective-permute-done.13.refs_2_, ...), custom_call_target="tpu_custom_call", output_to_operand_aliasing={{0}: (3, {})} | custom-call | flops 1048576 | bytes 8388608 | tf_op jit(solution)/shard_map/place/pallas_call | solution.py:58
  182.3 4.8 %place.13 = (bf16[2,4,4,4,2,256,256]{6,5,4,3,2,1,0:T(8,128)(2,1)}, f32[8,128]{1,0:T(8,128)}) custom-call(f32[2056,256]{1,0:T(8,128)} %copy-done.2, f32[2056,256]{1,0:T(8,128)} %copy-done.2, f32[2048,256]{1,0:T(8,128)} %collective-permute-done.14.refs_2_, bf16[2,4,4,4,2,256,256]{6,5,4,3,2,1,0:T(8,128)(2,1)} %get-tuple-element.107.refs_3_), custom_call_target="tpu_custom_call", output_to_operand_aliasing={{0}: (3, {})} | custom-call | flops 1048576 | bytes 8388608 | tf_op jit(solution)/shard_map/place/pallas_call | solution.py:58
  187.1 4.8 %place.14 = (bf16[2,4,4,4,2,256,256]{6,5,4,3,2,1,0:T(8,128)(2,1)}, f32[8,128]{1,0:T(8,128)}) custom-call(f32[2056,256]{1,0:T(8,128)} %copy-done.5, f32[2056,256]{1,0:T(8,128)} %copy-done.5, f32[2048,256]{1,0:T(8,128)} %collective-permute-done.16.refs_2_, bf16[2,4,4,4,2,256,256]{6,5,4,3,2,1,0:T(8,128)(2,1)} %get-tuple-element.108.refs_3_), custom_call_target="tpu_custom_call", output_to_operand_aliasing={{0}: (3, {})} | custom-call | flops 1048576 | bytes 8388608 | tf_op jit(solution)/shard_map/place/pallas_call | solution.py:58
  191.8 7.7 %plan.1 = (s32[1040]{0:T(1024)}, s32[64]{0:T(128)}) custom-call(s32[2]{0:T(128)} %pad_add_fusion.me_ref, f32[2056,256]{1,0:T(8,128)} %collective-permute-done.refs_0_.refs_1_, f32[2056,256]{1,0:T(8,128)} %copy-done, f32[2056,256]{1,0:T(8,128)} %collective-permute-done.5.refs_2_.refs_0_.refs_1_, f32[8,256]{1,0:T(8,128)} %copy-done.23, f32[2056,256]{1,0:T(8,128)} %copy-done.5, ...), custom_call_target="tpu_custom_call" | custom-call | tf_op jit(solution)/shard_map/plan/pallas_call | solution.py:138
  199.6 4.8 %place.15 = (bf16[2,4,4,4,2,256,256]{6,5,4,3,2,1,0:T(8,128)(2,1)}, f32[8,128]{1,0:T(8,128)}) custom-call(f32[2056,256]{1,0:T(8,128)} %copy-done.6, f32[2056,256]{1,0:T(8,128)} %copy-done.6, f32[2048,256]{1,0:T(8,128)} %collective-permute-done.18.refs_2_, bf16[2,4,4,4,2,256,256]{6,5,4,3,2,1,0:T(8,128)(2,1)} %get-tuple-element.109.refs_3_), custom_call_target="tpu_custom_call", output_to_operand_aliasing={{0}: (3, {})} | custom-call | flops 1048576 | bytes 8388608 | tf_op jit(solution)/shard_map/place/pallas_call | solution.py:58
  204.4 19.3 %product.5 = (f32[4,4,64,256]{3,2,1,0:T(8,128)}, f32[4,4,64,256]{3,2,1,0:T(8,128)}) custom-call(s32[2]{0:T(128)} %pad_add_fusion.me_ref, s32[1040]{0:T(1024)} %get-tuple-element.102.plan_ref, s32[64]{0:T(128)} %get-tuple-element.103.kept_ref, bf16[128,2,256,256]{3,2,1,0:T(8,128)(2,1)} %bitcast.17, f32[2056,256]{1,0:T(8,128)} %copy-done, ...), custom_call_target="tpu_custom_call" | custom-call | flops 6442450944 | bytes 16777216 | tf_op jit(solution)/shard_map/product/pallas_call | solution.py:246
  224.2 19.4 %product.6 = (f32[4,4,64,256]{3,2,1,0:T(8,128)}, f32[4,4,64,256]{3,2,1,0:T(8,128)}) custom-call(s32[2]{0:T(128)} %pad_add_fusion.me_ref, s32[1040]{0:T(1024)} %get-tuple-element.102.plan_ref, s32[64]{0:T(128)} %get-tuple-element.103.kept_ref, bf16[128,2,256,256]{3,2,1,0:T(8,128)(2,1)} %bitcast.18, f32[2056,256]{1,0:T(8,128)} %copy-done, ...), custom_call_target="tpu_custom_call" | custom-call | flops 6442450944 | bytes 16777216 | tf_op jit(solution)/shard_map/product/pallas_call | solution.py:246
  243.6 5.0 %collective-permute-done.23.other_ref = f32[4,4,64,256]{3,2,1,0:T(8,128)S(1)} collective-permute-done((f32[4,4,64,256]{3,2,1,0:T(8,128)}, f32[4,4,64,256]{3,2,1,0:T(8,128)S(1)}, u32[]{:S(2)}, u32[]{:S(2)}) %collective-permute-start.23) | collective-permute-done | bytes 1048608 | tf_op jit(solution)/shard_map/ppermute | solution.py:454
  248.6 1.0 copy-done.17
  249.6 3.6 inflate.5.refs_4_
  253.2 1.6 collective-permute-start.27
  255.1 0.8 collective-permute-start.31
  255.9 1.2 collective-permute-start.32
  257.1 21.4 %collective-permute-done.29.other_ref = f32[4,4,64,256]{3,2,1,0:T(8,128)} collective-permute-done((f32[4,4,64,256]{3,2,1,0:T(8,128)}, f32[4,4,64,256]{3,2,1,0:T(8,128)}, u32[]{:S(2)}, u32[]{:S(2)}) %collective-permute-start.29) | collective-permute-done | bytes 1048608 | tf_op jit(solution)/shard_map/ppermute | solution.py:454
  278.5 3.6 inflate.6.refs_8_
  282.1 19.1 %collective-permute-done.32.refs_3_ = f32[1024,256]{1,0:T(8,128)S(1)} collective-permute-done((f32[1024,256]{1,0:T(8,128)}, f32[1024,256]{1,0:T(8,128)S(1)}, u32[]{:S(2)}, u32[]{:S(2)}) %collective-permute-start.32) | collective-permute-done | bytes 1048608 | tf_op jit(solution)/shard_map/ppermute | solution.py:454
  301.2 1.5 collective-permute-start.37
  303.2 19.4 %product.7 = (f32[4,4,64,256]{3,2,1,0:T(8,128)}, f32[4,4,64,256]{3,2,1,0:T(8,128)}) custom-call(s32[2]{0:T(128)} %pad_add_fusion.me_ref, s32[1040]{0:T(1024)} %get-tuple-element.102.plan_ref, s32[64]{0:T(128)} %get-tuple-element.103.kept_ref, bf16[128,2,256,256]{3,2,1,0:T(8,128)(2,1)} %bitcast.19, f32[1024,256]{1,0:T(8,128)} %bitcast.34, ...), custom_call_target="tpu_custom_call" | custom-call | flops 6442450944 | bytes 16777216 | tf_op jit(solution)/shard_map/product/pallas_call | solution.py:246
  322.6 0.7 collective-permute-start.36
  324.0 1.0 copy-done.13
  325.0 14.4 %product.8 = (f32[4,4,32,256]{3,2,1,0:T(8,128)}, f32[4,4,32,256]{3,2,1,0:T(8,128)}) custom-call(s32[2]{0:T(128)} %pad_add_fusion.me_ref, s32[1040]{0:T(1024)} %get-tuple-element.102.plan_ref, s32[64]{0:T(128)} %get-tuple-element.103.kept_ref, bf16[128,2,256,256]{3,2,1,0:T(8,128)(2,1)} %bitcast.20, f32[1024,256]{1,0:T(8,128)} %bitcast.28, ...), custom_call_target="tpu_custom_call" | custom-call | flops 3221225472 | bytes 16777216 | tf_op jit(solution)/shard_map/product/pallas_call | solution.py:246
  339.5 6.1 %collective-permute-done.36.other_ref = f32[4,4,64,256]{3,2,1,0:T(8,128)} collective-permute-done((f32[4,4,64,256]{3,2,1,0:T(8,128)}, f32[4,4,64,256]{3,2,1,0:T(8,128)}, u32[]{:S(2)}, u32[]{:S(2)}) %collective-permute-start.36) | collective-permute-done | bytes 1048608 | tf_op jit(solution)/shard_map/ppermute | solution.py:556
  345.6 3.6 inflate.7.refs_12_
  349.2 1.5 collective-permute-start.39
  351.9 14.4 %product.9 = (f32[4,4,32,256]{3,2,1,0:T(8,128)}, f32[4,4,32,256]{3,2,1,0:T(8,128)}) custom-call(s32[2]{0:T(128)} %pad_add_fusion.me_ref, s32[1040]{0:T(1024)} %get-tuple-element.102.plan_ref, s32[64]{0:T(128)} %get-tuple-element.103.kept_ref, bf16[128,2,256,256]{3,2,1,0:T(8,128)(2,1)} %bitcast.21, f32[1024,256]{1,0:T(8,128)} %bitcast.29, ...), custom_call_target="tpu_custom_call" | custom-call | flops 3221225472 | bytes 16777216 | tf_op jit(solution)/shard_map/product/pallas_call | solution.py:246
  366.3 0.8 collective-permute-start.45
  367.1 3.3 inflate.8.refs_16_
  370.4 1.4 collective-permute-done.39.refs_14_
  371.8 1.5 collective-permute-start.43
  373.3 7.3 %collective-permute-done.45.other_ref = f32[4,4,32,256]{3,2,1,0:T(8,128)} collective-permute-done((f32[4,4,32,256]{3,2,1,0:T(8,128)}, f32[4,4,32,256]{3,2,1,0:T(8,128)}, u32[]{:S(2)}, u32[]{:S(2)}) %collective-permute-start.45) | collective-permute-done | bytes 524320 | tf_op jit(solution)/shard_map/ppermute | solution.py:556
  380.6 3.3 inflate.9.refs_20_
  383.9 1.9 collective-permute-done.43.refs_18_
  386.9 1.1 collective-permute-done.42.refs_17_
  388.5 12.6 %collective-permute-done.47.refs_22_ = f32[4,136,256]{2,1,0:T(8,128)S(1)} collective-permute-done((f32[4,136,256]{2,1,0:T(8,128)}, f32[4,136,256]{2,1,0:T(8,128)S(1)}, u32[]{:S(2)}, u32[]{:S(2)}) %collective-permute-start.47) | collective-permute-done | bytes 557088 | tf_op jit(solution)/shard_map/ppermute | solution.py:563
  401.1 1.9 collective-permute-done.48.refs_23_
  403.1 0.8 copy-done.22
  403.9 6.7 %owned.1 = f32[32,256,256]{2,1,0:T(8,128)} custom-call(s32[2]{0:T(128)} %pad_add_fusion.me_ref, f32[2056,256]{1,0:T(8,128)} %copy-done, f32[8,256]{1,0:T(8,128)} %copy-done.23, f32[2056,256]{1,0:T(8,128)} %copy-done.1, f32[2056,256]{1,0:T(8,128)} %copy-done.2, f32[4,264,256]{2,1,0:T(8,128)} %inflate.5.refs_4_, ...), custom_call_target="tpu_custom_call" | custom-call | flops 2097152 | bytes 16777216 | tf_op jit(solution)/shard_map/owned/pallas_call | solution.py:377
  (115 shorter events, 10.1 us)
Async XLA Ops:
  0.0 56.0 %collective-permute-start.1 = (f32[4096,256]{1,0:T(8,128)}, f32[4096,256]{1,0:T(8,128)}, u32[]{:S(2)}, u32[]{:S(2)}) collective-permute-start(f32[4096,256]{1,0:T(8,128)} %bitcast.22), channel_id=1, source_target_pairs={{0,8},{8,0},{16,24},{24,16},{1,9},{9,1},{17,25},{25,17},{2,10},{10... | collective-permute-start | bytes 12582920 | tf_op jit(solution)/shard_map/ppermute | solution.py:454
  6.8 60.3 %copy-start = (f32[2056,256]{1,0:T(8,128)}, f32[2056,256]{1,0:T(8,128)S(1)}, u32[]{:S(2)}) copy-start(f32[2056,256]{1,0:T(8,128)S(1)} %pad_maximum_fusion.refs_1_.refs_8_.refs_0_) | copy-start | bytes 6316036
  6.8 49.1 %collective-permute-start = (f32[2056,256]{1,0:T(8,128)S(1)}, f32[2056,256]{1,0:T(8,128)}, u32[]{:S(2)}, u32[]{:S(2)}) collective-permute-start(f32[2056,256]{1,0:T(8,128)S(1)} %pad_maximum_fusion.refs_1_.refs_8_.refs_0_), channel_id=1, source_target_pairs={{0,1},{1,0},{2,3},{3,2},{4,5},{5,4},{6,7},{7,6},{8,9},{9,8},{10,11... | collective-permute-start | bytes 6316040 | tf_op jit(solution)/shard_map/ppermute | solution.py:454
  9.4 47.9 %collective-permute-start.4 = (f32[2056,256]{1,0:T(8,128)S(1)}, f32[2056,256]{1,0:T(8,128)S(1)}, u32[]{:S(2)}, u32[]{:S(2)}) collective-permute-start(f32[2056,256]{1,0:T(8,128)S(1)} %pad_maximum_fusion.refs_1_.refs_8_.refs_0_), channel_id=1, source_target_pairs={{0,16},{8,24},{16,0},{24,8},{1,17},{9,25},{17,1},{25,9},{2,18},{10... | collective-permute-start | bytes 6316040 | tf_op jit(solution)/shard_map/ppermute | solution.py:454
  10.9 46.4 %collective-permute-start.3 = (f32[2056,256]{1,0:T(8,128)S(1)}, f32[2056,256]{1,0:T(8,128)S(1)}, u32[]{:S(2)}, u32[]{:S(2)}) collective-permute-start(f32[2056,256]{1,0:T(8,128)S(1)} %pad_maximum_fusion.refs_1_.refs_8_.refs_0_), channel_id=1, source_target_pairs={{0,8},{1,9},{2,4},{3,5},{4,2},{5,3},{6,14},{7,15},{8,0},{9,1},{10,... | collective-permute-start | bytes 6316040 | tf_op jit(solution)/shard_map/ppermute | solution.py:454
  10.9 48.9 %collective-permute-start.2 = (f32[2056,256]{1,0:T(8,128)S(1)}, f32[2056,256]{1,0:T(8,128)}, u32[]{:S(2)}, u32[]{:S(2)}) collective-permute-start(f32[2056,256]{1,0:T(8,128)S(1)} %pad_maximum_fusion.refs_1_.refs_8_.refs_0_), channel_id=1, source_target_pairs={{0,2},{1,3},{2,0},{3,1},{4,6},{5,7},{6,4},{7,5},{8,10},{9,11},{10,... | collective-permute-start | bytes 6316040 | tf_op jit(solution)/shard_map/ppermute | solution.py:454
  57.3 52.8 %copy-start.1 = (f32[2056,256]{1,0:T(8,128)}, f32[2056,256]{1,0:T(8,128)S(1)}, u32[]{:S(2)}) copy-start(f32[2056,256]{1,0:T(8,128)S(1)} %collective-permute-done.4.refs_0_.refs_1_.refs_5_.refs_2_) | copy-start | bytes 6316036
  57.3 9.9 %copy-start.3 = (f32[2056,256]{1,0:T(8,128)}, f32[2056,256]{1,0:T(8,128)S(1)}, u32[]{:S(2)}) copy-start(f32[2056,256]{1,0:T(8,128)S(1)} %collective-permute-done.3.refs_10_.refs_2_) | copy-start | bytes 6316036
  59.8 4.5 %collective-permute-start.5 = (f32[2056,256]{1,0:T(8,128)}, f32[2056,256]{1,0:T(8,128)}, u32[]{:S(2)}, u32[]{:S(2)}) collective-permute-start(f32[2056,256]{1,0:T(8,128)} %collective-permute-done.refs_0_.refs_1_), channel_id=1, source_target_pairs={{0,8},{8,0},{16,24},{24,16},{1,9},{9,1},{17,25},{25,17},{2,10},{10... | collective-permute-start | bytes 6316040 | tf_op jit(solution)/shard_map/ppermute | solution.py:454
  59.8 50.3 %collective-permute-start.7 = (f32[2056,256]{1,0:T(8,128)S(1)}, f32[2056,256]{1,0:T(8,128)}, u32[]{:S(2)}, u32[]{:S(2)}) collective-permute-start(f32[2056,256]{1,0:T(8,128)S(1)} %collective-permute-done.3.refs_10_.refs_2_), channel_id=1, source_target_pairs={{0,2},{1,3},{2,0},{3,1},{4,6},{5,7},{6,4},{7,5},{8,10},{9,11},{10,... | collective-permute-start | bytes 6316040 | tf_op jit(solution)/shard_map/ppermute | solution.py:454
  61.5 48.6 %collective-permute-start.8 = (f32[2056,256]{1,0:T(8,128)}, f32[2056,256]{1,0:T(8,128)}, u32[]{:S(2)}, u32[]{:S(2)}) collective-permute-start(f32[2056,256]{1,0:T(8,128)} %collective-permute-done.2.refs_9_.refs_1_), channel_id=1, source_target_pairs={{0,8},{1,9},{2,4},{3,5},{4,2},{5,3},{6,14},{7,15},{8,0},{9,1},{10,... | collective-permute-start | bytes 6316040 | tf_op jit(solution)/shard_map/ppermute | solution.py:454
  61.8 48.1 %collective-permute-start.10 = (f32[2048,256]{1,0:T(8,128)}, f32[2048,256]{1,0:T(8,128)}, u32[]{:S(2)}, u32[]{:S(2)}) collective-permute-start(f32[2048,256]{1,0:T(8,128)} %bitcast.36), channel_id=1, source_target_pairs={{0,16},{8,24},{16,0},{24,8},{1,17},{9,25},{17,1},{25,9},{2,18},{10... | collective-permute-start | bytes 6291464 | tf_op jit(solution)/shard_map/ppermute | solution.py:454
  62.3 47.9 %collective-permute-start.9 = (f32[2048,256]{1,0:T(8,128)}, f32[2048,256]{1,0:T(8,128)}, u32[]{:S(2)}, u32[]{:S(2)}) collective-permute-start(f32[2048,256]{1,0:T(8,128)} %bitcast.37), channel_id=1, source_target_pairs={{0,1},{1,0},{2,3},{3,2},{4,5},{5,4},{6,7},{7,6},{8,9},{9,8},{10,11... | collective-permute-start | bytes 6291464 | tf_op jit(solution)/shard_map/ppermute | solution.py:454
  64.3 8.2 %collective-permute-start.6 = (f32[8,256]{1,0:T(8,128)S(1)}, f32[8,256]{1,0:T(8,128)S(1)}, u32[]{:S(2)}, u32[]{:S(2)}) collective-permute-start(f32[8,256]{1,0:T(8,128)S(1)} %broadcast_in_dim.6), channel_id=1, source_target_pairs={{0,8},{8,0},{16,24},{24,16},{1,9},{9,1},{17,25},{25,17},{2,10},{10... | collective-permute-start | bytes 24584 | tf_op jit(solution)/shard_map/ppermute | solution.py:454
  67.2 107.9 %copy-start.7 = (f32[16,2,32,256]{3,2,0,1:T(8,128)}, f32[16,2,32,256]{3,2,0,1:T(8,128)S(1)}, u32[]{:S(2)}) copy-start(f32[16,2,32,256]{3,2,0,1:T(8,128)S(1)} %copy.13) | copy-start | bytes 3145732
  72.5 51.8 %copy-start.23 = (f32[8,256]{1,0:T(8,128)}, f32[8,256]{1,0:T(8,128)S(1)}, u32[]{:S(2)}) copy-start(f32[8,256]{1,0:T(8,128)S(1)} %collective-permute-done.6.refs_3_.refs_1_) | copy-start | bytes 24580
  110.1 4.2 %collective-permute-start.11 = (f32[2056,256]{1,0:T(8,128)S(1)}, f32[2056,256]{1,0:T(8,128)S(1)}, u32[]{:S(2)}, u32[]{:S(2)}) collective-permute-start(f32[2056,256]{1,0:T(8,128)S(1)} %collective-permute-done.4.refs_0_.refs_1_.refs_5_.refs_2_), channel_id=1, source_target_pairs={{0,8},{8,0},{16,24},{24,16},{1,9},{9,1},{17,25},{25,17},{2,10},{10... | collective-permute-start | bytes 6316040 | tf_op jit(solution)/shard_map/ppermute | solution.py:454
  114.4 10.0 %copy-start.2 = (f32[2056,256]{1,0:T(8,128)}, f32[2056,256]{1,0:T(8,128)S(1)}, u32[]{:S(2)}) copy-start(f32[2056,256]{1,0:T(8,128)S(1)} %collective-permute-done.11.refs_7_.refs_0_.refs_1_.refs_3_) | copy-start | bytes 6316036
  114.4 4.5 %collective-permute-start.13 = (f32[2048,256]{1,0:T(8,128)}, f32[2048,256]{1,0:T(8,128)}, u32[]{:S(2)}, u32[]{:S(2)}) collective-permute-start(f32[2048,256]{1,0:T(8,128)} %collective-permute-done.9.refs_2_), channel_id=1, source_target_pairs={{0,8},{8,0},{16,24},{24,16},{1,9},{9,1},{17,25},{25,17},{2,10},{10... | collective-permute-start | bytes 6291464 | tf_op jit(solution)/shard_map/ppermute | solution.py:454
  114.5 48.3 %collective-permute-start.12 = (f32[2056,256]{1,0:T(8,128)}, f32[2056,256]{1,0:T(8,128)S(1)}, u32[]{:S(2)}, u32[]{:S(2)}) collective-permute-start(f32[2056,256]{1,0:T(8,128)} %collective-permute-done.refs_0_.refs_1_), channel_id=1, source_target_pairs={{0,16},{8,24},{16,0},{24,8},{1,17},{9,25},{17,1},{25,9},{2,18},{10... | collective-permute-start | bytes 6316040 | tf_op jit(solution)/shard_map/ppermute | solution.py:454
  116.1 51.2 %collective-permute-start.15 = (f32[2056,256]{1,0:T(8,128)}, f32[2056,256]{1,0:T(8,128)S(1)}, u32[]{:S(2)}, u32[]{:S(2)}) collective-permute-start(f32[2056,256]{1,0:T(8,128)} %collective-permute-done.8.refs_12_.refs_4_), channel_id=1, source_target_pairs={{0,2},{1,3},{2,0},{3,1},{4,6},{5,7},{6,4},{7,5},{8,10},{9,11},{10,... | collective-permute-start | bytes 6316040 | tf_op jit(solution)/shard_map/ppermute | solution.py:454
  118.9 43.9 %collective-permute-start.14 = (f32[2048,256]{1,0:T(8,128)}, f32[2048,256]{1,0:T(8,128)}, u32[]{:S(2)}, u32[]{:S(2)}) collective-permute-start(f32[2048,256]{1,0:T(8,128)} %collective-permute-done.10.refs_2_), channel_id=1, source_target_pairs={{0,8},{8,0},{16,24},{24,16},{1,9},{9,1},{17,25},{25,17},{2,10},{10... | collective-permute-start | bytes 6291464 | tf_op jit(solution)/shard_map/ppermute | solution.py:454
  119.0 48.2 %collective-permute-start.16 = (f32[2048,256]{1,0:T(8,128)}, f32[2048,256]{1,0:T(8,128)}, u32[]{:S(2)}, u32[]{:S(2)}) collective-permute-start(f32[2048,256]{1,0:T(8,128)} %collective-permute-done.10.refs_2_), channel_id=1, source_target_pairs={{0,1},{1,0},{2,3},{3,2},{4,5},{5,4},{6,7},{7,6},{8,9},{9,8},{10,11... | collective-permute-start | bytes 6291464 | tf_op jit(solution)/shard_map/ppermute | solution.py:454
  162.8 4.4 %copy-start.5 = (f32[2056,256]{1,0:T(8,128)}, f32[2056,256]{1,0:T(8,128)S(1)}, u32[]{:S(2)}) copy-start(f32[2056,256]{1,0:T(8,128)S(1)} %collective-permute-done.12.refs_4_.refs_0_.refs_1_) | copy-start | bytes 6316036
  167.3 15.0 %copy-start.4 = (f32[2056,256]{1,0:T(8,128)}, f32[2056,256]{1,0:T(8,128)S(1)}, u32[]{:S(2)}) copy-start(f32[2056,256]{1,0:T(8,128)S(1)} %collective-permute-done.15.refs_13_.refs_5_) | copy-start | bytes 6316036
  167.3 4.2 %collective-permute-start.17 = (f32[2056,256]{1,0:T(8,128)S(1)}, f32[2056,256]{1,0:T(8,128)S(1)}, u32[]{:S(2)}, u32[]{:S(2)}) collective-permute-start(f32[2056,256]{1,0:T(8,128)S(1)} %collective-permute-done.12.refs_4_.refs_0_.refs_1_), channel_id=1, source_target_pairs={{0,8},{8,0},{16,24},{24,16},{1,9},{9,1},{17,25},{25,17},{2,10},{10... | collective-permute-start | bytes 6316040 | tf_op jit(solution)/shard_map/ppermute | solution.py:454
  172.8 26.8 %collective-permute-start.18 = (f32[2048,256]{1,0:T(8,128)}, f32[2048,256]{1,0:T(8,128)}, u32[]{:S(2)}, u32[]{:S(2)}) collective-permute-start(f32[2048,256]{1,0:T(8,128)} %collective-permute-done.16.refs_2_), channel_id=1, source_target_pairs={{0,8},{8,0},{16,24},{24,16},{1,9},{9,1},{17,25},{25,17},{2,10},{10... | collective-permute-start | bytes 6291464 | tf_op jit(solution)/shard_map/ppermute | solution.py:454
  172.9 50.8 %collective-permute-start.20 = (f32[1024,256]{1,0:T(8,128)}, f32[1024,256]{1,0:T(8,128)}, u32[]{:S(2)}, u32[]{:S(2)}) collective-permute-start(f32[1024,256]{1,0:T(8,128)} %bitcast.32), channel_id=1, source_target_pairs={{0,8},{1,9},{2,4},{3,5},{4,2},{5,3},{6,14},{7,15},{8,0},{9,1},{10,... | collective-permute-start | bytes 3145736 | tf_op jit(solution)/shard_map/ppermute | solution.py:454
  173.3 50.4 %collective-permute-start.19 = (f32[1024,256]{1,0:T(8,128)}, f32[1024,256]{1,0:T(8,128)}, u32[]{:S(2)}, u32[]{:S(2)}) collective-permute-start(f32[1024,256]{1,0:T(8,128)} %bitcast.33), channel_id=1, source_target_pairs={{0,2},{1,3},{2,0},{3,1},{4,6},{5,7},{6,4},{7,5},{8,10},{9,11},{10,... | collective-permute-start | bytes 3145736 | tf_op jit(solution)/shard_map/ppermute | solution.py:454
  175.1 48.6 %collective-permute-start.22 = (f32[1024,256]{1,0:T(8,128)S(1)}, f32[1024,256]{1,0:T(8,128)}, u32[]{:S(2)}, u32[]{:S(2)}) collective-permute-start(f32[1024,256]{1,0:T(8,128)S(1)} %bitcast.26), channel_id=1, source_target_pairs={{0,8},{1,9},{2,4},{3,5},{4,2},{5,3},{6,14},{7,15},{8,0},{9,1},{10,... | collective-permute-start | bytes 3145736 | tf_op jit(solution)/shard_map/ppermute | solution.py:454
  175.1 48.6 %collective-permute-start.21 = (f32[1024,256]{1,0:T(8,128)S(1)}, f32[1024,256]{1,0:T(8,128)}, u32[]{:S(2)}, u32[]{:S(2)}) collective-permute-start(f32[1024,256]{1,0:T(8,128)S(1)} %bitcast.27), channel_id=1, source_target_pairs={{0,2},{1,3},{2,0},{3,1},{4,6},{5,7},{6,4},{7,5},{8,10},{9,11},{10,... | collective-permute-start | bytes 3145736 | tf_op jit(solution)/shard_map/ppermute | solution.py:454
  223.8 24.9 %collective-permute-start.23 = (f32[4,4,64,256]{3,2,1,0:T(8,128)}, f32[4,4,64,256]{3,2,1,0:T(8,128)S(1)}, u32[]{:S(2)}, u32[]{:S(2)}) collective-permute-start(f32[4,4,64,256]{3,2,1,0:T(8,128)} %get-tuple-element.119), channel_id=1, source_target_pairs={{0,1},{1,0},{2,3},{3,2},{4,5},{5,4},{6,7},{7,6},{8,9},{9,8},{10,11... | collective-permute-start | bytes 3145736 | tf_op jit(solution)/shard_map/ppermute | solution.py:454
  223.8 29.3 %collective-permute-start.25 = (f32[1024,256]{1,0:T(8,128)}, f32[1024,256]{1,0:T(8,128)S(1)}, u32[]{:S(2)}, u32[]{:S(2)}) collective-permute-start(f32[1024,256]{1,0:T(8,128)} %collective-permute-done.20.refs_2_), channel_id=1, source_target_pairs={{0,2},{1,3},{2,0},{3,1},{4,6},{5,7},{6,4},{7,5},{8,10},{9,11},{10,... | collective-permute-start | bytes 3145736 | tf_op jit(solution)/shard_map/ppermute | solution.py:454
  224.2 29.0 %collective-permute-start.26 = (f32[1024,256]{1,0:T(8,128)}, f32[1024,256]{1,0:T(8,128)}, u32[]{:S(2)}, u32[]{:S(2)}) collective-permute-start(f32[1024,256]{1,0:T(8,128)} %collective-permute-done.19.refs_1_), channel_id=1, source_target_pairs={{0,8},{1,9},{2,4},{3,5},{4,2},{5,3},{6,14},{7,15},{8,0},{9,1},{10,... | collective-permute-start | bytes 3145736 | tf_op jit(solution)/shard_map/ppermute | solution.py:454
  253.2 50.0 %copy-start.16 = (f32[1024,256]{1,0:T(8,128)}, f32[1024,256]{1,0:T(8,128)S(1)}, u32[]{:S(2)}) copy-start(f32[1024,256]{1,0:T(8,128)S(1)} %collective-permute-done.25.refs_3_) | copy-start | bytes 3145732
  253.2 48.0 %collective-permute-start.27 = (f32[4,264,256]{2,1,0:T(8,128)}, f32[4,264,256]{2,1,0:T(8,128)}, u32[]{:S(2)}, u32[]{:S(2)}) collective-permute-start(f32[4,264,256]{2,1,0:T(8,128)} %inflate.5.refs_4_), channel_id=1, source_target_pairs={{0,16},{8,24},{16,0},{24,8},{1,17},{9,25},{17,1},{25,9},{2,18},{10... | collective-permute-start | bytes 3244040 | tf_op jit(solution)/shard_map/ppermute | solution.py:454
  254.8 23.7 %collective-permute-start.29 = (f32[4,4,64,256]{3,2,1,0:T(8,128)}, f32[4,4,64,256]{3,2,1,0:T(8,128)}, u32[]{:S(2)}, u32[]{:S(2)}) collective-permute-start(f32[4,4,64,256]{3,2,1,0:T(8,128)} %get-tuple-element.125), channel_id=1, source_target_pairs={{0,1},{1,0},{2,3},{3,2},{4,5},{5,4},{6,7},{7,6},{8,9},{9,8},{10,11... | collective-permute-start | bytes 3145736 | tf_op jit(solution)/shard_map/ppermute | solution.py:454
  255.1 27.0 %collective-permute-start.31 = (f32[1024,256]{1,0:T(8,128)}, f32[1024,256]{1,0:T(8,128)}, u32[]{:S(2)}, u32[]{:S(2)}) collective-permute-start(f32[1024,256]{1,0:T(8,128)} %collective-permute-done.26.refs_4_), channel_id=1, source_target_pairs={{0,2},{1,3},{2,0},{3,1},{4,6},{5,7},{6,4},{7,5},{8,10},{9,11},{10,... | collective-permute-start | bytes 3145736 | tf_op jit(solution)/shard_map/ppermute | solution.py:454
  255.9 45.3 %collective-permute-start.32 = (f32[1024,256]{1,0:T(8,128)}, f32[1024,256]{1,0:T(8,128)S(1)}, u32[]{:S(2)}, u32[]{:S(2)}) collective-permute-start(f32[1024,256]{1,0:T(8,128)} %collective-permute-done.22.refs_2_), channel_id=1, source_target_pairs={{0,2},{1,3},{2,0},{3,1},{4,6},{5,7},{6,4},{7,5},{8,10},{9,11},{10,... | collective-permute-start | bytes 3145736 | tf_op jit(solution)/shard_map/ppermute | solution.py:454
  257.1 44.1 %collective-permute-start.33 = (f32[1024,256]{1,0:T(8,128)}, f32[1024,256]{1,0:T(8,128)S(1)}, u32[]{:S(2)}, u32[]{:S(2)}) collective-permute-start(f32[1024,256]{1,0:T(8,128)} %collective-permute-done.21.refs_1_), channel_id=1, source_target_pairs={{0,8},{1,9},{2,4},{3,5},{4,2},{5,3},{6,14},{7,15},{8,0},{9,1},{10,... | collective-permute-start | bytes 3145736 | tf_op jit(solution)/shard_map/ppermute | solution.py:454
  301.2 21.5 %copy-start.11 = (f32[1024,256]{1,0:T(8,128)}, f32[1024,256]{1,0:T(8,128)S(1)}, u32[]{:S(2)}) copy-start(f32[1024,256]{1,0:T(8,128)S(1)} %collective-permute-done.32.refs_3_) | copy-start | bytes 3145732
  301.2 21.5 %copy-start.12 = (f32[1024,256]{1,0:T(8,128)}, f32[1024,256]{1,0:T(8,128)S(1)}, u32[]{:S(2)}) copy-start(f32[1024,256]{1,0:T(8,128)S(1)} %collective-permute-done.33.refs_4_) | copy-start | bytes 3145732
  301.2 22.9 %collective-permute-start.37 = (f32[1024,256]{1,0:T(8,128)S(1)}, f32[1024,256]{1,0:T(8,128)S(1)}, u32[]{:S(2)}, u32[]{:S(2)}) collective-permute-start(f32[1024,256]{1,0:T(8,128)S(1)} %collective-permute-done.33.refs_4_), channel_id=1, source_target_pairs={{0,2},{1,3},{2,0},{3,1},{4,6},{5,7},{6,4},{7,5},{8,10},{9,11},{10,... | collective-permute-start | bytes 3145736 | tf_op jit(solution)/shard_map/ppermute | solution.py:454
  302.7 46.5 %collective-permute-start.34 = (f32[4,264,256]{2,1,0:T(8,128)}, f32[4,264,256]{2,1,0:T(8,128)}, u32[]{:S(2)}, u32[]{:S(2)}) collective-permute-start(f32[4,264,256]{2,1,0:T(8,128)} %inflate.6.refs_8_), channel_id=1, source_target_pairs={{0,16},{8,24},{16,0},{24,8},{1,17},{9,25},{17,1},{25,9},{2,18},{10... | collective-permute-start | bytes 3244040 | tf_op jit(solution)/shard_map/ppermute | solution.py:454
  322.6 22.9 %collective-permute-start.36 = (f32[4,4,64,256]{3,2,1,0:T(8,128)}, f32[4,4,64,256]{3,2,1,0:T(8,128)}, u32[]{:S(2)}, u32[]{:S(2)}) collective-permute-start(f32[4,4,64,256]{3,2,1,0:T(8,128)} %get-tuple-element.132), channel_id=1, source_target_pairs={{0,1},{1,0},{2,3},{3,2},{4,5},{5,4},{6,7},{7,6},{8,9},{9,8},{10,11... | collective-permute-start | bytes 3145736 | tf_op jit(solution)/shard_map/ppermute | solution.py:556
  339.4 12.0 %copy-start.8 = (f32[4,264,256]{2,1,0:T(8,128)S(1)}, f32[4,264,256]{2,1,0:T(8,128)}, u32[]{:S(2)}) copy-start(f32[4,264,256]{2,1,0:T(8,128)} %inflate.5.refs_4_) | copy-start | bytes 3244036
  339.4 12.0 %copy-start.9 = (f32[4,264,256]{2,1,0:T(8,128)S(1)}, f32[4,264,256]{2,1,0:T(8,128)}, u32[]{:S(2)}) copy-start(f32[4,264,256]{2,1,0:T(8,128)} %inflate.6.refs_8_) | copy-start | bytes 3244036
  349.1 31.5 %copy-start.10 = (f32[4,264,256]{2,1,0:T(8,128)S(1)}, f32[4,264,256]{2,1,0:T(8,128)}, u32[]{:S(2)}) copy-start(f32[4,264,256]{2,1,0:T(8,128)} %inflate.7.refs_12_) | copy-start | bytes 3244036
  349.2 22.7 %collective-permute-start.39 = (f32[4,264,256]{2,1,0:T(8,128)}, f32[4,264,256]{2,1,0:T(8,128)}, u32[]{:S(2)}, u32[]{:S(2)}) collective-permute-start(f32[4,264,256]{2,1,0:T(8,128)} %inflate.7.refs_12_), channel_id=1, source_target_pairs={{0,16},{8,24},{16,0},{24,8},{1,17},{9,25},{17,1},{25,9},{2,18},{10... | collective-permute-start | bytes 3244040 | tf_op jit(solution)/shard_map/ppermute | solution.py:563
  350.7 15.6 %collective-permute-start.41 = (f32[4,4,32,256]{3,2,1,0:T(8,128)}, f32[4,4,32,256]{3,2,1,0:T(8,128)}, u32[]{:S(2)}, u32[]{:S(2)}) collective-permute-start(f32[4,4,32,256]{3,2,1,0:T(8,128)} %get-tuple-element.139), channel_id=1, source_target_pairs={{0,1},{1,0},{2,3},{3,2},{4,5},{5,4},{6,7},{7,6},{8,9},{9,8},{10,11... | collective-permute-start | bytes 1572872 | tf_op jit(solution)/shard_map/ppermute | solution.py:556
  351.4 34.4 %collective-permute-start.24 = (f32[4,264,256]{2,1,0:T(8,128)S(1)}, f32[4,264,256]{2,1,0:T(8,128)}, u32[]{:S(2)}, u32[]{:S(2)}) collective-permute-start(f32[4,264,256]{2,1,0:T(8,128)S(1)} %copy-done.8), channel_id=1, source_target_pairs={{0,8},{8,0},{16,24},{24,16},{1,9},{9,1},{17,25},{25,17},{2,10},{10... | collective-permute-start | bytes 3244040 | tf_op jit(solution)/shard_map/ppermute | solution.py:541
  351.4 35.0 %collective-permute-start.30 = (f32[4,264,256]{2,1,0:T(8,128)S(1)}, f32[4,264,256]{2,1,0:T(8,128)}, u32[]{:S(2)}, u32[]{:S(2)}) collective-permute-start(f32[4,264,256]{2,1,0:T(8,128)S(1)} %copy-done.9), channel_id=1, source_target_pairs={{0,8},{8,0},{16,24},{24,16},{1,9},{9,1},{17,25},{25,17},{2,10},{10... | collective-permute-start | bytes 3244040 | tf_op jit(solution)/shard_map/ppermute | solution.py:541
  366.3 14.3 %collective-permute-start.45 = (f32[4,4,32,256]{3,2,1,0:T(8,128)}, f32[4,4,32,256]{3,2,1,0:T(8,128)}, u32[]{:S(2)}, u32[]{:S(2)}) collective-permute-start(f32[4,4,32,256]{3,2,1,0:T(8,128)} %get-tuple-element.145), channel_id=1, source_target_pairs={{0,1},{1,0},{2,3},{3,2},{4,5},{5,4},{6,7},{7,6},{8,9},{9,8},{10,11... | collective-permute-start | bytes 1572872 | tf_op jit(solution)/shard_map/ppermute | solution.py:556
  367.1 19.5 %collective-permute-start.28 = (f32[4,264,256]{2,1,0:T(8,128)}, f32[4,264,256]{2,1,0:T(8,128)}, u32[]{:S(2)}, u32[]{:S(2)}) collective-permute-start(f32[4,264,256]{2,1,0:T(8,128)} %collective-permute-done.27.refs_6_), channel_id=1, source_target_pairs={{0,8},{8,0},{16,24},{24,16},{1,9},{9,1},{17,25},{25,17},{2,10},{10... | collective-permute-start | bytes 3244040 | tf_op jit(solution)/shard_map/ppermute | solution.py:541
  371.8 14.0 %collective-permute-start.43 = (f32[4,136,256]{2,1,0:T(8,128)}, f32[4,136,256]{2,1,0:T(8,128)}, u32[]{:S(2)}, u32[]{:S(2)}) collective-permute-start(f32[4,136,256]{2,1,0:T(8,128)} %inflate.8.refs_16_), channel_id=1, source_target_pairs={{0,16},{8,24},{16,0},{24,8},{1,17},{9,25},{17,1},{25,9},{2,18},{10... | collective-permute-start | bytes 1671176 | tf_op jit(solution)/shard_map/ppermute | solution.py:563
  380.6 7.5 %collective-permute-start.38 = (f32[4,264,256]{2,1,0:T(8,128)S(1)}, f32[4,264,256]{2,1,0:T(8,128)}, u32[]{:S(2)}, u32[]{:S(2)}) collective-permute-start(f32[4,264,256]{2,1,0:T(8,128)S(1)} %copy-done.10), channel_id=1, source_target_pairs={{0,8},{8,0},{16,24},{24,16},{1,9},{9,1},{17,25},{25,17},{2,10},{10... | collective-permute-start | bytes 3244040 | tf_op jit(solution)/shard_map/ppermute | solution.py:564
  385.8 2.2 collective-permute-start.42
  385.8 15.2 %collective-permute-start.47 = (f32[4,136,256]{2,1,0:T(8,128)}, f32[4,136,256]{2,1,0:T(8,128)S(1)}, u32[]{:S(2)}, u32[]{:S(2)}) collective-permute-start(f32[4,136,256]{2,1,0:T(8,128)} %inflate.9.refs_20_), channel_id=1, source_target_pairs={{0,16},{8,24},{16,0},{24,8},{1,17},{9,25},{17,1},{25,9},{2,18},{10... | collective-permute-start | bytes 1671176 | tf_op jit(solution)/shard_map/ppermute | solution.py:563
  386.4 14.7 %collective-permute-start.35 = (f32[4,264,256]{2,1,0:T(8,128)}, f32[4,264,256]{2,1,0:T(8,128)S(1)}, u32[]{:S(2)}, u32[]{:S(2)}) collective-permute-start(f32[4,264,256]{2,1,0:T(8,128)} %collective-permute-done.34.refs_10_), channel_id=1, source_target_pairs={{0,8},{8,0},{16,24},{24,16},{1,9},{9,1},{17,25},{25,17},{2,10},{10... | collective-permute-start | bytes 3244040 | tf_op jit(solution)/shard_map/ppermute | solution.py:541
  386.6 14.5 %collective-permute-start.40 = (f32[4,264,256]{2,1,0:T(8,128)}, f32[4,264,256]{2,1,0:T(8,128)S(1)}, u32[]{:S(2)}, u32[]{:S(2)}) collective-permute-start(f32[4,264,256]{2,1,0:T(8,128)} %collective-permute-done.39.refs_14_), channel_id=1, source_target_pairs={{0,8},{8,0},{16,24},{24,16},{1,9},{9,1},{17,25},{25,17},{2,10},{10... | collective-permute-start | bytes 3244040 | tf_op jit(solution)/shard_map/ppermute | solution.py:564
  388.0 15.1 %copy-start.18 = (f32[4,136,256]{2,1,0:T(8,128)}, f32[4,136,256]{2,1,0:T(8,128)S(1)}, u32[]{:S(2)}) copy-start(f32[4,136,256]{2,1,0:T(8,128)S(1)} %collective-permute-done.42.refs_17_) | copy-start | bytes 1671172
  388.0 13.1 %collective-permute-start.46 = (f32[4,136,256]{2,1,0:T(8,128)}, f32[4,136,256]{2,1,0:T(8,128)S(1)}, u32[]{:S(2)}, u32[]{:S(2)}) collective-permute-start(f32[4,136,256]{2,1,0:T(8,128)} %inflate.9.refs_20_), channel_id=1, source_target_pairs={{0,8},{8,0},{16,24},{24,16},{1,9},{9,1},{17,25},{25,17},{2,10},{10... | collective-permute-start | bytes 1671176 | tf_op jit(solution)/shard_map/ppermute | solution.py:564
  388.1 13.0 %collective-permute-start.44 = (f32[4,136,256]{2,1,0:T(8,128)}, f32[4,136,256]{2,1,0:T(8,128)S(1)}, u32[]{:S(2)}, u32[]{:S(2)}) collective-permute-start(f32[4,136,256]{2,1,0:T(8,128)} %collective-permute-done.43.refs_18_), channel_id=1, source_target_pairs={{0,8},{8,0},{16,24},{24,16},{1,9},{9,1},{17,25},{25,17},{2,10},{10... | collective-permute-start | bytes 1671176 | tf_op jit(solution)/shard_map/ppermute | solution.py:564
  401.1 2.0 collective-permute-start.48
  (10 other events, 14.4 us)

commit v4 on v3

--- a/solution.py
+++ b/solution.py
@@ -149,16 +149,18 @@
     )(me, *args)
 
 
-def product_kernel(line, grid_blocks, part, me_ref, plan_ref, kept_ref, b_ref, *refs):
+def product_kernel(line, groups, part, me_ref, plan_ref, kept_ref, b_ref, *refs):
     parts = 2 * line - 2
     a_refs = refs[:parts]
-    other_ref, own_ref, raw, halves, total, ring, a_sems, b_sems = refs[parts:]
-    group, j = pl.program_id(0), pl.program_id(1)
-    blocks, count, rows, width = (grid_blocks, *other_ref.shape[1:])
+    out_refs, (raw, halves, total, ring, a_sems, b_sems) = refs[parts:-6], refs[-6:]
+    blocks = (halves.shape[0] - 1) // line
+    count, rows, width = out_refs[0].shape[1:]
+    group, j = pl.program_id(0) + groups[0], pl.program_id(1)
     size = blocks * count * rows
-    last = 2 * blocks - 1
+    top, last = groups[0] * blocks, (groups[-1] + 1) * blocks - 1
     row = group * blocks + j
     q = me_ref[1] // 2
+    begun = kept_ref[FIELDS * (top - 1)] if top else 0
     end = kept_ref[FIELDS * last]
 
     def fetch(n):
@@ -166,7 +168,7 @@
         slot = n % RING
         return pltpu.make_async_copy(b_ref.at[tile], ring.at[slot], b_sems.at[slot])
 
-    @pl.when(row == 0)
+    @pl.when(row == top)
     def _():
         def each(act):
             for i in range(parts):
@@ -185,7 +187,7 @@
             fetch(n).start()
             return 0
 
-        lax.fori_loop(0, jnp.minimum(end, RING), begin, 0)
+        lax.fori_loop(begun, jnp.minimum(end, begun + RING), begin, 0)
         halves[line * blocks] = jnp.zeros(halves.shape[1:], halves.dtype)
         each(lambda copy: copy.wait())
 
@@ -199,7 +201,7 @@
         lax.fori_loop(0, line * blocks, convert, 0)
 
     total[...] = jnp.zeros_like(total)
-    first = jnp.where(row == 0, 0, kept_ref[FIELDS * jnp.maximum(row - 1, 0)])
+    first = jnp.where(row == top, begun, kept_ref[FIELDS * jnp.maximum(row - 1, 0)])
 
     def multiply(n):
         a = halves[plan_ref[FIELDS * n + 1]]
@@ -228,31 +230,29 @@
 
     lax.fori_loop(0, (kept_ref[FIELDS * row] - first) // 2, step, 0)
 
-    @pl.when(group == 0)
-    def _():
-        for m in range(count):
-            other_ref[0, m] = total[kept_ref[FIELDS * row + 1 + m]]
-
-    @pl.when(group == 1)
-    def _():
-        for m in range(count):
-            own_ref[0, m] = total[kept_ref[FIELDS * row + 1 + m]]
-
-
-def product(me, plan, panel, parts, line, part, rows):
+    for g, out_ref in zip(groups, out_refs):
+
+        @pl.when(group == g)
+        def _():
+            for m in range(count):
+                out_ref[0, m] = total[kept_ref[FIELDS * row + 1 + m]]
+
+
+def product(me, plan, panel, parts, line, part, rows, groups=(0, 1)):
     blocks, count, width = panel.shape[1], panel.shape[3], panel.shape[6]
     out = jax.ShapeDtypeStruct((blocks, count, rows, width), jnp.float32)
     smem = pl.BlockSpec(memory_space=pltpu.SMEM)
     return pl.pallas_call(
-        functools.partial(product_kernel, line, blocks, part),
-        grid=(2, blocks),
-        out_shape=(out, out),
+        functools.partial(product_kernel, line, groups, part),
+        grid=(len(groups), blocks),
+        out_shape=(out,) * len(groups),
         in_specs=[smem] * 3 + [pl.BlockSpec(memory_space=pl.ANY)] * (1 + len(parts)),
-        out_specs=(
+        out_specs=tuple(
             pl.BlockSpec(
-                (1, count, rows, width), lambda g, j: (jnp.where(g == 0, j, blocks - 1), 0, 0, 0)
-            ),
-            pl.BlockSpec((1, count, rows, width), lambda g, j: (jnp.where(g == 0, 0, j), 0, 0, 0)),
+                (1, count, rows, width),
+                lambda g, j, i=i: (jnp.where(g == i, j, 0 if i else blocks - 1), 0, 0, 0),
+            )
+            for i in range(len(groups))
         ),
         scratch_shapes=[
             pltpu.VMEM((line * blocks * count * rows, width), jnp.float32),
@@ -264,8 +264,8 @@
         ],
         compiler_params=pltpu.CompilerParams(vmem_limit_bytes=VMEM),
         cost_estimate=pl.CostEstimate(
-            flops=3 * 2 * 16 * blocks * count * rows * width * width,
-            bytes_accessed=panel.size,
+            flops=3 * len(groups) * 16 * blocks * count * rows * width * width,
+            bytes_accessed=len(groups) * panel.size // 2,
             transcendentals=0,
         ),
         name="product",
@@ -273,26 +273,24 @@
 
 
 def inflate_kernel(own_ref, other_ref, out_ref):
-    count, rows = own_ref.shape[1:3]
-    partial = jnp.zeros((8, own_ref.shape[3]), jnp.float32)
-    for m in range(count):
-        kept = own_ref[0, m] + other_ref[0, m]
-        inflated = kept * kept
-        out_ref[0, m * rows : (m + 1) * rows] = inflated
-        for i in range(0, rows, 8):
-            partial += inflated[i : i + 8]
-    out_ref[0, count * rows :] = partial
+    blocks, count, rows, width = own_ref.shape
+    for j in range(blocks):
+        partial = jnp.zeros((8, width), jnp.float32)
+        for m in range(count):
+            kept = own_ref[j, m] + other_ref[j, m]
+            inflated = kept * kept
+            out_ref[j, m * rows : (m + 1) * rows] = inflated
+            for i in range(0, rows, 8):
+                partial += inflated[i : i + 8]
+        out_ref[j, count * rows :] = partial
 
 
 def inflate(own, other):
     blocks, count, rows, width = own.shape
-    spec = pl.BlockSpec((1, count, rows, width), lambda j: (j, 0, 0, 0))
     return pl.pallas_call(
         inflate_kernel,
-        grid=(blocks,),
         out_shape=jax.ShapeDtypeStruct((blocks, count * rows + 8, width), jnp.float32),
-        in_specs=[spec, spec],
-        out_specs=pl.BlockSpec((1, count * rows + 8, width), lambda j: (j, 0, 0)),
+        compiler_params=pltpu.CompilerParams(vmem_limit_bytes=VMEM),
         cost_estimate=pl.CostEstimate(
             flops=3 * own.size, bytes_accessed=12 * own.size, transcendentals=0
         ),
@@ -457,7 +455,7 @@
 
     def swap(tick, x):
         x = tie(x, *swapped[-1:])
-        swapped.append(send(tick, core, x))
+        swapped.append(at(tick + 1, core(after(tick, x))))
         return swapped[-1]
 
     base = line - 1
@@ -486,6 +484,10 @@
 
     tick = 0
     while tick <= max(hops) + 1 or landed or flying:
+        if chunks > 1 and (1, line - 2) in hops.get(tick - 1, ()):
+            gathered = [own[1], *came[1]]
+            early, *_ = product(me, plan, panel, gathered, line, 0, rows[1], (0,))
+            at(tick - 1, early)
         for h, hop in hops.get(tick, ()):
             if hop:
                 operands = came[h][-1], came[h][-2]
@@ -495,7 +497,7 @@
                 came[h].append(send(tick, links[link], operands[link]))
         if tick == 0:
             whole = tiles.reshape(-1, width)
-            rest = tiles[:, :, half:].reshape(-1, width)
+            rest = tie(tiles, own[0])[:, :, half:].reshape(-1, width)
             b_pair, b_across = send(0, pair, own[0]), send(0, across, own[0])
             core_own = swap(0, whole)
             put(0, 1, 0, (whole, width, 0))
@@ -548,20 +550,18 @@
             theirs, mine = product(me, plan, panel, gathered, line, part, size)
             landed.append((tick, at(tick, theirs), mine))
         tick += 1
-    theirs, queue = None, []
+    theirs, last = [early], early
+    for gathered, part, size in waiting[1:]:
+        last, *_ = product(tie(me, last), plan, panel, gathered, line, part, size, (0,))
+        theirs.append(last)
+    last = early
     for n, (gathered, part, size) in enumerate(waiting):
-        theirs, mine = product(
-            me if theirs is None else tie(me, theirs), plan, panel, gathered, line, part, size
-        )
-        other = pair(tie(theirs, other))
-        queue.append((mine, other))
-        done = [theirs, *(waiting[n + 1][0] if n + 1 < len(waiting) else ())]
-        if n == 0 and len(waiting) > 1:
-            continue
-        for mine, ready in queue if n + 1 == len(waiting) else [queue.pop(0)]:
-            inflated = inflate(mine, tie(ready, *done) if ready is not other else ready)
-            opposite = across(tie(inflated, opposite))
-            sources += [inflated, core(inflated), opposite, core(opposite)]
+        last = theirs[-1] if n == 1 else last
+        last, *_ = product(tie(me, last), plan, panel, gathered, line, part, size, (1,))
+        other = pair(tie(theirs[n], other))
+        inflated = inflate(last, other)
+        opposite = across(tie(inflated, opposite))
+        sources += [inflated, core(inflated), opposite, core(opposite)]
     sizes = tuple(rows[h] for h in range(chunks) for _ in range(0, sizes[h], rows[h]))
     scale = float(4 * TR * width)
     owned = owned_tiles(me, known[1::2], sources, sizes, count, scale)

time: 415 us -> 399 us (0.961)
  waiting for transfers between devices: 206 us -> 179 us
  Pallas kernels: 158 us -> 167 us
    ppermute x33 -> x25, waiting for transfers between devices: 173 us -> 147 us  [send(): return at(tick, move(after(tick, x), *more))]
    pallas_call x10 -> x13, Pallas kernels: 104 us -> 113 us  [the longest x8 101 us: product(): pl.pallas_call(functools.partial(product_kernel, line, groups, part), gri...]
    ppermute x3 -> x11, waiting for transfers between devices: 13.4 us -> 17.9 us  [the longest x8 9.31 us: swap(): swapped.append(at(tick + 1, core(after(tick, x))))]
    ppermute x33 -> x25, starting transfers between devices: 25.6 us -> 27.5 us  [send(): return at(tick, move(after(tick, x), *more))]
  transfers between devices with their start and end apart: 49 -> 49, of which waited for: 22 -> 20; matrix products, arithmetic and copies ran while one was open for 2% -> 2% of each run, Pallas kernels for 37% -> 40%
where the time goes in v4:
time: 399 us; the launch traced here: 398 us
  waiting for transfers between devices  179 us (45%)
  Pallas kernels  167 us (42%)
  starting transfers between devices  35.8 us (9%)
  local copies, waits for them, and re-layouts  14.2 us (4%)
    ppermute x25, waiting for transfers between devices, send(): return at(tick, move(after(tick, x), *more))  147 us
    pallas_call x8, Pallas kernels, product(): pl.pallas_call(functools.partial(product_kernel, line, groups, part), gri...  101 us
    pallas_call x8, Pallas kernels, place(): pl.pallas_call(functools.partial(place_kernel, len(parts)), grid=(blocks,...  39.1 us
    ppermute x25, starting transfers between devices, send(): return at(tick, move(after(tick, x), *more))  27.5 us
    ppermute x3, waiting for transfers between devices, on_device(): opposite = across(tie(inflated, opposite))  13.8 us
    pallas_call x5, Pallas kernels, inflate(): pl.pallas_call(inflate_kernel, out_shape=jax.ShapeDtypeStruct((blocks, co...  12.2 us
    ppermute x8, waiting for transfers between devices, swap(): swapped.append(at(tick + 1, core(after(tick, x))))  9.31 us
    ppermute x3, waiting for transfers between devices, on_device(): other = pair(tie(theirs[n], other))  8.58 us
  transfers between devices with their start and end apart: 49, of which 20 were waited for; matrix products, arithmetic and copies ran while one was open for 2% of the time, Pallas kernels for 40%

profile of v4, /device:TPU:0, one launch (start us, length us, event | category | flops | bytes accessed | tf_op | source)
XLA Modules:
  0.0 397.7 jit_solution(10182661405976546556)
XLA Ops:
  1.2 0.8 reshape.37
  2.0 1.7 slice.16
  4.6 2.6 collective-permute-start
  7.2 1.5 collective-permute-start.4
  8.7 3.1 collective-permute-start.2
  11.8 4.9 %place.8 = (bf16[2,4,4,4,2,256,256]{6,5,4,3,2,1,0:T(8,128)(2,1)}, f32[8,128]{1,0:T(8,128)}) custom-call(f32[4096,256]{1,0:T(8,128)} %bitcast.33), custom_call_target="tpu_custom_call" | custom-call | flops 1048576 | bytes 8388608 | tf_op jit(solution)/shard_map/place/pallas_call | solution.py:58
  16.7 37.0 %collective-permute-done.refs_0_.refs_1_ = f32[2056,256]{1,0:T(8,128)} collective-permute-done((f32[2056,256]{1,0:T(8,128)S(1)}, f32[2056,256]{1,0:T(8,128)}, u32[]{:S(2)}, u32[]{:S(2)}) %collective-permute-start) | collective-permute-done | bytes 2105376 | tf_op jit(solution)/shard_map/ppermute | solution.py:452
  53.8 1.4 collective-permute-done.4.refs_0_.refs_1_.refs_5_.refs_2_
  55.1 2.5 collective-permute-done.2.refs_9_.refs_1_
  57.6 1.7 collective-permute-start.7
  59.6 3.1 slice.13
  63.7 1.3 fusion
  65.4 5.3 %place.9 = (bf16[2,4,4,4,2,256,256]{6,5,4,3,2,1,0:T(8,128)(2,1)}, f32[8,128]{1,0:T(8,128)}) custom-call(f32[4096,256]{1,0:T(8,128)} %collective-permute-done.1.refs_0_, bf16[2,4,4,4,2,256,256]{6,5,4,3,2,1,0:T(8,128)(2,1)} %get-tuple-element.81.refs_1_), custom_call_target="tpu_custom_call", output_to_operand_aliasing={{0}: (1, {})} | custom-call | flops 1048576 | bytes 8388608 | tf_op jit(solution)/shard_map/place/pallas_call | solution.py:58
  70.7 40.0 %collective-permute-done.10.refs_2_ = f32[2048,256]{1,0:T(8,128)S(1)} collective-permute-done((f32[2048,256]{1,0:T(8,128)}, f32[2048,256]{1,0:T(8,128)S(1)}, u32[]{:S(2)}, u32[]{:S(2)}) %collective-permute-start.10) | collective-permute-done | bytes 2097184 | tf_op jit(solution)/shard_map/ppermute | solution.py:452
  111.1 4.2 %collective-permute-done.11.refs_7_.refs_0_.refs_1_.refs_3_ = f32[2056,256]{1,0:T(8,128)S(1)} collective-permute-done((f32[2056,256]{1,0:T(8,128)S(1)}, f32[2056,256]{1,0:T(8,128)S(1)}, u32[]{:S(2)}, u32[]{:S(2)}) %collective-permute-start.11) | collective-permute-done | bytes 2105376 | tf_op jit(solution)/shard_map/ppermute | solution.py:458
  115.4 1.5 collective-permute-start.12
  116.9 1.9 collective-permute-start.15
  118.8 1.0 collective-permute-done.13.refs_2_
  120.4 4.8 %place.10 = (bf16[2,4,4,4,2,256,256]{6,5,4,3,2,1,0:T(8,128)(2,1)}, f32[8,128]{1,0:T(8,128)}) custom-call(f32[2056,256]{1,0:T(8,128)} %collective-permute-done.refs_0_.refs_1_, f32[2056,256]{1,0:T(8,128)} %collective-permute-done.refs_0_.refs_1_, f32[2048,256]{1,0:T(8,128)} %collective-permute-done.9.refs_2_, ...), custom_call_target="tpu_custom_call", output_to_operand_aliasing={{0}: (3, {})} | custom-call | flops 1048576 | bytes 8388608 | tf_op jit(solution)/shard_map/place/pallas_call | solution.py:58
  125.3 4.8 %place.11 = (bf16[2,4,4,4,2,256,256]{6,5,4,3,2,1,0:T(8,128)(2,1)}, f32[8,128]{1,0:T(8,128)}) custom-call(f32[2056,256]{1,0:T(8,128)} %copy-done.1, f32[2056,256]{1,0:T(8,128)} %copy-done.1, f32[2048,256]{1,0:T(8,128)} %copy-done.20, bf16[2,4,4,4,2,256,256]{6,5,4,3,2,1,0:T(8,128)(2,1)} %get-tuple-element.95.refs_3_), custom_call_target="tpu_custom_call", output_to_operand_aliasing={{0}: (3, {})} | custom-call | flops 1048576 | bytes 8388608 | tf_op jit(solution)/shard_map/place/pallas_call | solution.py:58
  130.1 33.6 %collective-permute-done.12.refs_4_.refs_0_.refs_1_ = f32[2056,256]{1,0:T(8,128)S(1)} collective-permute-done((f32[2056,256]{1,0:T(8,128)}, f32[2056,256]{1,0:T(8,128)S(1)}, u32[]{:S(2)}, u32[]{:S(2)}) %collective-permute-start.12) | collective-permute-done | bytes 2105376 | tf_op jit(solution)/shard_map/ppermute | solution.py:452
  163.7 4.4 %collective-permute-done.16.refs_2_ = f32[2048,256]{1,0:T(8,128)} collective-permute-done((f32[2048,256]{1,0:T(8,128)}, f32[2048,256]{1,0:T(8,128)}, u32[]{:S(2)}, u32[]{:S(2)}) %collective-permute-start.16) | collective-permute-done | bytes 2097184 | tf_op jit(solution)/shard_map/ppermute | solution.py:452
  168.1 4.2 %collective-permute-done.17.refs_6_.refs_0_.refs_1_ = f32[2056,256]{1,0:T(8,128)S(1)} collective-permute-done((f32[2056,256]{1,0:T(8,128)S(1)}, f32[2056,256]{1,0:T(8,128)S(1)}, u32[]{:S(2)}, u32[]{:S(2)}) %collective-permute-start.17) | collective-permute-done | bytes 2105376 | tf_op jit(solution)/shard_map/ppermute | solution.py:458
  172.8 1.8 collective-permute-start.19
  174.6 1.7 collective-permute-start.21
  177.0 4.9 %place.12 = (bf16[2,4,4,4,2,256,256]{6,5,4,3,2,1,0:T(8,128)(2,1)}, f32[8,128]{1,0:T(8,128)}) custom-call(f32[2056,256]{1,0:T(8,128)} %copy-done.6, f32[2056,256]{1,0:T(8,128)} %copy-done.6, f32[2048,256]{1,0:T(8,128)} %collective-permute-done.13.refs_2_, bf16[2,4,4,4,2,256,256]{6,5,4,3,2,1,0:T(8,128)(2,1)} %get-tuple-element.102.refs_3_), custom_call_target="tpu_custom_call", output_to_operand_aliasing={{0}: (3, {})} | custom-call | flops 1048576 | bytes 8388608 | tf_op jit(solution)/shard_map/place/pallas_call | solution.py:58
  181.9 4.8 %place.13 = (bf16[2,4,4,4,2,256,256]{6,5,4,3,2,1,0:T(8,128)(2,1)}, f32[8,128]{1,0:T(8,128)}) custom-call(f32[2056,256]{1,0:T(8,128)} %copy-done.2, f32[2056,256]{1,0:T(8,128)} %copy-done.2, f32[2048,256]{1,0:T(8,128)} %collective-permute-done.14.refs_2_, bf16[2,4,4,4,2,256,256]{6,5,4,3,2,1,0:T(8,128)(2,1)} %get-tuple-element.103.refs_3_), custom_call_target="tpu_custom_call", output_to_operand_aliasing={{0}: (3, {})} | custom-call | flops 1048576 | bytes 8388608 | tf_op jit(solution)/shard_map/place/pallas_call | solution.py:58
  186.7 4.8 %place.14 = (bf16[2,4,4,4,2,256,256]{6,5,4,3,2,1,0:T(8,128)(2,1)}, f32[8,128]{1,0:T(8,128)}) custom-call(f32[2056,256]{1,0:T(8,128)} %copy-done.8, f32[2056,256]{1,0:T(8,128)} %copy-done.8, f32[2048,256]{1,0:T(8,128)} %collective-permute-done.16.refs_2_, bf16[2,4,4,4,2,256,256]{6,5,4,3,2,1,0:T(8,128)(2,1)} %get-tuple-element.104.refs_3_), custom_call_target="tpu_custom_call", output_to_operand_aliasing={{0}: (3, {})} | custom-call | flops 1048576 | bytes 8388608 | tf_op jit(solution)/shard_map/place/pallas_call | solution.py:58
  191.5 7.7 %plan.1 = (s32[1040]{0:T(1024)}, s32[64]{0:T(128)}) custom-call(s32[2]{0:T(128)} %pad_add_fusion.me_ref, f32[2056,256]{1,0:T(8,128)} %collective-permute-done.refs_0_.refs_1_, f32[2056,256]{1,0:T(8,128)} %copy-done, f32[2056,256]{1,0:T(8,128)} %copy-done.6, f32[8,256]{1,0:T(8,128)} %copy-done.36, f32[2056,256]{1,0:T(8,128)} %copy-done.8, ...), custom_call_target="tpu_custom_call" | custom-call | tf_op jit(solution)/shard_map/plan/pallas_call | solution.py:138
  199.2 4.9 %place.15 = (bf16[2,4,4,4,2,256,256]{6,5,4,3,2,1,0:T(8,128)(2,1)}, f32[8,128]{1,0:T(8,128)}) custom-call(f32[2056,256]{1,0:T(8,128)} %copy-done.9, f32[2056,256]{1,0:T(8,128)} %copy-done.9, f32[2048,256]{1,0:T(8,128)} %collective-permute-done.18.refs_2_, bf16[2,4,4,4,2,256,256]{6,5,4,3,2,1,0:T(8,128)(2,1)} %get-tuple-element.105.refs_3_), custom_call_target="tpu_custom_call", output_to_operand_aliasing={{0}: (3, {})} | custom-call | flops 1048576 | bytes 8388608 | tf_op jit(solution)/shard_map/place/pallas_call | solution.py:58
  204.0 20.2 %product.8 = (f32[4,4,64,256]{3,2,1,0:T(8,128)}, f32[4,4,64,256]{3,2,1,0:T(8,128)}) custom-call(s32[2]{0:T(128)} %pad_add_fusion.me_ref, s32[1040]{0:T(1024)} %get-tuple-element.98.plan_ref, s32[64]{0:T(128)} %get-tuple-element.99.kept_ref, bf16[128,2,256,256]{3,2,1,0:T(8,128)(2,1)} %bitcast.17, f32[2056,256]{1,0:T(8,128)} %copy-done, ...), custom_call_target="tpu_custom_call" | custom-call | flops 6442450944 | bytes 16777216 | tf_op jit(solution)/shard_map/product/pallas_call | solution.py:245
  225.1 20.2 %product.9 = (f32[4,4,64,256]{3,2,1,0:T(8,128)}, f32[4,4,64,256]{3,2,1,0:T(8,128)}) custom-call(s32[2]{0:T(128)} %pad_add_fusion.me_ref, s32[1040]{0:T(1024)} %get-tuple-element.98.plan_ref, s32[64]{0:T(128)} %get-tuple-element.99.kept_ref, bf16[128,2,256,256]{3,2,1,0:T(8,128)(2,1)} %bitcast.18, f32[2056,256]{1,0:T(8,128)} %copy-done, ...), custom_call_target="tpu_custom_call" | custom-call | flops 6442450944 | bytes 16777216 | tf_op jit(solution)/shard_map/product/pallas_call | solution.py:245
  245.3 3.8 collective-permute-done.23.other_ref
  249.2 1.7 collective-permute-start.29
  251.0 1.7 collective-permute-start.31
  252.7 2.7 inflate.5.refs_4_
  255.3 1.5 collective-permute-start.27
  257.2 16.0 %collective-permute-done.29.other_ref = f32[4,4,64,256]{3,2,1,0:T(8,128)S(1)} collective-permute-done((f32[4,4,64,256]{3,2,1,0:T(8,128)}, f32[4,4,64,256]{3,2,1,0:T(8,128)S(1)}, u32[]{:S(2)}, u32[]{:S(2)}) %collective-permute-start.29) | collective-permute-done | bytes 1048608 | tf_op jit(solution)/shard_map/ppermute | solution.py:452
  273.2 1.0 copy-done.26
  274.1 2.7 inflate.6.refs_8_
  277.1 1.0 copy-done.18
  278.0 11.8 %product.10 = f32[4,4,64,256]{3,2,1,0:T(8,128)} custom-call(s32[2]{0:T(128)} %pad_add_fusion.me_ref, s32[1040]{0:T(1024)} %get-tuple-element.98.plan_ref, s32[64]{0:T(128)} %get-tuple-element.99.kept_ref, bf16[128,2,256,256]{3,2,1,0:T(8,128)(2,1)} %bitcast.19, f32[1024,256]{1,0:T(8,128)} %bitcast.38, f32[1024,256]{1,0:T(8,128)} %collective-permute-done.19.refs_1_, ...), custom_call_target="tpu_custom_call" | custom-call | flops 3221225472 | bytes 8388608 | tf_op jit(solution)/shard_map/product/pallas_call | solution.py:245
  289.8 7.1 %collective-permute-done.32.refs_3_ = f32[1024,256]{1,0:T(8,128)S(1)} collective-permute-done((f32[1024,256]{1,0:T(8,128)}, f32[1024,256]{1,0:T(8,128)S(1)}, u32[]{:S(2)}, u32[]{:S(2)}) %collective-permute-start.32) | collective-permute-done | bytes 1048608 | tf_op jit(solution)/shard_map/ppermute | solution.py:452
  297.0 1.6 collective-permute-start.34
  299.2 1.7 collective-permute-start.40
  301.0 12.6 %product.11.own_ref = f32[4,4,64,256]{3,2,1,0:T(8,128)} custom-call(s32[2]{0:T(128)} %pad_add_fusion.me_ref, s32[1040]{0:T(1024)} %get-tuple-element.98.plan_ref, s32[64]{0:T(128)} %get-tuple-element.99.kept_ref, bf16[128,2,256,256]{3,2,1,0:T(8,128)(2,1)} %bitcast.20, f32[1024,256]{1,0:T(8,128)} %bitcast.39, f32[1024,256]{1,0:T(8,128)} %collective-permute-done.19.refs_1_, ...), custom_call_target="tpu_custom_call" | custom-call | flops 3221225472 | bytes 8388608 | tf_op jit(solution)/shard_map/product/pallas_call | solution.py:245
  313.6 7.5 %collective-permute-done.36.other_ref = f32[4,4,64,256]{3,2,1,0:T(8,128)S(1)} collective-permute-done((f32[4,4,64,256]{3,2,1,0:T(8,128)}, f32[4,4,64,256]{3,2,1,0:T(8,128)S(1)}, u32[]{:S(2)}, u32[]{:S(2)}) %collective-permute-start.36) | collective-permute-done | bytes 1048608 | tf_op jit(solution)/shard_map/ppermute | solution.py:561
  321.1 1.0 copy-done.27
  322.1 2.6 inflate.7.refs_12_
  325.2 1.0 copy-done.12
  326.2 8.8 %product.12 = f32[4,4,32,256]{3,2,1,0:T(8,128)} custom-call(s32[2]{0:T(128)} %pad_add_fusion.me_ref, s32[1040]{0:T(1024)} %get-tuple-element.98.plan_ref, s32[64]{0:T(128)} %get-tuple-element.99.kept_ref, bf16[128,2,256,256]{3,2,1,0:T(8,128)(2,1)} %bitcast.21, f32[1024,256]{1,0:T(8,128)} %bitcast.27, f32[1024,256]{1,0:T(8,128)} %collective-permute-done.21.refs_1_, ...), custom_call_target="tpu_custom_call" | custom-call | flops 1610612736 | bytes 8388608 | tf_op jit(solution)/shard_map/product/pallas_call | solution.py:245
  335.4 8.8 %product.13 = f32[4,4,32,256]{3,2,1,0:T(8,128)} custom-call(s32[2]{0:T(128)} %pad_add_fusion.me_ref, s32[1040]{0:T(1024)} %get-tuple-element.98.plan_ref, s32[64]{0:T(128)} %get-tuple-element.99.kept_ref, bf16[128,2,256,256]{3,2,1,0:T(8,128)(2,1)} %bitcast.22, f32[1024,256]{1,0:T(8,128)} %bitcast.28, f32[1024,256]{1,0:T(8,128)} %collective-permute-done.21.refs_1_, ...), custom_call_target="tpu_custom_call" | custom-call | flops 1610612736 | bytes 8388608 | tf_op jit(solution)/shard_map/product/pallas_call | solution.py:245
  344.3 1.1 collective-permute-done.41.other_ref
  346.5 9.5 %product.14.own_ref = f32[4,4,32,256]{3,2,1,0:T(8,128)} custom-call(s32[2]{0:T(128)} %pad_add_fusion.me_ref, s32[1040]{0:T(1024)} %get-tuple-element.98.plan_ref, s32[64]{0:T(128)} %get-tuple-element.99.kept_ref, bf16[128,2,256,256]{3,2,1,0:T(8,128)(2,1)} %bitcast.23, f32[1024,256]{1,0:T(8,128)} %bitcast.29, f32[1024,256]{1,0:T(8,128)} %collective-permute-done.21.refs_1_, ...), custom_call_target="tpu_custom_call" | custom-call | flops 1610612736 | bytes 8388608 | tf_op jit(solution)/shard_map/product/pallas_call | solution.py:245
  356.0 2.1 inflate.8.refs_16_
  358.1 1.8 collective-permute-start.43
  360.0 9.5 %product.15.own_ref = f32[4,4,32,256]{3,2,1,0:T(8,128)} custom-call(s32[2]{0:T(128)} %pad_add_fusion.me_ref, s32[1040]{0:T(1024)} %get-tuple-element.98.plan_ref, s32[64]{0:T(128)} %get-tuple-element.99.kept_ref, bf16[128,2,256,256]{3,2,1,0:T(8,128)(2,1)} %bitcast.24, f32[1024,256]{1,0:T(8,128)} %bitcast.30, f32[1024,256]{1,0:T(8,128)} %collective-permute-done.21.refs_1_, ...), custom_call_target="tpu_custom_call" | custom-call | flops 1610612736 | bytes 8388608 | tf_op jit(solution)/shard_map/product/pallas_call | solution.py:245
  369.5 2.1 inflate.9.refs_20_
  371.6 1.3 collective-permute-done.43.refs_18_
  372.9 1.7 collective-permute-start.47
  375.7 12.5 %collective-permute-done.47.refs_22_ = f32[4,136,256]{2,1,0:T(8,128)S(1)} collective-permute-done((f32[4,136,256]{2,1,0:T(8,128)}, f32[4,136,256]{2,1,0:T(8,128)S(1)}, u32[]{:S(2)}, u32[]{:S(2)}) %collective-permute-start.47) | collective-permute-done | bytes 557088 | tf_op jit(solution)/shard_map/ppermute | solution.py:563
  389.0 1.2 collective-permute-done.48.refs_23_
  390.2 0.8 copy-done.33
  391.0 6.7 %owned.1 = f32[32,256,256]{2,1,0:T(8,128)} custom-call(s32[2]{0:T(128)} %pad_add_fusion.me_ref, f32[2056,256]{1,0:T(8,128)} %copy-done, f32[8,256]{1,0:T(8,128)} %copy-done.36, f32[2056,256]{1,0:T(8,128)} %copy-done.1, f32[2056,256]{1,0:T(8,128)} %copy-done.2, f32[4,264,256]{2,1,0:T(8,128)} %inflate.5.refs_4_, ...), custom_call_target="tpu_custom_call" | custom-call | flops 2097152 | bytes 16777216 | tf_op jit(solution)/shard_map/owned/pallas_call | solution.py:375
  (145 shorter events, 12.3 us)
Async XLA Ops:
  0.0 53.8 %collective-permute-start.1 = (f32[4096,256]{1,0:T(8,128)}, f32[4096,256]{1,0:T(8,128)}, u32[]{:S(2)}, u32[]{:S(2)}) collective-permute-start(f32[4096,256]{1,0:T(8,128)} %bitcast.31), channel_id=1, source_target_pairs={{0,8},{8,0},{16,24},{24,16},{1,9},{9,1},{17,25},{25,17},{2,10},{10... | collective-permute-start | bytes 12582920 | tf_op jit(solution)/shard_map/ppermute | solution.py:458
  4.6 58.0 %copy-start = (f32[2056,256]{1,0:T(8,128)}, f32[2056,256]{1,0:T(8,128)S(1)}, u32[]{:S(2)}) copy-start(f32[2056,256]{1,0:T(8,128)S(1)} %pad_maximum_fusion.refs_1_.refs_8_.refs_0_) | copy-start | bytes 6316036
  4.6 49.1 %collective-permute-start = (f32[2056,256]{1,0:T(8,128)S(1)}, f32[2056,256]{1,0:T(8,128)}, u32[]{:S(2)}, u32[]{:S(2)}) collective-permute-start(f32[2056,256]{1,0:T(8,128)S(1)} %pad_maximum_fusion.refs_1_.refs_8_.refs_0_), channel_id=1, source_target_pairs={{0,1},{1,0},{2,3},{3,2},{4,5},{5,4},{6,7},{7,6},{8,9},{9,8},{10,11... | collective-permute-start | bytes 6316040 | tf_op jit(solution)/shard_map/ppermute | solution.py:452
  7.2 47.9 %collective-permute-start.4 = (f32[2056,256]{1,0:T(8,128)S(1)}, f32[2056,256]{1,0:T(8,128)S(1)}, u32[]{:S(2)}, u32[]{:S(2)}) collective-permute-start(f32[2056,256]{1,0:T(8,128)S(1)} %pad_maximum_fusion.refs_1_.refs_8_.refs_0_), channel_id=1, source_target_pairs={{0,16},{8,24},{16,0},{24,8},{1,17},{9,25},{17,1},{25,9},{2,18},{10... | collective-permute-start | bytes 6316040 | tf_op jit(solution)/shard_map/ppermute | solution.py:452
  8.7 46.4 %collective-permute-start.3 = (f32[2056,256]{1,0:T(8,128)S(1)}, f32[2056,256]{1,0:T(8,128)S(1)}, u32[]{:S(2)}, u32[]{:S(2)}) collective-permute-start(f32[2056,256]{1,0:T(8,128)S(1)} %pad_maximum_fusion.refs_1_.refs_8_.refs_0_), channel_id=1, source_target_pairs={{0,8},{1,9},{2,4},{3,5},{4,2},{5,3},{6,14},{7,15},{8,0},{9,1},{10,... | collective-permute-start | bytes 6316040 | tf_op jit(solution)/shard_map/ppermute | solution.py:452
  8.7 48.9 %collective-permute-start.2 = (f32[2056,256]{1,0:T(8,128)S(1)}, f32[2056,256]{1,0:T(8,128)}, u32[]{:S(2)}, u32[]{:S(2)}) collective-permute-start(f32[2056,256]{1,0:T(8,128)S(1)} %pad_maximum_fusion.refs_1_.refs_8_.refs_0_), channel_id=1, source_target_pairs={{0,2},{1,3},{2,0},{3,1},{4,6},{5,7},{6,4},{7,5},{8,10},{9,11},{10,... | collective-permute-start | bytes 6316040 | tf_op jit(solution)/shard_map/ppermute | solution.py:452
  16.7 47.0 %copy-start.4 = (f32[1,4,4,256,256]{4,3,2,1,0:T(8,128)S(1)}, f32[1,4,4,256,256]{4,3,2,1,0:T(8,128)}, u32[]{:S(2)}) copy-start(f32[1,4,4,256,256]{4,3,2,1,0:T(8,128)} %param.4) | copy-start | bytes 12582916
  55.1 55.9 %copy-start.1 = (f32[2056,256]{1,0:T(8,128)}, f32[2056,256]{1,0:T(8,128)S(1)}, u32[]{:S(2)}) copy-start(f32[2056,256]{1,0:T(8,128)S(1)} %collective-permute-done.4.refs_0_.refs_1_.refs_5_.refs_2_) | copy-start | bytes 6316036
  57.6 6.1 %collective-permute-start.5 = (f32[2056,256]{1,0:T(8,128)}, f32[2056,256]{1,0:T(8,128)S(1)}, u32[]{:S(2)}, u32[]{:S(2)}) collective-permute-start(f32[2056,256]{1,0:T(8,128)} %collective-permute-done.refs_0_.refs_1_), channel_id=1, source_target_pairs={{0,8},{8,0},{16,24},{24,16},{1,9},{9,1},{17,25},{25,17},{2,10},{10... | collective-permute-start | bytes 6316040 | tf_op jit(solution)/shard_map/ppermute | solution.py:458
  57.6 53.4 %collective-permute-start.7 = (f32[2056,256]{1,0:T(8,128)S(1)}, f32[2056,256]{1,0:T(8,128)}, u32[]{:S(2)}, u32[]{:S(2)}) collective-permute-start(f32[2056,256]{1,0:T(8,128)S(1)} %collective-permute-done.3.refs_10_.refs_2_), channel_id=1, source_target_pairs={{0,2},{1,3},{2,0},{3,1},{4,6},{5,7},{6,4},{7,5},{8,10},{9,11},{10,... | collective-permute-start | bytes 6316040 | tf_op jit(solution)/shard_map/ppermute | solution.py:452
  59.3 51.7 %collective-permute-start.8 = (f32[2056,256]{1,0:T(8,128)}, f32[2056,256]{1,0:T(8,128)}, u32[]{:S(2)}, u32[]{:S(2)}) collective-permute-start(f32[2056,256]{1,0:T(8,128)} %collective-permute-done.2.refs_9_.refs_1_), channel_id=1, source_target_pairs={{0,8},{1,9},{2,4},{3,5},{4,2},{5,3},{6,14},{7,15},{8,0},{9,1},{10,... | collective-permute-start | bytes 6316040 | tf_op jit(solution)/shard_map/ppermute | solution.py:452
  62.6 48.0 %collective-permute-start.10 = (f32[2048,256]{1,0:T(8,128)}, f32[2048,256]{1,0:T(8,128)S(1)}, u32[]{:S(2)}, u32[]{:S(2)}) collective-permute-start(f32[2048,256]{1,0:T(8,128)} %bitcast.8), channel_id=1, source_target_pairs={{0,16},{8,24},{16,0},{24,8},{1,17},{9,25},{17,1},{25,9},{2,18},{10... | collective-permute-start | bytes 6291464 | tf_op jit(solution)/shard_map/ppermute | solution.py:452
  63.2 47.9 %collective-permute-start.9 = (f32[2048,256]{1,0:T(8,128)}, f32[2048,256]{1,0:T(8,128)}, u32[]{:S(2)}, u32[]{:S(2)}) collective-permute-start(f32[2048,256]{1,0:T(8,128)} %bitcast.8), channel_id=1, source_target_pairs={{0,1},{1,0},{2,3},{3,2},{4,5},{5,4},{6,7},{7,6},{8,9},{9,8},{10,11... | collective-permute-start | bytes 6291464 | tf_op jit(solution)/shard_map/ppermute | solution.py:452
  63.7 7.0 %collective-permute-start.6 = (f32[8,256]{1,0:T(8,128)S(1)}, f32[8,256]{1,0:T(8,128)S(1)}, u32[]{:S(2)}, u32[]{:S(2)}) collective-permute-start(f32[8,256]{1,0:T(8,128)S(1)} %broadcast_in_dim.6), channel_id=1, source_target_pairs={{0,8},{8,0},{16,24},{24,16},{1,9},{9,1},{17,25},{25,17},{2,10},{10... | collective-permute-start | bytes 24584 | tf_op jit(solution)/shard_map/ppermute | solution.py:458
  65.4 109.2 %copy-start.3 = (f32[16,2,32,256]{3,2,0,1:T(8,128)}, f32[16,2,32,256]{3,2,0,1:T(8,128)S(1)}, u32[]{:S(2)}) copy-start(f32[16,2,32,256]{3,2,0,1:T(8,128)S(1)} %copy.13) | copy-start | bytes 3145732
  70.7 54.6 %copy-start.36 = (f32[8,256]{1,0:T(8,128)}, f32[8,256]{1,0:T(8,128)S(1)}, u32[]{:S(2)}) copy-start(f32[8,256]{1,0:T(8,128)S(1)} %collective-permute-done.6.refs_3_.refs_1_) | copy-start | bytes 24580
  111.0 4.2 %collective-permute-start.11 = (f32[2056,256]{1,0:T(8,128)S(1)}, f32[2056,256]{1,0:T(8,128)S(1)}, u32[]{:S(2)}, u32[]{:S(2)}) collective-permute-start(f32[2056,256]{1,0:T(8,128)S(1)} %collective-permute-done.4.refs_0_.refs_1_.refs_5_.refs_2_), channel_id=1, source_target_pairs={{0,8},{8,0},{16,24},{24,16},{1,9},{9,1},{17,25},{25,17},{2,10},{10... | collective-permute-start | bytes 6316040 | tf_op jit(solution)/shard_map/ppermute | solution.py:458
  115.3 4.5 %collective-permute-start.13 = (f32[2048,256]{1,0:T(8,128)}, f32[2048,256]{1,0:T(8,128)}, u32[]{:S(2)}, u32[]{:S(2)}) collective-permute-start(f32[2048,256]{1,0:T(8,128)} %collective-permute-done.9.refs_2_), channel_id=1, source_target_pairs={{0,8},{8,0},{16,24},{24,16},{1,9},{9,1},{17,25},{25,17},{2,10},{10... | collective-permute-start | bytes 6291464 | tf_op jit(solution)/shard_map/ppermute | solution.py:458
  115.4 48.3 %collective-permute-start.12 = (f32[2056,256]{1,0:T(8,128)}, f32[2056,256]{1,0:T(8,128)S(1)}, u32[]{:S(2)}, u32[]{:S(2)}) collective-permute-start(f32[2056,256]{1,0:T(8,128)} %collective-permute-done.refs_0_.refs_1_), channel_id=1, source_target_pairs={{0,16},{8,24},{16,0},{24,8},{1,17},{9,25},{17,1},{25,9},{2,18},{10... | collective-permute-start | bytes 6316040 | tf_op jit(solution)/shard_map/ppermute | solution.py:452
  116.9 51.2 %collective-permute-start.15 = (f32[2056,256]{1,0:T(8,128)}, f32[2056,256]{1,0:T(8,128)S(1)}, u32[]{:S(2)}, u32[]{:S(2)}) collective-permute-start(f32[2056,256]{1,0:T(8,128)} %collective-permute-done.8.refs_12_.refs_4_), channel_id=1, source_target_pairs={{0,2},{1,3},{2,0},{3,1},{4,6},{5,7},{6,4},{7,5},{8,10},{9,11},{10,... | collective-permute-start | bytes 6316040 | tf_op jit(solution)/shard_map/ppermute | solution.py:452
  119.8 43.9 %collective-permute-start.14 = (f32[2048,256]{1,0:T(8,128)}, f32[2048,256]{1,0:T(8,128)}, u32[]{:S(2)}, u32[]{:S(2)}) collective-permute-start(f32[2048,256]{1,0:T(8,128)} %copy-done.20), channel_id=1, source_target_pairs={{0,8},{8,0},{16,24},{24,16},{1,9},{9,1},{17,25},{25,17},{2,10},{10... | collective-permute-start | bytes 6291464 | tf_op jit(solution)/shard_map/ppermute | solution.py:458
  119.9 48.2 %collective-permute-start.16 = (f32[2048,256]{1,0:T(8,128)}, f32[2048,256]{1,0:T(8,128)}, u32[]{:S(2)}, u32[]{:S(2)}) collective-permute-start(f32[2048,256]{1,0:T(8,128)} %copy-done.20), channel_id=1, source_target_pairs={{0,1},{1,0},{2,3},{3,2},{4,5},{5,4},{6,7},{7,6},{8,9},{9,8},{10,11... | collective-permute-start | bytes 6291464 | tf_op jit(solution)/shard_map/ppermute | solution.py:452
  168.1 4.2 %collective-permute-start.17 = (f32[2056,256]{1,0:T(8,128)S(1)}, f32[2056,256]{1,0:T(8,128)S(1)}, u32[]{:S(2)}, u32[]{:S(2)}) collective-permute-start(f32[2056,256]{1,0:T(8,128)S(1)} %collective-permute-done.12.refs_4_.refs_0_.refs_1_), channel_id=1, source_target_pairs={{0,8},{8,0},{16,24},{24,16},{1,9},{9,1},{17,25},{25,17},{2,10},{10... | collective-permute-start | bytes 6316040 | tf_op jit(solution)/shard_map/ppermute | solution.py:458
  172.3 26.9 %collective-permute-start.18 = (f32[2048,256]{1,0:T(8,128)}, f32[2048,256]{1,0:T(8,128)}, u32[]{:S(2)}, u32[]{:S(2)}) collective-permute-start(f32[2048,256]{1,0:T(8,128)} %collective-permute-done.16.refs_2_), channel_id=1, source_target_pairs={{0,8},{8,0},{16,24},{24,16},{1,9},{9,1},{17,25},{25,17},{2,10},{10... | collective-permute-start | bytes 6291464 | tf_op jit(solution)/shard_map/ppermute | solution.py:458
  172.4 51.8 %collective-permute-start.20 = (f32[1024,256]{1,0:T(8,128)}, f32[1024,256]{1,0:T(8,128)}, u32[]{:S(2)}, u32[]{:S(2)}) collective-permute-start(f32[1024,256]{1,0:T(8,128)} %bitcast.36), channel_id=1, source_target_pairs={{0,8},{1,9},{2,4},{3,5},{4,2},{5,3},{6,14},{7,15},{8,0},{9,1},{10,... | collective-permute-start | bytes 3145736 | tf_op jit(solution)/shard_map/ppermute | solution.py:452
  172.8 51.4 %collective-permute-start.19 = (f32[1024,256]{1,0:T(8,128)}, f32[1024,256]{1,0:T(8,128)}, u32[]{:S(2)}, u32[]{:S(2)}) collective-permute-start(f32[1024,256]{1,0:T(8,128)} %bitcast.37), channel_id=1, source_target_pairs={{0,2},{1,3},{2,0},{3,1},{4,6},{5,7},{6,4},{7,5},{8,10},{9,11},{10,... | collective-permute-start | bytes 3145736 | tf_op jit(solution)/shard_map/ppermute | solution.py:452
  174.6 49.7 %collective-permute-start.22 = (f32[1024,256]{1,0:T(8,128)S(1)}, f32[1024,256]{1,0:T(8,128)}, u32[]{:S(2)}, u32[]{:S(2)}) collective-permute-start(f32[1024,256]{1,0:T(8,128)S(1)} %bitcast.25), channel_id=1, source_target_pairs={{0,8},{1,9},{2,4},{3,5},{4,2},{5,3},{6,14},{7,15},{8,0},{9,1},{10,... | collective-permute-start | bytes 3145736 | tf_op jit(solution)/shard_map/ppermute | solution.py:452
  174.6 49.7 %collective-permute-start.21 = (f32[1024,256]{1,0:T(8,128)S(1)}, f32[1024,256]{1,0:T(8,128)}, u32[]{:S(2)}, u32[]{:S(2)}) collective-permute-start(f32[1024,256]{1,0:T(8,128)S(1)} %bitcast.26), channel_id=1, source_target_pairs={{0,2},{1,3},{2,0},{3,1},{4,6},{5,7},{6,4},{7,5},{8,10},{9,11},{10,... | collective-permute-start | bytes 3145736 | tf_op jit(solution)/shard_map/ppermute | solution.py:452
  224.3 24.9 %collective-permute-start.23 = (f32[4,4,64,256]{3,2,1,0:T(8,128)}, f32[4,4,64,256]{3,2,1,0:T(8,128)S(1)}, u32[]{:S(2)}, u32[]{:S(2)}) collective-permute-start(f32[4,4,64,256]{3,2,1,0:T(8,128)} %get-tuple-element.115), channel_id=1, source_target_pairs={{0,1},{1,0},{2,3},{3,2},{4,5},{5,4},{6,7},{7,6},{8,9},{9,8},{10,11... | collective-permute-start | bytes 3145736 | tf_op jit(solution)/shard_map/ppermute | solution.py:452
  224.4 24.9 %collective-permute-start.25 = (f32[1024,256]{1,0:T(8,128)}, f32[1024,256]{1,0:T(8,128)S(1)}, u32[]{:S(2)}, u32[]{:S(2)}) collective-permute-start(f32[1024,256]{1,0:T(8,128)} %collective-permute-done.20.refs_2_), channel_id=1, source_target_pairs={{0,2},{1,3},{2,0},{3,1},{4,6},{5,7},{6,4},{7,5},{8,10},{9,11},{10,... | collective-permute-start | bytes 3145736 | tf_op jit(solution)/shard_map/ppermute | solution.py:452
  225.1 24.1 %collective-permute-start.26 = (f32[1024,256]{1,0:T(8,128)}, f32[1024,256]{1,0:T(8,128)S(1)}, u32[]{:S(2)}, u32[]{:S(2)}) collective-permute-start(f32[1024,256]{1,0:T(8,128)} %collective-permute-done.19.refs_1_), channel_id=1, source_target_pairs={{0,8},{1,9},{2,4},{3,5},{4,2},{5,3},{6,14},{7,15},{8,0},{9,1},{10,... | collective-permute-start | bytes 3145736 | tf_op jit(solution)/shard_map/ppermute | solution.py:452
  249.2 27.6 %copy-start.16 = (f32[1024,256]{1,0:T(8,128)}, f32[1024,256]{1,0:T(8,128)S(1)}, u32[]{:S(2)}) copy-start(f32[1024,256]{1,0:T(8,128)S(1)} %collective-permute-done.25.refs_3_) | copy-start | bytes 3145732
  249.2 27.6 %copy-start.17 = (f32[1024,256]{1,0:T(8,128)}, f32[1024,256]{1,0:T(8,128)S(1)}, u32[]{:S(2)}) copy-start(f32[1024,256]{1,0:T(8,128)S(1)} %collective-permute-done.26.refs_4_) | copy-start | bytes 3145732
  249.2 23.9 %collective-permute-start.29 = (f32[4,4,64,256]{3,2,1,0:T(8,128)}, f32[4,4,64,256]{3,2,1,0:T(8,128)S(1)}, u32[]{:S(2)}, u32[]{:S(2)}) collective-permute-start(f32[4,4,64,256]{3,2,1,0:T(8,128)} %get-tuple-element.121), channel_id=1, source_target_pairs={{0,1},{1,0},{2,3},{3,2},{4,5},{5,4},{6,7},{7,6},{8,9},{9,8},{10,11... | collective-permute-start | bytes 3145736 | tf_op jit(solution)/shard_map/ppermute | solution.py:452
  251.0 26.1 %collective-permute-start.31 = (f32[1024,256]{1,0:T(8,128)S(1)}, f32[1024,256]{1,0:T(8,128)S(1)}, u32[]{:S(2)}, u32[]{:S(2)}) collective-permute-start(f32[1024,256]{1,0:T(8,128)S(1)} %collective-permute-done.26.refs_4_), channel_id=1, source_target_pairs={{0,2},{1,3},{2,0},{3,1},{4,6},{5,7},{6,4},{7,5},{8,10},{9,11},{10,... | collective-permute-start | bytes 3145736 | tf_op jit(solution)/shard_map/ppermute | solution.py:452
  255.3 41.6 %collective-permute-start.27 = (f32[4,264,256]{2,1,0:T(8,128)}, f32[4,264,256]{2,1,0:T(8,128)S(1)}, u32[]{:S(2)}, u32[]{:S(2)}) collective-permute-start(f32[4,264,256]{2,1,0:T(8,128)} %inflate.5.refs_4_), channel_id=1, source_target_pairs={{0,16},{8,24},{16,0},{24,8},{1,17},{9,25},{17,1},{25,9},{2,18},{10... | collective-permute-start | bytes 3244040 | tf_op jit(solution)/shard_map/ppermute | solution.py:452
  256.8 40.1 %collective-permute-start.32 = (f32[1024,256]{1,0:T(8,128)}, f32[1024,256]{1,0:T(8,128)S(1)}, u32[]{:S(2)}, u32[]{:S(2)}) collective-permute-start(f32[1024,256]{1,0:T(8,128)} %collective-permute-done.22.refs_2_), channel_id=1, source_target_pairs={{0,2},{1,3},{2,0},{3,1},{4,6},{5,7},{6,4},{7,5},{8,10},{9,11},{10,... | collective-permute-start | bytes 3145736 | tf_op jit(solution)/shard_map/ppermute | solution.py:452
  257.2 39.8 %collective-permute-start.33 = (f32[1024,256]{1,0:T(8,128)}, f32[1024,256]{1,0:T(8,128)S(1)}, u32[]{:S(2)}, u32[]{:S(2)}) collective-permute-start(f32[1024,256]{1,0:T(8,128)} %collective-permute-done.21.refs_1_), channel_id=1, source_target_pairs={{0,8},{1,9},{2,4},{3,5},{4,2},{5,3},{6,14},{7,15},{8,0},{9,1},{10,... | collective-permute-start | bytes 3145736 | tf_op jit(solution)/shard_map/ppermute | solution.py:452
  276.8 20.1 %copy-start.14 = (f32[4,264,256]{2,1,0:T(8,128)S(1)}, f32[4,264,256]{2,1,0:T(8,128)}, u32[]{:S(2)}) copy-start(f32[4,264,256]{2,1,0:T(8,128)} %inflate.6.refs_8_) | copy-start | bytes 3244036
  297.0 16.6 %copy-start.10 = (f32[1024,256]{1,0:T(8,128)}, f32[1024,256]{1,0:T(8,128)S(1)}, u32[]{:S(2)}) copy-start(f32[1024,256]{1,0:T(8,128)S(1)} %collective-permute-done.32.refs_3_) | copy-start | bytes 3145732
  297.0 16.6 %copy-start.11 = (f32[1024,256]{1,0:T(8,128)}, f32[1024,256]{1,0:T(8,128)S(1)}, u32[]{:S(2)}) copy-start(f32[1024,256]{1,0:T(8,128)S(1)} %collective-permute-done.33.refs_4_) | copy-start | bytes 3145732
  297.0 49.0 %copy-start.21 = (f32[4,264,256]{2,1,0:T(8,128)}, f32[4,264,256]{2,1,0:T(8,128)S(1)}, u32[]{:S(2)}) copy-start(f32[4,264,256]{2,1,0:T(8,128)S(1)} %collective-permute-done.27.refs_6_) | copy-start | bytes 3244036
  297.0 27.7 %collective-permute-start.34 = (f32[4,264,256]{2,1,0:T(8,128)S(1)}, f32[4,264,256]{2,1,0:T(8,128)}, u32[]{:S(2)}, u32[]{:S(2)}) collective-permute-start(f32[4,264,256]{2,1,0:T(8,128)S(1)} %copy-done.14), channel_id=1, source_target_pairs={{0,16},{8,24},{16,0},{24,8},{1,17},{9,25},{17,1},{25,9},{2,18},{10... | collective-permute-start | bytes 3244040 | tf_op jit(solution)/shard_map/ppermute | solution.py:452
  298.6 22.5 %collective-permute-start.36 = (f32[4,4,64,256]{3,2,1,0:T(8,128)}, f32[4,4,64,256]{3,2,1,0:T(8,128)S(1)}, u32[]{:S(2)}, u32[]{:S(2)}) collective-permute-start(f32[4,4,64,256]{3,2,1,0:T(8,128)} %product.10), channel_id=1, source_target_pairs={{0,1},{1,0},{2,3},{3,2},{4,5},{5,4},{6,7},{7,6},{8,9},{9,8},{10,11... | collective-permute-start | bytes 3145736 | tf_op jit(solution)/shard_map/ppermute | solution.py:561
  299.2 26.0 %collective-permute-start.40 = (f32[1024,256]{1,0:T(8,128)S(1)}, f32[1024,256]{1,0:T(8,128)S(1)}, u32[]{:S(2)}, u32[]{:S(2)}) collective-permute-start(f32[1024,256]{1,0:T(8,128)S(1)} %collective-permute-done.33.refs_4_), channel_id=1, source_target_pairs={{0,2},{1,3},{2,0},{3,1},{4,6},{5,7},{6,4},{7,5},{8,10},{9,11},{10,... | collective-permute-start | bytes 3145736 | tf_op jit(solution)/shard_map/ppermute | solution.py:452
  324.7 33.3 %collective-permute-start.38 = (f32[4,264,256]{2,1,0:T(8,128)}, f32[4,264,256]{2,1,0:T(8,128)S(1)}, u32[]{:S(2)}, u32[]{:S(2)}) collective-permute-start(f32[4,264,256]{2,1,0:T(8,128)} %inflate.7.refs_12_), channel_id=1, source_target_pairs={{0,16},{8,24},{16,0},{24,8},{1,17},{9,25},{17,1},{25,9},{2,18},{10... | collective-permute-start | bytes 3244040 | tf_op jit(solution)/shard_map/ppermute | solution.py:563
  335.0 10.4 %collective-permute-start.41 = (f32[4,4,32,256]{3,2,1,0:T(8,128)}, f32[4,4,32,256]{3,2,1,0:T(8,128)S(1)}, u32[]{:S(2)}, u32[]{:S(2)}) collective-permute-start(f32[4,4,32,256]{3,2,1,0:T(8,128)} %product.12), channel_id=1, source_target_pairs={{0,1},{1,0},{2,3},{3,2},{4,5},{5,4},{6,7},{7,6},{8,9},{9,8},{10,11... | collective-permute-start | bytes 1572872 | tf_op jit(solution)/shard_map/ppermute | solution.py:561
  335.4 37.5 %collective-permute-start.24 = (f32[4,264,256]{2,1,0:T(8,128)S(1)}, f32[4,264,256]{2,1,0:T(8,128)}, u32[]{:S(2)}, u32[]{:S(2)}) collective-permute-start(f32[4,264,256]{2,1,0:T(8,128)S(1)} %copy-done.13), channel_id=1, source_target_pairs={{0,8},{8,0},{16,24},{24,16},{1,9},{9,1},{17,25},{25,17},{2,10},{10... | collective-permute-start | bytes 3244040 | tf_op jit(solution)/shard_map/ppermute | solution.py:543
  344.3 15.6 %copy-start.15 = (f32[4,264,256]{2,1,0:T(8,128)S(1)}, f32[4,264,256]{2,1,0:T(8,128)}, u32[]{:S(2)}) copy-start(f32[4,264,256]{2,1,0:T(8,128)} %inflate.7.refs_12_) | copy-start | bytes 3244036
  345.4 14.5 %collective-permute-start.45 = (f32[4,4,32,256]{3,2,1,0:T(8,128)}, f32[4,4,32,256]{3,2,1,0:T(8,128)S(1)}, u32[]{:S(2)}, u32[]{:S(2)}) collective-permute-start(f32[4,4,32,256]{3,2,1,0:T(8,128)} %product.13), channel_id=1, source_target_pairs={{0,1},{1,0},{2,3},{3,2},{4,5},{5,4},{6,7},{7,6},{8,9},{9,8},{10,11... | collective-permute-start | bytes 1572872 | tf_op jit(solution)/shard_map/ppermute | solution.py:561
  346.0 28.7 %collective-permute-start.30 = (f32[4,264,256]{2,1,0:T(8,128)S(1)}, f32[4,264,256]{2,1,0:T(8,128)}, u32[]{:S(2)}, u32[]{:S(2)}) collective-permute-start(f32[4,264,256]{2,1,0:T(8,128)S(1)} %copy-done.14), channel_id=1, source_target_pairs={{0,8},{8,0},{16,24},{24,16},{1,9},{9,1},{17,25},{25,17},{2,10},{10... | collective-permute-start | bytes 3244040 | tf_op jit(solution)/shard_map/ppermute | solution.py:543
  346.0 28.8 %collective-permute-start.28 = (f32[4,264,256]{2,1,0:T(8,128)S(1)}, f32[4,264,256]{2,1,0:T(8,128)}, u32[]{:S(2)}, u32[]{:S(2)}) collective-permute-start(f32[4,264,256]{2,1,0:T(8,128)S(1)} %collective-permute-done.27.refs_6_), channel_id=1, source_target_pairs={{0,8},{8,0},{16,24},{24,16},{1,9},{9,1},{17,25},{25,17},{2,10},{10... | collective-permute-start | bytes 3244040 | tf_op jit(solution)/shard_map/ppermute | solution.py:543
  358.0 14.9 %copy-start.19 = (f32[4,136,256]{2,1,0:T(8,128)S(1)}, f32[4,136,256]{2,1,0:T(8,128)}, u32[]{:S(2)}) copy-start(f32[4,136,256]{2,1,0:T(8,128)} %inflate.8.refs_16_) | copy-start | bytes 1671172
  358.0 16.8 %copy-start.22 = (f32[4,264,256]{2,1,0:T(8,128)}, f32[4,264,256]{2,1,0:T(8,128)S(1)}, u32[]{:S(2)}) copy-start(f32[4,264,256]{2,1,0:T(8,128)S(1)} %collective-permute-done.38.refs_14_) | copy-start | bytes 3244036
  358.1 14.8 %collective-permute-start.43 = (f32[4,136,256]{2,1,0:T(8,128)}, f32[4,136,256]{2,1,0:T(8,128)S(1)}, u32[]{:S(2)}, u32[]{:S(2)}) collective-permute-start(f32[4,136,256]{2,1,0:T(8,128)} %inflate.8.refs_16_), channel_id=1, source_target_pairs={{0,16},{8,24},{16,0},{24,8},{1,17},{9,25},{17,1},{25,9},{2,18},{10... | collective-permute-start | bytes 1671176 | tf_op jit(solution)/shard_map/ppermute | solution.py:563
  359.9 15.3 %collective-permute-start.37 = (f32[4,264,256]{2,1,0:T(8,128)S(1)}, f32[4,264,256]{2,1,0:T(8,128)}, u32[]{:S(2)}, u32[]{:S(2)}) collective-permute-start(f32[4,264,256]{2,1,0:T(8,128)S(1)} %copy-done.15), channel_id=1, source_target_pairs={{0,8},{8,0},{16,24},{24,16},{1,9},{9,1},{17,25},{25,17},{2,10},{10... | collective-permute-start | bytes 3244040 | tf_op jit(solution)/shard_map/ppermute | solution.py:564
  372.9 17.2 %copy-start.28 = (f32[4,136,256]{2,1,0:T(8,128)}, f32[4,136,256]{2,1,0:T(8,128)S(1)}, u32[]{:S(2)}) copy-start(f32[4,136,256]{2,1,0:T(8,128)S(1)} %collective-permute-done.43.refs_18_) | copy-start | bytes 1671172
  372.9 2.4 collective-permute-start.42
  372.9 15.3 %collective-permute-start.47 = (f32[4,136,256]{2,1,0:T(8,128)}, f32[4,136,256]{2,1,0:T(8,128)S(1)}, u32[]{:S(2)}, u32[]{:S(2)}) collective-permute-start(f32[4,136,256]{2,1,0:T(8,128)} %inflate.9.refs_20_), channel_id=1, source_target_pairs={{0,16},{8,24},{16,0},{24,8},{1,17},{9,25},{17,1},{25,9},{2,18},{10... | collective-permute-start | bytes 1671176 | tf_op jit(solution)/shard_map/ppermute | solution.py:563
  374.6 13.5 %collective-permute-start.35 = (f32[4,264,256]{2,1,0:T(8,128)}, f32[4,264,256]{2,1,0:T(8,128)S(1)}, u32[]{:S(2)}, u32[]{:S(2)}) collective-permute-start(f32[4,264,256]{2,1,0:T(8,128)} %collective-permute-done.34.refs_10_), channel_id=1, source_target_pairs={{0,8},{8,0},{16,24},{24,16},{1,9},{9,1},{17,25},{25,17},{2,10},{10... | collective-permute-start | bytes 3244040 | tf_op jit(solution)/shard_map/ppermute | solution.py:543
  374.8 13.4 %collective-permute-start.39 = (f32[4,264,256]{2,1,0:T(8,128)S(1)}, f32[4,264,256]{2,1,0:T(8,128)S(1)}, u32[]{:S(2)}, u32[]{:S(2)}) collective-permute-start(f32[4,264,256]{2,1,0:T(8,128)S(1)} %collective-permute-done.38.refs_14_), channel_id=1, source_target_pairs={{0,8},{8,0},{16,24},{24,16},{1,9},{9,1},{17,25},{25,17},{2,10},{10... | collective-permute-start | bytes 3244040 | tf_op jit(solution)/shard_map/ppermute | solution.py:564
  375.2 13.0 %collective-permute-start.46 = (f32[4,136,256]{2,1,0:T(8,128)}, f32[4,136,256]{2,1,0:T(8,128)S(1)}, u32[]{:S(2)}, u32[]{:S(2)}) collective-permute-start(f32[4,136,256]{2,1,0:T(8,128)} %inflate.9.refs_20_), channel_id=1, source_target_pairs={{0,8},{8,0},{16,24},{24,16},{1,9},{9,1},{17,25},{25,17},{2,10},{10... | collective-permute-start | bytes 1671176 | tf_op jit(solution)/shard_map/ppermute | solution.py:564
  375.3 12.9 %collective-permute-start.44 = (f32[4,136,256]{2,1,0:T(8,128)S(1)}, f32[4,136,256]{2,1,0:T(8,128)S(1)}, u32[]{:S(2)}, u32[]{:S(2)}) collective-permute-start(f32[4,136,256]{2,1,0:T(8,128)S(1)} %collective-permute-done.43.refs_18_), channel_id=1, source_target_pairs={{0,8},{8,0},{16,24},{24,16},{1,9},{9,1},{17,25},{25,17},{2,10},{10... | collective-permute-start | bytes 1671176 | tf_op jit(solution)/shard_map/ppermute | solution.py:564
  388.2 2.0 collective-permute-start.48
  (23 other events, 119.2 us)

commit v5 on v4

--- a/solution.py
+++ b/solution.py
@@ -9,8 +9,10 @@
 
 TR = 8
 CHUNKS = (128, 64, 64)
-ROWS = (64, 64, 32)
+ROWS = (64, 64, 64)
+PIECES = 2
 FIELDS = 8
+ALL, EARLY, FINAL = 0, 1, 2
 RING = 16
 VMEM = 56 * 1024 * 1024
 
@@ -75,6 +77,7 @@
 
 def plan_kernel(line, blocks, count, me_ref, *refs):
     items = blocks * count
+    room = listed(blocks, count)
     known, shards = refs[:8], refs[8:-3]
     plan_ref, kept_ref, levels_ref = refs[-3:]
     r, c = me_ref[0], me_ref[1]
@@ -83,49 +86,61 @@
     for i, shard in enumerate(shards):
 
         def note(j, _, i=i, shard=shard):
-            levels_ref[i * items + j] = shard[0, j].astype(jnp.int32)
+            levels = jnp.int32(0)
+            for y in range(count):
+                levels += shard[0, j * count + y].astype(jnp.int32) << (4 * y)
+            levels_ref[i * blocks + j] = levels
             return 0
 
-        lax.fori_loop(0, items, note, 0)
+        lax.fori_loop(0, blocks, note, 0)
 
     def write(n, tile, at, levels):
         plan_ref[FIELDS * n] = tile
         plan_ref[FIELDS * n + 1] = at
-        for y in range(count):
-            plan_ref[FIELDS * n + 2 + y] = levels(y)
-
-    n = jnp.int32(0)
+        plan_ref[FIELDS * n + 2] = levels
+
+    ends = tuple(jnp.int32(i * room) for i in range(3))
     for group in range(2):
 
-        def column(j, n, group=group):
+        def column(j, ends, group=group):
             row = group * blocks + j
             for relative in range(4):
                 rr = jnp.bitwise_xor(r, relative)
 
-                def entry(z, n, relative=relative, rr=rr):
+                def entry(z, ends, relative=relative, rr=rr):
                     noted = known[2 * relative + group][0, j * count + z]
                     k = rr * TR + noted.astype(jnp.int32)
                     ck = k // blocks
-                    levels = arrival(q, ck // 2) * items + (k % blocks) * count
                     mine = ck % 2 == p
-                    write(
-                        n,
-                        (row * 4 + relative) * count + z,
-                        (ck // 2) * blocks + k % blocks,
-                        lambda y: levels_ref[jnp.where(mine, levels + y, 0)],
+                    came = jnp.where(mine, arrival(q, ck // 2), 0)
+                    final = came == 2 * line - 3
+                    tile = (row * 4 + relative) * count + z
+                    at = (ck // 2) * blocks + k % blocks
+                    levels = levels_ref[came * blocks + k % blocks]
+                    write(ends[0], tile, at, levels)
+                    write(jnp.where(final, ends[2], ends[1]), tile, at, levels)
+                    return (
+                        ends[0] + mine.astype(jnp.int32),
+                        ends[1] + (mine & ~final).astype(jnp.int32),
+                        ends[2] + (mine & final).astype(jnp.int32),
                     )
-                    return n + mine.astype(jnp.int32)
-
-                n = lax.fori_loop(0, count, entry, n)
-            write(n, row * 4 * count, line * blocks, lambda y: jnp.int32(0))
-            n = n + n % 2
-            kept_ref[FIELDS * row] = n
+
+                ends = lax.fori_loop(0, count, entry, ends)
+            filled = []
+            for i, n in enumerate(ends):
+                write(n, row * 4 * count, line * blocks, jnp.int32(0))
+                filled.append(n + n % 2)
+                kept_ref[FIELDS * (i * 2 * blocks + row)] = filled[-1]
             for m in range(count):
                 noted = known[group][0, items + j * count + m]
                 kept_ref[FIELDS * row + 1 + m] = noted.astype(jnp.int32)
-            return n
-
-        n = lax.fori_loop(0, blocks, column, n)
+            return tuple(filled)
+
+        ends = lax.fori_loop(0, blocks, column, ends)
+
+
+def listed(blocks, count):
+    return 2 * blocks * (4 * count + 1) + 2
 
 
 def noted(x, row):
@@ -139,49 +154,50 @@
         functools.partial(plan_kernel, line, blocks, count),
         grid=(1,),
         out_shape=(
-            jax.ShapeDtypeStruct((FIELDS * (2 * blocks * 4 * count + 2),), jnp.int32),
-            jax.ShapeDtypeStruct((FIELDS * 2 * blocks,), jnp.int32),
+            jax.ShapeDtypeStruct((3 * FIELDS * listed(blocks, count),), jnp.int32),
+            jax.ShapeDtypeStruct((3 * FIELDS * 2 * blocks,), jnp.int32),
         ),
         in_specs=[smem, *specs],
         out_specs=(smem, smem),
-        scratch_shapes=[pltpu.SMEM(((2 * line - 2) * blocks * count,), jnp.int32)],
+        scratch_shapes=[pltpu.SMEM(((2 * line - 2) * blocks,), jnp.int32)],
         name="plan",
     )(me, *args)
 
 
-def product_kernel(line, groups, part, me_ref, plan_ref, kept_ref, b_ref, *refs):
-    parts = 2 * line - 2
-    a_refs = refs[:parts]
-    out_refs, (raw, halves, total, ring, a_sems, b_sems) = refs[parts:-6], refs[-6:]
+def product_kernel(line, which, arrivals, pieces, part, me_ref, plan_ref, kept_ref, b_ref, *refs):
+    a_refs, refs = refs[: len(arrivals)], refs[len(arrivals) :]
+    before, refs = (refs[:2], refs[2:]) if which == FINAL else ((), refs)
+    out_refs, (raw, halves, total, ring, a_sems, b_sems) = refs[:-6], refs[-6:]
     blocks = (halves.shape[0] - 1) // line
-    count, rows, width = out_refs[0].shape[1:]
-    group, j = pl.program_id(0) + groups[0], pl.program_id(1)
+    count, piece, width = out_refs[0].shape[1:]
+    rows = pieces * piece
+    group, j = pl.program_id(0), pl.program_id(1)
     size = blocks * count * rows
-    top, last = groups[0] * blocks, (groups[-1] + 1) * blocks - 1
     row = group * blocks + j
     q = me_ref[1] // 2
-    begun = kept_ref[FIELDS * (top - 1)] if top else 0
-    end = kept_ref[FIELDS * last]
+    begun = which * listed(blocks, count)
+    ends = which * 2 * blocks
+    end = kept_ref[FIELDS * (ends + 2 * blocks - 1)]
 
     def fetch(n):
         tile = plan_ref[FIELDS * n]
         slot = n % RING
         return pltpu.make_async_copy(b_ref.at[tile], ring.at[slot], b_sems.at[slot])
 
-    @pl.when(row == top)
+    @pl.when(row == 0)
     def _():
         def each(act):
-            for i in range(parts):
+            for n, i in enumerate(arrivals):
                 steps, link = (i + 1) // 2, (i + 1) % 2
                 source = q if i == 0 else jnp.where(q % 2 == link, q + steps, q - steps)
 
                 @pl.when((source >= 0) & (source < line))
                 def _():
-                    rows_of = a_refs[i].at[part * size : (part + 1) * size]
+                    rows_of = a_refs[n].at[part * size : (part + 1) * size]
                     to = raw.at[pl.ds(pl.multiple_of(source * size, size), size)]
-                    act(pltpu.make_async_copy(rows_of, to, a_sems.at[i]))
-
-        each(lambda copy: copy.start())
+                    act(pltpu.make_async_copy(rows_of, to, a_sems.at[n]), source)
+
+        each(lambda copy, _: copy.start())
 
         def begin(n, _):
             fetch(n).start()
@@ -189,7 +205,6 @@
 
         lax.fori_loop(begun, jnp.minimum(end, begun + RING), begin, 0)
         halves[line * blocks] = jnp.zeros(halves.shape[1:], halves.dtype)
-        each(lambda copy: copy.wait())
 
         def convert(i, _):
             first = pl.multiple_of(i * count * rows, count * rows)
@@ -198,10 +213,14 @@
             halves[i, count * rows :] = low
             return 0
 
-        lax.fori_loop(0, line * blocks, convert, 0)
+        def use(copy, source):
+            copy.wait()
+            lax.fori_loop(source * blocks, (source + 1) * blocks, convert, 0)
+
+        each(use)
 
     total[...] = jnp.zeros_like(total)
-    first = jnp.where(row == top, begun, kept_ref[FIELDS * jnp.maximum(row - 1, 0)])
+    first = jnp.where(row == 0, begun, kept_ref[FIELDS * (ends + jnp.maximum(row - 1, 0))])
 
     def multiply(n):
         a = halves[plan_ref[FIELDS * n + 1]]
@@ -217,8 +236,9 @@
         fetch(n + 1).wait()
         products = [multiply(n), multiply(n + 1)]
         for e in range(2):
+            levels = plan_ref[FIELDS * (n + e) + 2]
             for y in range(count):
-                level = plan_ref[FIELDS * (n + e) + 2 + y]
+                level = (levels >> (4 * y)) & 15
                 total[level] += products[e][y * rows : (y + 1) * rows]
 
         @pl.when(n + RING < end)
@@ -228,48 +248,59 @@
 
         return 0
 
-    lax.fori_loop(0, (kept_ref[FIELDS * row] - first) // 2, step, 0)
-
-    for g, out_ref in zip(groups, out_refs):
+    lax.fori_loop(0, (kept_ref[FIELDS * (ends + row)] - first) // 2, step, 0)
+
+    for g in range(2):
 
         @pl.when(group == g)
         def _():
             for m in range(count):
-                out_ref[0, m] = total[kept_ref[FIELDS * row + 1 + m]]
-
-
-def product(me, plan, panel, parts, line, part, rows, groups=(0, 1)):
+                level = kept_ref[FIELDS * row + 1 + m]
+                for n in range(pieces):
+                    some = pl.ds(n * piece, piece)
+                    result = total[level, some]
+                    if before:
+                        result += before[g][0, m, some]
+                    out_refs[g * pieces + n][0, m] = result
+
+
+def product(me, plan, panel, parts, line, part, rows, which=ALL, before=(), pieces=1):
     blocks, count, width = panel.shape[1], panel.shape[3], panel.shape[6]
-    out = jax.ShapeDtypeStruct((blocks, count, rows, width), jnp.float32)
+    arrivals = list(range(2 * line - 2))
+    arrivals = {ALL: arrivals, EARLY: arrivals[:-1], FINAL: arrivals[-1:]}[which]
+    out = jax.ShapeDtypeStruct((blocks, count, rows // pieces, width), jnp.float32)
     smem = pl.BlockSpec(memory_space=pltpu.SMEM)
+
+    def tiles_of(group, size):
+        return pl.BlockSpec(
+            (1, count, size, width),
+            lambda g, j: (jnp.where(g == group, j, 0 if group else blocks - 1), 0, 0, 0),
+        )
+
     return pl.pallas_call(
-        functools.partial(product_kernel, line, groups, part),
-        grid=(len(groups), blocks),
-        out_shape=(out,) * len(groups),
-        in_specs=[smem] * 3 + [pl.BlockSpec(memory_space=pl.ANY)] * (1 + len(parts)),
-        out_specs=tuple(
-            pl.BlockSpec(
-                (1, count, rows, width),
-                lambda g, j, i=i: (jnp.where(g == i, j, 0 if i else blocks - 1), 0, 0, 0),
-            )
-            for i in range(len(groups))
-        ),
+        functools.partial(product_kernel, line, which, arrivals, pieces, part),
+        grid=(2, blocks),
+        out_shape=(out,) * (2 * pieces),
+        in_specs=[smem] * 3
+        + [pl.BlockSpec(memory_space=pl.ANY)] * (1 + len(arrivals))
+        + [tiles_of(g, rows) for g in range(len(before))],
+        out_specs=tuple(tiles_of(g, rows // pieces) for g in range(2) for _ in range(pieces)),
         scratch_shapes=[
             pltpu.VMEM((line * blocks * count * rows, width), jnp.float32),
             pltpu.VMEM((line * blocks + 1, 2 * count * rows, width), jnp.bfloat16),
             pltpu.VMEM((TR, rows, width), jnp.float32),
             pltpu.VMEM((RING, 2, width, width), jnp.bfloat16),
-            pltpu.SemaphoreType.DMA((len(parts),)),
+            pltpu.SemaphoreType.DMA((len(arrivals),)),
             pltpu.SemaphoreType.DMA((RING,)),
         ],
         compiler_params=pltpu.CompilerParams(vmem_limit_bytes=VMEM),
         cost_estimate=pl.CostEstimate(
-            flops=3 * len(groups) * 16 * blocks * count * rows * width * width,
-            bytes_accessed=len(groups) * panel.size // 2,
+            flops=3 * 32 * blocks * count * rows * width * width * len(arrivals) // (2 * line - 2),
+            bytes_accessed=panel.size * len(arrivals) // (2 * line - 2),
             transcendentals=0,
         ),
         name="product",
-    )(me, *plan, panel.reshape(-1, 2, width, width), *parts)
+    )(me, *plan, panel.reshape(-1, 2, width, width), *(parts[i] for i in arrivals), *before)
 
 
 def inflate_kernel(own_ref, other_ref, out_ref):
@@ -451,12 +482,8 @@
     def send(tick, move, x, *more):
         return at(tick, move(after(tick, x), *more))
 
-    swapped = []
-
-    def swap(tick, x):
-        x = tie(x, *swapped[-1:])
-        swapped.append(at(tick + 1, core(after(tick, x))))
-        return swapped[-1]
+    def swap(tick, x, *others):
+        return at(tick + 1, core(after(tick, tie(x, *others))))
 
     base = line - 1
     hops = {}
@@ -470,6 +497,7 @@
 
     panel = None
     sources, waiting, landed, flying = [], [], [], []
+    begun, made, cuts = {}, [], [1] * (chunks - 1) + [PIECES]
 
     def put(tick, group, relative, *parts):
         nonlocal panel
@@ -484,10 +512,13 @@
 
     tick = 0
     while tick <= max(hops) + 1 or landed or flying:
-        if chunks > 1 and (1, line - 2) in hops.get(tick - 1, ()):
-            gathered = [own[1], *came[1]]
-            early, *_ = product(me, plan, panel, gathered, line, 0, rows[1], (0,))
-            at(tick - 1, early)
+        for h in range(1, chunks):
+            if (h, line - 2) in hops.get(tick - 1, ()):
+                results = product(
+                    me, plan, panel, [own[h], *came[h]], line, 0, rows[h], FINAL, begun[h], cuts[h]
+                )
+                at(tick - 1, results[0])
+                made.append((results[: cuts[h]], results[cuts[h] :]))
         for h, hop in hops.get(tick, ()):
             if hop:
                 operands = came[h][-1], came[h][-2]
@@ -495,22 +526,28 @@
                 operands = own[h], own[h]
             for link in range(1 if hop == line - 2 else 2):
                 came[h].append(send(tick, links[link], operands[link]))
+            if h and hop == line - 2:
+                begun[h] = product(
+                    me, plan, panel, [own[h], *came[h][:-1]], line, 0, rows[h], EARLY
+                )
+                at(tick, begun[h][0])
         if tick == 0:
             whole = tiles.reshape(-1, width)
             rest = tie(tiles, own[0])[:, :, half:].reshape(-1, width)
             b_pair, b_across = send(0, pair, own[0]), send(0, across, own[0])
             core_own = swap(0, whole)
-            put(0, 1, 0, (whole, width, 0))
+            put(0, 1, 0, *halves(own[0], rest))
         if tick == 1:
             pair_rest, across_rest = send(1, pair, rest), send(1, across, rest)
-            core_pair, core_notes = swap(1, b_pair), swap(1, own[0][upper:])
+            core_pair = swap(1, b_pair)
             put(1, 1, 1, (core_own, width, 0))
             later = after(1, tiles)
             own += [at(1, cut(later, h)) for h in range(1, chunks)]
         if tick == 2:
             diagonal, diagonal_rest = send(2, across, b_pair), send(2, pair, across_rest)
             core_across, core_pair_rest = swap(2, b_across), swap(2, pair_rest)
-            core_across_rest = swap(2, across_rest)
+            core_across_rest = swap(2, across_rest, core_across)
+            core_notes = swap(2, own[0][upper:], core_pair_rest)
             put(2, 0, 0, *halves(b_pair, pair_rest))
             put(2, 1, 2, *halves(b_across, across_rest))
             put(3, 0, 1, *halves(core_pair, core_pair_rest))
@@ -518,7 +555,8 @@
         if tick == max(base, 3):
             core_diagonal = swap(tick, diagonal)
             put(tick, 0, 2, *halves(diagonal, diagonal_rest))
-            put(tick, 0, 3, *halves(core_diagonal, swap(tick, diagonal_rest)))
+            core_diagonal_rest = swap(tick, diagonal_rest, core_diagonal)
+            put(tick, 0, 3, *halves(core_diagonal, core_diagonal_rest))
             known = [
                 (b_pair, upper),
                 (own[0], upper),
@@ -532,10 +570,8 @@
             known = [noted(x, i) for x, i in known]
             shards = [noted(x, upper) for x in [own[0], *came[0]]]
             plan = make_plan(me, known, shards, line, blocks, count)
-        for h in range(chunks):
-            if tick == max(base, 3) if h == 0 else (h, line - 2) in hops.get(tick - 1, ()):
-                gathered = [own[h], *came[h]]
-                waiting += [(gathered, i, rows[h]) for i in range(sizes[h] // rows[h])]
+            gathered = [own[0], *came[0]]
+            waiting = [(gathered, i, rows[0]) for i in range(parts)]
         if flying and flying[0][0] < tick:
             _, mine, other = flying.pop(0)
             inflated = inflate(mine, other)
@@ -545,24 +581,22 @@
             _, theirs, mine = landed.pop(0)
             other = send(tick, pair, theirs)
             flying.append((tick, mine, other))
-        if waiting and tick < max(hops) - 1:
+        if waiting:
             gathered, part, size = waiting.pop(0)
             theirs, mine = product(me, plan, panel, gathered, line, part, size)
             landed.append((tick, at(tick, theirs), mine))
         tick += 1
-    theirs, last = [early], early
-    for gathered, part, size in waiting[1:]:
-        last, *_ = product(tie(me, last), plan, panel, gathered, line, part, size, (0,))
-        theirs.append(last)
-    last = early
-    for n, (gathered, part, size) in enumerate(waiting):
-        last = theirs[-1] if n == 1 else last
-        last, *_ = product(tie(me, last), plan, panel, gathered, line, part, size, (1,))
-        other = pair(tie(theirs[n], other))
-        inflated = inflate(last, other)
-        opposite = across(tie(inflated, opposite))
-        sources += [inflated, core(inflated), opposite, core(opposite)]
-    sizes = tuple(rows[h] for h in range(chunks) for _ in range(0, sizes[h], rows[h]))
+    for theirs, mine in made:
+        for x, y in zip(theirs, mine):
+            other = pair(tie(x, other))
+            inflated = inflate(y, other)
+            opposite = across(tie(inflated, opposite))
+            sources += [inflated, core(inflated), opposite, core(opposite)]
+    sizes = tuple(
+        rows[h] // cuts[h]
+        for h in range(chunks)
+        for _ in range(0, sizes[h], rows[h] // cuts[h])
+    )
     scale = float(4 * TR * width)
     owned = owned_tiles(me, known[1::2], sources, sizes, count, scale)
     return owned[None, None]

time: 399 us -> 387 us (0.970)
  Pallas kernels: 167 us -> 153 us
    ppermute x25, waiting for transfers between devices: 147 us -> 129 us  [send(): return at(tick, move(after(tick, x), *more))]
    pallas_call x8 -> x6, Pallas kernels: 101 us -> 86.9 us  [product(): pl.pallas_call(functools.partial(product_kernel, line, which, arrivals, p...]
    ppermute x11, waiting for transfers between devices: 17.9 us -> 24.7 us  [the longest x3 18.8 us: on_device(): other = pair(tie(x, other))]
    ppermute x3, waiting for transfers between devices: 13.8 us -> 20.3 us  [on_device(): opposite = across(tie(inflated, opposite))]
  transfers between devices with their start and end apart: 49 -> 49, of which waited for: 20 -> 19; matrix products, arithmetic and copies ran while one was open for 2% -> 2% of each run, Pallas kernels for 40% -> 38%
where the time goes in v5:
time: 387 us; the launch traced here: 384 us
  waiting for transfers between devices  176 us (45%)
  Pallas kernels  153 us (40%)
  starting transfers between devices  39.4 us (10%)
  local copies, waits for them, and re-layouts  15.2 us (4%)
    ppermute x25, waiting for transfers between devices, send(): return at(tick, move(after(tick, x), *more))  129 us
    pallas_call x6, Pallas kernels, product(): pl.pallas_call(functools.partial(product_kernel, line, which, arrivals, p...  86.9 us
    pallas_call x8, Pallas kernels, place(): pl.pallas_call(functools.partial(place_kernel, len(parts)), grid=(blocks,...  39 us
    ppermute x25, starting transfers between devices, send(): return at(tick, move(after(tick, x), *more))  28.1 us
    ppermute x3, waiting for transfers between devices, on_device(): opposite = across(tie(inflated, opposite))  20.3 us
    ppermute x3, waiting for transfers between devices, on_device(): other = pair(tie(x, other))  18.8 us
    pallas_call x5, Pallas kernels, inflate(): pl.pallas_call(inflate_kernel, out_shape=jax.ShapeDtypeStruct((blocks, co...  12.2 us
    pallas_call x1, Pallas kernels, make_plan(): pl.pallas_call(functools.partial(plan_kernel, line, blocks, count), grid=...  7.92 us
  transfers between devices with their start and end apart: 49, of which 19 were waited for; matrix products, arithmetic and copies ran while one was open for 2% of the time, Pallas kernels for 38%

profile of v5, /device:TPU:0, one launch (start us, length us, event | category | flops | bytes accessed | tf_op | source)
XLA Modules:
  0.0 384.1 jit_solution(2343985313334921693)
XLA Ops:
  0.0 0.8 reshape.28
  0.8 0.8 reshape.29
  1.5 1.7 slice.16
  4.2 3.0 collective-permute-start.3
  7.2 1.5 collective-permute-start.2
  8.7 3.1 collective-permute-start
  11.8 3.1 slice.13
  14.9 4.8 %place.8 = (bf16[2,4,4,4,2,256,256]{6,5,4,3,2,1,0:T(8,128)(2,1)}, f32[8,128]{1,0:T(8,128)}) custom-call(f32[2056,256]{1,0:T(8,128)} %copy-done, f32[2056,256]{1,0:T(8,128)} %copy-done, f32[2048,256]{1,0:T(8,128)} %bitcast.20), custom_call_target="tpu_custom_call" | custom-call | flops 1048576 | bytes 8388608 | tf_op jit(solution)/shard_map/place/pallas_call | solution.py:60
  19.7 33.3 %collective-permute-done.3.refs_0_.refs_1_.refs_5_.refs_2_ = f32[2056,256]{1,0:T(8,128)S(1)} collective-permute-done((f32[2056,256]{1,0:T(8,128)S(1)}, f32[2056,256]{1,0:T(8,128)S(1)}, u32[]{:S(2)}, u32[]{:S(2)}) %collective-permute-start.3) | collective-permute-done | bytes 2105376 | tf_op jit(solution)/shard_map/ppermute | solution.py:483
  53.0 1.6 collective-permute-done.2.refs_0_.refs_1_
  54.6 2.4 collective-permute-done.refs_9_.refs_1_
  57.0 1.6 collective-permute-start.6
  59.7 2.7 fusion
  62.4 5.3 %place.9 = (bf16[2,4,4,4,2,256,256]{6,5,4,3,2,1,0:T(8,128)(2,1)}, f32[8,128]{1,0:T(8,128)}) custom-call(f32[4096,256]{1,0:T(8,128)} %collective-permute-done.5.refs_0_, bf16[2,4,4,4,2,256,256]{6,5,4,3,2,1,0:T(8,128)(2,1)} %get-tuple-element.78.refs_1_), custom_call_target="tpu_custom_call", output_to_operand_aliasing={{0}: (1, {})} | custom-call | flops 1048576 | bytes 8388608 | tf_op jit(solution)/shard_map/place/pallas_call | solution.py:60
  67.7 39.3 %collective-permute-done.8.refs_2_ = f32[2048,256]{1,0:T(8,128)} collective-permute-done((f32[2048,256]{1,0:T(8,128)}, f32[2048,256]{1,0:T(8,128)}, u32[]{:S(2)}, u32[]{:S(2)}) %collective-permute-start.8) | collective-permute-done | bytes 2097184 | tf_op jit(solution)/shard_map/ppermute | solution.py:483
  107.3 1.6 collective-permute-start.13
  108.8 1.7 collective-permute-start.14
  111.1 4.8 %place.10 = (bf16[2,4,4,4,2,256,256]{6,5,4,3,2,1,0:T(8,128)(2,1)}, f32[8,128]{1,0:T(8,128)}) custom-call(f32[2056,256]{1,0:T(8,128)} %collective-permute-done.2.refs_0_.refs_1_, f32[2056,256]{1,0:T(8,128)} %collective-permute-done.2.refs_0_.refs_1_, f32[2048,256]{1,0:T(8,128)} %collective-permute-done.4.refs_2_, ...), custom_call_target="tpu_custom_call", output_to_operand_aliasing={{0}: (3, {})} | custom-call | flops 1048576 | bytes 8388608 | tf_op jit(solution)/shard_map/place/pallas_call | solution.py:60
  116.0 4.8 %place.11 = (bf16[2,4,4,4,2,256,256]{6,5,4,3,2,1,0:T(8,128)(2,1)}, f32[8,128]{1,0:T(8,128)}) custom-call(f32[2056,256]{1,0:T(8,128)} %copy-done.1, f32[2056,256]{1,0:T(8,128)} %copy-done.1, f32[2048,256]{1,0:T(8,128)} %collective-permute-done.8.refs_2_, bf16[2,4,4,4,2,256,256]{6,5,4,3,2,1,0:T(8,128)(2,1)} %get-tuple-element.91.refs_3_), custom_call_target="tpu_custom_call", output_to_operand_aliasing={{0}: (3, {})} | custom-call | flops 1048576 | bytes 8388608 | tf_op jit(solution)/shard_map/place/pallas_call | solution.py:60
  120.7 35.2 %collective-permute-done.15.refs_2_ = f32[2048,256]{1,0:T(8,128)} collective-permute-done((f32[2048,256]{1,0:T(8,128)}, f32[2048,256]{1,0:T(8,128)}, u32[]{:S(2)}, u32[]{:S(2)}) %collective-permute-start.15) | collective-permute-done | bytes 2097184 | tf_op jit(solution)/shard_map/ppermute | solution.py:483
  157.3 5.4 %collective-permute-done.16.refs_6_.refs_0_.refs_1_ = f32[2056,256]{1,0:T(8,128)} collective-permute-done((f32[2056,256]{1,0:T(8,128)}, f32[2056,256]{1,0:T(8,128)}, u32[]{:S(2)}, u32[]{:S(2)}) %collective-permute-start.16) | collective-permute-done | bytes 2105376 | tf_op jit(solution)/shard_map/ppermute | solution.py:486
  163.9 2.6 collective-permute-start.19
  166.6 2.7 collective-permute-start.21
  169.8 4.9 %place.12 = (bf16[2,4,4,4,2,256,256]{6,5,4,3,2,1,0:T(8,128)(2,1)}, f32[8,128]{1,0:T(8,128)}) custom-call(f32[2056,256]{1,0:T(8,128)} %collective-permute-done.12.refs_2_.refs_0_.refs_1_, f32[2056,256]{1,0:T(8,128)} %collective-permute-done.12.refs_2_.refs_0_.refs_1_, f32[2048,256]{1,0:T(8,128)} %copy-done.10, ...), custom_call_target="tpu_custom_call", output_to_operand_aliasing={{0}: (3, {})} | custom-call | flops 1048576 | bytes 8388608 | tf_op jit(solution)/shard_map/place/pallas_call | solution.py:60
  174.7 4.8 %place.13 = (bf16[2,4,4,4,2,256,256]{6,5,4,3,2,1,0:T(8,128)(2,1)}, f32[8,128]{1,0:T(8,128)}) custom-call(f32[2056,256]{1,0:T(8,128)} %copy-done.2, f32[2056,256]{1,0:T(8,128)} %copy-done.2, f32[2048,256]{1,0:T(8,128)} %copy-done.11, bf16[2,4,4,4,2,256,256]{6,5,4,3,2,1,0:T(8,128)(2,1)} %get-tuple-element.101.refs_3_), custom_call_target="tpu_custom_call", output_to_operand_aliasing={{0}: (3, {})} | custom-call | flops 1048576 | bytes 8388608 | tf_op jit(solution)/shard_map/place/pallas_call | solution.py:60
  179.5 4.8 %place.14 = (bf16[2,4,4,4,2,256,256]{6,5,4,3,2,1,0:T(8,128)(2,1)}, f32[8,128]{1,0:T(8,128)}) custom-call(f32[2056,256]{1,0:T(8,128)} %collective-permute-done.13.refs_4_.refs_0_.refs_1_, f32[2056,256]{1,0:T(8,128)} %collective-permute-done.13.refs_4_.refs_0_.refs_1_, f32[2048,256]{1,0:T(8,128)} %collective-permute-done.15.refs_2_, ...), custom_call_target="tpu_custom_call", output_to_operand_aliasing={{0}: (3, {})} | custom-call | flops 1048576 | bytes 8388608 | tf_op jit(solution)/shard_map/place/pallas_call | solution.py:60
  184.3 7.9 %plan.1 = (s32[3312]{0:T(1024)}, s32[192]{0:T(256)}) custom-call(s32[2]{0:T(128)} %pad_add_fusion.me_ref, f32[2056,256]{1,0:T(8,128)} %collective-permute-done.2.refs_0_.refs_1_, f32[2056,256]{1,0:T(8,128)} %copy-done, f32[2056,256]{1,0:T(8,128)} %collective-permute-done.12.refs_2_.refs_0_.refs_1_, f32[8,256]{1,0:T(8,128)} %copy-done.33, ...), custom_call_target="tpu_custom_call" | custom-call | tf_op jit(solution)/shard_map/plan/pallas_call | solution.py:153
  192.2 4.8 %place.15 = (bf16[2,4,4,4,2,256,256]{6,5,4,3,2,1,0:T(8,128)(2,1)}, f32[8,128]{1,0:T(8,128)}) custom-call(f32[2056,256]{1,0:T(8,128)} %collective-permute-done.16.refs_6_.refs_0_.refs_1_, f32[2056,256]{1,0:T(8,128)} %collective-permute-done.16.refs_6_.refs_0_.refs_1_, f32[2048,256]{1,0:T(8,128)} %collective-permute-done.17.refs_2_, ...), custom_call_target="tpu_custom_call", output_to_operand_aliasing={{0}: (3, {})} | custom-call | flops 1048576 | bytes 8388608 | tf_op jit(solution)/shard_map/place/pallas_call | solution.py:60
  197.0 18.7 %product.6 = (f32[4,4,64,256]{3,2,1,0:T(8,128)}, f32[4,4,64,256]{3,2,1,0:T(8,128)}) custom-call(s32[2]{0:T(128)} %pad_add_fusion.me_ref, s32[3312]{0:T(1024)} %get-tuple-element.94.plan_ref, s32[192]{0:T(256)} %get-tuple-element.95.kept_ref, bf16[128,2,256,256]{3,2,1,0:T(8,128)(2,1)} %bitcast.14, f32[2056,256]{1,0:T(8,128)} %copy-done, ...), custom_call_target="tpu_custom_call" | custom-call | flops 6442450944 | bytes 16777216 | tf_op jit(solution)/shard_map/product/pallas_call | solution.py:280
  215.8 2.2 collective-permute-start.23
  218.4 18.7 %product.7 = (f32[4,4,64,256]{3,2,1,0:T(8,128)}, f32[4,4,64,256]{3,2,1,0:T(8,128)}) custom-call(s32[2]{0:T(128)} %pad_add_fusion.me_ref, s32[3312]{0:T(1024)} %get-tuple-element.94.plan_ref, s32[192]{0:T(256)} %get-tuple-element.95.kept_ref, bf16[128,2,256,256]{3,2,1,0:T(8,128)(2,1)} %bitcast.15, f32[2056,256]{1,0:T(8,128)} %copy-done, ...), custom_call_target="tpu_custom_call" | custom-call | flops 6442450944 | bytes 16777216 | tf_op jit(solution)/shard_map/product/pallas_call | solution.py:280
  237.2 4.0 %collective-permute-done.23.other_ref = f32[4,4,64,256]{3,2,1,0:T(8,128)S(1)} collective-permute-done((f32[4,4,64,256]{3,2,1,0:T(8,128)}, f32[4,4,64,256]{3,2,1,0:T(8,128)S(1)}, u32[]{:S(2)}, u32[]{:S(2)}) %collective-permute-start.23) | collective-permute-done | bytes 1048608 | tf_op jit(solution)/shard_map/ppermute | solution.py:483
  241.2 1.5 collective-permute-done.25.refs_3_
  242.6 0.9 collective-permute-start.29
  243.6 1.7 collective-permute-start.31
  245.3 2.7 inflate.5.refs_4_
  248.9 15.6 %product.8 = (f32[4,4,64,256]{3,2,1,0:T(8,128)}, f32[4,4,64,256]{3,2,1,0:T(8,128)}) custom-call(s32[2]{0:T(128)} %pad_add_fusion.me_ref, s32[3312]{0:T(1024)} %get-tuple-element.94.plan_ref, s32[192]{0:T(256)} %get-tuple-element.95.kept_ref, bf16[128,2,256,256]{3,2,1,0:T(8,128)(2,1)} %bitcast.16, f32[1024,256]{1,0:T(8,128)} %bitcast.30, ...), custom_call_target="tpu_custom_call" | custom-call | flops 5368709120 | bytes 13981013 | tf_op jit(solution)/shard_map/product/pallas_call | solution.py:280
  264.5 1.9 collective-permute-done.29.other_ref
  266.4 1.0 copy-done.25
  267.3 2.6 inflate.6.refs_8_
  270.0 1.0 copy-done.22
  270.9 9.1 %product.9 = (f32[4,4,64,256]{3,2,1,0:T(8,128)}, f32[4,4,64,256]{3,2,1,0:T(8,128)}) custom-call(s32[2]{0:T(128)} %pad_add_fusion.me_ref, s32[3312]{0:T(1024)} %get-tuple-element.94.plan_ref, s32[192]{0:T(256)} %get-tuple-element.95.kept_ref, bf16[128,2,256,256]{3,2,1,0:T(8,128)(2,1)} %bitcast.17, f32[1024,256]{1,0:T(8,128)} %copy-done.22, ...), custom_call_target="tpu_custom_call" | custom-call | flops 1073741824 | bytes 2796202 | tf_op jit(solution)/shard_map/product/pallas_call | solution.py:280
  280.0 9.8 %collective-permute-done.32.refs_3_ = f32[1024,256]{1,0:T(8,128)S(1)} collective-permute-done((f32[1024,256]{1,0:T(8,128)}, f32[1024,256]{1,0:T(8,128)S(1)}, u32[]{:S(2)}, u32[]{:S(2)}) %collective-permute-start.32) | collective-permute-done | bytes 1048608 | tf_op jit(solution)/shard_map/ppermute | solution.py:483
  290.5 1.3 collective-permute-start.36
  291.8 1.4 collective-permute-start.40
  293.2 15.6 %product.10 = (f32[4,4,64,256]{3,2,1,0:T(8,128)}, f32[4,4,64,256]{3,2,1,0:T(8,128)}) custom-call(s32[2]{0:T(128)} %pad_add_fusion.me_ref, s32[3312]{0:T(1024)} %get-tuple-element.94.plan_ref, s32[192]{0:T(256)} %get-tuple-element.95.kept_ref, bf16[128,2,256,256]{3,2,1,0:T(8,128)(2,1)} %bitcast.18, f32[1024,256]{1,0:T(8,128)} %bitcast.27, ...), custom_call_target="tpu_custom_call" | custom-call | flops 5368709120 | bytes 13981013 | tf_op jit(solution)/shard_map/product/pallas_call | solution.py:280
  308.7 4.6 %collective-permute-done.36.other_ref = f32[4,4,64,256]{3,2,1,0:T(8,128)S(1)} collective-permute-done((f32[4,4,64,256]{3,2,1,0:T(8,128)}, f32[4,4,64,256]{3,2,1,0:T(8,128)S(1)}, u32[]{:S(2)}, u32[]{:S(2)}) %collective-permute-start.36) | collective-permute-done | bytes 1048608 | tf_op jit(solution)/shard_map/ppermute | solution.py:591
  313.3 1.0 copy-done.26
  314.3 2.7 inflate.7.refs_12_
  317.0 1.5 collective-permute-start.38
  318.5 1.0 copy-done.24
  319.4 9.2 %product.11 = (f32[4,4,32,256]{3,2,1,0:T(8,128)}, f32[4,4,32,256]{3,2,1,0:T(8,128)}, f32[4,4,32,256]{3,2,1,0:T(8,128)}, f32[4,4,32,256]{3,2,1,0:T(8,128)}) custom-call(s32[2]{0:T(128)} %pad_add_fusion.me_ref, s32[3312]{0:T(1024)} %get-tuple-element.94.plan_ref, s32[192]{0:T(256)} %get-tuple-element.95.kept_ref, bf16[128,2,256,256]{3,2,1,0:T(8,128)(2,1)} %bitcast.19, ...), custom_call_target="tpu_custom_call" | custom-call | flops 1073741824 | bytes 2796202 | tf_op jit(solution)/shard_map/product/pallas_call | solution.py:280
  328.6 1.9 collective-permute-start.41
  330.5 10.3 %collective-permute-done.41.other_ref = f32[4,4,32,256]{3,2,1,0:T(8,128)S(1)} collective-permute-done((f32[4,4,32,256]{3,2,1,0:T(8,128)}, f32[4,4,32,256]{3,2,1,0:T(8,128)S(1)}, u32[]{:S(2)}, u32[]{:S(2)}) %collective-permute-start.41) | collective-permute-done | bytes 524320 | tf_op jit(solution)/shard_map/ppermute | solution.py:591
  340.8 1.8 collective-permute-start.45
  343.1 2.1 inflate.8.refs_16_
  345.2 1.3 collective-permute-start.43
  346.5 3.9 %collective-permute-done.45.other_ref = f32[4,4,32,256]{3,2,1,0:T(8,128)} collective-permute-done((f32[4,4,32,256]{3,2,1,0:T(8,128)}, f32[4,4,32,256]{3,2,1,0:T(8,128)}, u32[]{:S(2)}, u32[]{:S(2)}) %collective-permute-start.45) | collective-permute-done | bytes 524320 | tf_op jit(solution)/shard_map/ppermute | solution.py:591
  350.4 2.1 inflate.9.refs_20_
  352.5 7.5 %collective-permute-done.43.refs_18_ = f32[4,136,256]{2,1,0:T(8,128)S(1)} collective-permute-done((f32[4,136,256]{2,1,0:T(8,128)}, f32[4,136,256]{2,1,0:T(8,128)S(1)}, u32[]{:S(2)}, u32[]{:S(2)}) %collective-permute-start.43) | collective-permute-done | bytes 557088 | tf_op jit(solution)/shard_map/ppermute | solution.py:593
  360.0 1.3 collective-permute-start.47
  362.4 12.9 %collective-permute-done.47.refs_22_ = f32[4,136,256]{2,1,0:T(8,128)S(1)} collective-permute-done((f32[4,136,256]{2,1,0:T(8,128)}, f32[4,136,256]{2,1,0:T(8,128)S(1)}, u32[]{:S(2)}, u32[]{:S(2)}) %collective-permute-start.47) | collective-permute-done | bytes 557088 | tf_op jit(solution)/shard_map/ppermute | solution.py:593
  376.0 1.3 collective-permute-done.48.refs_23_
  377.4 6.7 %owned.1 = f32[32,256,256]{2,1,0:T(8,128)} custom-call(s32[2]{0:T(128)} %pad_add_fusion.me_ref, f32[2056,256]{1,0:T(8,128)} %copy-done, f32[8,256]{1,0:T(8,128)} %copy-done.33, f32[2056,256]{1,0:T(8,128)} %copy-done.1, f32[2056,256]{1,0:T(8,128)} %copy-done.2, f32[4,264,256]{2,1,0:T(8,128)} %inflate.5.refs_4_, f32[4,264,256]{2,1,0:T(8,128)} %copy-done.15, ...), custom_call_target="tpu_custom_call" | custom-call | flops 2097152 | bytes 16777216 | tf_op jit(solution)/shard_map/owned/pallas_call | solution.py:406
  (136 shorter events, 10.1 us)
Async XLA Ops:
  4.2 10.8 %copy-start = (f32[2056,256]{1,0:T(8,128)}, f32[2056,256]{1,0:T(8,128)S(1)}, u32[]{:S(2)}) copy-start(f32[2056,256]{1,0:T(8,128)S(1)} %pad_maximum_fusion.refs_0_.refs_1_.refs_8_) | copy-start | bytes 6316036
  4.2 48.8 %collective-permute-start.3 = (f32[2056,256]{1,0:T(8,128)S(1)}, f32[2056,256]{1,0:T(8,128)S(1)}, u32[]{:S(2)}, u32[]{:S(2)}) collective-permute-start(f32[2056,256]{1,0:T(8,128)S(1)} %pad_maximum_fusion.refs_0_.refs_1_.refs_8_), channel_id=1, source_target_pairs={{0,16},{8,24},{16,0},{24,8},{1,17},{9,25},{17,1},{25,9},{2,18},{10... | collective-permute-start | bytes 6316040 | tf_op jit(solution)/shard_map/ppermute | solution.py:483
  7.2 47.4 %collective-permute-start.2 = (f32[2056,256]{1,0:T(8,128)S(1)}, f32[2056,256]{1,0:T(8,128)}, u32[]{:S(2)}, u32[]{:S(2)}) collective-permute-start(f32[2056,256]{1,0:T(8,128)S(1)} %pad_maximum_fusion.refs_0_.refs_1_.refs_8_), channel_id=1, source_target_pairs={{0,1},{1,0},{2,3},{3,2},{4,5},{5,4},{6,7},{7,6},{8,9},{9,8},{10,11... | collective-permute-start | bytes 6316040 | tf_op jit(solution)/shard_map/ppermute | solution.py:483
  8.7 45.9 %collective-permute-start.1 = (f32[2056,256]{1,0:T(8,128)S(1)}, f32[2056,256]{1,0:T(8,128)S(1)}, u32[]{:S(2)}, u32[]{:S(2)}) collective-permute-start(f32[2056,256]{1,0:T(8,128)S(1)} %pad_maximum_fusion.refs_0_.refs_1_.refs_8_), channel_id=1, source_target_pairs={{0,8},{1,9},{2,4},{3,5},{4,2},{5,3},{6,14},{7,15},{8,0},{9,1},{10,... | collective-permute-start | bytes 6316040 | tf_op jit(solution)/shard_map/ppermute | solution.py:483
  8.7 48.3 %collective-permute-start = (f32[2056,256]{1,0:T(8,128)S(1)}, f32[2056,256]{1,0:T(8,128)}, u32[]{:S(2)}, u32[]{:S(2)}) collective-permute-start(f32[2056,256]{1,0:T(8,128)S(1)} %pad_maximum_fusion.refs_0_.refs_1_.refs_8_), channel_id=1, source_target_pairs={{0,2},{1,3},{2,0},{3,1},{4,6},{5,7},{6,4},{7,5},{8,10},{9,11},{10,... | collective-permute-start | bytes 6316040 | tf_op jit(solution)/shard_map/ppermute | solution.py:483
  11.8 50.6 %collective-permute-start.5 = (f32[4096,256]{1,0:T(8,128)}, f32[4096,256]{1,0:T(8,128)}, u32[]{:S(2)}, u32[]{:S(2)}) collective-permute-start(f32[4096,256]{1,0:T(8,128)} %bitcast.8), channel_id=1, source_target_pairs={{0,8},{8,0},{16,24},{24,16},{1,9},{9,1},{17,25},{25,17},{2,10},{10... | collective-permute-start | bytes 12582920 | tf_op jit(solution)/shard_map/ppermute | solution.py:486
  53.0 58.1 %copy-start.1 = (f32[2056,256]{1,0:T(8,128)}, f32[2056,256]{1,0:T(8,128)S(1)}, u32[]{:S(2)}) copy-start(f32[2056,256]{1,0:T(8,128)S(1)} %collective-permute-done.3.refs_0_.refs_1_.refs_5_.refs_2_) | copy-start | bytes 6316036
  54.6 13.2 %copy-start.3 = (f32[2056,256]{1,0:T(8,128)}, f32[2056,256]{1,0:T(8,128)S(1)}, u32[]{:S(2)}) copy-start(f32[2056,256]{1,0:T(8,128)S(1)} %collective-permute-done.1.refs_10_.refs_2_) | copy-start | bytes 6316036
  57.0 50.2 %collective-permute-start.6 = (f32[2056,256]{1,0:T(8,128)S(1)}, f32[2056,256]{1,0:T(8,128)S(1)}, u32[]{:S(2)}, u32[]{:S(2)}) collective-permute-start(f32[2056,256]{1,0:T(8,128)S(1)} %collective-permute-done.1.refs_10_.refs_2_), channel_id=1, source_target_pairs={{0,2},{1,3},{2,0},{3,1},{4,6},{5,7},{6,4},{7,5},{8,10},{9,11},{10,... | collective-permute-start | bytes 6316040 | tf_op jit(solution)/shard_map/ppermute | solution.py:483
  58.7 48.6 %collective-permute-start.7 = (f32[2056,256]{1,0:T(8,128)}, f32[2056,256]{1,0:T(8,128)}, u32[]{:S(2)}, u32[]{:S(2)}) collective-permute-start(f32[2056,256]{1,0:T(8,128)} %collective-permute-done.refs_9_.refs_1_), channel_id=1, source_target_pairs={{0,8},{1,9},{2,4},{3,5},{4,2},{5,3},{6,14},{7,15},{8,0},{9,1},{10,... | collective-permute-start | bytes 6316040 | tf_op jit(solution)/shard_map/ppermute | solution.py:483
  58.7 48.4 %collective-permute-start.8 = (f32[2048,256]{1,0:T(8,128)}, f32[2048,256]{1,0:T(8,128)}, u32[]{:S(2)}, u32[]{:S(2)}) collective-permute-start(f32[2048,256]{1,0:T(8,128)} %bitcast.21), channel_id=1, source_target_pairs={{0,16},{8,24},{16,0},{24,8},{1,17},{9,25},{17,1},{25,9},{2,18},{10... | collective-permute-start | bytes 6291464 | tf_op jit(solution)/shard_map/ppermute | solution.py:483
  59.2 48.1 %collective-permute-start.4 = (f32[2048,256]{1,0:T(8,128)}, f32[2048,256]{1,0:T(8,128)}, u32[]{:S(2)}, u32[]{:S(2)}) collective-permute-start(f32[2048,256]{1,0:T(8,128)} %bitcast.22), channel_id=1, source_target_pairs={{0,1},{1,0},{2,3},{3,2},{4,5},{5,4},{6,7},{7,6},{8,9},{9,8},{10,11... | collective-permute-start | bytes 6291464 | tf_op jit(solution)/shard_map/ppermute | solution.py:483
  62.4 104.1 %copy-start.9 = (f32[4,4,64,256]{3,2,1,0:T(8,128)}, f32[4,4,64,256]{3,2,1,0:T(8,128)S(1)}, u32[]{:S(2)}) copy-start(f32[4,4,64,256]{3,2,1,0:T(8,128)S(1)} %get-tuple-element.141) | copy-start | bytes 3145732
  62.4 58.3 %collective-permute-start.12 = (f32[2056,256]{1,0:T(8,128)}, f32[2056,256]{1,0:T(8,128)}, u32[]{:S(2)}, u32[]{:S(2)}) collective-permute-start(f32[2056,256]{1,0:T(8,128)} %collective-permute-done.2.refs_0_.refs_1_), channel_id=1, source_target_pairs={{0,8},{8,0},{16,24},{24,16},{1,9},{9,1},{17,25},{25,17},{2,10},{10... | collective-permute-start | bytes 6316040 | tf_op jit(solution)/shard_map/ppermute | solution.py:486
  107.3 48.7 %collective-permute-start.13 = (f32[2056,256]{1,0:T(8,128)}, f32[2056,256]{1,0:T(8,128)}, u32[]{:S(2)}, u32[]{:S(2)}) collective-permute-start(f32[2056,256]{1,0:T(8,128)} %collective-permute-done.2.refs_0_.refs_1_), channel_id=1, source_target_pairs={{0,16},{8,24},{16,0},{24,8},{1,17},{9,25},{17,1},{25,9},{2,18},{10... | collective-permute-start | bytes 6316040 | tf_op jit(solution)/shard_map/ppermute | solution.py:483
  108.8 47.1 %collective-permute-start.14 = (f32[2056,256]{1,0:T(8,128)}, f32[2056,256]{1,0:T(8,128)S(1)}, u32[]{:S(2)}, u32[]{:S(2)}) collective-permute-start(f32[2056,256]{1,0:T(8,128)} %collective-permute-done.7.refs_12_.refs_4_), channel_id=1, source_target_pairs={{0,2},{1,3},{2,0},{3,1},{4,6},{5,7},{6,4},{7,5},{8,10},{9,11},{10,... | collective-permute-start | bytes 6316040 | tf_op jit(solution)/shard_map/ppermute | solution.py:483
  110.6 45.4 %collective-permute-start.15 = (f32[2048,256]{1,0:T(8,128)}, f32[2048,256]{1,0:T(8,128)}, u32[]{:S(2)}, u32[]{:S(2)}) collective-permute-start(f32[2048,256]{1,0:T(8,128)} %collective-permute-done.8.refs_2_), channel_id=1, source_target_pairs={{0,1},{1,0},{2,3},{3,2},{4,5},{5,4},{6,7},{7,6},{8,9},{9,8},{10,11... | collective-permute-start | bytes 6291464 | tf_op jit(solution)/shard_map/ppermute | solution.py:483
  111.1 45.4 %collective-permute-start.11 = (f32[2056,256]{1,0:T(8,128)S(1)}, f32[2056,256]{1,0:T(8,128)S(1)}, u32[]{:S(2)}, u32[]{:S(2)}) collective-permute-start(f32[2056,256]{1,0:T(8,128)S(1)} %collective-permute-done.3.refs_0_.refs_1_.refs_5_.refs_2_), channel_id=1, source_target_pairs={{0,8},{8,0},{16,24},{24,16},{1,9},{9,1},{17,25},{25,17},{2,10},{10... | collective-permute-start | bytes 6316040 | tf_op jit(solution)/shard_map/ppermute | solution.py:486
  156.0 6.8 %collective-permute-start.16 = (f32[2056,256]{1,0:T(8,128)}, f32[2056,256]{1,0:T(8,128)}, u32[]{:S(2)}, u32[]{:S(2)}) collective-permute-start(f32[2056,256]{1,0:T(8,128)} %collective-permute-done.13.refs_4_.refs_0_.refs_1_), channel_id=1, source_target_pairs={{0,8},{8,0},{16,24},{24,16},{1,9},{9,1},{17,25},{25,17},{2,10},{10... | collective-permute-start | bytes 6316040 | tf_op jit(solution)/shard_map/ppermute | solution.py:486
  156.0 7.4 %collective-permute-start.9 = (f32[2048,256]{1,0:T(8,128)}, f32[2048,256]{1,0:T(8,128)S(1)}, u32[]{:S(2)}, u32[]{:S(2)}) collective-permute-start(f32[2048,256]{1,0:T(8,128)} %collective-permute-done.4.refs_2_), channel_id=1, source_target_pairs={{0,8},{8,0},{16,24},{24,16},{1,9},{9,1},{17,25},{25,17},{2,10},{10... | collective-permute-start | bytes 6291464 | tf_op jit(solution)/shard_map/ppermute | solution.py:486
  157.3 17.4 %copy-start.2 = (f32[2056,256]{1,0:T(8,128)}, f32[2056,256]{1,0:T(8,128)S(1)}, u32[]{:S(2)}) copy-start(f32[2056,256]{1,0:T(8,128)S(1)} %collective-permute-done.11.refs_7_.refs_0_.refs_1_.refs_3_) | copy-start | bytes 6316036
  157.3 9.2 %collective-permute-start.18 = (f32[2048,256]{1,0:T(8,128)}, f32[2048,256]{1,0:T(8,128)S(1)}, u32[]{:S(2)}, u32[]{:S(2)}) collective-permute-start(f32[2048,256]{1,0:T(8,128)} %collective-permute-done.8.refs_2_), channel_id=1, source_target_pairs={{0,8},{8,0},{16,24},{24,16},{1,9},{9,1},{17,25},{25,17},{2,10},{10... | collective-permute-start | bytes 6291464 | tf_op jit(solution)/shard_map/ppermute | solution.py:486
  162.8 29.4 %collective-permute-start.17 = (f32[2048,256]{1,0:T(8,128)}, f32[2048,256]{1,0:T(8,128)}, u32[]{:S(2)}, u32[]{:S(2)}) collective-permute-start(f32[2048,256]{1,0:T(8,128)} %collective-permute-done.15.refs_2_), channel_id=1, source_target_pairs={{0,8},{8,0},{16,24},{24,16},{1,9},{9,1},{17,25},{25,17},{2,10},{10... | collective-permute-start | bytes 6291464 | tf_op jit(solution)/shard_map/ppermute | solution.py:486
  163.4 3.1 collective-permute-start.10
  163.6 52.2 %collective-permute-start.20 = (f32[1024,256]{1,0:T(8,128)}, f32[1024,256]{1,0:T(8,128)}, u32[]{:S(2)}, u32[]{:S(2)}) collective-permute-start(f32[1024,256]{1,0:T(8,128)} %bitcast.28), channel_id=1, source_target_pairs={{0,8},{1,9},{2,4},{3,5},{4,2},{5,3},{6,14},{7,15},{8,0},{9,1},{10,... | collective-permute-start | bytes 3145736 | tf_op jit(solution)/shard_map/ppermute | solution.py:483
  163.9 51.9 %collective-permute-start.19 = (f32[1024,256]{1,0:T(8,128)}, f32[1024,256]{1,0:T(8,128)}, u32[]{:S(2)}, u32[]{:S(2)}) collective-permute-start(f32[1024,256]{1,0:T(8,128)} %bitcast.29), channel_id=1, source_target_pairs={{0,2},{1,3},{2,0},{3,1},{4,6},{5,7},{6,4},{7,5},{8,10},{9,11},{10,... | collective-permute-start | bytes 3145736 | tf_op jit(solution)/shard_map/ppermute | solution.py:483
  166.5 8.1 %copy-start.33 = (f32[8,256]{1,0:T(8,128)}, f32[8,256]{1,0:T(8,128)S(1)}, u32[]{:S(2)}) copy-start(f32[8,256]{1,0:T(8,128)S(1)} %collective-permute-done.10.refs_3_.refs_1_) | copy-start | bytes 24580
  166.5 49.3 %collective-permute-start.22 = (f32[1024,256]{1,0:T(8,128)S(1)}, f32[1024,256]{1,0:T(8,128)}, u32[]{:S(2)}, u32[]{:S(2)}) collective-permute-start(f32[1024,256]{1,0:T(8,128)S(1)} %bitcast.25), channel_id=1, source_target_pairs={{0,8},{1,9},{2,4},{3,5},{4,2},{5,3},{6,14},{7,15},{8,0},{9,1},{10,... | collective-permute-start | bytes 3145736 | tf_op jit(solution)/shard_map/ppermute | solution.py:483
  166.6 49.3 %collective-permute-start.21 = (f32[1024,256]{1,0:T(8,128)S(1)}, f32[1024,256]{1,0:T(8,128)}, u32[]{:S(2)}, u32[]{:S(2)}) collective-permute-start(f32[1024,256]{1,0:T(8,128)S(1)} %bitcast.26), channel_id=1, source_target_pairs={{0,2},{1,3},{2,0},{3,1},{4,6},{5,7},{6,4},{7,5},{8,10},{9,11},{10,... | collective-permute-start | bytes 3145736 | tf_op jit(solution)/shard_map/ppermute | solution.py:483
  215.8 25.3 %collective-permute-start.23 = (f32[4,4,64,256]{3,2,1,0:T(8,128)}, f32[4,4,64,256]{3,2,1,0:T(8,128)S(1)}, u32[]{:S(2)}, u32[]{:S(2)}) collective-permute-start(f32[4,4,64,256]{3,2,1,0:T(8,128)} %get-tuple-element.113), channel_id=1, source_target_pairs={{0,1},{1,0},{2,3},{3,2},{4,5},{5,4},{6,7},{7,6},{8,9},{9,8},{10,11... | collective-permute-start | bytes 3145736 | tf_op jit(solution)/shard_map/ppermute | solution.py:483
  218.1 24.6 %collective-permute-start.25 = (f32[1024,256]{1,0:T(8,128)}, f32[1024,256]{1,0:T(8,128)S(1)}, u32[]{:S(2)}, u32[]{:S(2)}) collective-permute-start(f32[1024,256]{1,0:T(8,128)} %collective-permute-done.20.refs_2_), channel_id=1, source_target_pairs={{0,2},{1,3},{2,0},{3,1},{4,6},{5,7},{6,4},{7,5},{8,10},{9,11},{10,... | collective-permute-start | bytes 3145736 | tf_op jit(solution)/shard_map/ppermute | solution.py:483
  218.4 24.2 %collective-permute-start.26 = (f32[1024,256]{1,0:T(8,128)}, f32[1024,256]{1,0:T(8,128)S(1)}, u32[]{:S(2)}, u32[]{:S(2)}) collective-permute-start(f32[1024,256]{1,0:T(8,128)} %collective-permute-done.19.refs_1_), channel_id=1, source_target_pairs={{0,8},{1,9},{2,4},{3,5},{4,2},{5,3},{6,14},{7,15},{8,0},{9,1},{10,... | collective-permute-start | bytes 3145736 | tf_op jit(solution)/shard_map/ppermute | solution.py:483
  242.6 23.7 %collective-permute-start.29 = (f32[4,4,64,256]{3,2,1,0:T(8,128)}, f32[4,4,64,256]{3,2,1,0:T(8,128)S(1)}, u32[]{:S(2)}, u32[]{:S(2)}) collective-permute-start(f32[4,4,64,256]{3,2,1,0:T(8,128)} %get-tuple-element.119), channel_id=1, source_target_pairs={{0,1},{1,0},{2,3},{3,2},{4,5},{5,4},{6,7},{7,6},{8,9},{9,8},{10,11... | collective-permute-start | bytes 3145736 | tf_op jit(solution)/shard_map/ppermute | solution.py:483
  243.6 26.4 %collective-permute-start.31 = (f32[1024,256]{1,0:T(8,128)S(1)}, f32[1024,256]{1,0:T(8,128)S(1)}, u32[]{:S(2)}, u32[]{:S(2)}) collective-permute-start(f32[1024,256]{1,0:T(8,128)S(1)} %collective-permute-done.26.refs_4_), channel_id=1, source_target_pairs={{0,2},{1,3},{2,0},{3,1},{4,6},{5,7},{6,4},{7,5},{8,10},{9,11},{10,... | collective-permute-start | bytes 3145736 | tf_op jit(solution)/shard_map/ppermute | solution.py:483
  248.0 41.9 %collective-permute-start.27 = (f32[4,264,256]{2,1,0:T(8,128)}, f32[4,264,256]{2,1,0:T(8,128)S(1)}, u32[]{:S(2)}, u32[]{:S(2)}) collective-permute-start(f32[4,264,256]{2,1,0:T(8,128)} %inflate.5.refs_4_), channel_id=1, source_target_pairs={{0,16},{8,24},{16,0},{24,8},{1,17},{9,25},{17,1},{25,9},{2,18},{10... | collective-permute-start | bytes 3244040 | tf_op jit(solution)/shard_map/ppermute | solution.py:483
  248.6 41.2 %collective-permute-start.32 = (f32[1024,256]{1,0:T(8,128)}, f32[1024,256]{1,0:T(8,128)S(1)}, u32[]{:S(2)}, u32[]{:S(2)}) collective-permute-start(f32[1024,256]{1,0:T(8,128)} %collective-permute-done.22.refs_2_), channel_id=1, source_target_pairs={{0,2},{1,3},{2,0},{3,1},{4,6},{5,7},{6,4},{7,5},{8,10},{9,11},{10,... | collective-permute-start | bytes 3145736 | tf_op jit(solution)/shard_map/ppermute | solution.py:483
  248.9 41.0 %collective-permute-start.33 = (f32[1024,256]{1,0:T(8,128)}, f32[1024,256]{1,0:T(8,128)S(1)}, u32[]{:S(2)}, u32[]{:S(2)}) collective-permute-start(f32[1024,256]{1,0:T(8,128)} %collective-permute-done.21.refs_1_), channel_id=1, source_target_pairs={{0,8},{1,9},{2,4},{3,5},{4,2},{5,3},{6,14},{7,15},{8,0},{9,1},{10,... | collective-permute-start | bytes 3145736 | tf_op jit(solution)/shard_map/ppermute | solution.py:483
  270.9 18.9 %copy-start.7 = (f32[4,264,256]{2,1,0:T(8,128)S(1)}, f32[4,264,256]{2,1,0:T(8,128)}, u32[]{:S(2)}) copy-start(f32[4,264,256]{2,1,0:T(8,128)} %inflate.6.refs_8_) | copy-start | bytes 3244036
  289.9 52.8 %copy-start.12 = (f32[4,264,256]{2,1,0:T(8,128)}, f32[4,264,256]{2,1,0:T(8,128)S(1)}, u32[]{:S(2)}) copy-start(f32[4,264,256]{2,1,0:T(8,128)S(1)} %collective-permute-done.27.refs_6_) | copy-start | bytes 3244036
  289.9 27.1 %collective-permute-start.34 = (f32[4,264,256]{2,1,0:T(8,128)S(1)}, f32[4,264,256]{2,1,0:T(8,128)S(1)}, u32[]{:S(2)}, u32[]{:S(2)}) collective-permute-start(f32[4,264,256]{2,1,0:T(8,128)S(1)} %copy-done.7), channel_id=1, source_target_pairs={{0,16},{8,24},{16,0},{24,8},{1,17},{9,25},{17,1},{25,9},{2,18},{10... | collective-permute-start | bytes 3244040 | tf_op jit(solution)/shard_map/ppermute | solution.py:483
  290.5 22.8 %collective-permute-start.36 = (f32[4,4,64,256]{3,2,1,0:T(8,128)}, f32[4,4,64,256]{3,2,1,0:T(8,128)S(1)}, u32[]{:S(2)}, u32[]{:S(2)}) collective-permute-start(f32[4,4,64,256]{3,2,1,0:T(8,128)} %get-tuple-element.128), channel_id=1, source_target_pairs={{0,1},{1,0},{2,3},{3,2},{4,5},{5,4},{6,7},{7,6},{8,9},{9,8},{10,11... | collective-permute-start | bytes 3145736 | tf_op jit(solution)/shard_map/ppermute | solution.py:591
  291.8 26.7 %collective-permute-start.40 = (f32[1024,256]{1,0:T(8,128)S(1)}, f32[1024,256]{1,0:T(8,128)S(1)}, u32[]{:S(2)}, u32[]{:S(2)}) collective-permute-start(f32[1024,256]{1,0:T(8,128)S(1)} %collective-permute-done.33.refs_4_), channel_id=1, source_target_pairs={{0,2},{1,3},{2,0},{3,1},{4,6},{5,7},{6,4},{7,5},{8,10},{9,11},{10,... | collective-permute-start | bytes 3145736 | tf_op jit(solution)/shard_map/ppermute | solution.py:483
  317.0 44.3 %copy-start.13 = (f32[4,264,256]{2,1,0:T(8,128)}, f32[4,264,256]{2,1,0:T(8,128)S(1)}, u32[]{:S(2)}) copy-start(f32[4,264,256]{2,1,0:T(8,128)S(1)} %collective-permute-done.34.refs_10_) | copy-start | bytes 3244036
  317.0 28.2 %collective-permute-start.38 = (f32[4,264,256]{2,1,0:T(8,128)}, f32[4,264,256]{2,1,0:T(8,128)S(1)}, u32[]{:S(2)}, u32[]{:S(2)}) collective-permute-start(f32[4,264,256]{2,1,0:T(8,128)} %inflate.7.refs_12_), channel_id=1, source_target_pairs={{0,16},{8,24},{16,0},{24,8},{1,17},{9,25},{17,1},{25,9},{2,18},{10... | collective-permute-start | bytes 3244040 | tf_op jit(solution)/shard_map/ppermute | solution.py:593
  319.4 11.1 %copy-start.6 = (f32[4,264,256]{2,1,0:T(8,128)S(1)}, f32[4,264,256]{2,1,0:T(8,128)}, u32[]{:S(2)}) copy-start(f32[4,264,256]{2,1,0:T(8,128)} %inflate.5.refs_4_) | copy-start | bytes 3244036
  319.4 31.0 %copy-start.8 = (f32[4,264,256]{2,1,0:T(8,128)S(1)}, f32[4,264,256]{2,1,0:T(8,128)}, u32[]{:S(2)}) copy-start(f32[4,264,256]{2,1,0:T(8,128)} %inflate.7.refs_12_) | copy-start | bytes 3244036
  328.6 12.2 %collective-permute-start.41 = (f32[4,4,32,256]{3,2,1,0:T(8,128)}, f32[4,4,32,256]{3,2,1,0:T(8,128)S(1)}, u32[]{:S(2)}, u32[]{:S(2)}) collective-permute-start(f32[4,4,32,256]{3,2,1,0:T(8,128)} %get-tuple-element.135), channel_id=1, source_target_pairs={{0,1},{1,0},{2,3},{3,2},{4,5},{5,4},{6,7},{7,6},{8,9},{9,8},{10,11... | collective-permute-start | bytes 1572872 | tf_op jit(solution)/shard_map/ppermute | solution.py:591
  330.5 29.5 %collective-permute-start.24 = (f32[4,264,256]{2,1,0:T(8,128)S(1)}, f32[4,264,256]{2,1,0:T(8,128)S(1)}, u32[]{:S(2)}, u32[]{:S(2)}) collective-permute-start(f32[4,264,256]{2,1,0:T(8,128)S(1)} %copy-done.6), channel_id=1, source_target_pairs={{0,8},{8,0},{16,24},{24,16},{1,9},{9,1},{17,25},{25,17},{2,10},{10... | collective-permute-start | bytes 3244040 | tf_op jit(solution)/shard_map/ppermute | solution.py:579
  340.8 9.6 %collective-permute-start.45 = (f32[4,4,32,256]{3,2,1,0:T(8,128)}, f32[4,4,32,256]{3,2,1,0:T(8,128)}, u32[]{:S(2)}, u32[]{:S(2)}) collective-permute-start(f32[4,4,32,256]{3,2,1,0:T(8,128)} %get-tuple-element.139), channel_id=1, source_target_pairs={{0,1},{1,0},{2,3},{3,2},{4,5},{5,4},{6,7},{7,6},{8,9},{9,8},{10,11... | collective-permute-start | bytes 1572872 | tf_op jit(solution)/shard_map/ppermute | solution.py:591
  342.6 18.7 %collective-permute-start.30 = (f32[4,264,256]{2,1,0:T(8,128)S(1)}, f32[4,264,256]{2,1,0:T(8,128)}, u32[]{:S(2)}, u32[]{:S(2)}) collective-permute-start(f32[4,264,256]{2,1,0:T(8,128)S(1)} %copy-done.7), channel_id=1, source_target_pairs={{0,8},{8,0},{16,24},{24,16},{1,9},{9,1},{17,25},{25,17},{2,10},{10... | collective-permute-start | bytes 3244040 | tf_op jit(solution)/shard_map/ppermute | solution.py:579
  342.6 18.9 %collective-permute-start.28 = (f32[4,264,256]{2,1,0:T(8,128)S(1)}, f32[4,264,256]{2,1,0:T(8,128)}, u32[]{:S(2)}, u32[]{:S(2)}) collective-permute-start(f32[4,264,256]{2,1,0:T(8,128)S(1)} %collective-permute-done.27.refs_6_), channel_id=1, source_target_pairs={{0,8},{8,0},{16,24},{24,16},{1,9},{9,1},{17,25},{25,17},{2,10},{10... | collective-permute-start | bytes 3244040 | tf_op jit(solution)/shard_map/ppermute | solution.py:579
  345.2 32.1 %copy-start.14 = (f32[4,264,256]{2,1,0:T(8,128)}, f32[4,264,256]{2,1,0:T(8,128)S(1)}, u32[]{:S(2)}) copy-start(f32[4,264,256]{2,1,0:T(8,128)S(1)} %collective-permute-done.38.refs_14_) | copy-start | bytes 3244036
  345.2 14.7 %collective-permute-start.43 = (f32[4,136,256]{2,1,0:T(8,128)}, f32[4,136,256]{2,1,0:T(8,128)S(1)}, u32[]{:S(2)}, u32[]{:S(2)}) collective-permute-start(f32[4,136,256]{2,1,0:T(8,128)} %inflate.8.refs_16_), channel_id=1, source_target_pairs={{0,16},{8,24},{16,0},{24,8},{1,17},{9,25},{17,1},{25,9},{2,18},{10... | collective-permute-start | bytes 1671176 | tf_op jit(solution)/shard_map/ppermute | solution.py:593
  350.4 11.4 %collective-permute-start.37 = (f32[4,264,256]{2,1,0:T(8,128)S(1)}, f32[4,264,256]{2,1,0:T(8,128)}, u32[]{:S(2)}, u32[]{:S(2)}) collective-permute-start(f32[4,264,256]{2,1,0:T(8,128)S(1)} %copy-done.8), channel_id=1, source_target_pairs={{0,8},{8,0},{16,24},{24,16},{1,9},{9,1},{17,25},{25,17},{2,10},{10... | collective-permute-start | bytes 3244040 | tf_op jit(solution)/shard_map/ppermute | solution.py:594
  360.0 17.4 %copy-start.27 = (f32[4,136,256]{2,1,0:T(8,128)}, f32[4,136,256]{2,1,0:T(8,128)S(1)}, u32[]{:S(2)}) copy-start(f32[4,136,256]{2,1,0:T(8,128)S(1)} %collective-permute-done.43.refs_18_) | copy-start | bytes 1671172
  360.0 2.2 collective-permute-start.42
  360.0 17.4 %copy-start.15 = (f32[4,264,256]{2,1,0:T(8,128)}, f32[4,264,256]{2,1,0:T(8,128)S(1)}, u32[]{:S(2)}) copy-start(f32[4,264,256]{2,1,0:T(8,128)S(1)} %collective-permute-done.24.refs_5_) | copy-start | bytes 3244036
  360.0 15.3 %collective-permute-start.47 = (f32[4,136,256]{2,1,0:T(8,128)}, f32[4,136,256]{2,1,0:T(8,128)S(1)}, u32[]{:S(2)}, u32[]{:S(2)}) collective-permute-start(f32[4,136,256]{2,1,0:T(8,128)} %inflate.9.refs_20_), channel_id=1, source_target_pairs={{0,16},{8,24},{16,0},{24,8},{1,17},{9,25},{17,1},{25,9},{2,18},{10... | collective-permute-start | bytes 1671176 | tf_op jit(solution)/shard_map/ppermute | solution.py:593
  361.3 13.9 %collective-permute-start.35 = (f32[4,264,256]{2,1,0:T(8,128)S(1)}, f32[4,264,256]{2,1,0:T(8,128)S(1)}, u32[]{:S(2)}, u32[]{:S(2)}) collective-permute-start(f32[4,264,256]{2,1,0:T(8,128)S(1)} %collective-permute-done.34.refs_10_), channel_id=1, source_target_pairs={{0,8},{8,0},{16,24},{24,16},{1,9},{9,1},{17,25},{25,17},{2,10},{10... | collective-permute-start | bytes 3244040 | tf_op jit(solution)/shard_map/ppermute | solution.py:579
  361.5 13.8 %collective-permute-start.39 = (f32[4,264,256]{2,1,0:T(8,128)S(1)}, f32[4,264,256]{2,1,0:T(8,128)S(1)}, u32[]{:S(2)}, u32[]{:S(2)}) collective-permute-start(f32[4,264,256]{2,1,0:T(8,128)S(1)} %collective-permute-done.38.refs_14_), channel_id=1, source_target_pairs={{0,8},{8,0},{16,24},{24,16},{1,9},{9,1},{17,25},{25,17},{2,10},{10... | collective-permute-start | bytes 3244040 | tf_op jit(solution)/shard_map/ppermute | solution.py:594
  361.9 13.4 %collective-permute-start.46 = (f32[4,136,256]{2,1,0:T(8,128)}, f32[4,136,256]{2,1,0:T(8,128)S(1)}, u32[]{:S(2)}, u32[]{:S(2)}) collective-permute-start(f32[4,136,256]{2,1,0:T(8,128)} %inflate.9.refs_20_), channel_id=1, source_target_pairs={{0,8},{8,0},{16,24},{24,16},{1,9},{9,1},{17,25},{25,17},{2,10},{10... | collective-permute-start | bytes 1671176 | tf_op jit(solution)/shard_map/ppermute | solution.py:594
  362.1 13.2 %copy-start.28 = (f32[4,136,256]{2,1,0:T(8,128)}, f32[4,136,256]{2,1,0:T(8,128)S(1)}, u32[]{:S(2)}) copy-start(f32[4,136,256]{2,1,0:T(8,128)S(1)} %collective-permute-done.42.refs_17_) | copy-start | bytes 1671172
  362.1 13.2 %collective-permute-start.44 = (f32[4,136,256]{2,1,0:T(8,128)S(1)}, f32[4,136,256]{2,1,0:T(8,128)S(1)}, u32[]{:S(2)}, u32[]{:S(2)}) collective-permute-start(f32[4,136,256]{2,1,0:T(8,128)S(1)} %collective-permute-done.43.refs_18_), channel_id=1, source_target_pairs={{0,8},{8,0},{16,24},{24,16},{1,9},{9,1},{17,25},{25,17},{2,10},{10... | collective-permute-start | bytes 1671176 | tf_op jit(solution)/shard_map/ppermute | solution.py:594
  375.2 2.1 collective-permute-start.48
  (20 other events, 51.7 us)

commit v6 on v5

--- a/solution.py
+++ b/solution.py
@@ -10,10 +10,11 @@
 TR = 8
 CHUNKS = (128, 64, 64)
 ROWS = (64, 64, 64)
-PIECES = 2
+CUTS = (1, 1, 1)
 FIELDS = 8
 ALL, EARLY, FINAL = 0, 1, 2
 RING = 16
+COLUMNS = 2
 VMEM = 56 * 1024 * 1024
 
 
@@ -173,7 +174,7 @@
     rows = pieces * piece
     group, j = pl.program_id(0), pl.program_id(1)
     size = blocks * count * rows
-    row = group * blocks + j
+    columns = out_refs[0].shape[0]
     q = me_ref[1] // 2
     begun = which * listed(blocks, count)
     ends = which * 2 * blocks
@@ -184,7 +185,7 @@
         slot = n % RING
         return pltpu.make_async_copy(b_ref.at[tile], ring.at[slot], b_sems.at[slot])
 
-    @pl.when(row == 0)
+    @pl.when((group == 0) & (j == 0))
     def _():
         def each(act):
             for n, i in enumerate(arrivals):
@@ -218,9 +219,6 @@
             lax.fori_loop(source * blocks, (source + 1) * blocks, convert, 0)
 
         each(use)
-
-    total[...] = jnp.zeros_like(total)
-    first = jnp.where(row == 0, begun, kept_ref[FIELDS * (ends + jnp.maximum(row - 1, 0))])
 
     def multiply(n):
         a = halves[plan_ref[FIELDS * n + 1]]
@@ -230,7 +228,7 @@
         by_high = dot(a, b_high)
         return by_high[: count * rows] + by_high[count * rows :] + dot(a[: count * rows], b_low)
 
-    def step(i, _):
+    def step(first, i):
         n = first + 2 * i
         fetch(n).wait()
         fetch(n + 1).wait()
@@ -246,22 +244,30 @@
             fetch(n + RING).start()
             fetch(n + RING + 1).start()
 
-        return 0
-
-    lax.fori_loop(0, (kept_ref[FIELDS * (ends + row)] - first) // 2, step, 0)
-
-    for g in range(2):
-
-        @pl.when(group == g)
-        def _():
-            for m in range(count):
-                level = kept_ref[FIELDS * row + 1 + m]
-                for n in range(pieces):
-                    some = pl.ds(n * piece, piece)
-                    result = total[level, some]
-                    if before:
-                        result += before[g][0, m, some]
-                    out_refs[g * pieces + n][0, m] = result
+        return first
+
+    for u in range(columns):
+        row = group * blocks + j * columns + u
+        first = jnp.where(row == 0, begun, kept_ref[FIELDS * (ends + jnp.maximum(row - 1, 0))])
+        total[...] = jnp.zeros_like(total)
+        lax.fori_loop(
+            0,
+            (kept_ref[FIELDS * (ends + row)] - first) // 2,
+            lambda i, first: step(first, i),
+            first,
+        )
+        for g in range(2):
+
+            @pl.when(group == g)
+            def _():
+                for m in range(count):
+                    level = kept_ref[FIELDS * row + 1 + m]
+                    for n in range(pieces):
+                        some = pl.ds(n * piece, piece)
+                        result = total[level, some]
+                        if before:
+                            result += before[g][u, m, some]
+                        out_refs[g * pieces + n][u, m] = result
 
 
 def product(me, plan, panel, parts, line, part, rows, which=ALL, before=(), pieces=1):
@@ -271,15 +277,18 @@
     out = jax.ShapeDtypeStruct((blocks, count, rows // pieces, width), jnp.float32)
     smem = pl.BlockSpec(memory_space=pltpu.SMEM)
 
+    columns = min(COLUMNS, blocks)
+    steps = blocks // columns
+
     def tiles_of(group, size):
         return pl.BlockSpec(
-            (1, count, size, width),
-            lambda g, j: (jnp.where(g == group, j, 0 if group else blocks - 1), 0, 0, 0),
+            (columns, count, size, width),
+            lambda g, j: (jnp.where(g == group, j, 0 if group else steps - 1), 0, 0, 0),
         )
 
     return pl.pallas_call(
         functools.partial(product_kernel, line, which, arrivals, pieces, part),
-        grid=(2, blocks),
+        grid=(2, steps),
         out_shape=(out,) * (2 * pieces),
         in_specs=[smem] * 3
         + [pl.BlockSpec(memory_space=pl.ANY)] * (1 + len(arrivals))
@@ -497,7 +506,7 @@
 
     panel = None
     sources, waiting, landed, flying = [], [], [], []
-    begun, made, cuts = {}, [], [1] * (chunks - 1) + [PIECES]
+    begun, made, cuts = {}, [], CUTS
 
     def put(tick, group, relative, *parts):
         nonlocal panel
@@ -507,8 +516,9 @@
     items = blocks * count
     upper, parts = sizes[0] * items, sizes[0] // rows[0]
 
-    def halves(top, low):
-        return (*((top, rows[0], part * items) for part in range(parts)), (low, half, 0))
+    def halves(top, low, number=0):
+        upper_rows = ((top, rows[0], part * items) for part in range(parts))
+        return (*upper_rows, (low, half, number * items))
 
     tick = 0
     while tick <= max(hops) + 1 or landed or flying:
@@ -539,19 +549,18 @@
             put(0, 1, 0, *halves(own[0], rest))
         if tick == 1:
             pair_rest, across_rest = send(1, pair, rest), send(1, across, rest)
-            core_pair = swap(1, b_pair)
+            core_pair = at(1, swap(1, b_pair))
             put(1, 1, 1, (core_own, width, 0))
             later = after(1, tiles)
             own += [at(1, cut(later, h)) for h in range(1, chunks)]
         if tick == 2:
             diagonal, diagonal_rest = send(2, across, b_pair), send(2, pair, across_rest)
-            core_across, core_pair_rest = swap(2, b_across), swap(2, pair_rest)
-            core_across_rest = swap(2, across_rest, core_across)
-            core_notes = swap(2, own[0][upper:], core_pair_rest)
+            core_across = swap(2, b_across)
+            core_rest = swap(2, jnp.concatenate([pair_rest, across_rest, own[0][upper:]]))
             put(2, 0, 0, *halves(b_pair, pair_rest))
             put(2, 1, 2, *halves(b_across, across_rest))
-            put(3, 0, 1, *halves(core_pair, core_pair_rest))
-            put(3, 1, 3, *halves(core_across, core_across_rest))
+            put(2, 0, 1, *halves(core_pair, core_rest))
+            put(2, 1, 3, *halves(core_across, core_rest, 1))
         if tick == max(base, 3):
             core_diagonal = swap(tick, diagonal)
             put(tick, 0, 2, *halves(diagonal, diagonal_rest))
@@ -561,7 +570,7 @@
                 (b_pair, upper),
                 (own[0], upper),
                 (core_pair, upper),
-                (core_notes, 0),
+                (core_rest, 2 * half * items),
                 (diagonal, upper),
                 (b_across, upper),
                 (core_diagonal, upper),
@@ -587,11 +596,14 @@
             landed.append((tick, at(tick, theirs), mine))
         tick += 1
     for theirs, mine in made:
-        for x, y in zip(theirs, mine):
-            other = pair(tie(x, other))
-            inflated = inflate(y, other)
-            opposite = across(tie(inflated, opposite))
-            sources += [inflated, core(inflated), opposite, core(opposite)]
+        others = [pair(tie(x, other)) for x in theirs]
+        other = others[-1]
+        inflated = []
+        for x, y in zip(mine, others):
+            inflated.append(inflate(x, tie(y, *inflated[-1:])))
+        for x in inflated:
+            opposite = across(tie(x, opposite))
+            sources += [x, core(x), opposite, core(opposite)]
     sizes = tuple(
         rows[h] // cuts[h]
         for h in range(chunks)

time: 387 us -> 380 us (0.982)
  starting transfers between devices: 39.4 us -> 33 us
  other arithmetic: 0.77 us -> 5.59 us
  waiting for transfers between devices: 176 us -> 172 us
    ppermute x25, waiting for transfers between devices: 129 us -> 122 us  [send(): return at(tick, move(after(tick, x), *more))]
    ppermute x6 -> x8, waiting for transfers between devices: 39.1 us -> 45.1 us  [the longest x2 25.5 us: on_device(): others = [pair(tie(x, other)) for x in theirs]]
    ppermute x6 -> x8, starting transfers between devices: 9.03 us -> 3.35 us  [the longest x2 2.17 us: on_device(): opposite = across(tie(x, opposite))]
    concatenate x0 -> x1, other arithmetic: none -> 4.8 us  [on_device(): jnp.concatenate([pair_rest, across_rest, own[0][upper:]])]
    pallas_call x5 -> x4, Pallas kernels: 12.2 us -> 10.6 us  [inflate(): pl.pallas_call(inflate_kernel, out_shape=jax.ShapeDtypeStruct((blocks, co...]
  transfers between devices with their start and end apart: 49 -> 43, of which waited for: 19 -> 17; matrix products, arithmetic and copies ran while one was open for 2% -> 4% of each run, Pallas kernels for 38% -> 39%
where the time goes in v6:
time: 380 us; the launch traced here: 378 us
  waiting for transfers between devices  172 us (45%)
  Pallas kernels  152 us (40%)
  starting transfers between devices  33 us (9%)
  local copies, waits for them, and re-layouts  15.3 us (4%)
  other arithmetic  5.59 us (1%)
    ppermute x25, waiting for transfers between devices, send(): return at(tick, move(after(tick, x), *more))  122 us
    pallas_call x6, Pallas kernels, product(): pl.pallas_call(functools.partial(product_kernel, line, which, arrivals, p...  88.2 us
    pallas_call x8, Pallas kernels, place(): pl.pallas_call(functools.partial(place_kernel, len(parts)), grid=(blocks,...  39 us
    ppermute x25, starting transfers between devices, send(): return at(tick, move(after(tick, x), *more))  26.8 us
    ppermute x2, waiting for transfers between devices, on_device(): others = [pair(tie(x, other)) for x in theirs]  25.5 us
    ppermute x2, waiting for transfers between devices, on_device(): opposite = across(tie(x, opposite))  18.1 us
    pallas_call x4, Pallas kernels, inflate(): pl.pallas_call(inflate_kernel, out_shape=jax.ShapeDtypeStruct((blocks, co...  10.6 us
    pallas_call x1, Pallas kernels, make_plan(): pl.pallas_call(functools.partial(plan_kernel, line, blocks, count), grid=...  7.92 us
  transfers between devices with their start and end apart: 43, of which 17 were waited for; matrix products, arithmetic and copies ran while one was open for 4% of the time, Pallas kernels for 39%

profile of v6, /device:TPU:0, one launch (start us, length us, event | category | flops | bytes accessed | tf_op | source)
XLA Modules:
  0.0 378.3 jit_solution(15705681171098554959)
XLA Ops:
  0.5 0.8 reshape.28
  1.2 0.8 reshape.29
  2.0 1.7 slice.16
  4.6 2.6 collective-permute-start.3
  7.2 1.5 collective-permute-start.2
  8.7 3.1 collective-permute-start
  11.8 1.5 slice.13
  13.3 4.8 %place.8 = (bf16[2,4,4,4,2,256,256]{6,5,4,3,2,1,0:T(8,128)(2,1)}, f32[8,128]{1,0:T(8,128)}) custom-call(f32[2056,256]{1,0:T(8,128)} %copy-done, f32[2056,256]{1,0:T(8,128)} %copy-done, f32[2048,256]{1,0:T(8,128)} %bitcast.24), custom_call_target="tpu_custom_call" | custom-call | flops 1048576 | bytes 8388608 | tf_op jit(solution)/shard_map/place/pallas_call | solution.py:61
  18.1 35.6 %collective-permute-done.3.refs_0_.refs_1_.refs_5_.refs_2_ = f32[2056,256]{1,0:T(8,128)S(1)} collective-permute-done((f32[2056,256]{1,0:T(8,128)S(1)}, f32[2056,256]{1,0:T(8,128)S(1)}, u32[]{:S(2)}, u32[]{:S(2)}) %collective-permute-start.3) | collective-permute-done | bytes 2105376 | tf_op jit(solution)/shard_map/ppermute | solution.py:492
  53.7 1.6 collective-permute-done.2.refs_0_.refs_1_
  55.2 2.3 collective-permute-done.refs_9_.refs_1_
  58.6 1.7 collective-permute-start.7
  60.9 2.7 fusion
  63.6 5.3 %place.9 = (bf16[2,4,4,4,2,256,256]{6,5,4,3,2,1,0:T(8,128)(2,1)}, f32[8,128]{1,0:T(8,128)}) custom-call(f32[4096,256]{1,0:T(8,128)} %collective-permute-done.6.refs_0_, bf16[2,4,4,4,2,256,256]{6,5,4,3,2,1,0:T(8,128)(2,1)} %get-tuple-element.71.refs_1_), custom_call_target="tpu_custom_call", output_to_operand_aliasing={{0}: (1, {})} | custom-call | flops 1048576 | bytes 8388608 | tf_op jit(solution)/shard_map/place/pallas_call | solution.py:61
  68.9 35.5 %collective-permute-done.5.refs_2_ = f32[2048,256]{1,0:T(8,128)S(1)} collective-permute-done((f32[2048,256]{1,0:T(8,128)}, f32[2048,256]{1,0:T(8,128)S(1)}, u32[]{:S(2)}, u32[]{:S(2)}) %collective-permute-start.5) | collective-permute-done | bytes 2097184 | tf_op jit(solution)/shard_map/ppermute | solution.py:492
  104.8 4.8 %pad_maximum_fusion = f32[4104,256]{1,0:T(8,128)} fusion(f32[8,256]{1,0:T(8,128)S(1)} %broadcast_in_dim.6, f32[2048,256]{1,0:T(8,128)S(1)} %collective-permute-done.5.refs_2_, f32[2048,256]{1,0:T(8,128)} %collective-permute-done.4.refs_2_), kind=kLoop, calls=%fused_computation | loop fusion | flops 2101248 | bytes 8404992 | tf_op jit(solution)/shard_map/concatenate | solution.py:559
  110.2 0.6 collective-permute-start.12
  110.8 1.4 collective-permute-start.13
  112.8 4.8 %place.10 = (bf16[2,4,4,4,2,256,256]{6,5,4,3,2,1,0:T(8,128)(2,1)}, f32[8,128]{1,0:T(8,128)}) custom-call(f32[2056,256]{1,0:T(8,128)} %collective-permute-done.2.refs_0_.refs_1_, f32[2056,256]{1,0:T(8,128)} %collective-permute-done.2.refs_0_.refs_1_, f32[2048,256]{1,0:T(8,128)} %collective-permute-done.4.refs_2_, ...), custom_call_target="tpu_custom_call", output_to_operand_aliasing={{0}: (3, {})} | custom-call | flops 1048576 | bytes 8388608 | tf_op jit(solution)/shard_map/place/pallas_call | solution.py:61
  117.5 4.8 %place.11 = (bf16[2,4,4,4,2,256,256]{6,5,4,3,2,1,0:T(8,128)(2,1)}, f32[8,128]{1,0:T(8,128)}) custom-call(f32[2056,256]{1,0:T(8,128)} %copy-done.2, f32[2056,256]{1,0:T(8,128)} %copy-done.2, f32[2048,256]{1,0:T(8,128)} %copy-done.7, bf16[2,4,4,4,2,256,256]{6,5,4,3,2,1,0:T(8,128)(2,1)} %get-tuple-element.81.refs_3_), custom_call_target="tpu_custom_call", output_to_operand_aliasing={{0}: (3, {})} | custom-call | flops 1048576 | bytes 8388608 | tf_op jit(solution)/shard_map/place/pallas_call | solution.py:61
  122.4 2.0 copy-done.1
  124.4 4.8 %place.12 = (bf16[2,4,4,4,2,256,256]{6,5,4,3,2,1,0:T(8,128)(2,1)}, f32[8,128]{1,0:T(8,128)}) custom-call(f32[2056,256]{1,0:T(8,128)} %collective-permute-done.9.refs_0_.refs_1_.refs_2_, f32[2056,256]{1,0:T(8,128)} %collective-permute-done.9.refs_0_.refs_1_.refs_2_, f32[4104,256]{1,0:T(8,128)} %copy-done.1, ...), custom_call_target="tpu_custom_call", output_to_operand_aliasing={{0}: (3, {})} | custom-call | flops 1048576 | bytes 8388608 | tf_op jit(solution)/shard_map/place/pallas_call | solution.py:61
  129.2 4.8 %place.13 = (bf16[2,4,4,4,2,256,256]{6,5,4,3,2,1,0:T(8,128)(2,1)}, f32[8,128]{1,0:T(8,128)}) custom-call(f32[2056,256]{1,0:T(8,128)} %collective-permute-done.11.refs_0_.refs_1_.refs_7_.refs_3_, f32[2056,256]{1,0:T(8,128)} %collective-permute-done.11.refs_0_.refs_1_.refs_7_.refs_3_, f32[4104,256]{1,0:T(8,128)} %copy-done.1, ...), custom_call_target="tpu_custom_call", output_to_operand_aliasing={{0}: (3, {})} | custom-call | flops 1048576 | bytes 8388608 | tf_op jit(solution)/shard_map/place/pallas_call | solution.py:61
  134.0 25.6 %collective-permute-done.14.refs_2_ = f32[2048,256]{1,0:T(8,128)} collective-permute-done((f32[2048,256]{1,0:T(8,128)}, f32[2048,256]{1,0:T(8,128)}, u32[]{:S(2)}, u32[]{:S(2)}) %collective-permute-start.14) | collective-permute-done | bytes 2097184 | tf_op jit(solution)/shard_map/ppermute | solution.py:492
  159.6 4.4 %collective-permute-done.15.refs_6_.refs_0_.refs_1_ = f32[2056,256]{1,0:T(8,128)S(1)} collective-permute-done((f32[2056,256]{1,0:T(8,128)}, f32[2056,256]{1,0:T(8,128)S(1)}, u32[]{:S(2)}, u32[]{:S(2)}) %collective-permute-start.15) | collective-permute-done | bytes 2105376 | tf_op jit(solution)/shard_map/ppermute | solution.py:495
  164.5 3.0 collective-permute-start.17
  167.6 0.8 collective-permute-start.19
  168.3 0.6 pad_add_fusion.me_ref
  168.9 4.8 %place.14 = (bf16[2,4,4,4,2,256,256]{6,5,4,3,2,1,0:T(8,128)(2,1)}, f32[8,128]{1,0:T(8,128)}) custom-call(f32[2056,256]{1,0:T(8,128)} %collective-permute-done.12.refs_4_.refs_0_.refs_1_, f32[2056,256]{1,0:T(8,128)} %collective-permute-done.12.refs_4_.refs_0_.refs_1_, f32[2048,256]{1,0:T(8,128)} %collective-permute-done.14.refs_2_, ...), custom_call_target="tpu_custom_call", output_to_operand_aliasing={{0}: (3, {})} | custom-call | flops 1048576 | bytes 8388608 | tf_op jit(solution)/shard_map/place/pallas_call | solution.py:61
  173.7 7.9 %plan.1 = (s32[3312]{0:T(1024)}, s32[192]{0:T(256)}) custom-call(s32[2]{0:T(128)} %pad_add_fusion.me_ref, f32[2056,256]{1,0:T(8,128)} %collective-permute-done.2.refs_0_.refs_1_, f32[2056,256]{1,0:T(8,128)} %copy-done, f32[2056,256]{1,0:T(8,128)} %collective-permute-done.9.refs_0_.refs_1_.refs_2_, f32[4104,256]{1,0:T(8,128)} %copy-done.1, ...), custom_call_target="tpu_custom_call" | custom-call | tf_op jit(solution)/shard_map/plan/pallas_call | solution.py:154
  181.7 4.9 %place.15 = (bf16[2,4,4,4,2,256,256]{6,5,4,3,2,1,0:T(8,128)(2,1)}, f32[8,128]{1,0:T(8,128)}) custom-call(f32[2056,256]{1,0:T(8,128)} %copy-done.5, f32[2056,256]{1,0:T(8,128)} %copy-done.5, f32[2048,256]{1,0:T(8,128)} %collective-permute-done.16.refs_2_, bf16[2,4,4,4,2,256,256]{6,5,4,3,2,1,0:T(8,128)(2,1)} %get-tuple-element.93.refs_3_), custom_call_target="tpu_custom_call", output_to_operand_aliasing={{0}: (3, {})} | custom-call | flops 1048576 | bytes 8388608 | tf_op jit(solution)/shard_map/place/pallas_call | solution.py:61
  186.6 19.4 %product.6 = (f32[4,4,64,256]{3,2,1,0:T(8,128)}, f32[4,4,64,256]{3,2,1,0:T(8,128)}) custom-call(s32[2]{0:T(128)} %pad_add_fusion.me_ref, s32[3312]{0:T(1024)} %get-tuple-element.88.plan_ref, s32[192]{0:T(256)} %get-tuple-element.89.kept_ref, bf16[128,2,256,256]{3,2,1,0:T(8,128)(2,1)} %bitcast.14, f32[2056,256]{1,0:T(8,128)} %copy-done, ...), custom_call_target="tpu_custom_call" | custom-call | flops 6442450944 | bytes 16777216 | tf_op jit(solution)/shard_map/product/pallas_call | solution.py:289
  206.0 7.7 %collective-permute-done.19.refs_1_ = f32[1024,256]{1,0:T(8,128)} collective-permute-done((f32[1024,256]{1,0:T(8,128)S(1)}, f32[1024,256]{1,0:T(8,128)}, u32[]{:S(2)}, u32[]{:S(2)}) %collective-permute-start.19) | collective-permute-done | bytes 1048608 | tf_op jit(solution)/shard_map/ppermute | solution.py:492
  214.3 1.7 collective-permute-start.23
  216.0 19.4 %product.7 = (f32[4,4,64,256]{3,2,1,0:T(8,128)}, f32[4,4,64,256]{3,2,1,0:T(8,128)}) custom-call(s32[2]{0:T(128)} %pad_add_fusion.me_ref, s32[3312]{0:T(1024)} %get-tuple-element.88.plan_ref, s32[192]{0:T(256)} %get-tuple-element.89.kept_ref, bf16[128,2,256,256]{3,2,1,0:T(8,128)(2,1)} %bitcast.15, f32[2056,256]{1,0:T(8,128)} %copy-done, ...), custom_call_target="tpu_custom_call" | custom-call | flops 6442450944 | bytes 16777216 | tf_op jit(solution)/shard_map/product/pallas_call | solution.py:289
  235.4 3.2 collective-permute-done.21.other_ref
  238.8 1.6 collective-permute-start.27
  240.4 1.7 collective-permute-start.29
  242.1 2.6 inflate.4.refs_4_
  244.7 1.4 collective-permute-start.25
  246.5 15.1 %product.8 = (f32[4,4,64,256]{3,2,1,0:T(8,128)}, f32[4,4,64,256]{3,2,1,0:T(8,128)}) custom-call(s32[2]{0:T(128)} %pad_add_fusion.me_ref, s32[3312]{0:T(1024)} %get-tuple-element.88.plan_ref, s32[192]{0:T(256)} %get-tuple-element.89.kept_ref, bf16[128,2,256,256]{3,2,1,0:T(8,128)(2,1)} %bitcast.16, f32[1024,256]{1,0:T(8,128)} %bitcast.9.refs_0_, ...), custom_call_target="tpu_custom_call" | custom-call | flops 5368709120 | bytes 13981013 | tf_op jit(solution)/shard_map/product/pallas_call | solution.py:289
  261.5 1.1 collective-permute-done.27.other_ref
  262.6 1.0 copy-done.27
  263.6 2.7 inflate.5.refs_8_
  266.5 1.0 copy-done.25
  267.5 9.6 %product.9 = (f32[4,4,64,256]{3,2,1,0:T(8,128)}, f32[4,4,64,256]{3,2,1,0:T(8,128)}) custom-call(s32[2]{0:T(128)} %pad_add_fusion.me_ref, s32[3312]{0:T(1024)} %get-tuple-element.88.plan_ref, s32[192]{0:T(256)} %get-tuple-element.89.kept_ref, bf16[128,2,256,256]{3,2,1,0:T(8,128)(2,1)} %bitcast.17, f32[1024,256]{1,0:T(8,128)} %copy-done.25, ...), custom_call_target="tpu_custom_call" | custom-call | flops 1073741824 | bytes 2796202 | tf_op jit(solution)/shard_map/product/pallas_call | solution.py:289
  277.1 8.9 %collective-permute-done.30.refs_3_ = f32[1024,256]{1,0:T(8,128)S(1)} collective-permute-done((f32[1024,256]{1,0:T(8,128)}, f32[1024,256]{1,0:T(8,128)S(1)}, u32[]{:S(2)}, u32[]{:S(2)}) %collective-permute-start.30) | collective-permute-done | bytes 1048608 | tf_op jit(solution)/shard_map/ppermute | solution.py:492
  286.0 1.4 collective-permute-start.32
  287.5 0.6 collective-permute-start.34
  288.1 1.3 collective-permute-start.38
  289.4 15.1 %product.10 = (f32[4,4,64,256]{3,2,1,0:T(8,128)}, f32[4,4,64,256]{3,2,1,0:T(8,128)}) custom-call(s32[2]{0:T(128)} %pad_add_fusion.me_ref, s32[3312]{0:T(1024)} %get-tuple-element.88.plan_ref, s32[192]{0:T(256)} %get-tuple-element.89.kept_ref, bf16[128,2,256,256]{3,2,1,0:T(8,128)(2,1)} %bitcast.18, f32[1024,256]{1,0:T(8,128)} %bitcast.31, ...), custom_call_target="tpu_custom_call" | custom-call | flops 5368709120 | bytes 13981013 | tf_op jit(solution)/shard_map/product/pallas_call | solution.py:289
  304.5 5.1 %collective-permute-done.34.other_ref = f32[4,4,64,256]{3,2,1,0:T(8,128)S(1)} collective-permute-done((f32[4,4,64,256]{3,2,1,0:T(8,128)}, f32[4,4,64,256]{3,2,1,0:T(8,128)S(1)}, u32[]{:S(2)}, u32[]{:S(2)}) %collective-permute-start.34) | collective-permute-done | bytes 1048608 | tf_op jit(solution)/shard_map/ppermute | solution.py:599
  309.6 1.0 copy-done.29
  310.6 2.6 inflate.6.refs_12_
  313.2 0.6 collective-permute-start.36
  313.9 1.0 copy-done.28
  314.9 9.6 %product.11 = (f32[4,4,64,256]{3,2,1,0:T(8,128)}, f32[4,4,64,256]{3,2,1,0:T(8,128)}) custom-call(s32[2]{0:T(128)} %pad_add_fusion.me_ref, s32[3312]{0:T(1024)} %get-tuple-element.88.plan_ref, s32[192]{0:T(256)} %get-tuple-element.89.kept_ref, bf16[128,2,256,256]{3,2,1,0:T(8,128)(2,1)} %bitcast.19, f32[1024,256]{1,0:T(8,128)} %copy-done.28, ...), custom_call_target="tpu_custom_call" | custom-call | flops 1073741824 | bytes 2796202 | tf_op jit(solution)/shard_map/product/pallas_call | solution.py:289
  325.2 20.4 %collective-permute-done.39.other_ref = f32[4,4,64,256]{3,2,1,0:T(8,128)} collective-permute-done((f32[4,4,64,256]{3,2,1,0:T(8,128)}, f32[4,4,64,256]{3,2,1,0:T(8,128)}, u32[]{:S(2)}, u32[]{:S(2)}) %collective-permute-start.39) | collective-permute-done | bytes 1048608 | tf_op jit(solution)/shard_map/ppermute | solution.py:599
  345.6 2.6 inflate.7.refs_16_
  348.2 1.5 collective-permute-start.41
  350.9 18.1 %collective-permute-done.41.refs_18_ = f32[4,264,256]{2,1,0:T(8,128)S(1)} collective-permute-done((f32[4,264,256]{2,1,0:T(8,128)}, f32[4,264,256]{2,1,0:T(8,128)S(1)}, u32[]{:S(2)}, u32[]{:S(2)}) %collective-permute-start.41) | collective-permute-done | bytes 1081376 | tf_op jit(solution)/shard_map/ppermute | solution.py:605
  369.0 0.9 copy-done.16
  370.3 1.5 collective-permute-done.42.refs_19_
  371.8 6.4 %owned.1 = f32[32,256,256]{2,1,0:T(8,128)} custom-call(s32[2]{0:T(128)} %pad_add_fusion.me_ref, f32[2056,256]{1,0:T(8,128)} %copy-done, f32[4104,256]{1,0:T(8,128)} %copy-done.1, f32[2056,256]{1,0:T(8,128)} %copy-done.2, f32[2056,256]{1,0:T(8,128)} %collective-permute-done.11.refs_0_.refs_1_.refs_7_.refs_3_, f32[4,264,256]{2,1,0:T(8,128)} %inflate.4.refs_4_, ...), custom_call_target="tpu_custom_call" | custom-call | flops 2097152 | bytes 16777216 | tf_op jit(solution)/shard_map/owned/pallas_call | solution.py:415
  (116 shorter events, 8.5 us)
Async XLA Ops:
  0.0 60.4 %collective-permute-start.6 = (f32[4096,256]{1,0:T(8,128)}, f32[4096,256]{1,0:T(8,128)}, u32[]{:S(2)}, u32[]{:S(2)}) collective-permute-start(f32[4096,256]{1,0:T(8,128)} %bitcast.20), channel_id=1, source_target_pairs={{0,8},{8,0},{16,24},{24,16},{1,9},{9,1},{17,25},{25,17},{2,10},{10... | collective-permute-start | bytes 12582920 | tf_op jit(solution)/shard_map/ppermute | solution.py:495
  4.5 7.4 %copy-start.6 = (f32[1,4,4,256,256]{4,3,2,1,0:T(8,128)S(1)}, f32[1,4,4,256,256]{4,3,2,1,0:T(8,128)}, u32[]{:S(2)}) copy-start(f32[1,4,4,256,256]{4,3,2,1,0:T(8,128)} %param.4) | copy-start | bytes 12582916
  4.6 8.7 %copy-start = (f32[2056,256]{1,0:T(8,128)}, f32[2056,256]{1,0:T(8,128)S(1)}, u32[]{:S(2)}) copy-start(f32[2056,256]{1,0:T(8,128)S(1)} %pad_maximum_fusion.1.refs_0_.refs_1_.refs_8_) | copy-start | bytes 6316036
  4.6 49.1 %collective-permute-start.3 = (f32[2056,256]{1,0:T(8,128)S(1)}, f32[2056,256]{1,0:T(8,128)S(1)}, u32[]{:S(2)}, u32[]{:S(2)}) collective-permute-start(f32[2056,256]{1,0:T(8,128)S(1)} %pad_maximum_fusion.1.refs_0_.refs_1_.refs_8_), channel_id=1, source_target_pairs={{0,16},{8,24},{16,0},{24,8},{1,17},{9,25},{17,1},{25,9},{2,18},{10... | collective-permute-start | bytes 6316040 | tf_op jit(solution)/shard_map/ppermute | solution.py:492
  7.2 48.0 %collective-permute-start.2 = (f32[2056,256]{1,0:T(8,128)S(1)}, f32[2056,256]{1,0:T(8,128)}, u32[]{:S(2)}, u32[]{:S(2)}) collective-permute-start(f32[2056,256]{1,0:T(8,128)S(1)} %pad_maximum_fusion.1.refs_0_.refs_1_.refs_8_), channel_id=1, source_target_pairs={{0,1},{1,0},{2,3},{3,2},{4,5},{5,4},{6,7},{7,6},{8,9},{9,8},{10,11... | collective-permute-start | bytes 6316040 | tf_op jit(solution)/shard_map/ppermute | solution.py:492
  8.7 46.6 %collective-permute-start.1 = (f32[2056,256]{1,0:T(8,128)S(1)}, f32[2056,256]{1,0:T(8,128)S(1)}, u32[]{:S(2)}, u32[]{:S(2)}) collective-permute-start(f32[2056,256]{1,0:T(8,128)S(1)} %pad_maximum_fusion.1.refs_0_.refs_1_.refs_8_), channel_id=1, source_target_pairs={{0,8},{1,9},{2,4},{3,5},{4,2},{5,3},{6,14},{7,15},{8,0},{9,1},{10,... | collective-permute-start | bytes 6316040 | tf_op jit(solution)/shard_map/ppermute | solution.py:492
  8.7 48.9 %collective-permute-start = (f32[2056,256]{1,0:T(8,128)S(1)}, f32[2056,256]{1,0:T(8,128)}, u32[]{:S(2)}, u32[]{:S(2)}) collective-permute-start(f32[2056,256]{1,0:T(8,128)S(1)} %pad_maximum_fusion.1.refs_0_.refs_1_.refs_8_), channel_id=1, source_target_pairs={{0,2},{1,3},{2,0},{3,1},{4,6},{5,7},{6,4},{7,5},{8,10},{9,11},{10,... | collective-permute-start | bytes 6316040 | tf_op jit(solution)/shard_map/ppermute | solution.py:492
  53.7 15.2 %copy-start.2 = (f32[2056,256]{1,0:T(8,128)}, f32[2056,256]{1,0:T(8,128)S(1)}, u32[]{:S(2)}) copy-start(f32[2056,256]{1,0:T(8,128)S(1)} %collective-permute-done.3.refs_0_.refs_1_.refs_5_.refs_2_) | copy-start | bytes 6316036
  55.2 13.7 %copy-start.4 = (f32[2056,256]{1,0:T(8,128)}, f32[2056,256]{1,0:T(8,128)S(1)}, u32[]{:S(2)}) copy-start(f32[2056,256]{1,0:T(8,128)S(1)} %collective-permute-done.1.refs_10_.refs_2_) | copy-start | bytes 6316036
  57.6 46.8 %collective-permute-start.5 = (f32[2048,256]{1,0:T(8,128)}, f32[2048,256]{1,0:T(8,128)S(1)}, u32[]{:S(2)}, u32[]{:S(2)}) collective-permute-start(f32[2048,256]{1,0:T(8,128)} %bitcast.25), channel_id=1, source_target_pairs={{0,16},{8,24},{16,0},{24,8},{1,17},{9,25},{17,1},{25,9},{2,18},{10... | collective-permute-start | bytes 6291464 | tf_op jit(solution)/shard_map/ppermute | solution.py:492
  58.1 46.7 %collective-permute-start.4 = (f32[2048,256]{1,0:T(8,128)}, f32[2048,256]{1,0:T(8,128)}, u32[]{:S(2)}, u32[]{:S(2)}) collective-permute-start(f32[2048,256]{1,0:T(8,128)} %bitcast.26), channel_id=1, source_target_pairs={{0,1},{1,0},{2,3},{3,2},{4,5},{5,4},{6,7},{7,6},{8,9},{9,8},{10,11... | collective-permute-start | bytes 6291464 | tf_op jit(solution)/shard_map/ppermute | solution.py:492
  58.6 50.9 %collective-permute-start.7 = (f32[2056,256]{1,0:T(8,128)S(1)}, f32[2056,256]{1,0:T(8,128)}, u32[]{:S(2)}, u32[]{:S(2)}) collective-permute-start(f32[2056,256]{1,0:T(8,128)S(1)} %collective-permute-done.1.refs_10_.refs_2_), channel_id=1, source_target_pairs={{0,2},{1,3},{2,0},{3,1},{4,6},{5,7},{6,4},{7,5},{8,10},{9,11},{10,... | collective-permute-start | bytes 6316040 | tf_op jit(solution)/shard_map/ppermute | solution.py:492
  60.4 49.2 %collective-permute-start.8 = (f32[2056,256]{1,0:T(8,128)}, f32[2056,256]{1,0:T(8,128)}, u32[]{:S(2)}, u32[]{:S(2)}) collective-permute-start(f32[2056,256]{1,0:T(8,128)} %collective-permute-done.refs_9_.refs_1_), channel_id=1, source_target_pairs={{0,8},{1,9},{2,4},{3,5},{4,2},{5,3},{6,14},{7,15},{8,0},{9,1},{10,... | collective-permute-start | bytes 6316040 | tf_op jit(solution)/shard_map/ppermute | solution.py:492
  60.4 49.2 %collective-permute-start.9 = (f32[2056,256]{1,0:T(8,128)}, f32[2056,256]{1,0:T(8,128)}, u32[]{:S(2)}, u32[]{:S(2)}) collective-permute-start(f32[2056,256]{1,0:T(8,128)} %collective-permute-done.2.refs_0_.refs_1_), channel_id=1, source_target_pairs={{0,8},{8,0},{16,24},{24,16},{1,9},{9,1},{17,25},{25,17},{2,10},{10... | collective-permute-start | bytes 6316040 | tf_op jit(solution)/shard_map/ppermute | solution.py:495
  63.6 103.9 %copy-start.11 = (f32[4,4,64,256]{3,2,1,0:T(8,128)}, f32[4,4,64,256]{3,2,1,0:T(8,128)S(1)}, u32[]{:S(2)}) copy-start(f32[4,4,64,256]{3,2,1,0:T(8,128)S(1)} %get-tuple-element.125) | copy-start | bytes 3145732
  104.4 5.1 %copy-start.7 = (f32[2048,256]{1,0:T(8,128)}, f32[2048,256]{1,0:T(8,128)S(1)}, u32[]{:S(2)}) copy-start(f32[2048,256]{1,0:T(8,128)S(1)} %collective-permute-done.5.refs_2_) | copy-start | bytes 6291460
  104.4 5.2 %copy-start.3 = (f32[2056,256]{1,0:T(8,128)S(1)}, f32[2056,256]{1,0:T(8,128)}, u32[]{:S(2)}) copy-start(f32[2056,256]{1,0:T(8,128)} %copy-done.2) | copy-start | bytes 6316036
  109.6 12.8 %collective-permute-start.10 = (f32[4104,256]{1,0:T(8,128)}, f32[4104,256]{1,0:T(8,128)S(1)}, u32[]{:S(2)}, u32[]{:S(2)}) collective-permute-start(f32[4104,256]{1,0:T(8,128)} %pad_maximum_fusion), channel_id=1, source_target_pairs={{0,8},{8,0},{16,24},{24,16},{1,9},{9,1},{17,25},{25,17},{2,10},{10... | collective-permute-start | bytes 12607496 | tf_op jit(solution)/shard_map/ppermute | solution.py:495
  109.7 19.5 %collective-permute-start.11 = (f32[2056,256]{1,0:T(8,128)S(1)}, f32[2056,256]{1,0:T(8,128)}, u32[]{:S(2)}, u32[]{:S(2)}) collective-permute-start(f32[2056,256]{1,0:T(8,128)S(1)} %copy-done.3), channel_id=1, source_target_pairs={{0,8},{8,0},{16,24},{24,16},{1,9},{9,1},{17,25},{25,17},{2,10},{10... | collective-permute-start | bytes 6316040 | tf_op jit(solution)/shard_map/ppermute | solution.py:495
  110.2 49.5 %collective-permute-start.12 = (f32[2056,256]{1,0:T(8,128)}, f32[2056,256]{1,0:T(8,128)}, u32[]{:S(2)}, u32[]{:S(2)}) collective-permute-start(f32[2056,256]{1,0:T(8,128)} %collective-permute-done.2.refs_0_.refs_1_), channel_id=1, source_target_pairs={{0,16},{8,24},{16,0},{24,8},{1,17},{9,25},{17,1},{25,9},{2,18},{10... | collective-permute-start | bytes 6316040 | tf_op jit(solution)/shard_map/ppermute | solution.py:492
  110.8 48.8 %collective-permute-start.13 = (f32[2056,256]{1,0:T(8,128)}, f32[2056,256]{1,0:T(8,128)}, u32[]{:S(2)}, u32[]{:S(2)}) collective-permute-start(f32[2056,256]{1,0:T(8,128)} %collective-permute-done.8.refs_12_.refs_4_), channel_id=1, source_target_pairs={{0,2},{1,3},{2,0},{3,1},{4,6},{5,7},{6,4},{7,5},{8,10},{9,11},{10,... | collective-permute-start | bytes 6316040 | tf_op jit(solution)/shard_map/ppermute | solution.py:492
  112.2 47.4 %collective-permute-start.14 = (f32[2048,256]{1,0:T(8,128)}, f32[2048,256]{1,0:T(8,128)}, u32[]{:S(2)}, u32[]{:S(2)}) collective-permute-start(f32[2048,256]{1,0:T(8,128)} %copy-done.7), channel_id=1, source_target_pairs={{0,1},{1,0},{2,3},{3,2},{4,5},{5,4},{6,7},{7,6},{8,9},{9,8},{10,11... | collective-permute-start | bytes 6291464 | tf_op jit(solution)/shard_map/ppermute | solution.py:492
  159.6 4.4 %collective-permute-start.15 = (f32[2056,256]{1,0:T(8,128)}, f32[2056,256]{1,0:T(8,128)S(1)}, u32[]{:S(2)}, u32[]{:S(2)}) collective-permute-start(f32[2056,256]{1,0:T(8,128)} %collective-permute-done.12.refs_4_.refs_0_.refs_1_), channel_id=1, source_target_pairs={{0,8},{8,0},{16,24},{24,16},{1,9},{9,1},{17,25},{25,17},{2,10},{10... | collective-permute-start | bytes 6316040 | tf_op jit(solution)/shard_map/ppermute | solution.py:495
  164.0 9.7 %copy-start.5 = (f32[2056,256]{1,0:T(8,128)}, f32[2056,256]{1,0:T(8,128)S(1)}, u32[]{:S(2)}) copy-start(f32[2056,256]{1,0:T(8,128)S(1)} %collective-permute-done.15.refs_6_.refs_0_.refs_1_) | copy-start | bytes 6316036
  164.0 17.6 %collective-permute-start.16 = (f32[2048,256]{1,0:T(8,128)}, f32[2048,256]{1,0:T(8,128)}, u32[]{:S(2)}, u32[]{:S(2)}) collective-permute-start(f32[2048,256]{1,0:T(8,128)} %collective-permute-done.14.refs_2_), channel_id=1, source_target_pairs={{0,8},{8,0},{16,24},{24,16},{1,9},{9,1},{17,25},{25,17},{2,10},{10... | collective-permute-start | bytes 6291464 | tf_op jit(solution)/shard_map/ppermute | solution.py:495
  164.1 41.9 %collective-permute-start.18 = (f32[1024,256]{1,0:T(8,128)}, f32[1024,256]{1,0:T(8,128)}, u32[]{:S(2)}, u32[]{:S(2)}) collective-permute-start(f32[1024,256]{1,0:T(8,128)} %bitcast.9.refs_0_), channel_id=1, source_target_pairs={{0,8},{1,9},{2,4},{3,5},{4,2},{5,3},{6,14},{7,15},{8,0},{9,1},{10,... | collective-permute-start | bytes 3145736 | tf_op jit(solution)/shard_map/ppermute | solution.py:492
  164.5 41.5 %collective-permute-start.17 = (f32[1024,256]{1,0:T(8,128)}, f32[1024,256]{1,0:T(8,128)}, u32[]{:S(2)}, u32[]{:S(2)}) collective-permute-start(f32[1024,256]{1,0:T(8,128)} %bitcast.9.refs_0_), channel_id=1, source_target_pairs={{0,2},{1,3},{2,0},{3,1},{4,6},{5,7},{6,4},{7,5},{8,10},{9,11},{10,... | collective-permute-start | bytes 3145736 | tf_op jit(solution)/shard_map/ppermute | solution.py:492
  167.5 38.5 %collective-permute-start.20 = (f32[1024,256]{1,0:T(8,128)S(1)}, f32[1024,256]{1,0:T(8,128)}, u32[]{:S(2)}, u32[]{:S(2)}) collective-permute-start(f32[1024,256]{1,0:T(8,128)S(1)} %bitcast.29), channel_id=1, source_target_pairs={{0,8},{1,9},{2,4},{3,5},{4,2},{5,3},{6,14},{7,15},{8,0},{9,1},{10,... | collective-permute-start | bytes 3145736 | tf_op jit(solution)/shard_map/ppermute | solution.py:492
  167.6 46.2 %collective-permute-start.19 = (f32[1024,256]{1,0:T(8,128)S(1)}, f32[1024,256]{1,0:T(8,128)}, u32[]{:S(2)}, u32[]{:S(2)}) collective-permute-start(f32[1024,256]{1,0:T(8,128)S(1)} %bitcast.30), channel_id=1, source_target_pairs={{0,2},{1,3},{2,0},{3,1},{4,6},{5,7},{6,4},{7,5},{8,10},{9,11},{10,... | collective-permute-start | bytes 3145736 | tf_op jit(solution)/shard_map/ppermute | solution.py:492
  213.7 24.8 %collective-permute-start.21 = (f32[4,4,64,256]{3,2,1,0:T(8,128)}, f32[4,4,64,256]{3,2,1,0:T(8,128)S(1)}, u32[]{:S(2)}, u32[]{:S(2)}) collective-permute-start(f32[4,4,64,256]{3,2,1,0:T(8,128)} %get-tuple-element.101), channel_id=1, source_target_pairs={{0,1},{1,0},{2,3},{3,2},{4,5},{5,4},{6,7},{7,6},{8,9},{9,8},{10,11... | collective-permute-start | bytes 3145736 | tf_op jit(solution)/shard_map/ppermute | solution.py:492
  214.3 24.6 %collective-permute-start.23 = (f32[1024,256]{1,0:T(8,128)}, f32[1024,256]{1,0:T(8,128)S(1)}, u32[]{:S(2)}, u32[]{:S(2)}) collective-permute-start(f32[1024,256]{1,0:T(8,128)} %collective-permute-done.18.refs_2_), channel_id=1, source_target_pairs={{0,2},{1,3},{2,0},{3,1},{4,6},{5,7},{6,4},{7,5},{8,10},{9,11},{10,... | collective-permute-start | bytes 3145736 | tf_op jit(solution)/shard_map/ppermute | solution.py:492
  216.0 22.8 %collective-permute-start.24 = (f32[1024,256]{1,0:T(8,128)}, f32[1024,256]{1,0:T(8,128)S(1)}, u32[]{:S(2)}, u32[]{:S(2)}) collective-permute-start(f32[1024,256]{1,0:T(8,128)} %collective-permute-done.17.refs_1_), channel_id=1, source_target_pairs={{0,8},{1,9},{2,4},{3,5},{4,2},{5,3},{6,14},{7,15},{8,0},{9,1},{10,... | collective-permute-start | bytes 3145736 | tf_op jit(solution)/shard_map/ppermute | solution.py:492
  238.6 3.5 copy-start.26
  238.8 7.6 %copy-start.24 = (f32[1024,256]{1,0:T(8,128)}, f32[1024,256]{1,0:T(8,128)S(1)}, u32[]{:S(2)}) copy-start(f32[1024,256]{1,0:T(8,128)S(1)} %collective-permute-done.23.refs_3_) | copy-start | bytes 3145732
  238.8 7.6 %copy-start.22 = (f32[1024,256]{1,0:T(8,128)}, f32[1024,256]{1,0:T(8,128)S(1)}, u32[]{:S(2)}) copy-start(f32[1024,256]{1,0:T(8,128)S(1)} %collective-permute-done.24.refs_4_) | copy-start | bytes 3145732
  238.8 23.7 %collective-permute-start.27 = (f32[4,4,64,256]{3,2,1,0:T(8,128)}, f32[4,4,64,256]{3,2,1,0:T(8,128)S(1)}, u32[]{:S(2)}, u32[]{:S(2)}) collective-permute-start(f32[4,4,64,256]{3,2,1,0:T(8,128)} %get-tuple-element.107), channel_id=1, source_target_pairs={{0,1},{1,0},{2,3},{3,2},{4,5},{5,4},{6,7},{7,6},{8,9},{9,8},{10,11... | collective-permute-start | bytes 3145736 | tf_op jit(solution)/shard_map/ppermute | solution.py:492
  240.4 26.1 %collective-permute-start.29 = (f32[1024,256]{1,0:T(8,128)S(1)}, f32[1024,256]{1,0:T(8,128)S(1)}, u32[]{:S(2)}, u32[]{:S(2)}) collective-permute-start(f32[1024,256]{1,0:T(8,128)S(1)} %collective-permute-done.24.refs_4_), channel_id=1, source_target_pairs={{0,2},{1,3},{2,0},{3,1},{4,6},{5,7},{6,4},{7,5},{8,10},{9,11},{10,... | collective-permute-start | bytes 3145736 | tf_op jit(solution)/shard_map/ppermute | solution.py:492
  244.7 41.3 %collective-permute-start.25 = (f32[4,264,256]{2,1,0:T(8,128)}, f32[4,264,256]{2,1,0:T(8,128)S(1)}, u32[]{:S(2)}, u32[]{:S(2)}) collective-permute-start(f32[4,264,256]{2,1,0:T(8,128)} %inflate.4.refs_4_), channel_id=1, source_target_pairs={{0,16},{8,24},{16,0},{24,8},{1,17},{9,25},{17,1},{25,9},{2,18},{10... | collective-permute-start | bytes 3244040 | tf_op jit(solution)/shard_map/ppermute | solution.py:492
  246.1 39.9 %collective-permute-start.30 = (f32[1024,256]{1,0:T(8,128)}, f32[1024,256]{1,0:T(8,128)S(1)}, u32[]{:S(2)}, u32[]{:S(2)}) collective-permute-start(f32[1024,256]{1,0:T(8,128)} %collective-permute-done.20.refs_2_), channel_id=1, source_target_pairs={{0,2},{1,3},{2,0},{3,1},{4,6},{5,7},{6,4},{7,5},{8,10},{9,11},{10,... | collective-permute-start | bytes 3145736 | tf_op jit(solution)/shard_map/ppermute | solution.py:492
  246.4 39.6 %collective-permute-start.31 = (f32[1024,256]{1,0:T(8,128)}, f32[1024,256]{1,0:T(8,128)S(1)}, u32[]{:S(2)}, u32[]{:S(2)}) collective-permute-start(f32[1024,256]{1,0:T(8,128)} %collective-permute-done.19.refs_1_), channel_id=1, source_target_pairs={{0,8},{1,9},{2,4},{3,5},{4,2},{5,3},{6,14},{7,15},{8,0},{9,1},{10,... | collective-permute-start | bytes 3145736 | tf_op jit(solution)/shard_map/ppermute | solution.py:492
  267.5 18.6 %copy-start.9 = (f32[4,264,256]{2,1,0:T(8,128)S(1)}, f32[4,264,256]{2,1,0:T(8,128)}, u32[]{:S(2)}) copy-start(f32[4,264,256]{2,1,0:T(8,128)} %inflate.5.refs_8_) | copy-start | bytes 3244036
  286.0 3.4 copy-start.23
  286.0 3.4 copy-start.21
  286.0 39.2 %copy-start.12 = (f32[4,264,256]{2,1,0:T(8,128)}, f32[4,264,256]{2,1,0:T(8,128)S(1)}, u32[]{:S(2)}) copy-start(f32[4,264,256]{2,1,0:T(8,128)S(1)} %collective-permute-done.25.refs_6_) | copy-start | bytes 3244036
  286.0 27.2 %collective-permute-start.32 = (f32[4,264,256]{2,1,0:T(8,128)S(1)}, f32[4,264,256]{2,1,0:T(8,128)S(1)}, u32[]{:S(2)}, u32[]{:S(2)}) collective-permute-start(f32[4,264,256]{2,1,0:T(8,128)S(1)} %copy-done.9), channel_id=1, source_target_pairs={{0,16},{8,24},{16,0},{24,8},{1,17},{9,25},{17,1},{25,9},{2,18},{10... | collective-permute-start | bytes 3244040 | tf_op jit(solution)/shard_map/ppermute | solution.py:492
  287.5 22.1 %collective-permute-start.34 = (f32[4,4,64,256]{3,2,1,0:T(8,128)}, f32[4,4,64,256]{3,2,1,0:T(8,128)S(1)}, u32[]{:S(2)}, u32[]{:S(2)}) collective-permute-start(f32[4,4,64,256]{3,2,1,0:T(8,128)} %get-tuple-element.116), channel_id=1, source_target_pairs={{0,1},{1,0},{2,3},{3,2},{4,5},{5,4},{6,7},{7,6},{8,9},{9,8},{10,11... | collective-permute-start | bytes 3145736 | tf_op jit(solution)/shard_map/ppermute | solution.py:599
  288.1 25.8 %collective-permute-start.38 = (f32[1024,256]{1,0:T(8,128)S(1)}, f32[1024,256]{1,0:T(8,128)S(1)}, u32[]{:S(2)}, u32[]{:S(2)}) collective-permute-start(f32[1024,256]{1,0:T(8,128)S(1)} %collective-permute-done.31.refs_4_), channel_id=1, source_target_pairs={{0,2},{1,3},{2,0},{3,1},{4,6},{5,7},{6,4},{7,5},{8,10},{9,11},{10,... | collective-permute-start | bytes 3145736 | tf_op jit(solution)/shard_map/ppermute | solution.py:492
  313.2 36.6 %copy-start.13 = (f32[4,264,256]{2,1,0:T(8,128)}, f32[4,264,256]{2,1,0:T(8,128)S(1)}, u32[]{:S(2)}) copy-start(f32[4,264,256]{2,1,0:T(8,128)S(1)} %collective-permute-done.32.refs_10_) | copy-start | bytes 3244036
  313.2 35.0 %collective-permute-start.36 = (f32[4,264,256]{2,1,0:T(8,128)}, f32[4,264,256]{2,1,0:T(8,128)S(1)}, u32[]{:S(2)}, u32[]{:S(2)}) collective-permute-start(f32[4,264,256]{2,1,0:T(8,128)} %inflate.6.refs_12_), channel_id=1, source_target_pairs={{0,16},{8,24},{16,0},{24,8},{1,17},{9,25},{17,1},{25,9},{2,18},{10... | collective-permute-start | bytes 3244040 | tf_op jit(solution)/shard_map/ppermute | solution.py:605
  314.9 9.7 %copy-start.8 = (f32[4,264,256]{2,1,0:T(8,128)S(1)}, f32[4,264,256]{2,1,0:T(8,128)}, u32[]{:S(2)}) copy-start(f32[4,264,256]{2,1,0:T(8,128)} %inflate.4.refs_4_) | copy-start | bytes 3244036
  324.5 25.3 %copy-start.10 = (f32[4,264,256]{2,1,0:T(8,128)S(1)}, f32[4,264,256]{2,1,0:T(8,128)}, u32[]{:S(2)}) copy-start(f32[4,264,256]{2,1,0:T(8,128)} %inflate.6.refs_12_) | copy-start | bytes 3244036
  324.5 21.1 %collective-permute-start.39 = (f32[4,4,64,256]{3,2,1,0:T(8,128)}, f32[4,4,64,256]{3,2,1,0:T(8,128)}, u32[]{:S(2)}, u32[]{:S(2)}) collective-permute-start(f32[4,4,64,256]{3,2,1,0:T(8,128)} %get-tuple-element.123), channel_id=1, source_target_pairs={{0,1},{1,0},{2,3},{3,2},{4,5},{5,4},{6,7},{7,6},{8,9},{9,8},{10,11... | collective-permute-start | bytes 3145736 | tf_op jit(solution)/shard_map/ppermute | solution.py:599
  324.6 25.2 %collective-permute-start.22 = (f32[4,264,256]{2,1,0:T(8,128)S(1)}, f32[4,264,256]{2,1,0:T(8,128)S(1)}, u32[]{:S(2)}, u32[]{:S(2)}) collective-permute-start(f32[4,264,256]{2,1,0:T(8,128)S(1)} %copy-done.8), channel_id=1, source_target_pairs={{0,8},{8,0},{16,24},{24,16},{1,9},{9,1},{17,25},{25,17},{2,10},{10... | collective-permute-start | bytes 3244040 | tf_op jit(solution)/shard_map/ppermute | solution.py:588
  324.7 25.7 %collective-permute-start.28 = (f32[4,264,256]{2,1,0:T(8,128)S(1)}, f32[4,264,256]{2,1,0:T(8,128)}, u32[]{:S(2)}, u32[]{:S(2)}) collective-permute-start(f32[4,264,256]{2,1,0:T(8,128)S(1)} %copy-done.9), channel_id=1, source_target_pairs={{0,8},{8,0},{16,24},{24,16},{1,9},{9,1},{17,25},{25,17},{2,10},{10... | collective-permute-start | bytes 3244040 | tf_op jit(solution)/shard_map/ppermute | solution.py:588
  325.2 25.3 %collective-permute-start.26 = (f32[4,264,256]{2,1,0:T(8,128)S(1)}, f32[4,264,256]{2,1,0:T(8,128)}, u32[]{:S(2)}, u32[]{:S(2)}) collective-permute-start(f32[4,264,256]{2,1,0:T(8,128)S(1)} %collective-permute-done.25.refs_6_), channel_id=1, source_target_pairs={{0,8},{8,0},{16,24},{24,16},{1,9},{9,1},{17,25},{25,17},{2,10},{10... | collective-permute-start | bytes 3244040 | tf_op jit(solution)/shard_map/ppermute | solution.py:588
  348.2 23.6 %copy-start.14 = (f32[4,264,256]{2,1,0:T(8,128)}, f32[4,264,256]{2,1,0:T(8,128)S(1)}, u32[]{:S(2)}) copy-start(f32[4,264,256]{2,1,0:T(8,128)S(1)} %collective-permute-done.36.refs_14_) | copy-start | bytes 3244036
  348.2 20.7 %collective-permute-start.41 = (f32[4,264,256]{2,1,0:T(8,128)}, f32[4,264,256]{2,1,0:T(8,128)S(1)}, u32[]{:S(2)}, u32[]{:S(2)}) collective-permute-start(f32[4,264,256]{2,1,0:T(8,128)} %inflate.7.refs_16_), channel_id=1, source_target_pairs={{0,16},{8,24},{16,0},{24,8},{1,17},{9,25},{17,1},{25,9},{2,18},{10... | collective-permute-start | bytes 3244040 | tf_op jit(solution)/shard_map/ppermute | solution.py:605
  349.8 19.2 %collective-permute-start.35 = (f32[4,264,256]{2,1,0:T(8,128)S(1)}, f32[4,264,256]{2,1,0:T(8,128)S(1)}, u32[]{:S(2)}, u32[]{:S(2)}) collective-permute-start(f32[4,264,256]{2,1,0:T(8,128)S(1)} %copy-done.10), channel_id=1, source_target_pairs={{0,8},{8,0},{16,24},{24,16},{1,9},{9,1},{17,25},{25,17},{2,10},{10... | collective-permute-start | bytes 3244040 | tf_op jit(solution)/shard_map/ppermute | solution.py:606
  349.8 22.0 %copy-start.15 = (f32[4,264,256]{2,1,0:T(8,128)}, f32[4,264,256]{2,1,0:T(8,128)S(1)}, u32[]{:S(2)}) copy-start(f32[4,264,256]{2,1,0:T(8,128)S(1)} %collective-permute-done.22.refs_5_) | copy-start | bytes 3244036
  349.8 19.2 %collective-permute-start.33 = (f32[4,264,256]{2,1,0:T(8,128)S(1)}, f32[4,264,256]{2,1,0:T(8,128)S(1)}, u32[]{:S(2)}, u32[]{:S(2)}) collective-permute-start(f32[4,264,256]{2,1,0:T(8,128)S(1)} %collective-permute-done.32.refs_10_), channel_id=1, source_target_pairs={{0,8},{8,0},{16,24},{24,16},{1,9},{9,1},{17,25},{25,17},{2,10},{10... | collective-permute-start | bytes 3244040 | tf_op jit(solution)/shard_map/ppermute | solution.py:588
  350.4 18.7 %collective-permute-start.40 = (f32[4,264,256]{2,1,0:T(8,128)}, f32[4,264,256]{2,1,0:T(8,128)S(1)}, u32[]{:S(2)}, u32[]{:S(2)}) collective-permute-start(f32[4,264,256]{2,1,0:T(8,128)} %inflate.7.refs_16_), channel_id=1, source_target_pairs={{0,8},{8,0},{16,24},{24,16},{1,9},{9,1},{17,25},{25,17},{2,10},{10... | collective-permute-start | bytes 3244040 | tf_op jit(solution)/shard_map/ppermute | solution.py:606
  350.4 18.6 %collective-permute-start.37 = (f32[4,264,256]{2,1,0:T(8,128)S(1)}, f32[4,264,256]{2,1,0:T(8,128)S(1)}, u32[]{:S(2)}, u32[]{:S(2)}) collective-permute-start(f32[4,264,256]{2,1,0:T(8,128)S(1)} %collective-permute-done.36.refs_14_), channel_id=1, source_target_pairs={{0,8},{8,0},{16,24},{24,16},{1,9},{9,1},{17,25},{25,17},{2,10},{10... | collective-permute-start | bytes 3244040 | tf_op jit(solution)/shard_map/ppermute | solution.py:606
  369.0 2.8 collective-permute-start.42
  369.0 2.8 copy-start.18
  (10 other events, 13.2 us)

commit v7 on v6

--- a/solution.py
+++ b/solution.py
@@ -380,7 +380,7 @@
         lax.fori_loop(0, items, place_item, jnp.int32(0))
 
     partials(lambda copy: copy.wait())
-    factors = scale / jnp.sum(jnp.sum(partial[...], axis=0), axis=1)
+    totals = jnp.sum(jnp.sum(partial[...], axis=0), axis=1)
 
     def finish(s, _):
         j = whose[s]
@@ -394,7 +394,7 @@
             @pl.when(j == jj)
             def _():
                 pltpu.make_async_copy(slots.at[s], slots.at[s], in_sems.at[s]).wait()
-                slots[s] = slots[s] * factors[jj : jj + 1]
+                slots[s] = scale * slots[s] / totals[jj : jj + 1]
 
         pltpu.make_async_copy(slots.at[s], out_ref.at[s], out_sems.at[s]).start()
         return 0

time: 380 us -> 380 us (level)
  transfers between devices with their start and end apart: 43 -> 43, of which waited for: 17 -> 16; matrix products, arithmetic and copies ran while one was open for 4% -> 3% of each run, Pallas kernels for 39% -> 39%
where the time goes in v7:
time: 380 us; the launch traced here: 379 us
  waiting for transfers between devices  170 us (45%)
  Pallas kernels  155 us (41%)
  starting transfers between devices  33 us (9%)
  local copies, waits for them, and re-layouts  15.3 us (4%)
  other arithmetic  5.59 us (1%)
    ppermute x25, waiting for transfers between devices, send(): return at(tick, move(after(tick, x), *more))  121 us
    pallas_call x6, Pallas kernels, product(): pl.pallas_call(functools.partial(product_kernel, line, which, arrivals, p...  89.7 us
    pallas_call x8, Pallas kernels, place(): pl.pallas_call(functools.partial(place_kernel, len(parts)), grid=(blocks,...  39 us
    ppermute x25, starting transfers between devices, send(): return at(tick, move(after(tick, x), *more))  26.8 us
    ppermute x2, waiting for transfers between devices, on_device(): others = [pair(tie(x, other)) for x in theirs]  24.2 us
    ppermute x2, waiting for transfers between devices, on_device(): opposite = across(tie(x, opposite))  18.2 us
    pallas_call x4, Pallas kernels, inflate(): pl.pallas_call(inflate_kernel, out_shape=jax.ShapeDtypeStruct((blocks, co...  10.6 us
    pallas_call x1, Pallas kernels, owned_tiles(): pl.pallas_call(functools.partial(owned_kernel, sizes, blocks, count, scal...  8.03 us
  transfers between devices with their start and end apart: 43, of which 16 were waited for; matrix products, arithmetic and copies ran while one was open for 3% of the time, Pallas kernels for 39%

profile of v7, /device:TPU:0, one launch (start us, length us, event | category | flops | bytes accessed | tf_op | source)
XLA Modules:
  0.0 379.0 jit_solution(13643274742064900846)
XLA Ops:
  0.5 0.8 reshape.28
  1.2 0.8 reshape.29
  2.0 1.7 slice.16
  4.6 2.6 collective-permute-start.3
  7.2 1.5 collective-permute-start.2
  8.7 3.1 collective-permute-start
  11.8 1.5 slice.13
  13.3 4.8 %place.8 = (bf16[2,4,4,4,2,256,256]{6,5,4,3,2,1,0:T(8,128)(2,1)}, f32[8,128]{1,0:T(8,128)}) custom-call(f32[2056,256]{1,0:T(8,128)} %copy-done, f32[2056,256]{1,0:T(8,128)} %copy-done, f32[2048,256]{1,0:T(8,128)} %bitcast.24), custom_call_target="tpu_custom_call" | custom-call | flops 1048576 | bytes 8388608 | tf_op jit(solution)/shard_map/place/pallas_call | solution.py:61
  18.1 35.6 %collective-permute-done.3.refs_0_.refs_1_.refs_5_.refs_2_ = f32[2056,256]{1,0:T(8,128)S(1)} collective-permute-done((f32[2056,256]{1,0:T(8,128)S(1)}, f32[2056,256]{1,0:T(8,128)S(1)}, u32[]{:S(2)}, u32[]{:S(2)}) %collective-permute-start.3) | collective-permute-done | bytes 2105376 | tf_op jit(solution)/shard_map/ppermute | solution.py:492
  53.7 1.6 collective-permute-done.2.refs_0_.refs_1_
  55.2 2.3 collective-permute-done.refs_9_.refs_1_
  58.6 1.7 collective-permute-start.7
  60.9 2.7 fusion
  63.6 5.3 %place.9 = (bf16[2,4,4,4,2,256,256]{6,5,4,3,2,1,0:T(8,128)(2,1)}, f32[8,128]{1,0:T(8,128)}) custom-call(f32[4096,256]{1,0:T(8,128)} %collective-permute-done.6.refs_0_, bf16[2,4,4,4,2,256,256]{6,5,4,3,2,1,0:T(8,128)(2,1)} %get-tuple-element.71.refs_1_), custom_call_target="tpu_custom_call", output_to_operand_aliasing={{0}: (1, {})} | custom-call | flops 1048576 | bytes 8388608 | tf_op jit(solution)/shard_map/place/pallas_call | solution.py:61
  68.9 35.5 %collective-permute-done.5.refs_2_ = f32[2048,256]{1,0:T(8,128)S(1)} collective-permute-done((f32[2048,256]{1,0:T(8,128)}, f32[2048,256]{1,0:T(8,128)S(1)}, u32[]{:S(2)}, u32[]{:S(2)}) %collective-permute-start.5) | collective-permute-done | bytes 2097184 | tf_op jit(solution)/shard_map/ppermute | solution.py:492
  104.8 4.8 %pad_maximum_fusion = f32[4104,256]{1,0:T(8,128)} fusion(f32[8,256]{1,0:T(8,128)S(1)} %broadcast_in_dim.6, f32[2048,256]{1,0:T(8,128)S(1)} %collective-permute-done.5.refs_2_, f32[2048,256]{1,0:T(8,128)} %collective-permute-done.4.refs_2_), kind=kLoop, calls=%fused_computation | loop fusion | flops 2101248 | bytes 8404992 | tf_op jit(solution)/shard_map/concatenate | solution.py:559
  110.2 0.6 collective-permute-start.12
  110.8 1.4 collective-permute-start.13
  112.8 4.8 %place.10 = (bf16[2,4,4,4,2,256,256]{6,5,4,3,2,1,0:T(8,128)(2,1)}, f32[8,128]{1,0:T(8,128)}) custom-call(f32[2056,256]{1,0:T(8,128)} %collective-permute-done.2.refs_0_.refs_1_, f32[2056,256]{1,0:T(8,128)} %collective-permute-done.2.refs_0_.refs_1_, f32[2048,256]{1,0:T(8,128)} %collective-permute-done.4.refs_2_, ...), custom_call_target="tpu_custom_call", output_to_operand_aliasing={{0}: (3, {})} | custom-call | flops 1048576 | bytes 8388608 | tf_op jit(solution)/shard_map/place/pallas_call | solution.py:61
  117.5 4.8 %place.11 = (bf16[2,4,4,4,2,256,256]{6,5,4,3,2,1,0:T(8,128)(2,1)}, f32[8,128]{1,0:T(8,128)}) custom-call(f32[2056,256]{1,0:T(8,128)} %copy-done.2, f32[2056,256]{1,0:T(8,128)} %copy-done.2, f32[2048,256]{1,0:T(8,128)} %copy-done.7, bf16[2,4,4,4,2,256,256]{6,5,4,3,2,1,0:T(8,128)(2,1)} %get-tuple-element.81.refs_3_), custom_call_target="tpu_custom_call", output_to_operand_aliasing={{0}: (3, {})} | custom-call | flops 1048576 | bytes 8388608 | tf_op jit(solution)/shard_map/place/pallas_call | solution.py:61
  122.4 2.0 copy-done.1
  124.4 4.8 %place.12 = (bf16[2,4,4,4,2,256,256]{6,5,4,3,2,1,0:T(8,128)(2,1)}, f32[8,128]{1,0:T(8,128)}) custom-call(f32[2056,256]{1,0:T(8,128)} %collective-permute-done.9.refs_0_.refs_1_.refs_2_, f32[2056,256]{1,0:T(8,128)} %collective-permute-done.9.refs_0_.refs_1_.refs_2_, f32[4104,256]{1,0:T(8,128)} %copy-done.1, ...), custom_call_target="tpu_custom_call", output_to_operand_aliasing={{0}: (3, {})} | custom-call | flops 1048576 | bytes 8388608 | tf_op jit(solution)/shard_map/place/pallas_call | solution.py:61
  129.2 4.8 %place.13 = (bf16[2,4,4,4,2,256,256]{6,5,4,3,2,1,0:T(8,128)(2,1)}, f32[8,128]{1,0:T(8,128)}) custom-call(f32[2056,256]{1,0:T(8,128)} %collective-permute-done.11.refs_0_.refs_1_.refs_7_.refs_3_, f32[2056,256]{1,0:T(8,128)} %collective-permute-done.11.refs_0_.refs_1_.refs_7_.refs_3_, f32[4104,256]{1,0:T(8,128)} %copy-done.1, ...), custom_call_target="tpu_custom_call", output_to_operand_aliasing={{0}: (3, {})} | custom-call | flops 1048576 | bytes 8388608 | tf_op jit(solution)/shard_map/place/pallas_call | solution.py:61
  134.0 25.6 %collective-permute-done.14.refs_2_ = f32[2048,256]{1,0:T(8,128)} collective-permute-done((f32[2048,256]{1,0:T(8,128)}, f32[2048,256]{1,0:T(8,128)}, u32[]{:S(2)}, u32[]{:S(2)}) %collective-permute-start.14) | collective-permute-done | bytes 2097184 | tf_op jit(solution)/shard_map/ppermute | solution.py:492
  159.6 4.4 %collective-permute-done.15.refs_6_.refs_0_.refs_1_ = f32[2056,256]{1,0:T(8,128)S(1)} collective-permute-done((f32[2056,256]{1,0:T(8,128)}, f32[2056,256]{1,0:T(8,128)S(1)}, u32[]{:S(2)}, u32[]{:S(2)}) %collective-permute-start.15) | collective-permute-done | bytes 2105376 | tf_op jit(solution)/shard_map/ppermute | solution.py:495
  164.5 3.0 collective-permute-start.17
  167.6 0.8 collective-permute-start.19
  168.3 0.6 pad_add_fusion.me_ref
  168.9 4.8 %place.14 = (bf16[2,4,4,4,2,256,256]{6,5,4,3,2,1,0:T(8,128)(2,1)}, f32[8,128]{1,0:T(8,128)}) custom-call(f32[2056,256]{1,0:T(8,128)} %collective-permute-done.12.refs_4_.refs_0_.refs_1_, f32[2056,256]{1,0:T(8,128)} %collective-permute-done.12.refs_4_.refs_0_.refs_1_, f32[2048,256]{1,0:T(8,128)} %collective-permute-done.14.refs_2_, ...), custom_call_target="tpu_custom_call", output_to_operand_aliasing={{0}: (3, {})} | custom-call | flops 1048576 | bytes 8388608 | tf_op jit(solution)/shard_map/place/pallas_call | solution.py:61
  173.7 7.9 %plan.1 = (s32[3312]{0:T(1024)}, s32[192]{0:T(256)}) custom-call(s32[2]{0:T(128)} %pad_add_fusion.me_ref, f32[2056,256]{1,0:T(8,128)} %collective-permute-done.2.refs_0_.refs_1_, f32[2056,256]{1,0:T(8,128)} %copy-done, f32[2056,256]{1,0:T(8,128)} %collective-permute-done.9.refs_0_.refs_1_.refs_2_, f32[4104,256]{1,0:T(8,128)} %copy-done.1, ...), custom_call_target="tpu_custom_call" | custom-call | tf_op jit(solution)/shard_map/plan/pallas_call | solution.py:154
  181.7 4.9 %place.15 = (bf16[2,4,4,4,2,256,256]{6,5,4,3,2,1,0:T(8,128)(2,1)}, f32[8,128]{1,0:T(8,128)}) custom-call(f32[2056,256]{1,0:T(8,128)} %copy-done.5, f32[2056,256]{1,0:T(8,128)} %copy-done.5, f32[2048,256]{1,0:T(8,128)} %collective-permute-done.16.refs_2_, bf16[2,4,4,4,2,256,256]{6,5,4,3,2,1,0:T(8,128)(2,1)} %get-tuple-element.93.refs_3_), custom_call_target="tpu_custom_call", output_to_operand_aliasing={{0}: (3, {})} | custom-call | flops 1048576 | bytes 8388608 | tf_op jit(solution)/shard_map/place/pallas_call | solution.py:61
  186.6 19.8 %product.6 = (f32[4,4,64,256]{3,2,1,0:T(8,128)}, f32[4,4,64,256]{3,2,1,0:T(8,128)}) custom-call(s32[2]{0:T(128)} %pad_add_fusion.me_ref, s32[3312]{0:T(1024)} %get-tuple-element.88.plan_ref, s32[192]{0:T(256)} %get-tuple-element.89.kept_ref, bf16[128,2,256,256]{3,2,1,0:T(8,128)(2,1)} %bitcast.14, f32[2056,256]{1,0:T(8,128)} %copy-done, ...), custom_call_target="tpu_custom_call" | custom-call | flops 6442450944 | bytes 16777216 | tf_op jit(solution)/shard_map/product/pallas_call | solution.py:289
  206.4 7.3 %collective-permute-done.19.refs_1_ = f32[1024,256]{1,0:T(8,128)} collective-permute-done((f32[1024,256]{1,0:T(8,128)S(1)}, f32[1024,256]{1,0:T(8,128)}, u32[]{:S(2)}, u32[]{:S(2)}) %collective-permute-start.19) | collective-permute-done | bytes 1048608 | tf_op jit(solution)/shard_map/ppermute | solution.py:492
  214.3 1.7 collective-permute-start.23
  216.0 19.8 %product.7 = (f32[4,4,64,256]{3,2,1,0:T(8,128)}, f32[4,4,64,256]{3,2,1,0:T(8,128)}) custom-call(s32[2]{0:T(128)} %pad_add_fusion.me_ref, s32[3312]{0:T(1024)} %get-tuple-element.88.plan_ref, s32[192]{0:T(256)} %get-tuple-element.89.kept_ref, bf16[128,2,256,256]{3,2,1,0:T(8,128)(2,1)} %bitcast.15, f32[2056,256]{1,0:T(8,128)} %copy-done, ...), custom_call_target="tpu_custom_call" | custom-call | flops 6442450944 | bytes 16777216 | tf_op jit(solution)/shard_map/product/pallas_call | solution.py:289
  235.8 2.8 collective-permute-done.21.other_ref
  238.8 1.6 collective-permute-start.27
  240.4 1.7 collective-permute-start.29
  242.1 2.6 inflate.4.refs_4_
  244.7 1.4 collective-permute-start.25
  246.5 16.3 %product.8 = (f32[4,4,64,256]{3,2,1,0:T(8,128)}, f32[4,4,64,256]{3,2,1,0:T(8,128)}) custom-call(s32[2]{0:T(128)} %pad_add_fusion.me_ref, s32[3312]{0:T(1024)} %get-tuple-element.88.plan_ref, s32[192]{0:T(256)} %get-tuple-element.89.kept_ref, bf16[128,2,256,256]{3,2,1,0:T(8,128)(2,1)} %bitcast.16, f32[1024,256]{1,0:T(8,128)} %bitcast.9.refs_0_, ...), custom_call_target="tpu_custom_call" | custom-call | flops 5368709120 | bytes 13981013 | tf_op jit(solution)/shard_map/product/pallas_call | solution.py:289
  262.7 1.0 copy-done.27
  263.7 2.7 inflate.5.refs_8_
  266.5 1.0 copy-done.25
  267.5 8.8 %product.9 = (f32[4,4,64,256]{3,2,1,0:T(8,128)}, f32[4,4,64,256]{3,2,1,0:T(8,128)}) custom-call(s32[2]{0:T(128)} %pad_add_fusion.me_ref, s32[3312]{0:T(1024)} %get-tuple-element.88.plan_ref, s32[192]{0:T(256)} %get-tuple-element.89.kept_ref, bf16[128,2,256,256]{3,2,1,0:T(8,128)(2,1)} %bitcast.17, f32[1024,256]{1,0:T(8,128)} %copy-done.25, ...), custom_call_target="tpu_custom_call" | custom-call | flops 1073741824 | bytes 2796202 | tf_op jit(solution)/shard_map/product/pallas_call | solution.py:289
  276.2 9.8 %collective-permute-done.30.refs_3_ = f32[1024,256]{1,0:T(8,128)S(1)} collective-permute-done((f32[1024,256]{1,0:T(8,128)}, f32[1024,256]{1,0:T(8,128)S(1)}, u32[]{:S(2)}, u32[]{:S(2)}) %collective-permute-start.30) | collective-permute-done | bytes 1048608 | tf_op jit(solution)/shard_map/ppermute | solution.py:492
  286.0 1.4 collective-permute-start.32
  287.5 0.6 collective-permute-start.34
  288.1 1.3 collective-permute-start.38
  289.4 16.3 %product.10 = (f32[4,4,64,256]{3,2,1,0:T(8,128)}, f32[4,4,64,256]{3,2,1,0:T(8,128)}) custom-call(s32[2]{0:T(128)} %pad_add_fusion.me_ref, s32[3312]{0:T(1024)} %get-tuple-element.88.plan_ref, s32[192]{0:T(256)} %get-tuple-element.89.kept_ref, bf16[128,2,256,256]{3,2,1,0:T(8,128)(2,1)} %bitcast.18, f32[1024,256]{1,0:T(8,128)} %bitcast.31, ...), custom_call_target="tpu_custom_call" | custom-call | flops 5368709120 | bytes 13981013 | tf_op jit(solution)/shard_map/product/pallas_call | solution.py:289
  305.7 3.9 %collective-permute-done.34.other_ref = f32[4,4,64,256]{3,2,1,0:T(8,128)S(1)} collective-permute-done((f32[4,4,64,256]{3,2,1,0:T(8,128)}, f32[4,4,64,256]{3,2,1,0:T(8,128)S(1)}, u32[]{:S(2)}, u32[]{:S(2)}) %collective-permute-start.34) | collective-permute-done | bytes 1048608 | tf_op jit(solution)/shard_map/ppermute | solution.py:599
  309.6 1.0 copy-done.29
  310.6 2.6 inflate.6.refs_12_
  313.2 0.6 collective-permute-start.36
  313.9 1.0 copy-done.28
  314.9 8.8 %product.11 = (f32[4,4,64,256]{3,2,1,0:T(8,128)}, f32[4,4,64,256]{3,2,1,0:T(8,128)}) custom-call(s32[2]{0:T(128)} %pad_add_fusion.me_ref, s32[3312]{0:T(1024)} %get-tuple-element.88.plan_ref, s32[192]{0:T(256)} %get-tuple-element.89.kept_ref, bf16[128,2,256,256]{3,2,1,0:T(8,128)(2,1)} %bitcast.19, f32[1024,256]{1,0:T(8,128)} %copy-done.28, ...), custom_call_target="tpu_custom_call" | custom-call | flops 1073741824 | bytes 2796202 | tf_op jit(solution)/shard_map/product/pallas_call | solution.py:289
  324.5 20.3 %collective-permute-done.39.other_ref = f32[4,4,64,256]{3,2,1,0:T(8,128)} collective-permute-done((f32[4,4,64,256]{3,2,1,0:T(8,128)}, f32[4,4,64,256]{3,2,1,0:T(8,128)}, u32[]{:S(2)}, u32[]{:S(2)}) %collective-permute-start.39) | collective-permute-done | bytes 1048608 | tf_op jit(solution)/shard_map/ppermute | solution.py:599
  344.8 2.6 inflate.7.refs_16_
  347.4 1.4 collective-permute-start.41
  348.8 0.6 collective-permute-start.33
  349.9 18.2 %collective-permute-done.41.refs_18_ = f32[4,264,256]{2,1,0:T(8,128)S(1)} collective-permute-done((f32[4,264,256]{2,1,0:T(8,128)}, f32[4,264,256]{2,1,0:T(8,128)S(1)}, u32[]{:S(2)}, u32[]{:S(2)}) %collective-permute-start.41) | collective-permute-done | bytes 1081376 | tf_op jit(solution)/shard_map/ppermute | solution.py:605
  368.2 0.9 copy-done.16
  369.5 1.5 collective-permute-done.42.refs_19_
  371.0 8.0 %owned.1 = f32[32,256,256]{2,1,0:T(8,128)} custom-call(s32[2]{0:T(128)} %pad_add_fusion.me_ref, f32[2056,256]{1,0:T(8,128)} %copy-done, f32[4104,256]{1,0:T(8,128)} %copy-done.1, f32[2056,256]{1,0:T(8,128)} %copy-done.2, f32[2056,256]{1,0:T(8,128)} %collective-permute-done.11.refs_0_.refs_1_.refs_7_.refs_3_, f32[4,264,256]{2,1,0:T(8,128)} %inflate.4.refs_4_, ...), custom_call_target="tpu_custom_call" | custom-call | flops 2097152 | bytes 16777216 | tf_op jit(solution)/shard_map/owned/pallas_call | solution.py:415
  (116 shorter events, 7.9 us)
Async XLA Ops:
  0.0 60.4 %collective-permute-start.6 = (f32[4096,256]{1,0:T(8,128)}, f32[4096,256]{1,0:T(8,128)}, u32[]{:S(2)}, u32[]{:S(2)}) collective-permute-start(f32[4096,256]{1,0:T(8,128)} %bitcast.20), channel_id=1, source_target_pairs={{0,8},{8,0},{16,24},{24,16},{1,9},{9,1},{17,25},{25,17},{2,10},{10... | collective-permute-start | bytes 12582920 | tf_op jit(solution)/shard_map/ppermute | solution.py:495
  4.5 7.4 %copy-start.6 = (f32[1,4,4,256,256]{4,3,2,1,0:T(8,128)S(1)}, f32[1,4,4,256,256]{4,3,2,1,0:T(8,128)}, u32[]{:S(2)}) copy-start(f32[1,4,4,256,256]{4,3,2,1,0:T(8,128)} %param.4) | copy-start | bytes 12582916
  4.6 8.7 %copy-start = (f32[2056,256]{1,0:T(8,128)}, f32[2056,256]{1,0:T(8,128)S(1)}, u32[]{:S(2)}) copy-start(f32[2056,256]{1,0:T(8,128)S(1)} %pad_maximum_fusion.1.refs_0_.refs_1_.refs_8_) | copy-start | bytes 6316036
  4.6 49.1 %collective-permute-start.3 = (f32[2056,256]{1,0:T(8,128)S(1)}, f32[2056,256]{1,0:T(8,128)S(1)}, u32[]{:S(2)}, u32[]{:S(2)}) collective-permute-start(f32[2056,256]{1,0:T(8,128)S(1)} %pad_maximum_fusion.1.refs_0_.refs_1_.refs_8_), channel_id=1, source_target_pairs={{0,16},{8,24},{16,0},{24,8},{1,17},{9,25},{17,1},{25,9},{2,18},{10... | collective-permute-start | bytes 6316040 | tf_op jit(solution)/shard_map/ppermute | solution.py:492
  7.2 48.0 %collective-permute-start.2 = (f32[2056,256]{1,0:T(8,128)S(1)}, f32[2056,256]{1,0:T(8,128)}, u32[]{:S(2)}, u32[]{:S(2)}) collective-permute-start(f32[2056,256]{1,0:T(8,128)S(1)} %pad_maximum_fusion.1.refs_0_.refs_1_.refs_8_), channel_id=1, source_target_pairs={{0,1},{1,0},{2,3},{3,2},{4,5},{5,4},{6,7},{7,6},{8,9},{9,8},{10,11... | collective-permute-start | bytes 6316040 | tf_op jit(solution)/shard_map/ppermute | solution.py:492
  8.7 46.6 %collective-permute-start.1 = (f32[2056,256]{1,0:T(8,128)S(1)}, f32[2056,256]{1,0:T(8,128)S(1)}, u32[]{:S(2)}, u32[]{:S(2)}) collective-permute-start(f32[2056,256]{1,0:T(8,128)S(1)} %pad_maximum_fusion.1.refs_0_.refs_1_.refs_8_), channel_id=1, source_target_pairs={{0,8},{1,9},{2,4},{3,5},{4,2},{5,3},{6,14},{7,15},{8,0},{9,1},{10,... | collective-permute-start | bytes 6316040 | tf_op jit(solution)/shard_map/ppermute | solution.py:492
  8.7 48.9 %collective-permute-start = (f32[2056,256]{1,0:T(8,128)S(1)}, f32[2056,256]{1,0:T(8,128)}, u32[]{:S(2)}, u32[]{:S(2)}) collective-permute-start(f32[2056,256]{1,0:T(8,128)S(1)} %pad_maximum_fusion.1.refs_0_.refs_1_.refs_8_), channel_id=1, source_target_pairs={{0,2},{1,3},{2,0},{3,1},{4,6},{5,7},{6,4},{7,5},{8,10},{9,11},{10,... | collective-permute-start | bytes 6316040 | tf_op jit(solution)/shard_map/ppermute | solution.py:492
  53.7 15.2 %copy-start.2 = (f32[2056,256]{1,0:T(8,128)}, f32[2056,256]{1,0:T(8,128)S(1)}, u32[]{:S(2)}) copy-start(f32[2056,256]{1,0:T(8,128)S(1)} %collective-permute-done.3.refs_0_.refs_1_.refs_5_.refs_2_) | copy-start | bytes 6316036
  55.2 13.7 %copy-start.4 = (f32[2056,256]{1,0:T(8,128)}, f32[2056,256]{1,0:T(8,128)S(1)}, u32[]{:S(2)}) copy-start(f32[2056,256]{1,0:T(8,128)S(1)} %collective-permute-done.1.refs_10_.refs_2_) | copy-start | bytes 6316036
  57.6 46.8 %collective-permute-start.5 = (f32[2048,256]{1,0:T(8,128)}, f32[2048,256]{1,0:T(8,128)S(1)}, u32[]{:S(2)}, u32[]{:S(2)}) collective-permute-start(f32[2048,256]{1,0:T(8,128)} %bitcast.25), channel_id=1, source_target_pairs={{0,16},{8,24},{16,0},{24,8},{1,17},{9,25},{17,1},{25,9},{2,18},{10... | collective-permute-start | bytes 6291464 | tf_op jit(solution)/shard_map/ppermute | solution.py:492
  58.1 46.7 %collective-permute-start.4 = (f32[2048,256]{1,0:T(8,128)}, f32[2048,256]{1,0:T(8,128)}, u32[]{:S(2)}, u32[]{:S(2)}) collective-permute-start(f32[2048,256]{1,0:T(8,128)} %bitcast.26), channel_id=1, source_target_pairs={{0,1},{1,0},{2,3},{3,2},{4,5},{5,4},{6,7},{7,6},{8,9},{9,8},{10,11... | collective-permute-start | bytes 6291464 | tf_op jit(solution)/shard_map/ppermute | solution.py:492
  58.6 50.9 %collective-permute-start.7 = (f32[2056,256]{1,0:T(8,128)S(1)}, f32[2056,256]{1,0:T(8,128)}, u32[]{:S(2)}, u32[]{:S(2)}) collective-permute-start(f32[2056,256]{1,0:T(8,128)S(1)} %collective-permute-done.1.refs_10_.refs_2_), channel_id=1, source_target_pairs={{0,2},{1,3},{2,0},{3,1},{4,6},{5,7},{6,4},{7,5},{8,10},{9,11},{10,... | collective-permute-start | bytes 6316040 | tf_op jit(solution)/shard_map/ppermute | solution.py:492
  60.4 49.2 %collective-permute-start.8 = (f32[2056,256]{1,0:T(8,128)}, f32[2056,256]{1,0:T(8,128)}, u32[]{:S(2)}, u32[]{:S(2)}) collective-permute-start(f32[2056,256]{1,0:T(8,128)} %collective-permute-done.refs_9_.refs_1_), channel_id=1, source_target_pairs={{0,8},{1,9},{2,4},{3,5},{4,2},{5,3},{6,14},{7,15},{8,0},{9,1},{10,... | collective-permute-start | bytes 6316040 | tf_op jit(solution)/shard_map/ppermute | solution.py:492
  60.4 49.2 %collective-permute-start.9 = (f32[2056,256]{1,0:T(8,128)}, f32[2056,256]{1,0:T(8,128)}, u32[]{:S(2)}, u32[]{:S(2)}) collective-permute-start(f32[2056,256]{1,0:T(8,128)} %collective-permute-done.2.refs_0_.refs_1_), channel_id=1, source_target_pairs={{0,8},{8,0},{16,24},{24,16},{1,9},{9,1},{17,25},{25,17},{2,10},{10... | collective-permute-start | bytes 6316040 | tf_op jit(solution)/shard_map/ppermute | solution.py:495
  63.6 103.9 %copy-start.11 = (f32[4,4,64,256]{3,2,1,0:T(8,128)}, f32[4,4,64,256]{3,2,1,0:T(8,128)S(1)}, u32[]{:S(2)}) copy-start(f32[4,4,64,256]{3,2,1,0:T(8,128)S(1)} %get-tuple-element.125) | copy-start | bytes 3145732
  104.4 5.1 %copy-start.7 = (f32[2048,256]{1,0:T(8,128)}, f32[2048,256]{1,0:T(8,128)S(1)}, u32[]{:S(2)}) copy-start(f32[2048,256]{1,0:T(8,128)S(1)} %collective-permute-done.5.refs_2_) | copy-start | bytes 6291460
  104.4 5.2 %copy-start.3 = (f32[2056,256]{1,0:T(8,128)S(1)}, f32[2056,256]{1,0:T(8,128)}, u32[]{:S(2)}) copy-start(f32[2056,256]{1,0:T(8,128)} %copy-done.2) | copy-start | bytes 6316036
  109.6 12.8 %collective-permute-start.10 = (f32[4104,256]{1,0:T(8,128)}, f32[4104,256]{1,0:T(8,128)S(1)}, u32[]{:S(2)}, u32[]{:S(2)}) collective-permute-start(f32[4104,256]{1,0:T(8,128)} %pad_maximum_fusion), channel_id=1, source_target_pairs={{0,8},{8,0},{16,24},{24,16},{1,9},{9,1},{17,25},{25,17},{2,10},{10... | collective-permute-start | bytes 12607496 | tf_op jit(solution)/shard_map/ppermute | solution.py:495
  109.7 19.5 %collective-permute-start.11 = (f32[2056,256]{1,0:T(8,128)S(1)}, f32[2056,256]{1,0:T(8,128)}, u32[]{:S(2)}, u32[]{:S(2)}) collective-permute-start(f32[2056,256]{1,0:T(8,128)S(1)} %copy-done.3), channel_id=1, source_target_pairs={{0,8},{8,0},{16,24},{24,16},{1,9},{9,1},{17,25},{25,17},{2,10},{10... | collective-permute-start | bytes 6316040 | tf_op jit(solution)/shard_map/ppermute | solution.py:495
  110.2 49.5 %collective-permute-start.12 = (f32[2056,256]{1,0:T(8,128)}, f32[2056,256]{1,0:T(8,128)}, u32[]{:S(2)}, u32[]{:S(2)}) collective-permute-start(f32[2056,256]{1,0:T(8,128)} %collective-permute-done.2.refs_0_.refs_1_), channel_id=1, source_target_pairs={{0,16},{8,24},{16,0},{24,8},{1,17},{9,25},{17,1},{25,9},{2,18},{10... | collective-permute-start | bytes 6316040 | tf_op jit(solution)/shard_map/ppermute | solution.py:492
  110.8 48.8 %collective-permute-start.13 = (f32[2056,256]{1,0:T(8,128)}, f32[2056,256]{1,0:T(8,128)}, u32[]{:S(2)}, u32[]{:S(2)}) collective-permute-start(f32[2056,256]{1,0:T(8,128)} %collective-permute-done.8.refs_12_.refs_4_), channel_id=1, source_target_pairs={{0,2},{1,3},{2,0},{3,1},{4,6},{5,7},{6,4},{7,5},{8,10},{9,11},{10,... | collective-permute-start | bytes 6316040 | tf_op jit(solution)/shard_map/ppermute | solution.py:492
  112.2 47.4 %collective-permute-start.14 = (f32[2048,256]{1,0:T(8,128)}, f32[2048,256]{1,0:T(8,128)}, u32[]{:S(2)}, u32[]{:S(2)}) collective-permute-start(f32[2048,256]{1,0:T(8,128)} %copy-done.7), channel_id=1, source_target_pairs={{0,1},{1,0},{2,3},{3,2},{4,5},{5,4},{6,7},{7,6},{8,9},{9,8},{10,11... | collective-permute-start | bytes 6291464 | tf_op jit(solution)/shard_map/ppermute | solution.py:492
  159.6 4.4 %collective-permute-start.15 = (f32[2056,256]{1,0:T(8,128)}, f32[2056,256]{1,0:T(8,128)S(1)}, u32[]{:S(2)}, u32[]{:S(2)}) collective-permute-start(f32[2056,256]{1,0:T(8,128)} %collective-permute-done.12.refs_4_.refs_0_.refs_1_), channel_id=1, source_target_pairs={{0,8},{8,0},{16,24},{24,16},{1,9},{9,1},{17,25},{25,17},{2,10},{10... | collective-permute-start | bytes 6316040 | tf_op jit(solution)/shard_map/ppermute | solution.py:495
  164.0 9.7 %copy-start.5 = (f32[2056,256]{1,0:T(8,128)}, f32[2056,256]{1,0:T(8,128)S(1)}, u32[]{:S(2)}) copy-start(f32[2056,256]{1,0:T(8,128)S(1)} %collective-permute-done.15.refs_6_.refs_0_.refs_1_) | copy-start | bytes 6316036
  164.0 17.6 %collective-permute-start.16 = (f32[2048,256]{1,0:T(8,128)}, f32[2048,256]{1,0:T(8,128)}, u32[]{:S(2)}, u32[]{:S(2)}) collective-permute-start(f32[2048,256]{1,0:T(8,128)} %collective-permute-done.14.refs_2_), channel_id=1, source_target_pairs={{0,8},{8,0},{16,24},{24,16},{1,9},{9,1},{17,25},{25,17},{2,10},{10... | collective-permute-start | bytes 6291464 | tf_op jit(solution)/shard_map/ppermute | solution.py:495
  164.1 42.2 %collective-permute-start.18 = (f32[1024,256]{1,0:T(8,128)}, f32[1024,256]{1,0:T(8,128)}, u32[]{:S(2)}, u32[]{:S(2)}) collective-permute-start(f32[1024,256]{1,0:T(8,128)} %bitcast.9.refs_0_), channel_id=1, source_target_pairs={{0,8},{1,9},{2,4},{3,5},{4,2},{5,3},{6,14},{7,15},{8,0},{9,1},{10,... | collective-permute-start | bytes 3145736 | tf_op jit(solution)/shard_map/ppermute | solution.py:492
  164.5 41.9 %collective-permute-start.17 = (f32[1024,256]{1,0:T(8,128)}, f32[1024,256]{1,0:T(8,128)}, u32[]{:S(2)}, u32[]{:S(2)}) collective-permute-start(f32[1024,256]{1,0:T(8,128)} %bitcast.9.refs_0_), channel_id=1, source_target_pairs={{0,2},{1,3},{2,0},{3,1},{4,6},{5,7},{6,4},{7,5},{8,10},{9,11},{10,... | collective-permute-start | bytes 3145736 | tf_op jit(solution)/shard_map/ppermute | solution.py:492
  167.5 38.9 %collective-permute-start.20 = (f32[1024,256]{1,0:T(8,128)S(1)}, f32[1024,256]{1,0:T(8,128)}, u32[]{:S(2)}, u32[]{:S(2)}) collective-permute-start(f32[1024,256]{1,0:T(8,128)S(1)} %bitcast.29), channel_id=1, source_target_pairs={{0,8},{1,9},{2,4},{3,5},{4,2},{5,3},{6,14},{7,15},{8,0},{9,1},{10,... | collective-permute-start | bytes 3145736 | tf_op jit(solution)/shard_map/ppermute | solution.py:492
  167.6 46.2 %collective-permute-start.19 = (f32[1024,256]{1,0:T(8,128)S(1)}, f32[1024,256]{1,0:T(8,128)}, u32[]{:S(2)}, u32[]{:S(2)}) collective-permute-start(f32[1024,256]{1,0:T(8,128)S(1)} %bitcast.30), channel_id=1, source_target_pairs={{0,2},{1,3},{2,0},{3,1},{4,6},{5,7},{6,4},{7,5},{8,10},{9,11},{10,... | collective-permute-start | bytes 3145736 | tf_op jit(solution)/shard_map/ppermute | solution.py:492
  213.7 24.8 %collective-permute-start.21 = (f32[4,4,64,256]{3,2,1,0:T(8,128)}, f32[4,4,64,256]{3,2,1,0:T(8,128)S(1)}, u32[]{:S(2)}, u32[]{:S(2)}) collective-permute-start(f32[4,4,64,256]{3,2,1,0:T(8,128)} %get-tuple-element.101), channel_id=1, source_target_pairs={{0,1},{1,0},{2,3},{3,2},{4,5},{5,4},{6,7},{7,6},{8,9},{9,8},{10,11... | collective-permute-start | bytes 3145736 | tf_op jit(solution)/shard_map/ppermute | solution.py:492
  214.3 24.6 %collective-permute-start.23 = (f32[1024,256]{1,0:T(8,128)}, f32[1024,256]{1,0:T(8,128)S(1)}, u32[]{:S(2)}, u32[]{:S(2)}) collective-permute-start(f32[1024,256]{1,0:T(8,128)} %collective-permute-done.18.refs_2_), channel_id=1, source_target_pairs={{0,2},{1,3},{2,0},{3,1},{4,6},{5,7},{6,4},{7,5},{8,10},{9,11},{10,... | collective-permute-start | bytes 3145736 | tf_op jit(solution)/shard_map/ppermute | solution.py:492
  216.0 22.8 %collective-permute-start.24 = (f32[1024,256]{1,0:T(8,128)}, f32[1024,256]{1,0:T(8,128)S(1)}, u32[]{:S(2)}, u32[]{:S(2)}) collective-permute-start(f32[1024,256]{1,0:T(8,128)} %collective-permute-done.17.refs_1_), channel_id=1, source_target_pairs={{0,8},{1,9},{2,4},{3,5},{4,2},{5,3},{6,14},{7,15},{8,0},{9,1},{10,... | collective-permute-start | bytes 3145736 | tf_op jit(solution)/shard_map/ppermute | solution.py:492
  238.6 3.5 copy-start.26
  238.8 7.6 %copy-start.24 = (f32[1024,256]{1,0:T(8,128)}, f32[1024,256]{1,0:T(8,128)S(1)}, u32[]{:S(2)}) copy-start(f32[1024,256]{1,0:T(8,128)S(1)} %collective-permute-done.23.refs_3_) | copy-start | bytes 3145732
  238.8 7.6 %copy-start.22 = (f32[1024,256]{1,0:T(8,128)}, f32[1024,256]{1,0:T(8,128)S(1)}, u32[]{:S(2)}) copy-start(f32[1024,256]{1,0:T(8,128)S(1)} %collective-permute-done.24.refs_4_) | copy-start | bytes 3145732
  238.8 23.9 %collective-permute-start.27 = (f32[4,4,64,256]{3,2,1,0:T(8,128)}, f32[4,4,64,256]{3,2,1,0:T(8,128)S(1)}, u32[]{:S(2)}, u32[]{:S(2)}) collective-permute-start(f32[4,4,64,256]{3,2,1,0:T(8,128)} %get-tuple-element.107), channel_id=1, source_target_pairs={{0,1},{1,0},{2,3},{3,2},{4,5},{5,4},{6,7},{7,6},{8,9},{9,8},{10,11... | collective-permute-start | bytes 3145736 | tf_op jit(solution)/shard_map/ppermute | solution.py:492
  240.4 26.1 %collective-permute-start.29 = (f32[1024,256]{1,0:T(8,128)S(1)}, f32[1024,256]{1,0:T(8,128)S(1)}, u32[]{:S(2)}, u32[]{:S(2)}) collective-permute-start(f32[1024,256]{1,0:T(8,128)S(1)} %collective-permute-done.24.refs_4_), channel_id=1, source_target_pairs={{0,2},{1,3},{2,0},{3,1},{4,6},{5,7},{6,4},{7,5},{8,10},{9,11},{10,... | collective-permute-start | bytes 3145736 | tf_op jit(solution)/shard_map/ppermute | solution.py:492
  244.7 41.3 %collective-permute-start.25 = (f32[4,264,256]{2,1,0:T(8,128)}, f32[4,264,256]{2,1,0:T(8,128)S(1)}, u32[]{:S(2)}, u32[]{:S(2)}) collective-permute-start(f32[4,264,256]{2,1,0:T(8,128)} %inflate.4.refs_4_), channel_id=1, source_target_pairs={{0,16},{8,24},{16,0},{24,8},{1,17},{9,25},{17,1},{25,9},{2,18},{10... | collective-permute-start | bytes 3244040 | tf_op jit(solution)/shard_map/ppermute | solution.py:492
  246.1 39.9 %collective-permute-start.30 = (f32[1024,256]{1,0:T(8,128)}, f32[1024,256]{1,0:T(8,128)S(1)}, u32[]{:S(2)}, u32[]{:S(2)}) collective-permute-start(f32[1024,256]{1,0:T(8,128)} %collective-permute-done.20.refs_2_), channel_id=1, source_target_pairs={{0,2},{1,3},{2,0},{3,1},{4,6},{5,7},{6,4},{7,5},{8,10},{9,11},{10,... | collective-permute-start | bytes 3145736 | tf_op jit(solution)/shard_map/ppermute | solution.py:492
  246.4 39.6 %collective-permute-start.31 = (f32[1024,256]{1,0:T(8,128)}, f32[1024,256]{1,0:T(8,128)S(1)}, u32[]{:S(2)}, u32[]{:S(2)}) collective-permute-start(f32[1024,256]{1,0:T(8,128)} %collective-permute-done.19.refs_1_), channel_id=1, source_target_pairs={{0,8},{1,9},{2,4},{3,5},{4,2},{5,3},{6,14},{7,15},{8,0},{9,1},{10,... | collective-permute-start | bytes 3145736 | tf_op jit(solution)/shard_map/ppermute | solution.py:492
  267.5 18.6 %copy-start.9 = (f32[4,264,256]{2,1,0:T(8,128)S(1)}, f32[4,264,256]{2,1,0:T(8,128)}, u32[]{:S(2)}) copy-start(f32[4,264,256]{2,1,0:T(8,128)} %inflate.5.refs_8_) | copy-start | bytes 3244036
  286.0 3.4 copy-start.23
  286.0 3.4 copy-start.21
  286.0 38.5 %copy-start.12 = (f32[4,264,256]{2,1,0:T(8,128)}, f32[4,264,256]{2,1,0:T(8,128)S(1)}, u32[]{:S(2)}) copy-start(f32[4,264,256]{2,1,0:T(8,128)S(1)} %collective-permute-done.25.refs_6_) | copy-start | bytes 3244036
  286.0 27.2 %collective-permute-start.32 = (f32[4,264,256]{2,1,0:T(8,128)S(1)}, f32[4,264,256]{2,1,0:T(8,128)S(1)}, u32[]{:S(2)}, u32[]{:S(2)}) collective-permute-start(f32[4,264,256]{2,1,0:T(8,128)S(1)} %copy-done.9), channel_id=1, source_target_pairs={{0,16},{8,24},{16,0},{24,8},{1,17},{9,25},{17,1},{25,9},{2,18},{10... | collective-permute-start | bytes 3244040 | tf_op jit(solution)/shard_map/ppermute | solution.py:492
  287.5 22.1 %collective-permute-start.34 = (f32[4,4,64,256]{3,2,1,0:T(8,128)}, f32[4,4,64,256]{3,2,1,0:T(8,128)S(1)}, u32[]{:S(2)}, u32[]{:S(2)}) collective-permute-start(f32[4,4,64,256]{3,2,1,0:T(8,128)} %get-tuple-element.116), channel_id=1, source_target_pairs={{0,1},{1,0},{2,3},{3,2},{4,5},{5,4},{6,7},{7,6},{8,9},{9,8},{10,11... | collective-permute-start | bytes 3145736 | tf_op jit(solution)/shard_map/ppermute | solution.py:599
  288.1 25.8 %collective-permute-start.38 = (f32[1024,256]{1,0:T(8,128)S(1)}, f32[1024,256]{1,0:T(8,128)S(1)}, u32[]{:S(2)}, u32[]{:S(2)}) collective-permute-start(f32[1024,256]{1,0:T(8,128)S(1)} %collective-permute-done.31.refs_4_), channel_id=1, source_target_pairs={{0,2},{1,3},{2,0},{3,1},{4,6},{5,7},{6,4},{7,5},{8,10},{9,11},{10,... | collective-permute-start | bytes 3145736 | tf_op jit(solution)/shard_map/ppermute | solution.py:492
  313.2 35.6 %copy-start.13 = (f32[4,264,256]{2,1,0:T(8,128)}, f32[4,264,256]{2,1,0:T(8,128)S(1)}, u32[]{:S(2)}) copy-start(f32[4,264,256]{2,1,0:T(8,128)S(1)} %collective-permute-done.32.refs_10_) | copy-start | bytes 3244036
  313.2 34.2 %collective-permute-start.36 = (f32[4,264,256]{2,1,0:T(8,128)}, f32[4,264,256]{2,1,0:T(8,128)S(1)}, u32[]{:S(2)}, u32[]{:S(2)}) collective-permute-start(f32[4,264,256]{2,1,0:T(8,128)} %inflate.6.refs_12_), channel_id=1, source_target_pairs={{0,16},{8,24},{16,0},{24,8},{1,17},{9,25},{17,1},{25,9},{2,18},{10... | collective-permute-start | bytes 3244040 | tf_op jit(solution)/shard_map/ppermute | solution.py:605
  314.9 9.1 %copy-start.8 = (f32[4,264,256]{2,1,0:T(8,128)S(1)}, f32[4,264,256]{2,1,0:T(8,128)}, u32[]{:S(2)}) copy-start(f32[4,264,256]{2,1,0:T(8,128)} %inflate.4.refs_4_) | copy-start | bytes 3244036
  323.7 25.1 %copy-start.10 = (f32[4,264,256]{2,1,0:T(8,128)S(1)}, f32[4,264,256]{2,1,0:T(8,128)}, u32[]{:S(2)}) copy-start(f32[4,264,256]{2,1,0:T(8,128)} %inflate.6.refs_12_) | copy-start | bytes 3244036
  323.7 21.1 %collective-permute-start.39 = (f32[4,4,64,256]{3,2,1,0:T(8,128)}, f32[4,4,64,256]{3,2,1,0:T(8,128)}, u32[]{:S(2)}, u32[]{:S(2)}) collective-permute-start(f32[4,4,64,256]{3,2,1,0:T(8,128)} %get-tuple-element.123), channel_id=1, source_target_pairs={{0,1},{1,0},{2,3},{3,2},{4,5},{5,4},{6,7},{7,6},{8,9},{9,8},{10,11... | collective-permute-start | bytes 3145736 | tf_op jit(solution)/shard_map/ppermute | solution.py:599
  324.0 24.8 %collective-permute-start.22 = (f32[4,264,256]{2,1,0:T(8,128)S(1)}, f32[4,264,256]{2,1,0:T(8,128)S(1)}, u32[]{:S(2)}, u32[]{:S(2)}) collective-permute-start(f32[4,264,256]{2,1,0:T(8,128)S(1)} %copy-done.8), channel_id=1, source_target_pairs={{0,8},{8,0},{16,24},{24,16},{1,9},{9,1},{17,25},{25,17},{2,10},{10... | collective-permute-start | bytes 3244040 | tf_op jit(solution)/shard_map/ppermute | solution.py:588
  324.0 25.4 %collective-permute-start.28 = (f32[4,264,256]{2,1,0:T(8,128)S(1)}, f32[4,264,256]{2,1,0:T(8,128)}, u32[]{:S(2)}, u32[]{:S(2)}) collective-permute-start(f32[4,264,256]{2,1,0:T(8,128)S(1)} %copy-done.9), channel_id=1, source_target_pairs={{0,8},{8,0},{16,24},{24,16},{1,9},{9,1},{17,25},{25,17},{2,10},{10... | collective-permute-start | bytes 3244040 | tf_op jit(solution)/shard_map/ppermute | solution.py:588
  324.5 25.0 %collective-permute-start.26 = (f32[4,264,256]{2,1,0:T(8,128)S(1)}, f32[4,264,256]{2,1,0:T(8,128)}, u32[]{:S(2)}, u32[]{:S(2)}) collective-permute-start(f32[4,264,256]{2,1,0:T(8,128)S(1)} %collective-permute-done.25.refs_6_), channel_id=1, source_target_pairs={{0,8},{8,0},{16,24},{24,16},{1,9},{9,1},{17,25},{25,17},{2,10},{10... | collective-permute-start | bytes 3244040 | tf_op jit(solution)/shard_map/ppermute | solution.py:588
  347.4 23.6 %copy-start.14 = (f32[4,264,256]{2,1,0:T(8,128)}, f32[4,264,256]{2,1,0:T(8,128)S(1)}, u32[]{:S(2)}) copy-start(f32[4,264,256]{2,1,0:T(8,128)S(1)} %collective-permute-done.36.refs_14_) | copy-start | bytes 3244036
  347.4 20.7 %collective-permute-start.41 = (f32[4,264,256]{2,1,0:T(8,128)}, f32[4,264,256]{2,1,0:T(8,128)S(1)}, u32[]{:S(2)}, u32[]{:S(2)}) collective-permute-start(f32[4,264,256]{2,1,0:T(8,128)} %inflate.7.refs_16_), channel_id=1, source_target_pairs={{0,16},{8,24},{16,0},{24,8},{1,17},{9,25},{17,1},{25,9},{2,18},{10... | collective-permute-start | bytes 3244040 | tf_op jit(solution)/shard_map/ppermute | solution.py:605
  348.8 19.3 %collective-permute-start.35 = (f32[4,264,256]{2,1,0:T(8,128)S(1)}, f32[4,264,256]{2,1,0:T(8,128)S(1)}, u32[]{:S(2)}, u32[]{:S(2)}) collective-permute-start(f32[4,264,256]{2,1,0:T(8,128)S(1)} %copy-done.10), channel_id=1, source_target_pairs={{0,8},{8,0},{16,24},{24,16},{1,9},{9,1},{17,25},{25,17},{2,10},{10... | collective-permute-start | bytes 3244040 | tf_op jit(solution)/shard_map/ppermute | solution.py:606
  348.8 22.2 %copy-start.15 = (f32[4,264,256]{2,1,0:T(8,128)}, f32[4,264,256]{2,1,0:T(8,128)S(1)}, u32[]{:S(2)}) copy-start(f32[4,264,256]{2,1,0:T(8,128)S(1)} %collective-permute-done.22.refs_5_) | copy-start | bytes 3244036
  348.8 19.3 %collective-permute-start.33 = (f32[4,264,256]{2,1,0:T(8,128)S(1)}, f32[4,264,256]{2,1,0:T(8,128)S(1)}, u32[]{:S(2)}, u32[]{:S(2)}) collective-permute-start(f32[4,264,256]{2,1,0:T(8,128)S(1)} %collective-permute-done.32.refs_10_), channel_id=1, source_target_pairs={{0,8},{8,0},{16,24},{24,16},{1,9},{9,1},{17,25},{25,17},{2,10},{10... | collective-permute-start | bytes 3244040 | tf_op jit(solution)/shard_map/ppermute | solution.py:588
  349.4 18.8 %collective-permute-start.40 = (f32[4,264,256]{2,1,0:T(8,128)}, f32[4,264,256]{2,1,0:T(8,128)S(1)}, u32[]{:S(2)}, u32[]{:S(2)}) collective-permute-start(f32[4,264,256]{2,1,0:T(8,128)} %inflate.7.refs_16_), channel_id=1, source_target_pairs={{0,8},{8,0},{16,24},{24,16},{1,9},{9,1},{17,25},{25,17},{2,10},{10... | collective-permute-start | bytes 3244040 | tf_op jit(solution)/shard_map/ppermute | solution.py:606
  349.5 18.7 %collective-permute-start.37 = (f32[4,264,256]{2,1,0:T(8,128)S(1)}, f32[4,264,256]{2,1,0:T(8,128)S(1)}, u32[]{:S(2)}, u32[]{:S(2)}) collective-permute-start(f32[4,264,256]{2,1,0:T(8,128)S(1)} %collective-permute-done.36.refs_14_), channel_id=1, source_target_pairs={{0,8},{8,0},{16,24},{24,16},{1,9},{9,1},{17,25},{25,17},{2,10},{10... | collective-permute-start | bytes 3244040 | tf_op jit(solution)/shard_map/ppermute | solution.py:606
  368.2 2.8 collective-permute-start.42
  368.2 2.8 copy-start.18
  (10 other events, 13.2 us)

commit v8 on v7

--- a/solution.py
+++ b/solution.py
@@ -74,6 +74,37 @@
         cost_estimate=pl.CostEstimate(flops=size, bytes_accessed=8 * size, transcendentals=0),
         name="place",
     )(*args)
+
+
+def join_kernel(firsts, *refs):
+    out_ref, sems = refs[-2:]
+    start, copies = 0, []
+    for i, (first, x_ref) in enumerate(zip(firsts, refs)):
+        rows = x_ref.shape[0] - first
+        to = out_ref.at[start : start + rows]
+        copies.append(pltpu.make_async_copy(x_ref.at[first : first + rows], to, sems.at[i]))
+        start += rows
+    for copy in copies:
+        copy.start()
+    for copy in copies:
+        copy.wait()
+
+
+def join(*parts):
+    arrays, firsts = zip(*parts)
+    rows = sum(x.shape[0] - first for x, first in parts)
+    return pl.pallas_call(
+        functools.partial(join_kernel, firsts),
+        out_shape=jax.ShapeDtypeStruct((rows, arrays[0].shape[1]), arrays[0].dtype),
+        in_specs=[pl.BlockSpec(memory_space=pl.ANY)] * len(parts),
+        out_specs=pl.BlockSpec(memory_space=pl.ANY),
+        scratch_shapes=[pltpu.SemaphoreType.DMA((len(parts),))],
+        compiler_params=pltpu.CompilerParams(vmem_limit_bytes=VMEM),
+        cost_estimate=pl.CostEstimate(
+            flops=0, bytes_accessed=8 * rows * arrays[0].shape[1], transcendentals=0
+        ),
+        name="join",
+    )(*arrays)
 
 
 def plan_kernel(line, blocks, count, me_ref, *refs):
@@ -556,7 +587,7 @@
         if tick == 2:
             diagonal, diagonal_rest = send(2, across, b_pair), send(2, pair, across_rest)
             core_across = swap(2, b_across)
-            core_rest = swap(2, jnp.concatenate([pair_rest, across_rest, own[0][upper:]]))
+            core_rest = swap(2, join((pair_rest, 0), (across_rest, 0), (own[0], upper)))
             put(2, 0, 0, *halves(b_pair, pair_rest))
             put(2, 1, 2, *halves(b_across, across_rest))
             put(2, 0, 1, *halves(core_pair, core_rest))

time: 380 us -> 506 us (1.33)
  Pallas kernels: 155 us -> 280 us
  waiting for transfers between devices: 170 us -> 176 us
    pallas_call x0 -> x1, Pallas kernels: none -> 128 us  [join(): pl.pallas_call(functools.partial(join_kernel, firsts), out_shape=jax.Shap...]
    ppermute x25, waiting for transfers between devices: 121 us -> 127 us  [send(): return at(tick, move(after(tick, x), *more))]
  transfers between devices with their start and end apart: 43 -> 43, of which waited for: 16 -> 17; matrix products, arithmetic and copies ran while one was open for 3% -> 2% of each run, Pallas kernels for 39% -> 54%
where the time goes in v8:
time: 506 us; the launch traced here: 504 us
  Pallas kernels  280 us (55%)
  waiting for transfers between devices  176 us (35%)
  starting transfers between devices  30.8 us (6%)
  local copies, waits for them, and re-layouts  16.3 us (3%)
    pallas_call x1, Pallas kernels, join(): pl.pallas_call(functools.partial(join_kernel, firsts), out_shape=jax.Shap...  128 us
    ppermute x25, waiting for transfers between devices, send(): return at(tick, move(after(tick, x), *more))  127 us
    pallas_call x6, Pallas kernels, product(): pl.pallas_call(functools.partial(product_kernel, line, which, arrivals, p...  88.1 us
    pallas_call x8, Pallas kernels, place(): pl.pallas_call(functools.partial(place_kernel, len(parts)), grid=(blocks,...  39 us
    ppermute x25, starting transfers between devices, send(): return at(tick, move(after(tick, x), *more))  24.8 us
    ppermute x2, waiting for transfers between devices, on_device(): others = [pair(tie(x, other)) for x in theirs]  24.7 us
    ppermute x2, waiting for transfers between devices, on_device(): opposite = across(tie(x, opposite))  18.1 us
    pallas_call x4, Pallas kernels, inflate(): pl.pallas_call(inflate_kernel, out_shape=jax.ShapeDtypeStruct((blocks, co...  10.6 us
  transfers between devices with their start and end apart: 43, of which 17 were waited for; matrix products, arithmetic and copies ran while one was open for 2% of the time, Pallas kernels for 54%

profile of v8, /device:TPU:0, one launch (start us, length us, event | category | flops | bytes accessed | tf_op | source)
XLA Modules:
  0.0 504.3 jit_solution(982959515354339273)
XLA Ops:
  0.5 0.8 reshape.28
  1.2 0.8 reshape.29
  2.0 1.7 slice.16
  4.6 2.6 collective-permute-start.3
  7.2 1.5 collective-permute-start.2
  8.7 3.1 collective-permute-start
  11.8 1.5 slice.13
  13.3 4.8 place.8
  18.1 35.6 %collective-permute-done.3.refs_0_.refs_1_.refs_5_.refs_2_ = f32[2056,256]{1,0:T(8,128)S(1)} collective-permute-done((f32[2056,256]{1,0:T(8,128)S(1)}, f32[2056,256]{1,0:T(8,128)S(1)}, u32[]{:S(2)}, u32[]{:S(2)}) %collective-permute-start.3) | collective-permute-done | bytes 2105376 | tf_op jit(solution)/shard_map/ppermute | solution.py:523
  53.7 1.6 collective-permute-done.2.refs_0_.refs_1_
  55.2 2.3 collective-permute-done.refs_9_.refs_1_
  57.6 1.7 collective-permute-start.7
  60.4 0.5 collective-permute-start.4
  60.9 2.7 fusion
  63.6 5.3 %place.9 = (bf16[2,4,4,4,2,256,256]{6,5,4,3,2,1,0:T(8,128)(2,1)}, f32[8,128]{1,0:T(8,128)}) custom-call(f32[4096,256]{1,0:T(8,128)} %collective-permute-done.6.refs_0_, bf16[2,4,4,4,2,256,256]{6,5,4,3,2,1,0:T(8,128)(2,1)} %get-tuple-element.71.refs_1_), custom_call_target="tpu_custom_call", output_to_operand_aliasing={{0}: (1, {})} | custom-call | flops 1048576 | bytes 8388608 | tf_op jit(solution)/shard_map/place/pallas_call | solution.py:61
  68.9 38.7 %collective-permute-done.5.refs_1_.refs_2_ = f32[2048,256]{1,0:T(8,128)S(1)} collective-permute-done((f32[2048,256]{1,0:T(8,128)}, f32[2048,256]{1,0:T(8,128)S(1)}, u32[]{:S(2)}, u32[]{:S(2)}) %collective-permute-start.5) | collective-permute-done | bytes 2097184 | tf_op jit(solution)/shard_map/ppermute | solution.py:523
  107.9 1.0 copy-done.7
  108.9 128.4 %join.1 = f32[4104,256]{1,0:T(8,128)} custom-call(f32[2048,256]{1,0:T(8,128)} %collective-permute-done.4.refs_0_.refs_2_, f32[2048,256]{1,0:T(8,128)} %copy-done.7, f32[2056,256]{1,0:T(8,128)} %copy-done), custom_call_target="tpu_custom_call" | custom-call | bytes 8404992 | tf_op jit(solution)/shard_map/join/pallas_call | solution.py:96
  238.0 0.5 collective-permute-start.12
  238.5 2.4 collective-permute-start.13
  241.4 4.8 place.10
  246.2 4.8 place.11
  251.0 2.0 copy-done.1
  253.1 4.8 place.12
  257.9 4.8 place.13
  262.7 25.6 %collective-permute-done.14.refs_2_ = f32[2048,256]{1,0:T(8,128)} collective-permute-done((f32[2048,256]{1,0:T(8,128)}, f32[2048,256]{1,0:T(8,128)}, u32[]{:S(2)}, u32[]{:S(2)}) %collective-permute-start.14) | collective-permute-done | bytes 2097184 | tf_op jit(solution)/shard_map/ppermute | solution.py:523
  288.3 4.4 collective-permute-done.15.refs_6_.refs_0_.refs_1_
  293.4 1.9 collective-permute-start.19
  295.3 0.6 pad_add_fusion.me_ref
  295.9 4.8 place.14
  300.7 7.9 %plan.1 = (s32[3312]{0:T(1024)}, s32[192]{0:T(256)}) custom-call(s32[2]{0:T(128)} %pad_add_fusion.me_ref, f32[2056,256]{1,0:T(8,128)} %collective-permute-done.2.refs_0_.refs_1_, f32[2056,256]{1,0:T(8,128)} %copy-done, f32[2056,256]{1,0:T(8,128)} %collective-permute-done.9.refs_0_.refs_1_.refs_2_, f32[4104,256]{1,0:T(8,128)} %copy-done.1, ...), custom_call_target="tpu_custom_call" | custom-call | tf_op jit(solution)/shard_map/plan/pallas_call | solution.py:185
  308.6 4.9 place.15
  313.6 19.4 %product.6 = (f32[4,4,64,256]{3,2,1,0:T(8,128)}, f32[4,4,64,256]{3,2,1,0:T(8,128)}) custom-call(s32[2]{0:T(128)} %pad_add_fusion.me_ref, s32[3312]{0:T(1024)} %get-tuple-element.88.plan_ref, s32[192]{0:T(256)} %get-tuple-element.89.kept_ref, bf16[128,2,256,256]{3,2,1,0:T(8,128)(2,1)} %bitcast.14, f32[2056,256]{1,0:T(8,128)} %copy-done, ...), custom_call_target="tpu_custom_call" | custom-call | flops 6442450944 | bytes 16777216 | tf_op jit(solution)/shard_map/product/pallas_call | solution.py:320
  333.0 8.2 %collective-permute-done.19.refs_1_ = f32[1024,256]{1,0:T(8,128)} collective-permute-done((f32[1024,256]{1,0:T(8,128)S(1)}, f32[1024,256]{1,0:T(8,128)}, u32[]{:S(2)}, u32[]{:S(2)}) %collective-permute-start.19) | collective-permute-done | bytes 1048608 | tf_op jit(solution)/shard_map/ppermute | solution.py:523
  342.0 19.4 %product.7 = (f32[4,4,64,256]{3,2,1,0:T(8,128)}, f32[4,4,64,256]{3,2,1,0:T(8,128)}) custom-call(s32[2]{0:T(128)} %pad_add_fusion.me_ref, s32[3312]{0:T(1024)} %get-tuple-element.88.plan_ref, s32[192]{0:T(256)} %get-tuple-element.89.kept_ref, bf16[128,2,256,256]{3,2,1,0:T(8,128)(2,1)} %bitcast.15, f32[2056,256]{1,0:T(8,128)} %copy-done, ...), custom_call_target="tpu_custom_call" | custom-call | flops 6442450944 | bytes 16777216 | tf_op jit(solution)/shard_map/product/pallas_call | solution.py:320
  361.4 4.3 collective-permute-done.21.other_ref
  366.0 1.6 collective-permute-start.27
  367.6 1.7 collective-permute-start.29
  369.3 2.6 inflate.4.refs_4_
  371.9 1.5 collective-permute-start.25
  373.8 15.5 %product.8 = (f32[4,4,64,256]{3,2,1,0:T(8,128)}, f32[4,4,64,256]{3,2,1,0:T(8,128)}) custom-call(s32[2]{0:T(128)} %pad_add_fusion.me_ref, s32[3312]{0:T(1024)} %get-tuple-element.88.plan_ref, s32[192]{0:T(256)} %get-tuple-element.89.kept_ref, bf16[128,2,256,256]{3,2,1,0:T(8,128)(2,1)} %bitcast.16, f32[1024,256]{1,0:T(8,128)} %bitcast.9.refs_0_, ...), custom_call_target="tpu_custom_call" | custom-call | flops 5368709120 | bytes 13981013 | tf_op jit(solution)/shard_map/product/pallas_call | solution.py:320
  389.5 1.0 copy-done.27
  390.5 2.7 inflate.5.refs_8_
  393.7 1.0 copy-done.25
  394.7 9.2 %product.9 = (f32[4,4,64,256]{3,2,1,0:T(8,128)}, f32[4,4,64,256]{3,2,1,0:T(8,128)}) custom-call(s32[2]{0:T(128)} %pad_add_fusion.me_ref, s32[3312]{0:T(1024)} %get-tuple-element.88.plan_ref, s32[192]{0:T(256)} %get-tuple-element.89.kept_ref, bf16[128,2,256,256]{3,2,1,0:T(8,128)(2,1)} %bitcast.17, f32[1024,256]{1,0:T(8,128)} %copy-done.25, ...), custom_call_target="tpu_custom_call" | custom-call | flops 1073741824 | bytes 2796202 | tf_op jit(solution)/shard_map/product/pallas_call | solution.py:320
  403.9 9.1 %collective-permute-done.30.refs_3_ = f32[1024,256]{1,0:T(8,128)S(1)} collective-permute-done((f32[1024,256]{1,0:T(8,128)}, f32[1024,256]{1,0:T(8,128)S(1)}, u32[]{:S(2)}, u32[]{:S(2)}) %collective-permute-start.30) | collective-permute-done | bytes 1048608 | tf_op jit(solution)/shard_map/ppermute | solution.py:523
  413.0 1.6 collective-permute-start.32
  414.5 0.6 collective-permute-start.34
  415.1 1.4 collective-permute-start.38
  416.5 15.5 %product.10 = (f32[4,4,64,256]{3,2,1,0:T(8,128)}, f32[4,4,64,256]{3,2,1,0:T(8,128)}) custom-call(s32[2]{0:T(128)} %pad_add_fusion.me_ref, s32[3312]{0:T(1024)} %get-tuple-element.88.plan_ref, s32[192]{0:T(256)} %get-tuple-element.89.kept_ref, bf16[128,2,256,256]{3,2,1,0:T(8,128)(2,1)} %bitcast.18, f32[1024,256]{1,0:T(8,128)} %bitcast.31, ...), custom_call_target="tpu_custom_call" | custom-call | flops 5368709120 | bytes 13981013 | tf_op jit(solution)/shard_map/product/pallas_call | solution.py:320
  431.9 4.5 collective-permute-done.34.other_ref
  436.4 1.0 copy-done.29
  437.4 2.6 inflate.6.refs_12_
  440.0 0.5 collective-permute-start.36
  440.6 1.0 copy-done.28
  441.6 9.2 %product.11 = (f32[4,4,64,256]{3,2,1,0:T(8,128)}, f32[4,4,64,256]{3,2,1,0:T(8,128)}) custom-call(s32[2]{0:T(128)} %pad_add_fusion.me_ref, s32[3312]{0:T(1024)} %get-tuple-element.88.plan_ref, s32[192]{0:T(256)} %get-tuple-element.89.kept_ref, bf16[128,2,256,256]{3,2,1,0:T(8,128)(2,1)} %bitcast.19, f32[1024,256]{1,0:T(8,128)} %copy-done.28, ...), custom_call_target="tpu_custom_call" | custom-call | flops 1073741824 | bytes 2796202 | tf_op jit(solution)/shard_map/product/pallas_call | solution.py:320
  451.5 20.2 %collective-permute-done.39.other_ref = f32[4,4,64,256]{3,2,1,0:T(8,128)} collective-permute-done((f32[4,4,64,256]{3,2,1,0:T(8,128)}, f32[4,4,64,256]{3,2,1,0:T(8,128)}, u32[]{:S(2)}, u32[]{:S(2)}) %collective-permute-start.39) | collective-permute-done | bytes 1048608 | tf_op jit(solution)/shard_map/ppermute | solution.py:630
  471.8 2.6 inflate.7.refs_16_
  474.4 1.4 collective-permute-start.41
  475.8 0.6 collective-permute-start.33
  476.9 18.1 %collective-permute-done.41.refs_18_ = f32[4,264,256]{2,1,0:T(8,128)S(1)} collective-permute-done((f32[4,264,256]{2,1,0:T(8,128)}, f32[4,264,256]{2,1,0:T(8,128)S(1)}, u32[]{:S(2)}, u32[]{:S(2)}) %collective-permute-start.41) | collective-permute-done | bytes 1081376 | tf_op jit(solution)/shard_map/ppermute | solution.py:636
  495.0 0.9 copy-done.16
  496.3 1.5 collective-permute-done.42.refs_19_
  497.8 6.4 %owned.1 = f32[32,256,256]{2,1,0:T(8,128)} custom-call(s32[2]{0:T(128)} %pad_add_fusion.me_ref, f32[2056,256]{1,0:T(8,128)} %copy-done, f32[4104,256]{1,0:T(8,128)} %copy-done.1, f32[2056,256]{1,0:T(8,128)} %copy-done.2, f32[2056,256]{1,0:T(8,128)} %collective-permute-done.11.refs_0_.refs_1_.refs_7_.refs_3_, f32[4,264,256]{2,1,0:T(8,128)} %inflate.4.refs_4_, ...), custom_call_target="tpu_custom_call" | custom-call | flops 2097152 | bytes 16777216 | tf_op jit(solution)/shard_map/owned/pallas_call | solution.py:446
  (116 shorter events, 8.5 us)
Async XLA Ops:
  0.0 60.3 %collective-permute-start.6 = (f32[4096,256]{1,0:T(8,128)}, f32[4096,256]{1,0:T(8,128)}, u32[]{:S(2)}, u32[]{:S(2)}) collective-permute-start(f32[4096,256]{1,0:T(8,128)} %bitcast.20), channel_id=1, source_target_pairs={{0,8},{8,0},{16,24},{24,16},{1,9},{9,1},{17,25},{25,17},{2,10},{10... | collective-permute-start | bytes 12582920 | tf_op jit(solution)/shard_map/ppermute | solution.py:526
  4.5 7.4 %copy-start.6 = (f32[1,4,4,256,256]{4,3,2,1,0:T(8,128)S(1)}, f32[1,4,4,256,256]{4,3,2,1,0:T(8,128)}, u32[]{:S(2)}) copy-start(f32[1,4,4,256,256]{4,3,2,1,0:T(8,128)} %param.4) | copy-start | bytes 12582916
  4.6 8.7 %copy-start = (f32[2056,256]{1,0:T(8,128)}, f32[2056,256]{1,0:T(8,128)S(1)}, u32[]{:S(2)}) copy-start(f32[2056,256]{1,0:T(8,128)S(1)} %pad_maximum_fusion.refs_0_.refs_1_.refs_2_.refs_8_) | copy-start | bytes 6316036
  4.6 49.1 %collective-permute-start.3 = (f32[2056,256]{1,0:T(8,128)S(1)}, f32[2056,256]{1,0:T(8,128)S(1)}, u32[]{:S(2)}, u32[]{:S(2)}) collective-permute-start(f32[2056,256]{1,0:T(8,128)S(1)} %pad_maximum_fusion.refs_0_.refs_1_.refs_2_.refs_8_), channel_id=1, source_target_pairs={{0,16},{8,24},{16,0},{24,8},{1,17},{9,25},{17,1},{25,9},{2,18},{10... | collective-permute-start | bytes 6316040 | tf_op jit(solution)/shard_map/ppermute | solution.py:523
  7.2 48.0 %collective-permute-start.2 = (f32[2056,256]{1,0:T(8,128)S(1)}, f32[2056,256]{1,0:T(8,128)}, u32[]{:S(2)}, u32[]{:S(2)}) collective-permute-start(f32[2056,256]{1,0:T(8,128)S(1)} %pad_maximum_fusion.refs_0_.refs_1_.refs_2_.refs_8_), channel_id=1, source_target_pairs={{0,1},{1,0},{2,3},{3,2},{4,5},{5,4},{6,7},{7,6},{8,9},{9,8},{10,11... | collective-permute-start | bytes 6316040 | tf_op jit(solution)/shard_map/ppermute | solution.py:523
  8.7 46.6 %collective-permute-start.1 = (f32[2056,256]{1,0:T(8,128)S(1)}, f32[2056,256]{1,0:T(8,128)S(1)}, u32[]{:S(2)}, u32[]{:S(2)}) collective-permute-start(f32[2056,256]{1,0:T(8,128)S(1)} %pad_maximum_fusion.refs_0_.refs_1_.refs_2_.refs_8_), channel_id=1, source_target_pairs={{0,8},{1,9},{2,4},{3,5},{4,2},{5,3},{6,14},{7,15},{8,0},{9,1},{10,... | collective-permute-start | bytes 6316040 | tf_op jit(solution)/shard_map/ppermute | solution.py:523
  8.7 48.9 %collective-permute-start = (f32[2056,256]{1,0:T(8,128)S(1)}, f32[2056,256]{1,0:T(8,128)}, u32[]{:S(2)}, u32[]{:S(2)}) collective-permute-start(f32[2056,256]{1,0:T(8,128)S(1)} %pad_maximum_fusion.refs_0_.refs_1_.refs_2_.refs_8_), channel_id=1, source_target_pairs={{0,2},{1,3},{2,0},{3,1},{4,6},{5,7},{6,4},{7,5},{8,10},{9,11},{10,... | collective-permute-start | bytes 6316040 | tf_op jit(solution)/shard_map/ppermute | solution.py:523
  53.7 15.2 %copy-start.2 = (f32[2056,256]{1,0:T(8,128)}, f32[2056,256]{1,0:T(8,128)S(1)}, u32[]{:S(2)}) copy-start(f32[2056,256]{1,0:T(8,128)S(1)} %collective-permute-done.3.refs_0_.refs_1_.refs_5_.refs_2_) | copy-start | bytes 6316036
  55.2 13.7 %copy-start.4 = (f32[2056,256]{1,0:T(8,128)}, f32[2056,256]{1,0:T(8,128)S(1)}, u32[]{:S(2)}) copy-start(f32[2056,256]{1,0:T(8,128)S(1)} %collective-permute-done.1.refs_10_.refs_2_) | copy-start | bytes 6316036
  57.6 179.8 %collective-permute-start.7 = (f32[2056,256]{1,0:T(8,128)S(1)}, f32[2056,256]{1,0:T(8,128)}, u32[]{:S(2)}, u32[]{:S(2)}) collective-permute-start(f32[2056,256]{1,0:T(8,128)S(1)} %collective-permute-done.1.refs_10_.refs_2_), channel_id=1, source_target_pairs={{0,2},{1,3},{2,0},{3,1},{4,6},{5,7},{6,4},{7,5},{8,10},{9,11},{10,... | collective-permute-start | bytes 6316040 | tf_op jit(solution)/shard_map/ppermute | solution.py:523
  59.3 178.0 %collective-permute-start.8 = (f32[2056,256]{1,0:T(8,128)}, f32[2056,256]{1,0:T(8,128)}, u32[]{:S(2)}, u32[]{:S(2)}) collective-permute-start(f32[2056,256]{1,0:T(8,128)} %collective-permute-done.refs_9_.refs_1_), channel_id=1, source_target_pairs={{0,8},{1,9},{2,4},{3,5},{4,2},{5,3},{6,14},{7,15},{8,0},{9,1},{10,... | collective-permute-start | bytes 6316040 | tf_op jit(solution)/shard_map/ppermute | solution.py:523
  59.3 178.0 %collective-permute-start.9 = (f32[2056,256]{1,0:T(8,128)}, f32[2056,256]{1,0:T(8,128)}, u32[]{:S(2)}, u32[]{:S(2)}) collective-permute-start(f32[2056,256]{1,0:T(8,128)} %collective-permute-done.2.refs_0_.refs_1_), channel_id=1, source_target_pairs={{0,8},{8,0},{16,24},{24,16},{1,9},{9,1},{17,25},{25,17},{2,10},{10... | collective-permute-start | bytes 6316040 | tf_op jit(solution)/shard_map/ppermute | solution.py:526
  59.8 47.7 %collective-permute-start.5 = (f32[2048,256]{1,0:T(8,128)}, f32[2048,256]{1,0:T(8,128)S(1)}, u32[]{:S(2)}, u32[]{:S(2)}) collective-permute-start(f32[2048,256]{1,0:T(8,128)} %bitcast.25), channel_id=1, source_target_pairs={{0,16},{8,24},{16,0},{24,8},{1,17},{9,25},{17,1},{25,9},{2,18},{10... | collective-permute-start | bytes 6291464 | tf_op jit(solution)/shard_map/ppermute | solution.py:523
  60.4 47.6 %collective-permute-start.4 = (f32[2048,256]{1,0:T(8,128)}, f32[2048,256]{1,0:T(8,128)}, u32[]{:S(2)}, u32[]{:S(2)}) collective-permute-start(f32[2048,256]{1,0:T(8,128)} %bitcast.26), channel_id=1, source_target_pairs={{0,1},{1,0},{2,3},{3,2},{4,5},{5,4},{6,7},{7,6},{8,9},{9,8},{10,11... | collective-permute-start | bytes 6291464 | tf_op jit(solution)/shard_map/ppermute | solution.py:523
  63.6 229.8 %copy-start.11 = (f32[4,4,64,256]{3,2,1,0:T(8,128)}, f32[4,4,64,256]{3,2,1,0:T(8,128)S(1)}, u32[]{:S(2)}) copy-start(f32[4,4,64,256]{3,2,1,0:T(8,128)S(1)} %get-tuple-element.125) | copy-start | bytes 3145732
  107.6 129.9 %copy-start.3 = (f32[2056,256]{1,0:T(8,128)S(1)}, f32[2056,256]{1,0:T(8,128)}, u32[]{:S(2)}) copy-start(f32[2056,256]{1,0:T(8,128)} %copy-done.2) | copy-start | bytes 6316036
  237.4 13.7 %collective-permute-start.10 = (f32[4104,256]{1,0:T(8,128)}, f32[4104,256]{1,0:T(8,128)S(1)}, u32[]{:S(2)}, u32[]{:S(2)}) collective-permute-start(f32[4104,256]{1,0:T(8,128)} %join.1), channel_id=1, source_target_pairs={{0,8},{8,0},{16,24},{24,16},{1,9},{9,1},{17,25},{25,17},{2,10},{10... | collective-permute-start | bytes 12607496 | tf_op jit(solution)/shard_map/ppermute | solution.py:526
  237.5 20.4 %collective-permute-start.11 = (f32[2056,256]{1,0:T(8,128)S(1)}, f32[2056,256]{1,0:T(8,128)}, u32[]{:S(2)}, u32[]{:S(2)}) collective-permute-start(f32[2056,256]{1,0:T(8,128)S(1)} %copy-done.3), channel_id=1, source_target_pairs={{0,8},{8,0},{16,24},{24,16},{1,9},{9,1},{17,25},{25,17},{2,10},{10... | collective-permute-start | bytes 6316040 | tf_op jit(solution)/shard_map/ppermute | solution.py:526
  238.0 50.3 %collective-permute-start.12 = (f32[2056,256]{1,0:T(8,128)}, f32[2056,256]{1,0:T(8,128)}, u32[]{:S(2)}, u32[]{:S(2)}) collective-permute-start(f32[2056,256]{1,0:T(8,128)} %collective-permute-done.2.refs_0_.refs_1_), channel_id=1, source_target_pairs={{0,16},{8,24},{16,0},{24,8},{1,17},{9,25},{17,1},{25,9},{2,18},{10... | collective-permute-start | bytes 6316040 | tf_op jit(solution)/shard_map/ppermute | solution.py:523
  238.5 49.8 %collective-permute-start.13 = (f32[2056,256]{1,0:T(8,128)}, f32[2056,256]{1,0:T(8,128)}, u32[]{:S(2)}, u32[]{:S(2)}) collective-permute-start(f32[2056,256]{1,0:T(8,128)} %collective-permute-done.8.refs_12_.refs_4_), channel_id=1, source_target_pairs={{0,2},{1,3},{2,0},{3,1},{4,6},{5,7},{6,4},{7,5},{8,10},{9,11},{10,... | collective-permute-start | bytes 6316040 | tf_op jit(solution)/shard_map/ppermute | solution.py:523
  240.9 47.4 %collective-permute-start.14 = (f32[2048,256]{1,0:T(8,128)}, f32[2048,256]{1,0:T(8,128)}, u32[]{:S(2)}, u32[]{:S(2)}) collective-permute-start(f32[2048,256]{1,0:T(8,128)} %copy-done.7), channel_id=1, source_target_pairs={{0,1},{1,0},{2,3},{3,2},{4,5},{5,4},{6,7},{7,6},{8,9},{9,8},{10,11... | collective-permute-start | bytes 6291464 | tf_op jit(solution)/shard_map/ppermute | solution.py:523
  288.3 4.4 collective-permute-start.15
  292.7 8.0 %copy-start.5 = (f32[2056,256]{1,0:T(8,128)}, f32[2056,256]{1,0:T(8,128)S(1)}, u32[]{:S(2)}) copy-start(f32[2056,256]{1,0:T(8,128)S(1)} %collective-permute-done.15.refs_6_.refs_0_.refs_1_) | copy-start | bytes 6316036
  292.7 15.9 %collective-permute-start.16 = (f32[2048,256]{1,0:T(8,128)}, f32[2048,256]{1,0:T(8,128)}, u32[]{:S(2)}, u32[]{:S(2)}) collective-permute-start(f32[2048,256]{1,0:T(8,128)} %collective-permute-done.14.refs_2_), channel_id=1, source_target_pairs={{0,8},{8,0},{16,24},{24,16},{1,9},{9,1},{17,25},{25,17},{2,10},{10... | collective-permute-start | bytes 6291464 | tf_op jit(solution)/shard_map/ppermute | solution.py:526
  292.8 40.1 %collective-permute-start.18 = (f32[1024,256]{1,0:T(8,128)}, f32[1024,256]{1,0:T(8,128)}, u32[]{:S(2)}, u32[]{:S(2)}) collective-permute-start(f32[1024,256]{1,0:T(8,128)} %bitcast.9.refs_0_), channel_id=1, source_target_pairs={{0,8},{1,9},{2,4},{3,5},{4,2},{5,3},{6,14},{7,15},{8,0},{9,1},{10,... | collective-permute-start | bytes 3145736 | tf_op jit(solution)/shard_map/ppermute | solution.py:523
  293.2 39.8 %collective-permute-start.17 = (f32[1024,256]{1,0:T(8,128)}, f32[1024,256]{1,0:T(8,128)}, u32[]{:S(2)}, u32[]{:S(2)}) collective-permute-start(f32[1024,256]{1,0:T(8,128)} %bitcast.9.refs_0_), channel_id=1, source_target_pairs={{0,2},{1,3},{2,0},{3,1},{4,6},{5,7},{6,4},{7,5},{8,10},{9,11},{10,... | collective-permute-start | bytes 3145736 | tf_op jit(solution)/shard_map/ppermute | solution.py:523
  293.3 39.7 %collective-permute-start.20 = (f32[1024,256]{1,0:T(8,128)S(1)}, f32[1024,256]{1,0:T(8,128)}, u32[]{:S(2)}, u32[]{:S(2)}) collective-permute-start(f32[1024,256]{1,0:T(8,128)S(1)} %bitcast.29), channel_id=1, source_target_pairs={{0,8},{1,9},{2,4},{3,5},{4,2},{5,3},{6,14},{7,15},{8,0},{9,1},{10,... | collective-permute-start | bytes 3145736 | tf_op jit(solution)/shard_map/ppermute | solution.py:523
  293.4 47.8 %collective-permute-start.19 = (f32[1024,256]{1,0:T(8,128)S(1)}, f32[1024,256]{1,0:T(8,128)}, u32[]{:S(2)}, u32[]{:S(2)}) collective-permute-start(f32[1024,256]{1,0:T(8,128)S(1)} %bitcast.30), channel_id=1, source_target_pairs={{0,2},{1,3},{2,0},{3,1},{4,6},{5,7},{6,4},{7,5},{8,10},{9,11},{10,... | collective-permute-start | bytes 3145736 | tf_op jit(solution)/shard_map/ppermute | solution.py:523
  341.2 24.6 %collective-permute-start.21 = (f32[4,4,64,256]{3,2,1,0:T(8,128)}, f32[4,4,64,256]{3,2,1,0:T(8,128)S(1)}, u32[]{:S(2)}, u32[]{:S(2)}) collective-permute-start(f32[4,4,64,256]{3,2,1,0:T(8,128)} %get-tuple-element.101), channel_id=1, source_target_pairs={{0,1},{1,0},{2,3},{3,2},{4,5},{5,4},{6,7},{7,6},{8,9},{9,8},{10,11... | collective-permute-start | bytes 3145736 | tf_op jit(solution)/shard_map/ppermute | solution.py:523
  341.7 24.3 %collective-permute-start.23 = (f32[1024,256]{1,0:T(8,128)}, f32[1024,256]{1,0:T(8,128)S(1)}, u32[]{:S(2)}, u32[]{:S(2)}) collective-permute-start(f32[1024,256]{1,0:T(8,128)} %collective-permute-done.18.refs_2_), channel_id=1, source_target_pairs={{0,2},{1,3},{2,0},{3,1},{4,6},{5,7},{6,4},{7,5},{8,10},{9,11},{10,... | collective-permute-start | bytes 3145736 | tf_op jit(solution)/shard_map/ppermute | solution.py:523
  342.0 24.0 %collective-permute-start.24 = (f32[1024,256]{1,0:T(8,128)}, f32[1024,256]{1,0:T(8,128)S(1)}, u32[]{:S(2)}, u32[]{:S(2)}) collective-permute-start(f32[1024,256]{1,0:T(8,128)} %collective-permute-done.17.refs_1_), channel_id=1, source_target_pairs={{0,8},{1,9},{2,4},{3,5},{4,2},{5,3},{6,14},{7,15},{8,0},{9,1},{10,... | collective-permute-start | bytes 3145736 | tf_op jit(solution)/shard_map/ppermute | solution.py:523
  365.8 3.5 copy-start.26
  366.0 7.7 %copy-start.24 = (f32[1024,256]{1,0:T(8,128)}, f32[1024,256]{1,0:T(8,128)S(1)}, u32[]{:S(2)}) copy-start(f32[1024,256]{1,0:T(8,128)S(1)} %collective-permute-done.23.refs_3_) | copy-start | bytes 3145732
  366.0 7.7 %copy-start.22 = (f32[1024,256]{1,0:T(8,128)}, f32[1024,256]{1,0:T(8,128)S(1)}, u32[]{:S(2)}) copy-start(f32[1024,256]{1,0:T(8,128)S(1)} %collective-permute-done.24.refs_4_) | copy-start | bytes 3145732
  366.0 23.5 %collective-permute-start.27 = (f32[4,4,64,256]{3,2,1,0:T(8,128)}, f32[4,4,64,256]{3,2,1,0:T(8,128)S(1)}, u32[]{:S(2)}, u32[]{:S(2)}) collective-permute-start(f32[4,4,64,256]{3,2,1,0:T(8,128)} %get-tuple-element.107), channel_id=1, source_target_pairs={{0,1},{1,0},{2,3},{3,2},{4,5},{5,4},{6,7},{7,6},{8,9},{9,8},{10,11... | collective-permute-start | bytes 3145736 | tf_op jit(solution)/shard_map/ppermute | solution.py:523
  367.6 26.1 %collective-permute-start.29 = (f32[1024,256]{1,0:T(8,128)S(1)}, f32[1024,256]{1,0:T(8,128)S(1)}, u32[]{:S(2)}, u32[]{:S(2)}) collective-permute-start(f32[1024,256]{1,0:T(8,128)S(1)} %collective-permute-done.24.refs_4_), channel_id=1, source_target_pairs={{0,2},{1,3},{2,0},{3,1},{4,6},{5,7},{6,4},{7,5},{8,10},{9,11},{10,... | collective-permute-start | bytes 3145736 | tf_op jit(solution)/shard_map/ppermute | solution.py:523
  371.9 41.0 %collective-permute-start.25 = (f32[4,264,256]{2,1,0:T(8,128)}, f32[4,264,256]{2,1,0:T(8,128)S(1)}, u32[]{:S(2)}, u32[]{:S(2)}) collective-permute-start(f32[4,264,256]{2,1,0:T(8,128)} %inflate.4.refs_4_), channel_id=1, source_target_pairs={{0,16},{8,24},{16,0},{24,8},{1,17},{9,25},{17,1},{25,9},{2,18},{10... | collective-permute-start | bytes 3244040 | tf_op jit(solution)/shard_map/ppermute | solution.py:523
  373.4 39.5 %collective-permute-start.30 = (f32[1024,256]{1,0:T(8,128)}, f32[1024,256]{1,0:T(8,128)S(1)}, u32[]{:S(2)}, u32[]{:S(2)}) collective-permute-start(f32[1024,256]{1,0:T(8,128)} %collective-permute-done.20.refs_2_), channel_id=1, source_target_pairs={{0,2},{1,3},{2,0},{3,1},{4,6},{5,7},{6,4},{7,5},{8,10},{9,11},{10,... | collective-permute-start | bytes 3145736 | tf_op jit(solution)/shard_map/ppermute | solution.py:523
  373.8 39.2 %collective-permute-start.31 = (f32[1024,256]{1,0:T(8,128)}, f32[1024,256]{1,0:T(8,128)S(1)}, u32[]{:S(2)}, u32[]{:S(2)}) collective-permute-start(f32[1024,256]{1,0:T(8,128)} %collective-permute-done.19.refs_1_), channel_id=1, source_target_pairs={{0,8},{1,9},{2,4},{3,5},{4,2},{5,3},{6,14},{7,15},{8,0},{9,1},{10,... | collective-permute-start | bytes 3145736 | tf_op jit(solution)/shard_map/ppermute | solution.py:523
  394.6 18.3 %copy-start.9 = (f32[4,264,256]{2,1,0:T(8,128)S(1)}, f32[4,264,256]{2,1,0:T(8,128)}, u32[]{:S(2)}) copy-start(f32[4,264,256]{2,1,0:T(8,128)} %inflate.5.refs_8_) | copy-start | bytes 3244036
  412.9 3.5 copy-start.23
  413.0 3.5 copy-start.21
  413.0 38.5 %copy-start.12 = (f32[4,264,256]{2,1,0:T(8,128)}, f32[4,264,256]{2,1,0:T(8,128)S(1)}, u32[]{:S(2)}) copy-start(f32[4,264,256]{2,1,0:T(8,128)S(1)} %collective-permute-done.25.refs_6_) | copy-start | bytes 3244036
  413.0 27.1 %collective-permute-start.32 = (f32[4,264,256]{2,1,0:T(8,128)S(1)}, f32[4,264,256]{2,1,0:T(8,128)S(1)}, u32[]{:S(2)}, u32[]{:S(2)}) collective-permute-start(f32[4,264,256]{2,1,0:T(8,128)S(1)} %copy-done.9), channel_id=1, source_target_pairs={{0,16},{8,24},{16,0},{24,8},{1,17},{9,25},{17,1},{25,9},{2,18},{10... | collective-permute-start | bytes 3244040 | tf_op jit(solution)/shard_map/ppermute | solution.py:523
  414.5 21.9 %collective-permute-start.34 = (f32[4,4,64,256]{3,2,1,0:T(8,128)}, f32[4,4,64,256]{3,2,1,0:T(8,128)S(1)}, u32[]{:S(2)}, u32[]{:S(2)}) collective-permute-start(f32[4,4,64,256]{3,2,1,0:T(8,128)} %get-tuple-element.116), channel_id=1, source_target_pairs={{0,1},{1,0},{2,3},{3,2},{4,5},{5,4},{6,7},{7,6},{8,9},{9,8},{10,11... | collective-permute-start | bytes 3145736 | tf_op jit(solution)/shard_map/ppermute | solution.py:630
  415.1 25.5 %collective-permute-start.38 = (f32[1024,256]{1,0:T(8,128)S(1)}, f32[1024,256]{1,0:T(8,128)S(1)}, u32[]{:S(2)}, u32[]{:S(2)}) collective-permute-start(f32[1024,256]{1,0:T(8,128)S(1)} %collective-permute-done.31.refs_4_), channel_id=1, source_target_pairs={{0,2},{1,3},{2,0},{3,1},{4,6},{5,7},{6,4},{7,5},{8,10},{9,11},{10,... | collective-permute-start | bytes 3145736 | tf_op jit(solution)/shard_map/ppermute | solution.py:523
  440.0 35.8 %copy-start.13 = (f32[4,264,256]{2,1,0:T(8,128)}, f32[4,264,256]{2,1,0:T(8,128)S(1)}, u32[]{:S(2)}) copy-start(f32[4,264,256]{2,1,0:T(8,128)S(1)} %collective-permute-done.32.refs_10_) | copy-start | bytes 3244036
  440.0 34.3 %collective-permute-start.36 = (f32[4,264,256]{2,1,0:T(8,128)}, f32[4,264,256]{2,1,0:T(8,128)S(1)}, u32[]{:S(2)}, u32[]{:S(2)}) collective-permute-start(f32[4,264,256]{2,1,0:T(8,128)} %inflate.6.refs_12_), channel_id=1, source_target_pairs={{0,16},{8,24},{16,0},{24,8},{1,17},{9,25},{17,1},{25,9},{2,18},{10... | collective-permute-start | bytes 3244040 | tf_op jit(solution)/shard_map/ppermute | solution.py:636
  441.6 9.3 %copy-start.8 = (f32[4,264,256]{2,1,0:T(8,128)S(1)}, f32[4,264,256]{2,1,0:T(8,128)}, u32[]{:S(2)}) copy-start(f32[4,264,256]{2,1,0:T(8,128)} %inflate.4.refs_4_) | copy-start | bytes 3244036
  450.8 25.0 %copy-start.10 = (f32[4,264,256]{2,1,0:T(8,128)S(1)}, f32[4,264,256]{2,1,0:T(8,128)}, u32[]{:S(2)}) copy-start(f32[4,264,256]{2,1,0:T(8,128)} %inflate.6.refs_12_) | copy-start | bytes 3244036
  450.8 21.0 %collective-permute-start.39 = (f32[4,4,64,256]{3,2,1,0:T(8,128)}, f32[4,4,64,256]{3,2,1,0:T(8,128)}, u32[]{:S(2)}, u32[]{:S(2)}) collective-permute-start(f32[4,4,64,256]{3,2,1,0:T(8,128)} %get-tuple-element.123), channel_id=1, source_target_pairs={{0,1},{1,0},{2,3},{3,2},{4,5},{5,4},{6,7},{7,6},{8,9},{9,8},{10,11... | collective-permute-start | bytes 3145736 | tf_op jit(solution)/shard_map/ppermute | solution.py:630
  450.9 24.9 %collective-permute-start.22 = (f32[4,264,256]{2,1,0:T(8,128)S(1)}, f32[4,264,256]{2,1,0:T(8,128)S(1)}, u32[]{:S(2)}, u32[]{:S(2)}) collective-permute-start(f32[4,264,256]{2,1,0:T(8,128)S(1)} %copy-done.8), channel_id=1, source_target_pairs={{0,8},{8,0},{16,24},{24,16},{1,9},{9,1},{17,25},{25,17},{2,10},{10... | collective-permute-start | bytes 3244040 | tf_op jit(solution)/shard_map/ppermute | solution.py:619
  451.0 25.4 %collective-permute-start.28 = (f32[4,264,256]{2,1,0:T(8,128)S(1)}, f32[4,264,256]{2,1,0:T(8,128)}, u32[]{:S(2)}, u32[]{:S(2)}) collective-permute-start(f32[4,264,256]{2,1,0:T(8,128)S(1)} %copy-done.9), channel_id=1, source_target_pairs={{0,8},{8,0},{16,24},{24,16},{1,9},{9,1},{17,25},{25,17},{2,10},{10... | collective-permute-start | bytes 3244040 | tf_op jit(solution)/shard_map/ppermute | solution.py:619
  451.5 25.0 %collective-permute-start.26 = (f32[4,264,256]{2,1,0:T(8,128)S(1)}, f32[4,264,256]{2,1,0:T(8,128)}, u32[]{:S(2)}, u32[]{:S(2)}) collective-permute-start(f32[4,264,256]{2,1,0:T(8,128)S(1)} %collective-permute-done.25.refs_6_), channel_id=1, source_target_pairs={{0,8},{8,0},{16,24},{24,16},{1,9},{9,1},{17,25},{25,17},{2,10},{10... | collective-permute-start | bytes 3244040 | tf_op jit(solution)/shard_map/ppermute | solution.py:619
  474.4 23.4 %copy-start.14 = (f32[4,264,256]{2,1,0:T(8,128)}, f32[4,264,256]{2,1,0:T(8,128)S(1)}, u32[]{:S(2)}) copy-start(f32[4,264,256]{2,1,0:T(8,128)S(1)} %collective-permute-done.36.refs_14_) | copy-start | bytes 3244036
  474.4 20.6 %collective-permute-start.41 = (f32[4,264,256]{2,1,0:T(8,128)}, f32[4,264,256]{2,1,0:T(8,128)S(1)}, u32[]{:S(2)}, u32[]{:S(2)}) collective-permute-start(f32[4,264,256]{2,1,0:T(8,128)} %inflate.7.refs_16_), channel_id=1, source_target_pairs={{0,16},{8,24},{16,0},{24,8},{1,17},{9,25},{17,1},{25,9},{2,18},{10... | collective-permute-start | bytes 3244040 | tf_op jit(solution)/shard_map/ppermute | solution.py:636
  475.8 19.2 %collective-permute-start.35 = (f32[4,264,256]{2,1,0:T(8,128)S(1)}, f32[4,264,256]{2,1,0:T(8,128)S(1)}, u32[]{:S(2)}, u32[]{:S(2)}) collective-permute-start(f32[4,264,256]{2,1,0:T(8,128)S(1)} %copy-done.10), channel_id=1, source_target_pairs={{0,8},{8,0},{16,24},{24,16},{1,9},{9,1},{17,25},{25,17},{2,10},{10... | collective-permute-start | bytes 3244040 | tf_op jit(solution)/shard_map/ppermute | solution.py:637
  475.8 22.0 %copy-start.15 = (f32[4,264,256]{2,1,0:T(8,128)}, f32[4,264,256]{2,1,0:T(8,128)S(1)}, u32[]{:S(2)}) copy-start(f32[4,264,256]{2,1,0:T(8,128)S(1)} %collective-permute-done.22.refs_5_) | copy-start | bytes 3244036
  475.8 19.2 %collective-permute-start.33 = (f32[4,264,256]{2,1,0:T(8,128)S(1)}, f32[4,264,256]{2,1,0:T(8,128)S(1)}, u32[]{:S(2)}, u32[]{:S(2)}) collective-permute-start(f32[4,264,256]{2,1,0:T(8,128)S(1)} %collective-permute-done.32.refs_10_), channel_id=1, source_target_pairs={{0,8},{8,0},{16,24},{24,16},{1,9},{9,1},{17,25},{25,17},{2,10},{10... | collective-permute-start | bytes 3244040 | tf_op jit(solution)/shard_map/ppermute | solution.py:619
  476.4 18.6 %collective-permute-start.40 = (f32[4,264,256]{2,1,0:T(8,128)}, f32[4,264,256]{2,1,0:T(8,128)S(1)}, u32[]{:S(2)}, u32[]{:S(2)}) collective-permute-start(f32[4,264,256]{2,1,0:T(8,128)} %inflate.7.refs_16_), channel_id=1, source_target_pairs={{0,8},{8,0},{16,24},{24,16},{1,9},{9,1},{17,25},{25,17},{2,10},{10... | collective-permute-start | bytes 3244040 | tf_op jit(solution)/shard_map/ppermute | solution.py:637
  476.5 18.6 %collective-permute-start.37 = (f32[4,264,256]{2,1,0:T(8,128)S(1)}, f32[4,264,256]{2,1,0:T(8,128)S(1)}, u32[]{:S(2)}, u32[]{:S(2)}) collective-permute-start(f32[4,264,256]{2,1,0:T(8,128)S(1)} %collective-permute-done.36.refs_14_), channel_id=1, source_target_pairs={{0,8},{8,0},{16,24},{24,16},{1,9},{9,1},{17,25},{25,17},{2,10},{10... | collective-permute-start | bytes 3244040 | tf_op jit(solution)/shard_map/ppermute | solution.py:637
  495.0 2.8 collective-permute-start.42
  495.0 2.8 copy-start.18
  495.0 2.8 copy-start.19
  (10 other events, 11.7 us)
